TPU v7x, 32 devices: a whole 2x2x4 slice. The times are simulated.
32 devices in a mesh: seq: 16 (over z, y, core), head: 2 (over x).
Axes of the slice: x: 2, y: 2, z: 4, core: 2. Of those that a mesh axis runs over, the one named last changes fastest.
Arguments:
- queries: bfloat16 [4096, 32, 128], P('seq', 'head'), may hold values from -16 to 16
- keys: bfloat16 [4096, 32, 128], P('seq', 'head'), may hold values from -40 to 40
- values: bfloat16 [4096, 32, 128], P('seq', 'head'), may hold values from -6 to 6
- cluster_ids: int32 [4096, 32], P('seq', 'head'), may hold values from 0 to 511, as said below
- out_weight: bfloat16 [4096, 4096], P('seq', 'head'), may hold values from -0.09375 to 0.09375
Outputs:
- mixed: bfloat16 [4096, 4096], P('seq', 'head')
Inputs may be any that keep to these rules, and one draw needn't show every extreme that they name: `cluster_ids`: in each head h, the ids j with j % 16 equal to one residue, drawn from the seed for that head, are never used.
All inputs are finite; a program needn't handle non-finite values.
Results may differ from a plain program's by a relative error of at most 0.008.
The roundings to bfloat16 on the way count: a program that leaves them out, or rounds other values in their place, can miss the bound.
Values may be sent and summed in bfloat16 or wider, within the bound.
No kernel may reach another device: no remote copies, remote signals or barrier semaphores. Data moves between devices by JAX's collectives and lax.ppermute only.
A program may use at most 320 MiB of HBM per device.

v0:
```python
import math

import jax
import jax.numpy as jnp
from jax import lax
from jax.sharding import PartitionSpec as P

C = 512


def on_device(queries, keys, values, cluster_ids, out_weight):
    tok_rows, head_count, e_width = queries.shape
    score_scale = 1.0 / math.sqrt(e_width)
    labels = lax.broadcasted_iota(jnp.int32, (head_count, tok_rows, C), 2)
    onehot = (cluster_ids.T[:, :, None] == labels).astype(jnp.bfloat16)
    totals = jnp.einsum("htc,the->hce", onehot, queries, preferred_element_type=jnp.float32)
    counts = jnp.sum(onehot, axis=1, dtype=jnp.float32)
    all_totals, all_counts = lax.psum((totals, counts), "seq")
    centroid = (all_totals / jnp.maximum(all_counts, 1.0)[:, :, None]).astype(jnp.bfloat16)
    scores = (
        jnp.einsum("hce,the->hct", centroid, keys, preferred_element_type=jnp.float32) * score_scale
    )
    local_max = jnp.max(scores, axis=2)
    weights = jnp.exp(scores - local_max[:, :, None])
    local_total = jnp.sum(weights, axis=2)
    local_out = jnp.einsum(
        "hct,the->hce", weights.astype(jnp.bfloat16), values, preferred_element_type=jnp.float32
    )
    global_max = lax.pmax(local_max, "seq")
    factor = jnp.exp(local_max - global_max)
    share_out, share_total = (
        lax.psum_scatter(local_out * factor[:, :, None], "seq", scatter_dimension=1, tiled=True),
        lax.psum_scatter(local_total * factor, "seq", scatter_dimension=1, tiled=True),
    )
    share_attended = (share_out / share_total[:, :, None]).astype(jnp.bfloat16)
    attended = lax.all_gather(share_attended, "seq", axis=1, tiled=True)
    expanded = jnp.einsum(
        "htc,hce->the", onehot, attended, preferred_element_type=jnp.float32
    ).astype(jnp.bfloat16)
    flat = expanded.reshape(tok_rows, head_count * e_width)
    features = lax.all_gather(flat, "head", axis=1, tiled=True)
    mixed = jnp.dot(
        features,
        lax.all_gather(out_weight, "seq", axis=0, tiled=True),
        preferred_element_type=jnp.float32,
    )
    return mixed.astype(jnp.bfloat16)


def solution(mesh):
    placed = (
        P("seq", "head", None),
        P("seq", "head", None),
        P("seq", "head", None),
        P("seq", "head"),
        P("seq", "head"),
    )
    return jax.shard_map(
        on_device, mesh=mesh, in_specs=placed, out_specs=P("seq", "head"), check_vma=False
    )
```

profile of v0, /device:TPU:0, one launch (start us, length us, event | category | flops | bytes accessed | tf_op | source)
XLA Modules:
  0.0 553.4 jit_solution(10244484791630498231)
XLA Ops:
  6.5 0.0 copy-start
  6.5 0.0 all-reduce.2.cloned.1.call-start
  6.5 0.0 copy-start.2
  6.5 5.6 %fusion.2 = f32[16,512,128]{2,1,0:T(8,128)} fusion(s32[16,256]{1,0:T(8,128)} %bitcast.11, bf16[256,16,128]{2,1,0:T(8,128)(2,1)} %param.5), kind=kOutput, calls=%fused_computation.5 | convolution fusion | flops 538968064 | bytes 5259264 | tf_op jit(solution)/shard_map/htc,the->hce/dot_general | solution.py:16
  12.1 0.0 all-reduce.2.cloned.1.call-update
  12.2 0.0 reduce-scatter.7.cloned.1.call-start
  12.2 0.0 copy-done.2
  12.2 1.3 convert_reduce_fusion
  13.5 64.3 %psum.15 = f32[16,512]{1,0:T(8,128)S(1)} all-reduce(f32[16,512]{1,0:T(8,128)S(1)} %convert_reduce_fusion), channel_id=1, replica_groups=mesh['seq'=16,'head'=2] {'seq'}, use_global_device_ids=true, to_apply=%region_2.0 | all-reduce | flops 8192 | bytes 65536 | tf_op jit(solution)/shard_map/psum | solution.py:18
  77.8 48.9 %all-reduce.2.cloned.1.call-done = f32[16,512,128]{2,1,0:T(8,128)} async-done(((f32[16,512,128]{2,1,0:T(8,128)}), f32[16,512,128]{2,1,0:T(8,128)}) %all-reduce.2.cloned.1.call-update) | async-done | bytes 4194320 | tf_op jit(solution)/shard_map/psum | solution.py:18
  126.7 0.0 copy-done
  126.7 5.7 %multiply_reduce_fusion = (f32[16,512]{1,0:T(8,128)S(1)}, f32[16,512,256]{1,2,0:T(8,128)}) fusion(bf16[256,16,128]{2,1,0:T(8,128)(2,1)S(1)} %copy-done, f32[16,512,128]{2,1,0:T(8,128)} %all-reduce.2.cloned.1.call-done, f32[16,512]{1,0:T(8,128)S(1)} %broadcast_maximum_fusion), kind=kOutput, calls=%fused_computation.6 | convolution fusion | flops 543154176 | bytes 13697024 | tf_op jit(solution)/shard_map/hce,the->hct/dot_general | solution.py:21
  132.3 59.3 %pmax.7 = f32[16,512]{1,0:T(8,128)S(1)} all-reduce(f32[16,512]{1,0:T(8,128)S(1)} %get-tuple-element.7), channel_id=1, replica_groups=mesh['seq'=16,'head'=2] {'seq'}, use_global_device_ids=true, to_apply=%region_4.0 | all-reduce | flops 8192 | bytes 65536 | tf_op jit(solution)/shard_map/pmax | solution.py:29
  191.6 0.0 copy-start.1
  191.6 4.9 fusion.3
  196.6 0.8 copy.10
  197.4 0.0 reduce-scatter.7.cloned.1.call-update
  197.4 0.0 reduce-scatter.5.cloned.1.call-start
  197.5 0.0 copy-done.1
  197.5 6.5 %broadcast_multiply_fusion = f32[16,512,128]{2,1,0:T(8,128)} fusion(f32[16,512]{1,0:T(8,128)S(1)} %get-tuple-element.6, f32[16,512,256]{1,2,0:T(8,128)} %get-tuple-element.8, f32[16,512]{1,0:T(8,128)S(1)} %get-tuple-element.7, bf16[256,16,128]{2,1,0:T(8,128)(2,1)S(1)} %copy-done.1), kind=kOutput, calls=%fused_computation.17 | convolution fusion | flops 544210944 | bytes 13697024 | tf_op jit(solution)/shard_map/hct,the->hce/dot_general | solution.py:26
  204.0 0.0 reduce-scatter.5.cloned.1.call-update
  204.0 0.0 all-gather.4.cloned.1.call-start
  204.0 46.1 %reduce-scatter.7.cloned.1.call-done = f32[32,16]{1,0:T(8,128)} async-done(((f32[512,16]{1,0:T(8,128)}), f32[32,16]{1,0:T(8,128)}) %reduce-scatter.7.cloned.1.call-update) | async-done | bytes 2064
  250.1 0.8 copy.11
  250.9 75.3 %reduce-scatter.5.cloned.1.call-done = f32[16,32,128]{2,1,0:T(8,128)} async-done(((f32[16,512,128]{2,1,0:T(8,128)}), f32[16,32,128]{2,1,0:T(8,128)}) %reduce-scatter.5.cloned.1.call-update) | async-done | bytes 262160 | tf_op jit(solution)/shard_map/reduce_scatter | solution.py:32
  326.2 1.7 divide_convert_fusion.2
  328.0 0.0 all-gather.4.cloned.1.call-update
  328.0 0.0 all-gather.6.cloned.1.call-start
  328.0 40.4 %all-gather.4.cloned.1.call-done = bf16[16,512,128]{2,1,0:T(8,128)(2,1)} async-done(((bf16[16,32,128]{2,1,0:T(8,128)(2,1)}), bf16[16,512,128]{2,1,0:T(8,128)(2,1)}) %all-gather.4.cloned.1.call-update) | async-done | bytes 2097168 | tf_op jit(solution)/shard_map/all_gather | solution.py:36
  368.5 5.1 fusion.15
  373.5 0.0 all-gather.6.cloned.1.call-update
  373.6 0.0 all-gather.8.cloned.1.call-start
  373.6 0.5 all-gather.8.cloned.1.call-update
  374.1 31.6 %all-gather.6.cloned.1.call-done = bf16[256,4096]{0,1:T(8,128)(2,1)} async-done(((bf16[256,2048]{0,1:T(8,128)(2,1)}), bf16[256,4096]{0,1:T(8,128)(2,1)}) %all-gather.6.cloned.1.call-update) | async-done | bytes 2097168 | tf_op jit(solution)/shard_map/all_gather | solution.py:41
  405.7 128.9 %all-gather.8.cloned.1.call-done = bf16[4096,2048]{1,0:T(8,128)(2,1)} async-done(((bf16[256,2048]{1,0:T(8,128)(2,1)}), bf16[4096,2048]{1,0:T(8,128)(2,1)}) %all-gather.8.cloned.1.call-update) | async-done | bytes 16777232 | tf_op jit(solution)/shard_map/all_gather | solution.py:44
  534.7 11.9 %convolution_convert_fusion = bf16[256,2048]{1,0:T(8,128)(2,1)} fusion(bf16[256,4096]{0,1:T(8,128)(2,1)} %all-gather.6.cloned.1.call-done, bf16[4096,2048]{1,0:T(8,128)(2,1)} %all-gather.8.cloned.1.call-done), kind=kOutput, calls=%fused_computation.15 | convolution fusion | flops 4295491584 | bytes 19922944 | tf_op jit(solution)/shard_map/dot_general | solution.py:42
  (2 shorter events, 0.0 us)
Async XLA Ops:
  6.5 120.1 %copy-start = (bf16[256,16,128]{2,1,0:T(8,128)(2,1)S(1)}, bf16[256,16,128]{2,1,0:T(8,128)(2,1)}, u32[]{:S(2)}) copy-start(bf16[256,16,128]{2,1,0:T(8,128)(2,1)} %param.6) | copy-start | bytes 3145732
  6.5 120.1 %all-reduce.2.cloned.1.call-start = ((), (), s32[]{:S(2)}) async-start(), calls=%async_computation.2 | async-start | bytes 8388608 | tf_op jit(solution)/shard_map/psum | solution.py:18
  6.5 5.7 %copy-start.2 = (s32[256,16]{0,1:T(8,128)S(1)}, s32[256,16]{0,1:T(8,128)}, u32[]{:S(2)}) copy-start(s32[256,16]{0,1:T(8,128)} %param.8) | copy-start | bytes 49156
  12.2 238.0 %reduce-scatter.7.cloned.1.call-start = ((), (), s32[]{:S(2)}) async-start(), calls=%async_computation.7 | async-start | bytes 278528
  191.6 5.8 %copy-start.1 = (bf16[256,16,128]{2,1,0:T(8,128)(2,1)S(1)}, bf16[256,16,128]{2,1,0:T(8,128)(2,1)}, u32[]{:S(2)}) copy-start(bf16[256,16,128]{2,1,0:T(8,128)(2,1)} %param.7) | copy-start | bytes 3145732
  197.4 128.8 %reduce-scatter.5.cloned.1.call-start = ((), (), s32[]{:S(2)}) async-start(), calls=%async_computation.3 | async-start | bytes 4456448 | tf_op jit(solution)/shard_map/reduce_scatter | solution.py:32
  204.0 164.5 %all-gather.4.cloned.1.call-start = ((), (), s32[]{:S(2)}) async-start(), calls=%async_computation.4 | async-start | bytes 2228224 | tf_op jit(solution)/shard_map/all_gather | solution.py:36
  328.0 77.8 %all-gather.6.cloned.1.call-start = ((), (), s32[]{:S(2)}) async-start(), calls=%async_computation.5 | async-start | bytes 3145728 | tf_op jit(solution)/shard_map/all_gather | solution.py:41
  373.6 161.1 %all-gather.8.cloned.1.call-start = ((), (), s32[]{:S(2)}) async-start(), calls=%async_computation.6 | async-start | bytes 17825792 | tf_op jit(solution)/shard_map/all_gather | solution.py:44
Sparse Core Ops, SparseCore 0:
  12.3 114.3 all-reduce.1
  197.5 52.5 reduce-scatter.6
  254.5 71.7 reduce-scatter.4
  328.2 40.1 all-gather.3
  373.7 32.0 all-gather.5
  407.8 126.8 all-gather.7
where the time goes:
time: 554 us; the launch traced here: 553 us
  waiting for transfers between devices  372 us (67%)
  blocking collectives  124 us (22%)
  matrix products  34.7 us (6%)
  between operations  13.5 us (2%)
  other arithmetic  7.92 us (1%)
    all_gather x1, waiting for transfers between devices, on_device(): lax.all_gather(out_weight, 'seq', axis=0, tiled=True)  129 us
    reduce_scatter x1, waiting for transfers between devices, on_device(): lax.psum_scatter(local_out * factor[:, :, None], 'seq', scatter_dimension...  75.3 us
    psum x1, blocking collectives, on_device(): all_totals, all_counts = lax.psum((totals, counts), 'seq')  64.3 us
    pmax x1, blocking collectives, on_device(): global_max = lax.pmax(local_max, 'seq')  59.3 us
    psum x1, waiting for transfers between devices, on_device(): all_totals, all_counts = lax.psum((totals, counts), 'seq')  48.9 us
    unnamed x7, waiting for transfers between devices  46.7 us
    all_gather x1, waiting for transfers between devices, on_device(): attended = lax.all_gather(share_attended, 'seq', axis=1, tiled=True)  40.4 us
    all_gather x1, waiting for transfers between devices, on_device(): features = lax.all_gather(flat, 'head', axis=1, tiled=True)  31.6 us
  transfers between devices with their start and end apart: 6, of which 6 were waited for; matrix products, arithmetic and copies ran while one was open for 2% of the time, Pallas kernels for 0%

commit v1 on v0

v1 whole, which is shorter than its diff:
```python
import math

import jax
import jax.numpy as jnp
from jax import lax
from jax.sharding import PartitionSpec as P

C = 512


def expand_and_project(ids, attended, weight):
    tok_rows = ids.shape[0]
    heads, _, e_width = attended.shape
    labels = lax.broadcasted_iota(jnp.int32, (heads, tok_rows, C), 2)
    onehot = (ids.T[:, :, None] == labels).astype(jnp.bfloat16)
    features = jnp.einsum("htc,hce->the", onehot, attended, preferred_element_type=jnp.float32).astype(
        jnp.bfloat16
    )
    flat = features.reshape(tok_rows, heads * e_width)
    return jnp.dot(flat, weight, preferred_element_type=jnp.float32).astype(jnp.bfloat16)


def by_reduction(queries, keys, values, cluster_ids, out_weight):
    tok_rows, head_count, e_width = queries.shape
    score_scale = 1.0 / math.sqrt(e_width)
    labels = lax.broadcasted_iota(jnp.int32, (head_count, tok_rows, C), 2)
    onehot = (cluster_ids.T[:, :, None] == labels).astype(jnp.bfloat16)
    totals = jnp.einsum("htc,the->hce", onehot, queries, preferred_element_type=jnp.float32)
    counts = jnp.sum(onehot, axis=1, dtype=jnp.float32)
    all_totals, all_counts = lax.psum((totals, counts), "seq")
    centroid = (all_totals / jnp.maximum(all_counts, 1.0)[:, :, None]).astype(jnp.bfloat16)
    scores = jnp.einsum("hce,the->hct", centroid, keys, preferred_element_type=jnp.float32) * score_scale
    local_max = jnp.max(scores, axis=2)
    weights = jnp.exp(scores - local_max[:, :, None])
    local_total = jnp.sum(weights, axis=2)
    local_out = jnp.einsum(
        "hct,the->hce", weights.astype(jnp.bfloat16), values, preferred_element_type=jnp.float32
    )
    global_max = lax.pmax(local_max, "seq")
    factor = jnp.exp(local_max - global_max)
    share_out = lax.psum_scatter(local_out * factor[:, :, None], "seq", scatter_dimension=1, tiled=True)
    share_total = lax.psum_scatter(local_total * factor, "seq", scatter_dimension=1, tiled=True)
    share_attended = (share_out / share_total[:, :, None]).astype(jnp.bfloat16)
    attended = lax.all_gather(share_attended, "seq", axis=1, tiled=True)
    attended = lax.all_gather(attended, "head", axis=0, tiled=True)
    ids = lax.all_gather(cluster_ids, "head", axis=1, tiled=True)
    weight = lax.all_gather(out_weight, "seq", axis=0, tiled=True)
    return expand_and_project(ids, attended, weight)


def by_head(queries, keys, values, cluster_ids, out_weight):
    tok_rows, head_count, e_width = queries.shape
    n_seq = lax.axis_size("seq")
    per = head_count // n_seq
    score_scale = 1.0 / math.sqrt(e_width)
    weight = lax.all_gather(out_weight, "seq", axis=0, tiled=True)
    ids = lax.all_gather(cluster_ids, "head", axis=1, tiled=True)

    packed = jnp.stack([queries, keys, values]).transpose(2, 0, 1, 3)
    moved = lax.all_to_all(packed, "seq", split_axis=0, concat_axis=2, tiled=True)
    q, k, v = moved[:, 0], moved[:, 1], moved[:, 2]
    own_ids = lax.all_to_all(cluster_ids.T, "seq", split_axis=0, concat_axis=1, tiled=True)

    labels = lax.broadcasted_iota(jnp.int32, (per, C, own_ids.shape[1]), 1)
    onehot = (own_ids[:, None, :] == labels).astype(jnp.bfloat16)
    totals = jnp.einsum("hct,hte->hce", onehot, q, preferred_element_type=jnp.float32)
    counts = jnp.sum(onehot, axis=2, dtype=jnp.float32)
    centroid = (totals / jnp.maximum(counts, 1.0)[:, :, None]).astype(jnp.bfloat16)
    scores = jnp.einsum("hce,hte->hct", centroid, k, preferred_element_type=jnp.float32) * score_scale
    weights = jnp.exp(scores - jnp.max(scores, axis=2)[:, :, None])
    total = jnp.sum(weights, axis=2)
    summed = jnp.einsum("hct,hte->hce", weights.astype(jnp.bfloat16), v, preferred_element_type=jnp.float32)
    own = (summed / total[:, :, None]).astype(jnp.bfloat16)
    attended = lax.all_gather(own, ("head", "seq"), axis=0, tiled=True)
    return expand_and_project(ids, attended, weight)


def on_device(queries, keys, values, cluster_ids, out_weight):
    if queries.shape[1] % lax.axis_size("seq") == 0:
        return by_head(queries, keys, values, cluster_ids, out_weight)
    return by_reduction(queries, keys, values, cluster_ids, out_weight)


def solution(mesh):
    placed = (
        P("seq", "head", None),
        P("seq", "head", None),
        P("seq", "head", None),
        P("seq", "head"),
        P("seq", "head"),
    )
    return jax.shard_map(
        on_device, mesh=mesh, in_specs=placed, out_specs=P("seq", "head"), check_vma=False
    )
```

time: 554 us -> 324 us (0.58)
  waiting for transfers between devices: 372 us -> 249 us
  blocking collectives: 124 us -> 4.6 us
  starting transfers between devices: 0.21 us -> 12.6 us
  matrix products: 34.7 us -> 27.8 us
  local copies, waits for them, and re-layouts: 1.63 us -> 7.74 us
    reduce_scatter x1 -> x0, waiting for transfers between devices: 75.3 us -> none  [on_device(): lax.psum_scatter(local_out * factor[:, :, None], 'seq', scatter_dimension...]
    psum x1 -> x0, blocking collectives: 64.3 us -> none  [on_device(): all_totals, all_counts = lax.psum((totals, counts), 'seq')]
    pmax x1 -> x0, blocking collectives: 59.3 us -> none  [on_device(): global_max = lax.pmax(local_max, 'seq')]
    all_to_all x0 -> x2, waiting for transfers between devices: none -> 59.3 us  [the longest x1 58.4 us: by_head(): lax.all_to_all(packed, 'seq', split_axis=0, concat_axis=2, tiled=True)]
    psum x1 -> x0, waiting for transfers between devices: 48.9 us -> none  [on_device(): all_totals, all_counts = lax.psum((totals, counts), 'seq')]
    unnamed x7 -> x2, waiting for transfers between devices: 46.7 us -> 0.71 us
    all_to_all x0 -> x2, starting transfers between devices: none -> 12.5 us  [the longest x1 7.39 us: by_head(): lax.all_to_all(cluster_ids.T, 'seq', split_axis=0, concat_axis=1, tiled=T...]
    all_gather x3 -> x2, waiting for transfers between devices: 201 us -> 189 us  [the longest x1 122 us: by_head(): weight = lax.all_gather(out_weight, 'seq', axis=0, tiled=True)]
  transfers between devices with their start and end apart: 6 -> 4, of which waited for: 6 -> 4; matrix products, arithmetic and copies ran while one was open for 2% -> 4% of each run, Pallas kernels for 0% -> 0%
where the time goes in v1:
time: 324 us; the launch traced here: 323 us
  waiting for transfers between devices  249 us (77%)
  matrix products  27.8 us (9%)
  between operations  13.5 us (4%)
  starting transfers between devices  12.6 us (4%)
  other arithmetic  7.94 us (2%)
  local copies, waits for them, and re-layouts  7.74 us (2%)
  blocking collectives  4.6 us (1%)
    all_gather x1, waiting for transfers between devices, by_head(): weight = lax.all_gather(out_weight, 'seq', axis=0, tiled=True)  122 us
    all_gather x1, waiting for transfers between devices, by_head(): attended = lax.all_gather(own, ('head', 'seq'), axis=0, tiled=True)  67.6 us
    all_to_all x1, waiting for transfers between devices, by_head(): lax.all_to_all(packed, 'seq', split_axis=0, concat_axis=2, tiled=True)  58.4 us
    dot_general x1, matrix products, expand_and_project(): jnp.dot(flat, weight, preferred_element_type=jnp.float32)  9.25 us
    dot_general x1, matrix products, by_head(): jnp.einsum('hce,hte->hct', centroid, k, preferred_element_type=jnp.float32)  9.24 us
    all_to_all x1, starting transfers between devices, by_head(): lax.all_to_all(cluster_ids.T, 'seq', split_axis=0, concat_axis=1, tiled=T...  7.39 us
  transfers between devices with their start and end apart: 4, of which 4 were waited for; matrix products, arithmetic and copies ran while one was open for 4% of the time, Pallas kernels for 0%

profile of v1, /device:TPU:0, one launch (start us, length us, event | category | flops | bytes accessed | tf_op | source)
XLA Modules:
  0.0 323.4 jit_solution(11268808167526256796)
XLA Ops:
  6.5 1.3 all_to_all.23
  7.9 7.4 %all-to-all-start = ((s32[16,1,256]{2,1,0:T(1,128)}), s32[16,1,256]{2,1,0:T(1,128)S(1)}, u32[]{:S(2)}, u32[]{:S(2)}) async-start(s32[16,1,256]{2,1,0:T(1,128)} %all_to_all.23), calls=%async_computation | async-start | bytes 32768 | tf_op jit(solution)/shard_map/all_to_all | solution.py:62
  15.3 1.5 copy.25
  16.8 2.1 copy_bitcast_fusion
  18.8 2.0 maximum_bitcast_fusion
  20.8 0.9 all-to-all-done
  21.8 5.1 %all-to-all-start.1 = ((bf16[16,3,256,128]{3,2,1,0:T(8,128)(2,1)}), bf16[16,3,256,128]{3,2,1,0:T(8,128)(2,1)S(1)}, u32[]{:S(2)}, u32[]{:S(2)}) async-start(bf16[16,3,256,128]{3,2,1,0:T(8,128)(2,1)} %maximum_bitcast_fusion), calls=%async_computation.1 | async-start | bytes 6291456 | tf_op jit(solution)/shard_map/all_to_all | solution.py:60
  26.9 0.0 all-gather.6.cloned.1.call-start
  26.9 0.9 convert_reduce_fusion
  27.8 58.4 %all-to-all-done.1 = bf16[16,3,256,128]{3,2,1,0:T(8,128)(2,1)S(1)} async-done(((bf16[16,3,256,128]{3,2,1,0:T(8,128)(2,1)}), bf16[16,3,256,128]{3,2,1,0:T(8,128)(2,1)S(1)}, u32[]{:S(2)}, u32[]{:S(2)}) %all-to-all-start.1) | async-done | bytes 3145760 | tf_op jit(solution)/shard_map/all_to_all | solution.py:60
  86.2 2.1 copy.19
  88.3 9.2 %multiply_reduce_fusion = (f32[512]{0:T(512)S(1)}, f32[512,4096]{1,0:T(8,128)}) fusion(bf16[1,3,4096,128]{3,2,1,0:T(8,128)(2,1)} %bitcast.40, s32[4096]{0:T(1024)S(1)} %bitcast.45, f32[512]{0:T(512)S(1)} %broadcast_maximum_fusion), kind=kOutput, calls=%fused_computation.9 | convolution fusion | flops 1080163840 | bytes 10506240 | tf_op jit(solution)/shard_map/hce,hte->hct/dot_general | solution.py:69
  97.5 0.0 copy-start
  97.5 5.0 %fusion.4 = f32[512]{0:T(512)S(1)} fusion(f32[512,4096]{1,0:T(8,128)} %get-tuple-element.6, f32[512]{0:T(512)S(1)} %get-tuple-element.5), kind=kLoop, calls=%fused_computation.10 | loop fusion | flops 6290944 | bytes 8392704 | tf_op jit(solution)/shard_map/reduce_sum | solution.py:71
  102.6 0.7 copy-done
  103.3 0.0 copy-start.1
  103.3 3.4 %fusion.16 = bf16[512,128]{1,0:T(8,128)(2,1)} fusion(f32[512,4096]{1,0:T(8,128)S(1)} %copy-done, f32[512]{0:T(512)S(1)} %get-tuple-element.5, bf16[1,3,4096,128]{3,2,1,0:T(8,128)(2,1)} %bitcast.41, f32[512]{0:T(512)S(1)} %fusion.4), kind=kOutput, calls=%fused_computation.21 | convolution fusion | flops 543293440 | bytes 9572352 | tf_op jit(solution)/shard_map/hct,hte->hce/dot_general | solution.py:72
  106.7 0.0 all-gather.6.cloned.1.call-update
  106.7 0.0 all-gather.4.cloned.1.call-start
  106.8 0.7 all-gather.4.cloned.1.call-update
  107.5 0.0 copy-done.1
  107.5 4.6 %all_gather.10 = s32[256,32]{0,1:T(8,128)S(1)} all-gather(s32[256,16]{0,1:T(8,128)S(1)} %copy-done.1), channel_id=1, replica_groups=mesh['seq'=16,'head'=2] {'head'}, dimensions={1}, use_global_device_ids=true | all-gather | bytes 49152 | tf_op jit(solution)/shard_map/all_gather | solution.py:57
  112.1 67.6 %all-gather.6.cloned.1.call-done = bf16[16384,128]{1,0:T(8,128)(2,1)} async-done(((bf16[512,128]{1,0:T(8,128)(2,1)}), bf16[16384,128]{1,0:T(8,128)(2,1)}) %all-gather.6.cloned.1.call-update) | async-done | bytes 4194320 | tf_op jit(solution)/shard_map/all_gather | solution.py:74
  179.7 6.0 %fusion.9 = bf16[32,128,256]{2,1,0:T(8,128)(2,1)S(1)} fusion(bf16[32,512,128]{2,1,0:T(8,128)(2,1)} %bitcast.46, s32[32,256]{1,0:T(8,128)S(1)} %bitcast.43), kind=kOutput, calls=%fused_computation.16 | convolution fusion | flops 1078984704 | bytes 6324224 | tf_op jit(solution)/shard_map/htc,hce->the/dot_general | solution.py:16
  185.6 121.7 %all-gather.4.cloned.1.call-done = bf16[4096,2048]{1,0:T(8,128)(2,1)} async-done(((bf16[256,2048]{1,0:T(8,128)(2,1)}), bf16[4096,2048]{1,0:T(8,128)(2,1)}) %all-gather.4.cloned.1.call-update) | async-done | bytes 16777232 | tf_op jit(solution)/shard_map/all_gather | solution.py:56
  307.3 9.2 %convolution_convert_fusion = bf16[256,2048]{1,0:T(8,128)(2,1)} fusion(bf16[256,4096]{0,1:T(8,128)(2,1)S(1)} %bitcast.39, bf16[4096,2048]{1,0:T(8,128)(2,1)} %all-gather.4.cloned.1.call-done), kind=kOutput, calls=%fused_computation.15 | convolution fusion | flops 4295491584 | bytes 19922944 | tf_op jit(solution)/shard_map/dot_general | solution.py:20
  (1 shorter events, 0.0 us)
Async XLA Ops:
  7.9 13.9 %all-to-all-start = ((s32[16,1,256]{2,1,0:T(1,128)}), s32[16,1,256]{2,1,0:T(1,128)S(1)}, u32[]{:S(2)}, u32[]{:S(2)}) async-start(s32[16,1,256]{2,1,0:T(1,128)} %all_to_all.23), calls=%async_computation | async-start | bytes 32768 | tf_op jit(solution)/shard_map/all_to_all | solution.py:62
  21.8 64.5 %all-to-all-start.1 = ((bf16[16,3,256,128]{3,2,1,0:T(8,128)(2,1)}), bf16[16,3,256,128]{3,2,1,0:T(8,128)(2,1)S(1)}, u32[]{:S(2)}, u32[]{:S(2)}) async-start(bf16[16,3,256,128]{3,2,1,0:T(8,128)(2,1)} %maximum_bitcast_fusion), calls=%async_computation.1 | async-start | bytes 6291456 | tf_op jit(solution)/shard_map/all_to_all | solution.py:60
  26.9 152.8 %all-gather.6.cloned.1.call-start = ((), (), s32[]{:S(2)}) async-start(), calls=%async_computation.3 | async-start | bytes 4325376 | tf_op jit(solution)/shard_map/all_gather | solution.py:74
  97.5 5.8 %copy-start = (f32[512,4096]{1,0:T(8,128)S(1)}, f32[512,4096]{1,0:T(8,128)}, u32[]{:S(2)}) copy-start(f32[512,4096]{1,0:T(8,128)} %get-tuple-element.6) | copy-start | bytes 25165828
  103.3 4.2 %copy-start.1 = (s32[256,16]{0,1:T(8,128)S(1)}, s32[256,16]{0,1:T(8,128)}, u32[]{:S(2)}) copy-start(s32[256,16]{0,1:T(8,128)} %param.8) | copy-start | bytes 49156
  106.7 200.6 %all-gather.4.cloned.1.call-start = ((), (), s32[]{:S(2)}) async-start(), calls=%async_computation.2 | async-start | bytes 17825792 | tf_op jit(solution)/shard_map/all_gather | solution.py:56
Sparse Core Ops, SparseCore 0:
  106.9 72.7 all-gather.5
  181.8 125.4 all-gather.3

commit v2 on v1

--- a/solution.py
+++ b/solution.py
@@ -48,20 +48,47 @@
     return expand_and_project(ids, attended, weight)
 
 
+def gather_heads(part):
+    n_head = lax.axis_size("head")
+    me = lax.axis_index("head")
+    whole = jnp.zeros((n_head,) + part.shape, part.dtype)
+    whole = lax.dynamic_update_index_in_dim(whole, part, me, 0)
+    for shift in range(1, n_head):
+        moved = lax.ppermute(part, "head", [(i, (i + shift) % n_head) for i in range(n_head)])
+        whole = lax.dynamic_update_index_in_dim(whole, moved, lax.rem(me + n_head - shift, n_head), 0)
+    return whole
+
+
 def by_head(queries, keys, values, cluster_ids, out_weight):
     tok_rows, head_count, e_width = queries.shape
     n_seq = lax.axis_size("seq")
+    n_head = lax.axis_size("head")
     per = head_count // n_seq
+    tokens = n_seq * tok_rows
     score_scale = 1.0 / math.sqrt(e_width)
     weight = lax.all_gather(out_weight, "seq", axis=0, tiled=True)
-    ids = lax.all_gather(cluster_ids, "head", axis=1, tiled=True)
 
-    packed = jnp.stack([queries, keys, values]).transpose(2, 0, 1, 3)
-    moved = lax.all_to_all(packed, "seq", split_axis=0, concat_axis=2, tiled=True)
-    q, k, v = moved[:, 0], moved[:, 1], moved[:, 2]
-    own_ids = lax.all_to_all(cluster_ids.T, "seq", split_axis=0, concat_axis=1, tiled=True)
+    ids_t = cluster_ids.T
+    high, low = ids_t // 16, ids_t % 16
+    id_rows = -(-2 * tok_rows // (16 * e_width)) * 16
+    coded = jnp.concatenate([high, low], axis=1).astype(jnp.bfloat16)
+    coded = jnp.pad(coded, ((0, 0), (0, id_rows * e_width - 2 * tok_rows)))
+    packed = jnp.concatenate(
+        [x.transpose(1, 0, 2) for x in (queries, keys, values)] + [coded.reshape(head_count, id_rows, e_width)],
+        axis=1,
+    )
+    rows = packed.shape[1]
+    packed = packed.reshape(n_seq, per, rows, e_width)
+    moved = lax.all_to_all(packed, "seq", split_axis=0, concat_axis=0)
+    moved = moved.reshape(n_seq, per, rows, e_width).transpose(1, 0, 2, 3)
+    q, k, v = (
+        moved[:, :, i * tok_rows : (i + 1) * tok_rows].reshape(per, tokens, e_width) for i in range(3)
+    )
+    coded = moved[:, :, 3 * tok_rows :].reshape(per, n_seq, id_rows * e_width)[:, :, : 2 * tok_rows]
+    coded = coded.reshape(per, n_seq, 2, tok_rows).astype(jnp.int32)
+    own_ids = (coded[:, :, 0] * 16 + coded[:, :, 1]).reshape(per, tokens)
 
-    labels = lax.broadcasted_iota(jnp.int32, (per, C, own_ids.shape[1]), 1)
+    labels = lax.broadcasted_iota(jnp.int32, (per, C, tokens), 1)
     onehot = (own_ids[:, None, :] == labels).astype(jnp.bfloat16)
     totals = jnp.einsum("hct,hte->hce", onehot, q, preferred_element_type=jnp.float32)
     counts = jnp.sum(onehot, axis=2, dtype=jnp.float32)
@@ -71,8 +98,15 @@
     total = jnp.sum(weights, axis=2)
     summed = jnp.einsum("hct,hte->hce", weights.astype(jnp.bfloat16), v, preferred_element_type=jnp.float32)
     own = (summed / total[:, :, None]).astype(jnp.bfloat16)
-    attended = lax.all_gather(own, ("head", "seq"), axis=0, tiled=True)
-    return expand_and_project(ids, attended, weight)
+    labels = lax.broadcasted_iota(jnp.int32, (per, tokens, C), 2)
+    onehot = (own_ids[:, :, None] == labels).astype(jnp.bfloat16)
+    expanded = jnp.einsum("htc,hce->hte", onehot, own, preferred_element_type=jnp.float32).astype(jnp.bfloat16)
+    sent = expanded.reshape(per, n_seq, tok_rows, e_width).transpose(1, 0, 2, 3)
+    received = lax.all_to_all(sent, "seq", split_axis=0, concat_axis=0).reshape(head_count, tok_rows, e_width)
+    features = gather_heads(received.transpose(1, 0, 2).reshape(tok_rows, head_count * e_width))
+    features = features.transpose(1, 0, 2).reshape(tok_rows, n_head * head_count * e_width)
+    mixed = jnp.dot(features, weight, preferred_element_type=jnp.float32)
+    return mixed.astype(jnp.bfloat16)
 
 
 def on_device(queries, keys, values, cluster_ids, out_weight):

time: 324 us -> 257 us (0.79)
  waiting for transfers between devices: 249 us -> 24.3 us
  blocking collectives: 4.6 us -> 176 us
  starting transfers between devices: 12.6 us -> 1.5 us
    all_to_all x0 -> x2, blocking collectives: none -> 176 us  [the longest x1 140 us: by_head(): moved = lax.all_to_all(packed, 'seq', split_axis=0, concat_axis=0)]
    all_gather x1, waiting for transfers between devices: 122 us -> 0.02 us  [by_head(): weight = lax.all_gather(out_weight, 'seq', axis=0, tiled=True)]
    all_gather x1 -> x0, waiting for transfers between devices: 67.6 us -> none  [by_head(): attended = lax.all_gather(own, ('head', 'seq'), axis=0, tiled=True)]
    all_to_all x2 -> x0, waiting for transfers between devices: 59.3 us -> none  [the longest x1 58.4 us: by_head(): lax.all_to_all(packed, 'seq', split_axis=0, concat_axis=2, tiled=True)]
    ppermute x0 -> x1, waiting for transfers between devices: none -> 23.6 us  [gather_heads(): lax.ppermute(part, 'head', [(i, (i + shift) % n_head) for i in range(n_he...]
    all_to_all x2 -> x0, starting transfers between devices: 12.5 us -> none  [the longest x1 7.39 us: by_head(): lax.all_to_all(cluster_ids.T, 'seq', split_axis=0, concat_axis=1, tiled=T...]
    all_gather x1 -> x0, blocking collectives: 4.6 us -> none  [by_head(): ids = lax.all_gather(cluster_ids, 'head', axis=1, tiled=True)]
    all_to_all x2 -> x0, local copies, waits for them, and re-layouts: 3.41 us -> none  [the longest x1 2.08 us: by_head(): lax.all_to_all(packed, 'seq', split_axis=0, concat_axis=2, tiled=True)]
  transfers between devices with their start and end apart: 4 -> 2, of which waited for: 4 -> 1; matrix products, arithmetic and copies ran while one was open for 4% -> 12% of each run, Pallas kernels for 0% -> 0%
where the time goes in v2:
time: 257 us
  blocking collectives  176 us (68%)
  matrix products  26.6 us (10%)
  waiting for transfers between devices  24.3 us (9%)
  between operations  13.5 us (5%)
  local copies, waits for them, and re-layouts  7.66 us (3%)
  other arithmetic  7.17 us (3%)
    all_to_all x1, blocking collectives, by_head(): moved = lax.all_to_all(packed, 'seq', split_axis=0, concat_axis=0)  140 us
    all_to_all x1, blocking collectives, by_head(): lax.all_to_all(sent, 'seq', split_axis=0, concat_axis=0)  36.4 us
    ppermute x1, waiting for transfers between devices, gather_heads(): lax.ppermute(part, 'head', [(i, (i + shift) % n_head) for i in range(n_he...  23.6 us
    dot_general x1, matrix products, by_head(): mixed = jnp.dot(features, weight, preferred_element_type=jnp.float32)  9.25 us
    dot_general x1, matrix products, by_head(): jnp.einsum('hce,hte->hct', centroid, k, preferred_element_type=jnp.float32)  9.23 us
    dot_general x1, matrix products, by_head(): jnp.einsum('htc,hce->hte', onehot, own, preferred_element_type=jnp.float32)  8.08 us
    reduce_sum x1, other arithmetic, by_head(): total = jnp.sum(weights, axis=2)  5.21 us
  transfers between devices with their start and end apart: 2, of which 1 were waited for; matrix products, arithmetic and copies ran while one was open for 12% of the time, Pallas kernels for 0%

profile of v2, /device:TPU:0, one launch (start us, length us, event | category | flops | bytes accessed | tf_op | source)
XLA Modules:
  0.0 257.1 jit_solution(18098206514507353061)
XLA Ops:
  6.5 0.0 all-gather.2.cloned.1.call-start
  6.5 0.7 all-gather.2.cloned.1.call-update
  7.3 0.7 fusion.27
  8.0 1.5 copy.23
  9.5 2.1 copy_bitcast_fusion
  11.6 0.3 maximum_bitcast_fusion
  11.9 140.0 %all_to_all.10 = bf16[16,1,784,128]{3,2,1,0:T(8,128)(2,1)S(1)} all-to-all(bf16[16,1,784,128]{3,2,1,0:T(8,128)(2,1)S(1)} %maximum_bitcast_fusion), channel_id=1, replica_groups=mesh['seq'=16,'head'=2] {'seq'}, dimensions={0} | all-to-all | bytes 6422528 | tf_op jit(solution)/shard_map/all_to_all | solution.py:82
  152.0 0.9 convert_reduce_fusion
  152.9 1.8 fusion.34
  154.7 9.2 %multiply_reduce_fusion = (f32[512]{0:T(512)S(1)}, f32[512,4096]{1,0:T(8,128)}) fusion(bf16[4096,128]{1,0:T(8,128)(2,1)} %bitcast.70, bf16[4096,128]{1,0:T(8,128)(2,1)} %bitcast.69, s32[4096]{0:T(1024)S(1)} %bitcast.75, f32[512]{0:T(512)S(1)} %broadcast_maximum_fusion), kind=kOutput, calls=%fused_computation.8 | convolution fusion | flops 1080163840 | bytes 10506240 | tf_op jit(solution)/shard_map/hce,hte->hct/dot_general | solution.py:96
  163.9 0.0 copy-start
  163.9 5.2 %fusion.3 = f32[512]{0:T(512)S(1)} fusion(f32[512,4096]{1,0:T(8,128)} %get-tuple-element.11, f32[512]{0:T(512)S(1)} %get-tuple-element.10), kind=kLoop, calls=%fused_computation.9 | loop fusion | flops 6290944 | bytes 8392704 | tf_op jit(solution)/shard_map/reduce_sum | solution.py:98
  169.1 0.0 copy-done
  169.1 8.1 %fusion.5 = bf16[4096,128]{1,0:T(8,128)(2,1)S(1)} fusion(s32[4096]{0:T(1024)S(1)} %bitcast.76, bf16[4096,128]{1,0:T(8,128)(2,1)S(1)} %bitcast.72, f32[512,4096]{1,0:T(8,128)} %get-tuple-element.11, f32[512]{0:T(512)S(1)} %get-tuple-element.10, f32[512]{0:T(512)S(1)} %fusion.3), kind=kOutput, calls=%fused_computation.11 | convolution fusion | flops 1082785792 | bytes 10506240 | tf_op jit(solution)/shard_map/htc,hce->hte/dot_general | solution.py:103
  177.2 0.7 copy.18
  177.9 36.4 %all_to_all.11 = bf16[16,1,256,128]{2,3,1,0:T(8,128)(2,1)S(1)} all-to-all(bf16[16,1,256,128]{2,3,1,0:T(8,128)(2,1)S(1)} %copy.18), channel_id=1, replica_groups=mesh['seq'=16,'head'=2] {'seq'}, dimensions={0} | all-to-all | bytes 2097152 | tf_op jit(solution)/shard_map/all_to_all | solution.py:105
  214.3 1.5 collective-permute-start
  215.8 0.1 broadcast_in_dim.13
  216.0 0.1 constant_dynamic-update-slice_fusion
  216.1 23.6 %collective-permute-done = bf16[256,2048]{0,1:T(8,128)(2,1)} collective-permute-done((bf16[256,2048]{0,1:T(8,128)(2,1)S(1)}, bf16[256,2048]{0,1:T(8,128)(2,1)}, u32[]{:S(2)}, u32[]{:S(2)}) %collective-permute-start) | collective-permute-done | bytes 1048608 | tf_op jit(solution)/shard_map/ppermute | solution.py:57
  239.7 1.3 bitcast_dynamic-update-slice_fusion
  241.0 0.0 all-gather.2.cloned.1.call-done
  241.0 9.3 %convolution_convert_fusion = bf16[256,2048]{1,0:T(8,128)(2,1)} fusion(bf16[256,4096]{0,1:T(8,128)(2,1)S(1)} %bitcast.65, bf16[4096,2048]{1,0:T(8,128)(2,1)} %all-gather.2.cloned.1.call-done), kind=kOutput, calls=%fused_computation.16 | convolution fusion | flops 4295491584 | bytes 19922944 | tf_op jit(solution)/shard_map/dot_general | solution.py:108
  (8 shorter events, 0.1 us)
Async XLA Ops:
  6.5 234.4 %all-gather.2.cloned.1.call-start = ((), (), s32[]{:S(2)}) async-start(), calls=%async_computation.2 | async-start | bytes 17825792 | tf_op jit(solution)/shard_map/all_gather | solution.py:69
  163.9 5.2 %copy-start = (bf16[1,16,256,128]{3,2,1,0:T(8,128)(2,1)S(1)}, bf16[1,16,256,128]{3,2,1,0:T(8,128)(2,1)}, u32[]{:S(2)}) copy-start(bf16[1,16,256,128]{3,2,1,0:T(8,128)(2,1)} %get-tuple-element.6) | copy-start | bytes 3145732
  214.3 25.3 %collective-permute-start = (bf16[256,2048]{0,1:T(8,128)(2,1)S(1)}, bf16[256,2048]{0,1:T(8,128)(2,1)}, u32[]{:S(2)}, u32[]{:S(2)}) collective-permute-start(bf16[256,2048]{0,1:T(8,128)(2,1)S(1)} %bitcast.67), channel_id=1, source_target_pairs={{0,1},{1,0},{2,3},{3,2},{4,5},{5,4},{6,7},{7,6},{8,9},{9,8},{10,11... | collective-permute-start | bytes 3145736 | tf_op jit(solution)/shard_map/ppermute | solution.py:57
Sparse Core Ops, SparseCore 0:
  9.5 202.7 all-gather.1

commit v3 on v1

--- a/solution.py
+++ b/solution.py
@@ -3,6 +3,8 @@
 import jax
 import jax.numpy as jnp
 from jax import lax
+from jax.experimental import pallas as pl
+from jax.experimental.pallas import tpu as pltpu
 from jax.sharding import PartitionSpec as P
 
 C = 512
@@ -48,35 +50,186 @@
     return expand_and_project(ids, attended, weight)
 
 
+def attend_kernel(tok_rows, moved_ref, out_ref, sums_ref, scores_ref, acc_ref):
+    n_src, _, e_width = moved_ref.shape
+    lanes = e_width
+    blocks = tok_rows // lanes
+    scale = 1.0 / math.sqrt(e_width)
+    cluster = lax.broadcasted_iota(jnp.int32, (C, lanes), 0)
+    ones = jnp.ones((tok_rows, e_width), jnp.bfloat16)
+
+    sums_ref[...] = jnp.zeros_like(sums_ref)
+
+    @pl.loop(0, n_src)
+    def _(src):
+        coded = moved_ref[src, 3 * tok_rows :, :].astype(jnp.float32).astype(jnp.int32)
+        parts = []
+        for i in range(blocks):
+            ids = coded[i : i + 1] * 16 + coded[blocks + i : blocks + i + 1]
+            parts.append(jnp.where(cluster == ids, 1.0, 0.0).astype(jnp.bfloat16))
+        onehot = jnp.concatenate(parts, axis=1)
+        wide = jnp.concatenate([moved_ref[src, :tok_rows, :], ones], axis=1)
+        sums_ref[...] += jnp.dot(onehot, wide, preferred_element_type=jnp.float32)
+
+    centroid = (sums_ref[:, :e_width] / jnp.maximum(sums_ref[:, e_width:], 1.0)).astype(jnp.bfloat16)
+
+    def score(src, top):
+        keys = moved_ref[src, tok_rows : 2 * tok_rows, :]
+        scores = lax.dot_general(centroid, keys, (((1,), (1,)), ((), ())), preferred_element_type=jnp.float32)
+        scores_ref[src] = scores
+        for i in range(blocks):
+            top = jnp.maximum(top, scores[:, i * lanes : (i + 1) * lanes])
+        return top
+
+    top = lax.fori_loop(0, n_src, score, jnp.full((C, lanes), -jnp.inf, jnp.float32))
+    top = jnp.broadcast_to(jnp.max(top, axis=1, keepdims=True), (C, tok_rows))
+
+    acc_ref[...] = jnp.zeros_like(acc_ref)
+
+    def weigh(src, total):
+        weights = jnp.exp((scores_ref[src] - top) * scale)
+        for i in range(blocks):
+            total += weights[:, i * lanes : (i + 1) * lanes]
+        values = moved_ref[src, 2 * tok_rows : 3 * tok_rows, :]
+        acc_ref[...] += jnp.dot(weights.astype(jnp.bfloat16), values, preferred_element_type=jnp.float32)
+        return total
+
+    total = lax.fori_loop(0, n_src, weigh, jnp.zeros((C, lanes), jnp.float32))
+    out_ref[...] = (acc_ref[...] / jnp.sum(total, axis=1, keepdims=True)).astype(jnp.bfloat16)
+
+
+def attend(moved, tok_rows):
+    n_src, _, e_width = moved.shape
+    tokens = n_src * tok_rows
+    return pl.pallas_call(
+        lambda *refs: attend_kernel(tok_rows, *refs),
+        out_shape=jax.ShapeDtypeStruct((C, e_width), jnp.bfloat16),
+        in_specs=[pl.BlockSpec(memory_space=pltpu.VMEM)],
+        out_specs=pl.BlockSpec(memory_space=pltpu.VMEM),
+        scratch_shapes=[
+            pltpu.VMEM((C, 2 * e_width), jnp.float32),
+            pltpu.VMEM((n_src, C, tok_rows), jnp.float32),
+            pltpu.VMEM((C, e_width), jnp.float32),
+        ],
+        compiler_params=pltpu.CompilerParams(vmem_limit_bytes=40 * 2**20),
+        cost_estimate=pl.CostEstimate(
+            flops=8 * C * tokens * e_width, bytes_accessed=moved.size * 2, transcendentals=C * tokens
+        ),
+        name="attend",
+    )(moved)
+
+
+def lookup_kernel(ids_ref, attended_ref, weight_ref, out_ref, table_ref):
+    heads, clusters, e_width = attended_ref.shape
+    tok_tile = ids_ref.shape[0]
+
+    @pl.when(pl.program_id(0) == 0)
+    def _():
+        @pl.loop(0, heads)
+        def _(h):
+            part = weight_ref[pl.ds(pl.multiple_of(h * e_width, e_width), e_width), :]
+            product = jnp.dot(attended_ref[h], part, preferred_element_type=jnp.float32)
+            table_ref[pl.ds(pl.multiple_of(h * clusters, clusters), clusters), :] = product.astype(jnp.bfloat16)
+
+    labels = lax.broadcasted_iota(jnp.int32, (tok_tile, clusters), 1)
+    total = None
+    for h in range(0, heads, 2):
+        onehot = jnp.concatenate(
+            [jnp.where(ids_ref[:, i : i + 1] == labels, 1.0, 0.0).astype(jnp.bfloat16) for i in (h, h + 1)], axis=1
+        )
+        term = jnp.dot(
+            onehot, table_ref[h * clusters : (h + 2) * clusters, :], preferred_element_type=jnp.float32
+        )
+        total = term if total is None else total + term
+    out_ref[...] = total.astype(jnp.bfloat16)
+
+
+def lookup(ids, attended, weight, tok_tile):
+    tokens, heads = ids.shape
+    _, clusters, e_width = attended.shape
+    cols = weight.shape[1]
+    return pl.pallas_call(
+        lookup_kernel,
+        out_shape=jax.ShapeDtypeStruct((tokens, cols), jnp.bfloat16),
+        grid=(tokens // tok_tile,),
+        in_specs=[
+            pl.BlockSpec((tok_tile, heads), lambda i: (i, 0)),
+            pl.BlockSpec((heads, clusters, e_width), lambda i: (0, 0, 0)),
+            pl.BlockSpec((heads * e_width, cols), lambda i: (0, 0)),
+        ],
+        out_specs=pl.BlockSpec((tok_tile, cols), lambda i: (i, 0)),
+        scratch_shapes=[pltpu.VMEM((heads * clusters, cols), jnp.bfloat16)],
+        compiler_params=pltpu.CompilerParams(vmem_limit_bytes=48 * 2**20),
+        cost_estimate=pl.CostEstimate(
+            flops=2 * tokens * heads * clusters * cols,
+            bytes_accessed=2 * (attended.size + weight.size + tokens * cols),
+            transcendentals=0,
+        ),
+        name="lookup",
+    )(ids, attended, weight)
+
+
 def by_head(queries, keys, values, cluster_ids, out_weight):
     tok_rows, head_count, e_width = queries.shape
     n_seq = lax.axis_size("seq")
-    per = head_count // n_seq
-    score_scale = 1.0 / math.sqrt(e_width)
-    weight = lax.all_gather(out_weight, "seq", axis=0, tiled=True)
-    ids = lax.all_gather(cluster_ids, "head", axis=1, tiled=True)
-
-    packed = jnp.stack([queries, keys, values]).transpose(2, 0, 1, 3)
-    moved = lax.all_to_all(packed, "seq", split_axis=0, concat_axis=2, tiled=True)
-    q, k, v = moved[:, 0], moved[:, 1], moved[:, 2]
-    own_ids = lax.all_to_all(cluster_ids.T, "seq", split_axis=0, concat_axis=1, tiled=True)
-
-    labels = lax.broadcasted_iota(jnp.int32, (per, C, own_ids.shape[1]), 1)
-    onehot = (own_ids[:, None, :] == labels).astype(jnp.bfloat16)
-    totals = jnp.einsum("hct,hte->hce", onehot, q, preferred_element_type=jnp.float32)
-    counts = jnp.sum(onehot, axis=2, dtype=jnp.float32)
-    centroid = (totals / jnp.maximum(counts, 1.0)[:, :, None]).astype(jnp.bfloat16)
-    scores = jnp.einsum("hce,hte->hct", centroid, k, preferred_element_type=jnp.float32) * score_scale
-    weights = jnp.exp(scores - jnp.max(scores, axis=2)[:, :, None])
-    total = jnp.sum(weights, axis=2)
-    summed = jnp.einsum("hct,hte->hce", weights.astype(jnp.bfloat16), v, preferred_element_type=jnp.float32)
-    own = (summed / total[:, :, None]).astype(jnp.bfloat16)
-    attended = lax.all_gather(own, ("head", "seq"), axis=0, tiled=True)
-    return expand_and_project(ids, attended, weight)
+    n_head = lax.axis_size("head")
+    half = n_seq // 2
+    rows, cols = out_weight.shape
+    cols_each = cols // half
+    seq_at = lax.axis_index("seq")
+
+    ids_t = cluster_ids.T
+    all_ids = lax.all_gather(ids_t, ("head", "seq"), axis=0, tiled=False)
+    all_ids = all_ids.reshape(n_head, n_seq, head_count, tok_rows)
+    near_ids = lax.dynamic_slice_in_dim(all_ids, (seq_at // half) * half, half, axis=1)
+    near_ids = near_ids.transpose(1, 3, 0, 2).reshape(half * tok_rows, n_head * head_count)
+
+    high, low = ids_t // 16, ids_t % 16
+    id_rows = -(-2 * tok_rows // (16 * e_width)) * 16
+    coded = jnp.concatenate([high, low], axis=1).astype(jnp.bfloat16)
+    coded = jnp.pad(coded, ((0, 0), (0, id_rows * e_width - 2 * tok_rows)))
+    packed = jnp.concatenate(
+        [x.transpose(1, 0, 2) for x in (queries, keys, values)] + [coded.reshape(head_count, id_rows, e_width)],
+        axis=1,
+    )
+    moved = lax.all_to_all(packed, "seq", split_axis=0, concat_axis=0, tiled=True)
+
+    moved, out_weight = lax.optimization_barrier((moved, out_weight))
+    blocks = out_weight.reshape(rows, half, cols_each).transpose(1, 0, 2)
+    blocks = jnp.concatenate([blocks, blocks], axis=0)
+    weight = lax.all_to_all(blocks, "seq", split_axis=0, concat_axis=0, tiled=True)
+    weight = weight.reshape(n_seq * rows, cols_each)
+
+    own = attend(moved, tok_rows)
+    attended = lax.all_gather(own, ("head", "seq"), axis=0, tiled=False)
+    near = lookup(near_ids, attended, weight, 2 * tok_rows)
+
+    groups = [list(range(half)), list(range(half, n_seq))]
+    mixed = lax.all_to_all(
+        near.reshape(half, tok_rows, cols_each),
+        "seq",
+        split_axis=0,
+        concat_axis=0,
+        axis_index_groups=groups,
+        tiled=True,
+    )
+    return mixed.transpose(1, 0, 2).reshape(tok_rows, cols)
+
+
+def fits(queries, out_weight):
+    n_seq = lax.axis_size("seq")
+    tok_rows, head_count, e_width = queries.shape
+    return (
+        head_count == n_seq
+        and n_seq % 2 == 0
+        and e_width == 128
+        and tok_rows % e_width == 0
+        and out_weight.shape[1] % (n_seq // 2 * 128) == 0
+    )
 
 
 def on_device(queries, keys, values, cluster_ids, out_weight):
-    if queries.shape[1] % lax.axis_size("seq") == 0:
+    if fits(queries, out_weight):
         return by_head(queries, keys, values, cluster_ids, out_weight)
     return by_reduction(queries, keys, values, cluster_ids, out_weight)
 

time: 324 us -> 250 us (0.77)
  waiting for transfers between devices: 249 us -> 0.04 us
  blocking collectives: 4.6 us -> 184 us
  Pallas kernels: 0 us -> 40.3 us
  matrix products: 27.8 us -> 0 us
  starting transfers between devices: 12.6 us -> 3.72 us
  other arithmetic: 7.94 us -> 2.51 us
    all_gather x2 -> x1, waiting for transfers between devices: 189 us -> 0.02 us  [by_head(): attended = lax.all_gather(own, ('head', 'seq'), axis=0, tiled=False)]
    all_to_all x0 -> x2, blocking collectives: none -> 97.7 us  [the longest x1 80.7 us: by_head(): lax.all_to_all(packed, 'seq', split_axis=0, concat_axis=0, tiled=True)]
    all_gather x1, blocking collectives: 4.6 us -> 86.4 us  [by_head(): all_ids = lax.all_gather(ids_t, ('head', 'seq'), axis=0, tiled=False)]
    all_to_all x2 -> x1, waiting for transfers between devices: 59.3 us -> 0.01 us  [by_head(): lax.all_to_all(blocks, 'seq', split_axis=0, concat_axis=0, tiled=True)]
    pallas_call x0 -> x2, Pallas kernels: none -> 40.3 us  [the longest x1 27.5 us: lookup(): pl.pallas_call(lookup_kernel, out_shape=jax.ShapeDtypeStruct((tokens, col...]
    dot_general x4 -> x0, matrix products: 27.8 us -> none  [the longest x1 9.25 us: expand_and_project(): jnp.dot(flat, weight, preferred_element_type=jnp.float32)]
    all_to_all x2 -> x1, starting transfers between devices: 12.5 us -> 3.72 us  [by_head(): lax.all_to_all(blocks, 'seq', split_axis=0, concat_axis=0, tiled=True)]
    reduce_sum x2 -> x0, other arithmetic: 5.94 us -> none  [the longest x1 5.03 us: by_head(): total = jnp.sum(weights, axis=2)]
  transfers between devices with their start and end apart: 4 -> 2, of which waited for: 4 -> 0; matrix products, arithmetic and copies ran while one was open for 4% -> 1% of each run, Pallas kernels for 0% -> 0%
where the time goes in v3:
time: 250 us
  blocking collectives  184 us (74%)
  Pallas kernels  40.3 us (16%)
  between operations  13.5 us (5%)
  local copies, waits for them, and re-layouts  5.36 us (2%)
  starting transfers between devices  3.72 us (1%)
  other arithmetic  2.51 us (1%)
    all_gather x1, blocking collectives, by_head(): all_ids = lax.all_gather(ids_t, ('head', 'seq'), axis=0, tiled=False)  86.4 us
    all_to_all x1, blocking collectives, by_head(): lax.all_to_all(packed, 'seq', split_axis=0, concat_axis=0, tiled=True)  80.7 us
    pallas_call x1, Pallas kernels, lookup(): pl.pallas_call(lookup_kernel, out_shape=jax.ShapeDtypeStruct((tokens, col...  27.5 us
    all_to_all x1, blocking collectives, by_head(): lax.all_to_all(near.reshape(half, tok_rows, cols_each), 'seq', split_axis...  17 us
    pallas_call x1, Pallas kernels, attend(): pl.pallas_call(lambda *refs: attend_kernel(tok_rows, *refs), out_shape=ja...  12.8 us
  transfers between devices with their start and end apart: 2, of which 0 were waited for; matrix products, arithmetic and copies ran while one was open for 1% of the time, Pallas kernels for 0%

profile of v3, /device:TPU:0, one launch (start us, length us, event | category | flops | bytes accessed | tf_op | source)
XLA Modules:
  0.0 249.5 jit_solution(12535039953432797908)
XLA Ops:
  6.5 0.0 all-gather.4.cloned.1.call-start
  6.5 0.7 fusion.4
  7.3 1.5 copy.29
  8.8 2.1 copy_bitcast_fusion
  10.9 0.3 pad_maximum_fusion
  11.2 80.7 %all_to_all.15.refs_0_ = bf16[16,784,128]{2,1,0:T(8,128)(2,1)S(1)} all-to-all(bf16[16,784,128]{2,1,0:T(8,128)(2,1)S(1)} %pad_maximum_fusion), channel_id=1, replica_groups=mesh['seq'=16,'head'=2] {'seq'}, dimensions={0} | all-to-all | bytes 6422528 | tf_op jit(solution)/shard_map/all_to_all | solution.py:195
  91.8 0.0 copy-start
  91.8 12.8 %attend.1 = bf16[512,128]{1,0:T(8,128)(2,1)} custom-call(bf16[16,784,128]{2,1,0:T(8,128)(2,1)S(1)} %all_to_all.15.refs_0_), custom_call_target="tpu_custom_call" | custom-call | flops 2147483648 | bytes 3211264 | tf_op jit(solution)/shard_map/attend/pallas_call | solution.py:104
  104.6 0.0 all-gather.4.cloned.1.call-update
  104.7 0.0 copy-done
  104.7 0.1 copy.28
  104.8 0.0 copy-start.1
  104.8 1.5 pad_maximum_fusion.1
  106.3 3.7 %all-to-all-start.1 = ((bf16[16,256,256]{2,1,0:T(8,128)(2,1)}), bf16[16,256,256]{2,1,0:T(8,128)(2,1)S(1)}, u32[]{:S(2)}, u32[]{:S(2)}) async-start(bf16[16,256,256]{2,1,0:T(8,128)(2,1)} %pad_maximum_fusion.1), calls=%async_computation.1 | async-start | bytes 4194304 | tf_op jit(solution)/shard_map/all_to_all | solution.py:200
  110.0 0.0 copy-done.1
  110.0 86.4 %all-gather = s32[512,256]{1,0:T(8,128)S(1)} all-gather(s32[16,256]{1,0:T(8,128)S(1)} %bitcast.43), channel_id=2, replica_groups=mesh['seq'=16,'head'=2] {'head','seq'}, dimensions={0}, use_global_device_ids=true | all-gather | bytes 540672 | tf_op jit(solution)/shard_map/all_gather | solution.py:182
  196.5 0.2 copy.19
  196.6 0.1 copy.22
  196.7 0.3 copy.17.ids_ref
  197.1 0.0 all-to-all-done.1
  197.1 0.0 all-gather.4.cloned.1.call-done
  197.1 27.5 %lookup.1 = bf16[2048,256]{1,0:T(8,128)(2,1)S(1)} custom-call(s32[2048,32]{1,0:T(8,128)S(1)} %copy.17.ids_ref, bf16[32,512,128]{2,1,0:T(8,128)(2,1)} %bitcast.44, bf16[4096,256]{1,0:T(8,128)(2,1)S(1)} %bitcast.33), custom_call_target="tpu_custom_call" | custom-call | flops 17179869184 | bytes 7340032 | tf_op jit(solution)/shard_map/lookup/pallas_call | solution.py:151
  224.6 17.0 %all_to_all.16 = bf16[8,256,256]{2,1,0:T(8,128)(2,1)S(1)} all-to-all(bf16[8,256,256]{2,1,0:T(8,128)(2,1)S(1)} %bitcast.34), channel_id=1, replica_groups={{0,2,4,6,8,10,12,14},{16,18,20,22,24,26,28,30},{1,3,5,7,9,11,13,15},{17..., dimensions={0} | all-to-all | bytes 2097152 | tf_op jit(solution)/shard_map/all_to_all | solution.py:208
  241.6 1.1 copy.21
  (3 shorter events, 0.0 us)
Async XLA Ops:
  6.5 190.6 %all-gather.4.cloned.1.call-start = ((), (), s32[]{:S(2)}) async-start(), calls=%async_computation.3 | async-start | bytes 4325376 | tf_op jit(solution)/shard_map/all_gather | solution.py:204
  91.8 12.8 %copy-start = (bf16[256,2048]{1,0:T(8,128)(2,1)S(1)}, bf16[256,2048]{1,0:T(8,128)(2,1)}, u32[]{:S(2)}) copy-start(bf16[256,2048]{1,0:T(8,128)(2,1)} %param.9) | copy-start | bytes 3145732
  104.8 5.3 %copy-start.1 = (s32[256,16]{0,1:T(8,128)S(1)}, s32[256,16]{0,1:T(8,128)}, u32[]{:S(2)}) copy-start(s32[256,16]{0,1:T(8,128)} %param.8) | copy-start | bytes 49156
  106.3 90.8 %all-to-all-start.1 = ((bf16[16,256,256]{2,1,0:T(8,128)(2,1)}), bf16[16,256,256]{2,1,0:T(8,128)(2,1)S(1)}, u32[]{:S(2)}, u32[]{:S(2)}) async-start(bf16[16,256,256]{2,1,0:T(8,128)(2,1)} %pad_maximum_fusion.1), calls=%async_computation.1 | async-start | bytes 4194304 | tf_op jit(solution)/shard_map/all_to_all | solution.py:200
Sparse Core Ops, SparseCore 0:
  104.8 80.3 all-gather.3

commit v4 on v3

--- a/solution.py
+++ b/solution.py
@@ -119,70 +119,110 @@
     )(moved)
 
 
-def lookup_kernel(ids_ref, attended_ref, weight_ref, out_ref, table_ref):
+def expand_kernel(ids_ref, attended_ref, *refs):
+    out_ref = refs[-1]
     heads, clusters, e_width = attended_ref.shape
     tok_tile = ids_ref.shape[0]
-
-    @pl.when(pl.program_id(0) == 0)
-    def _():
-        @pl.loop(0, heads)
-        def _(h):
-            part = weight_ref[pl.ds(pl.multiple_of(h * e_width, e_width), e_width), :]
-            product = jnp.dot(attended_ref[h], part, preferred_element_type=jnp.float32)
-            table_ref[pl.ds(pl.multiple_of(h * clusters, clusters), clusters), :] = product.astype(jnp.bfloat16)
-
-    labels = lax.broadcasted_iota(jnp.int32, (tok_tile, clusters), 1)
-    total = None
-    for h in range(0, heads, 2):
-        onehot = jnp.concatenate(
-            [jnp.where(ids_ref[:, i : i + 1] == labels, 1.0, 0.0).astype(jnp.bfloat16) for i in (h, h + 1)], axis=1
-        )
-        term = jnp.dot(
-            onehot, table_ref[h * clusters : (h + 2) * clusters, :], preferred_element_type=jnp.float32
-        )
-        total = term if total is None else total + term
-    out_ref[...] = total.astype(jnp.bfloat16)
-
-
-def lookup(ids, attended, weight, tok_tile):
+    labels = lax.broadcasted_iota(jnp.int32, (tok_tile, e_width), 1).astype(jnp.int16)
+    one, zero = jnp.bfloat16(1.0), jnp.bfloat16(0.0)
+    for h in range(heads):
+        ids = jnp.broadcast_to(ids_ref[:, h : h + 1], (tok_tile, e_width)).astype(jnp.int16)
+        parts = [
+            jnp.where(ids == labels + jnp.int16(at), one, zero) for at in range(0, clusters, e_width)
+        ]
+        onehot = jnp.concatenate(parts, axis=1)
+        found = jnp.dot(onehot, attended_ref[h], preferred_element_type=jnp.float32)
+        out_ref[h] = found.astype(jnp.bfloat16)
+
+
+def expand(ids, attended, store, piece, pieces, tok_tile):
     tokens, heads = ids.shape
     _, clusters, e_width = attended.shape
-    cols = weight.shape[1]
+    held = () if store is None else (store,)
     return pl.pallas_call(
-        lookup_kernel,
-        out_shape=jax.ShapeDtypeStruct((tokens, cols), jnp.bfloat16),
+        expand_kernel,
+        out_shape=jax.ShapeDtypeStruct((pieces * heads, tokens, e_width), jnp.bfloat16),
         grid=(tokens // tok_tile,),
         in_specs=[
             pl.BlockSpec((tok_tile, heads), lambda i: (i, 0)),
             pl.BlockSpec((heads, clusters, e_width), lambda i: (0, 0, 0)),
-            pl.BlockSpec((heads * e_width, cols), lambda i: (0, 0)),
-        ],
-        out_specs=pl.BlockSpec((tok_tile, cols), lambda i: (i, 0)),
-        scratch_shapes=[pltpu.VMEM((heads * clusters, cols), jnp.bfloat16)],
-        compiler_params=pltpu.CompilerParams(vmem_limit_bytes=48 * 2**20),
+        ]
+        + [pl.BlockSpec(memory_space=pl.ANY) for _ in held],
+        out_specs=pl.BlockSpec((heads, tok_tile, e_width), lambda i: (piece, i, 0)),
+        input_output_aliases={2: 0} if held else {},
+        compiler_params=pltpu.CompilerParams(vmem_limit_bytes=50 * 2**20),
         cost_estimate=pl.CostEstimate(
-            flops=2 * tokens * heads * clusters * cols,
-            bytes_accessed=2 * (attended.size + weight.size + tokens * cols),
+            flops=4 * tokens * heads * clusters * e_width,
+            bytes_accessed=2 * (attended.size + heads * tokens * e_width),
             transcendentals=0,
         ),
-        name="lookup",
-    )(ids, attended, weight)
+        name="expand",
+    )(ids, attended, *held)
+
+
+def project_kernel(heads_ref, features_ref, weight_ref, out_ref):
+    heads, _, e_width = features_ref.shape
+    total = None
+    for slot in range(0, heads, 2):
+        left = jnp.concatenate([features_ref[slot], features_ref[slot + 1]], axis=1)
+        starts = [pl.multiple_of(heads_ref[slot + j] * e_width, e_width) for j in range(2)]
+        right = jnp.concatenate([weight_ref[pl.ds(at, e_width), :] for at in starts], axis=0)
+        term = jnp.dot(left, right, preferred_element_type=jnp.float32)
+        total = term if total is None else total + term
+    out_ref[...] = total.astype(jnp.bfloat16)
+
+
+def project(slot_heads, features, weight, tok_tile):
+    heads, tokens, e_width = features.shape
+    cols = weight.shape[1]
+    return pl.pallas_call(
+        project_kernel,
+        out_shape=jax.ShapeDtypeStruct((tokens, cols), jnp.bfloat16),
+        grid_spec=pltpu.PrefetchScalarGridSpec(
+            num_scalar_prefetch=1,
+            grid=(tokens // tok_tile,),
+            in_specs=[
+                pl.BlockSpec((heads, tok_tile, e_width), lambda i, _: (0, i, 0)),
+                pl.BlockSpec(weight.shape, lambda i, _: (0, 0)),
+            ],
+            out_specs=pl.BlockSpec((tok_tile, cols), lambda i, _: (i, 0)),
+        ),
+        compiler_params=pltpu.CompilerParams(vmem_limit_bytes=50 * 2**20),
+        cost_estimate=pl.CostEstimate(
+            flops=2 * tokens * weight.size,
+            bytes_accessed=2 * (features.size + weight.size + tokens * cols),
+            transcendentals=0,
+        ),
+        name="project",
+    )(slot_heads, features, weight)
 
 
 def by_head(queries, keys, values, cluster_ids, out_weight):
     tok_rows, head_count, e_width = queries.shape
     n_seq = lax.axis_size("seq")
-    n_head = lax.axis_size("head")
     half = n_seq // 2
     rows, cols = out_weight.shape
     cols_each = cols // half
     seq_at = lax.axis_index("seq")
+    head_at = lax.axis_index("head")
+    core = lax.rem(seq_at, 2)
+    swap_heads = [(0, 1), (1, 0)]
+    swap_cores = [(i, i ^ 1) for i in range(n_seq)]
 
     ids_t = cluster_ids.T
-    all_ids = lax.all_gather(ids_t, ("head", "seq"), axis=0, tiled=False)
-    all_ids = all_ids.reshape(n_head, n_seq, head_count, tok_rows)
-    near_ids = lax.dynamic_slice_in_dim(all_ids, (seq_at // half) * half, half, axis=1)
-    near_ids = near_ids.transpose(1, 3, 0, 2).reshape(half * tok_rows, n_head * head_count)
+    groups = [list(range(half)), list(range(half, n_seq))]
+    near_ids = lax.all_to_all(
+        jnp.broadcast_to(ids_t[None], (half,) + ids_t.shape),
+        "seq",
+        split_axis=0,
+        concat_axis=0,
+        axis_index_groups=groups,
+        tiled=True,
+    )
+    chips = 2 * jnp.arange(half, dtype=jnp.int32)
+    slot_heads = jnp.concatenate(
+        [plane * head_count + chips + at for plane in (head_at, 1 - head_at) for at in (core, 1 - core)]
+    )
 
     high, low = ids_t // 16, ids_t % 16
     id_rows = -(-2 * tok_rows // (16 * e_width)) * 16
@@ -192,19 +232,39 @@
         [x.transpose(1, 0, 2) for x in (queries, keys, values)] + [coded.reshape(head_count, id_rows, e_width)],
         axis=1,
     )
+    near_ids, packed = lax.optimization_barrier((near_ids, packed))
+    near_ids = near_ids.transpose(1, 0, 2).reshape(half, 2, half * tok_rows)
+    far_ids = lax.ppermute(near_ids, "head", swap_heads)
     moved = lax.all_to_all(packed, "seq", split_axis=0, concat_axis=0, tiled=True)
-
-    moved, out_weight = lax.optimization_barrier((moved, out_weight))
+    own = attend(moved, tok_rows)
+    own, far_ids = lax.optimization_barrier((own, far_ids))
+    slot_ids = [
+        lax.dynamic_index_in_dim(x, at, 1, keepdims=False).T for x in (near_ids, far_ids) for at in (core, 1 - core)
+    ]
+
+    same_core = [list(range(at, n_seq, 2)) for at in range(2)]
+    spread = jnp.broadcast_to(own[None], (half,) + own.shape)
+    first = lax.all_to_all(
+        spread, "seq", split_axis=0, concat_axis=0, axis_index_groups=same_core, tiled=True
+    )
+
     blocks = out_weight.reshape(rows, half, cols_each).transpose(1, 0, 2)
     blocks = jnp.concatenate([blocks, blocks], axis=0)
+    first, blocks, slot_ids = lax.optimization_barrier((first, blocks, slot_ids))
     weight = lax.all_to_all(blocks, "seq", split_axis=0, concat_axis=0, tiled=True)
     weight = weight.reshape(n_seq * rows, cols_each)
 
-    own = attend(moved, tok_rows)
-    attended = lax.all_gather(own, ("head", "seq"), axis=0, tiled=False)
-    near = lookup(near_ids, attended, weight, 2 * tok_rows)
-
-    groups = [list(range(half)), list(range(half, n_seq))]
+    third = lax.ppermute(first, "head", swap_heads)
+    second = lax.ppermute(first, "seq", swap_cores)
+    pieces = len(slot_ids)
+    tok_tile = 2 * tok_rows
+    features = expand(slot_ids[0], first, None, 0, pieces, tok_tile)
+    features = expand(slot_ids[1], second, features, 1, pieces, tok_tile)
+    features, third = lax.optimization_barrier((features, third))
+    fourth = lax.ppermute(third, "seq", swap_cores)
+    features = expand(slot_ids[2], third, features, 2, pieces, tok_tile)
+    features = expand(slot_ids[3], fourth, features, 3, pieces, tok_tile)
+    near = project(slot_heads, features, weight, 2 * tok_rows)
     mixed = lax.all_to_all(
         near.reshape(half, tok_rows, cols_each),
         "seq",
@@ -221,7 +281,8 @@
     tok_rows, head_count, e_width = queries.shape
     return (
         head_count == n_seq
-        and n_seq % 2 == 0
+        and lax.axis_size("head") == 2
+        and n_seq % 4 == 0
         and e_width == 128
         and tok_rows % e_width == 0
         and out_weight.shape[1] % (n_seq // 2 * 128) == 0

time: 250 us -> 214 us (0.86)
  blocking collectives: 184 us -> 24.4 us
  waiting for transfers between devices: 0.04 us -> 88 us
  starting transfers between devices: 3.72 us -> 33.8 us
  between operations: 13.5 us -> 0.16 us
  local copies, waits for them, and re-layouts: 5.36 us -> 14.1 us
  Pallas kernels: 40.3 us -> 48.3 us
    all_gather x1 -> x0, blocking collectives: 86.4 us -> none  [by_head(): all_ids = lax.all_gather(ids_t, ('head', 'seq'), axis=0, tiled=False)]
    all_to_all x1 -> x0, blocking collectives: 80.7 us -> none  [by_head(): lax.all_to_all(packed, 'seq', split_axis=0, concat_axis=0, tiled=True)]
    all_to_all x0 -> x3, waiting for transfers between devices: none -> 78.4 us  [the longest x1 58.8 us: by_head(): lax.all_to_all(packed, 'seq', split_axis=0, concat_axis=0, tiled=True)]
    all_to_all x0 -> x3, starting transfers between devices: none -> 26.6 us  [the longest x1 15.6 us: by_head(): lax.all_to_all(spread, 'seq', split_axis=0, concat_axis=0, axis_index_gro...]
    ppermute x0 -> x4, waiting for transfers between devices: none -> 9.69 us  [the longest x1 9.68 us: by_head(): third = lax.ppermute(first, 'head', swap_heads)]
    pallas_call x1 -> x5, Pallas kernels: 27.5 us -> 36.1 us  [the longest x4 27.1 us: expand(): pl.pallas_call(expand_kernel, out_shape=jax.ShapeDtypeStruct((pieces * he...]
    all_to_all x1, blocking collectives: 17 us -> 24.4 us  [by_head(): lax.all_to_all(near.reshape(half, tok_rows, cols_each), 'seq', split_axis...]
    dynamic_slice x1 -> x6, local copies, waits for them, and re-layouts: 0.02 us -> 5.6 us  [by_head(): lax.dynamic_index_in_dim(x, at, 1, keepdims=False)]
  transfers between devices with their start and end apart: 2 -> 8, of which waited for: 0 -> 4; matrix products, arithmetic and copies ran while one was open for 1% -> 6% of each run, Pallas kernels for 0% -> 18%
where the time goes in v4:
time: 214 us; the launch traced here: 213 us
  waiting for transfers between devices  88 us (41%)
  Pallas kernels  48.3 us (23%)
  starting transfers between devices  33.8 us (16%)
  blocking collectives  24.4 us (11%)
  local copies, waits for them, and re-layouts  14.1 us (7%)
  other arithmetic  4.14 us (2%)
    all_to_all x1, waiting for transfers between devices, by_head(): lax.all_to_all(packed, 'seq', split_axis=0, concat_axis=0, tiled=True)  58.8 us
    pallas_call x4, Pallas kernels, expand(): pl.pallas_call(expand_kernel, out_shape=jax.ShapeDtypeStruct((pieces * he...  27.1 us
    all_to_all x1, blocking collectives, by_head(): lax.all_to_all(near.reshape(half, tok_rows, cols_each), 'seq', split_axis...  24.4 us
    all_to_all x1, waiting for transfers between devices, by_head(): lax.all_to_all(spread, 'seq', split_axis=0, concat_axis=0, axis_index_gro...  19 us
    all_to_all x1, starting transfers between devices, by_head(): lax.all_to_all(spread, 'seq', split_axis=0, concat_axis=0, axis_index_gro...  15.6 us
    pallas_call x1, Pallas kernels, attend(): pl.pallas_call(lambda *refs: attend_kernel(tok_rows, *refs), out_shape=ja...  12.2 us
    ppermute x1, waiting for transfers between devices, by_head(): third = lax.ppermute(first, 'head', swap_heads)  9.68 us
    pallas_call x1, Pallas kernels, project(): pl.pallas_call(project_kernel, out_shape=jax.ShapeDtypeStruct((tokens, co...  8.97 us
  transfers between devices with their start and end apart: 8, of which 4 were waited for; matrix products, arithmetic and copies ran while one was open for 6% of the time, Pallas kernels for 18%

profile of v4, /device:TPU:0, one launch (start us, length us, event | category | flops | bytes accessed | tf_op | source)
XLA Modules:
  0.0 213.0 jit_solution(2768366933964211252)
XLA Ops:
  0.0 0.0 copy-start.5
  0.0 0.0 copy-start.6
  0.0 1.5 broadcast_in_dim.4
  1.5 5.3 %all-to-all-start = ((s32[8,16,256]{2,1,0:T(8,128)}), s32[8,16,256]{2,1,0:T(8,128)S(1)}, u32[]{:S(2)}, u32[]{:S(2)}) async-start(s32[8,16,256]{2,1,0:T(8,128)} %broadcast_in_dim.4), calls=%async_computation | async-start | bytes 262144 | tf_op jit(solution)/shard_map/all_to_all | solution.py:214
  6.8 0.7 fusion.4
  7.6 1.5 copy.41
  9.1 0.0 copy-done.5
  9.1 0.0 copy-done.6
  9.1 0.5 copy_bitcast_fusion
  9.6 1.8 pad_maximum_fusion
  11.4 0.6 all-to-all-done
  12.0 5.8 %all-to-all-start.1 = ((bf16[16,784,128]{2,1,0:T(8,128)(2,1)}), bf16[16,784,128]{2,1,0:T(8,128)(2,1)S(1)}, u32[]{:S(2)}, u32[]{:S(2)}) async-start(bf16[16,784,128]{2,1,0:T(8,128)(2,1)} %pad_maximum_fusion), calls=%async_computation.1 | async-start | bytes 6422528 | tf_op jit(solution)/shard_map/all_to_all | solution.py:238
  17.8 0.1 copy.26
  17.8 0.1 reshape.21
  17.9 1.6 collective-permute-start
  19.5 58.8 %all-to-all-done.1.refs_0_ = bf16[16,784,128]{2,1,0:T(8,128)(2,1)S(1)} async-done(((bf16[16,784,128]{2,1,0:T(8,128)(2,1)}), bf16[16,784,128]{2,1,0:T(8,128)(2,1)S(1)}, u32[]{:S(2)}, u32[]{:S(2)}) %all-to-all-start.1) | async-done | bytes 3211296 | tf_op jit(solution)/shard_map/all_to_all | solution.py:238
  78.3 12.2 %attend.1 = bf16[512,128]{1,0:T(8,128)(2,1)S(1)} custom-call(bf16[16,784,128]{2,1,0:T(8,128)(2,1)S(1)} %all-to-all-done.1.refs_0_), custom_call_target="tpu_custom_call" | custom-call | flops 2147483648 | bytes 3211264 | tf_op jit(solution)/shard_map/attend/pallas_call | solution.py:104
  90.4 0.0 copy-start.4
  90.4 0.0 collective-permute-done
  90.4 1.1 broadcast_in_dim.5
  91.6 15.6 %all-to-all-start.2 = ((bf16[8,512,128]{2,1,0:T(8,128)(2,1)}), bf16[8,512,128]{2,1,0:T(8,128)(2,1)S(1)}, u32[]{:S(2)}, u32[]{:S(2)}) async-start(bf16[8,512,128]{2,1,0:T(8,128)(2,1)} %broadcast_in_dim.5), calls=%async_computation.2 | async-start | bytes 2097152 | tf_op jit(solution)/shard_map/all_to_all | solution.py:247
  107.1 0.0 copy-done.4
  107.2 0.1 copy.40
  107.2 1.5 pad_maximum_fusion.1
  108.8 0.1 constant_dynamic-slice_fusion.2
  108.9 1.4 copy.29
  110.2 1.3 copy.28
  111.6 0.1 constant_dynamic-slice_fusion
  111.7 1.3 copy.31
  113.0 1.3 copy.30
  114.4 19.0 %all-to-all-done.2.attended_ref = bf16[8,512,128]{2,1,0:T(8,128)(2,1)S(1)} async-done(((bf16[8,512,128]{2,1,0:T(8,128)(2,1)}), bf16[8,512,128]{2,1,0:T(8,128)(2,1)S(1)}, u32[]{:S(2)}, u32[]{:S(2)}) %all-to-all-start.2) | async-done | bytes 1048608 | tf_op jit(solution)/shard_map/all_to_all | solution.py:247
  133.4 3.7 %all-to-all-start.3 = ((bf16[16,256,256]{2,1,0:T(8,128)(2,1)}), bf16[16,256,256]{2,1,0:T(8,128)(2,1)S(1)}, u32[]{:S(2)}, u32[]{:S(2)}) async-start(bf16[16,256,256]{2,1,0:T(8,128)(2,1)} %pad_maximum_fusion.1), calls=%async_computation.3 | async-start | bytes 4194304 | tf_op jit(solution)/shard_map/all_to_all | solution.py:254
  137.2 0.0 copy-start.2
  137.2 0.5 collective-permute-start.1
  137.6 1.5 collective-permute-start.2
  139.1 0.0 copy-start.3
  139.1 1.2 copy-done.3
  140.3 6.4 %expand.4.refs_0_ = bf16[32,2048,128]{2,1,0:T(8,128)(2,1)} custom-call(s32[2048,8]{1,0:T(8,128)S(1)} %bitcast.42, bf16[8,512,128]{2,1,0:T(8,128)(2,1)S(1)} %all-to-all-done.2.attended_ref), custom_call_target="tpu_custom_call" | custom-call | flops 4294967296 | bytes 5242880 | tf_op jit(solution)/shard_map/expand/pallas_call | solution.py:142
  146.7 0.0 collective-permute-done.1.attended_ref
  146.7 0.0 copy-done.2
  146.7 6.5 %expand.5.refs_0_ = bf16[32,2048,128]{2,1,0:T(8,128)(2,1)} custom-call(s32[2048,8]{1,0:T(8,128)S(1)} %bitcast.41, bf16[8,512,128]{2,1,0:T(8,128)(2,1)S(1)} %collective-permute-done.1.attended_ref, bf16[32,2048,128]{2,1,0:T(8,128)(2,1)} %expand.4.refs_0_), custom_call_target="tpu_custom_call", output_to_operand_aliasing={{}: (2, {})} | custom-call | flops 4294967296 | bytes 5242880 | tf_op jit(solution)/shard_map/expand/pallas_call | solution.py:142
  153.2 9.7 %collective-permute-done.2.attended_ref = bf16[8,512,128]{2,1,0:T(8,128)(2,1)} collective-permute-done((bf16[8,512,128]{2,1,0:T(8,128)(2,1)S(1)}, bf16[8,512,128]{2,1,0:T(8,128)(2,1)}, u32[]{:S(2)}, u32[]{:S(2)}) %collective-permute-start.2) | collective-permute-done | bytes 1048608 | tf_op jit(solution)/shard_map/ppermute | solution.py:257
  162.9 0.0 collective-permute-start.3
  162.9 0.1 pad_add_fusion.heads_ref
  163.0 0.0 copy-start.1
  163.0 1.2 copy-done.1
  164.2 0.0 copy-start
  164.2 7.8 %expand.6.refs_0_ = bf16[32,2048,128]{2,1,0:T(8,128)(2,1)} custom-call(s32[2048,8]{1,0:T(8,128)S(1)} %bitcast.40, bf16[8,512,128]{2,1,0:T(8,128)(2,1)} %collective-permute-done.2.attended_ref, bf16[32,2048,128]{2,1,0:T(8,128)(2,1)} %expand.5.refs_0_), custom_call_target="tpu_custom_call", output_to_operand_aliasing={{}: (2, {})} | custom-call | flops 4294967296 | bytes 5242880 | tf_op jit(solution)/shard_map/expand/pallas_call | solution.py:142
  172.0 0.0 collective-permute-done.3.attended_ref
  172.0 0.0 copy-done
  172.0 6.5 %expand.7.features_ref = bf16[32,2048,128]{2,1,0:T(8,128)(2,1)} custom-call(s32[2048,8]{1,0:T(8,128)S(1)} %bitcast.39, bf16[8,512,128]{2,1,0:T(8,128)(2,1)S(1)} %collective-permute-done.3.attended_ref, bf16[32,2048,128]{2,1,0:T(8,128)(2,1)} %expand.6.refs_0_), custom_call_target="tpu_custom_call", output_to_operand_aliasing={{}: (2, {})} | custom-call | flops 4294967296 | bytes 5242880 | tf_op jit(solution)/shard_map/expand/pallas_call | solution.py:142
  178.5 0.0 all-to-all-done.3
  178.5 9.0 %project.1 = bf16[2048,256]{1,0:T(8,128)(2,1)S(1)} custom-call(s32[32]{0:T(128)S(1)} %pad_add_fusion.heads_ref, bf16[32,2048,128]{2,1,0:T(8,128)(2,1)} %expand.7.features_ref, bf16[4096,256]{1,0:T(8,128)(2,1)S(1)} %bitcast.38), custom_call_target="tpu_custom_call" | custom-call | flops 4294967296 | bytes 19922944 | tf_op jit(solution)/shard_map/project/pallas_call | solution.py:178
  187.5 24.4 %all_to_all.25 = bf16[8,256,256]{2,1,0:T(8,128)(2,1)S(1)} all-to-all(bf16[8,256,256]{2,1,0:T(8,128)(2,1)S(1)} %bitcast.43), channel_id=1, replica_groups={{0,2,4,6,8,10,12,14},{16,18,20,22,24,26,28,30},{1,3,5,7,9,11,13,15},{17..., dimensions={0} | all-to-all | bytes 2097152 | tf_op jit(solution)/shard_map/all_to_all | solution.py:268
  211.9 1.1 copy.34
  (4 shorter events, 0.0 us)
Async XLA Ops:
  0.0 9.1 %copy-start.5 = (bf16[256,16,128]{2,1,0:T(8,128)(2,1)S(1)}, bf16[256,16,128]{2,1,0:T(8,128)(2,1)}, u32[]{:S(2)}) copy-start(bf16[256,16,128]{2,1,0:T(8,128)(2,1)} %param.7) | copy-start | bytes 3145732
  0.0 9.1 %copy-start.6 = (bf16[256,16,128]{2,1,0:T(8,128)(2,1)S(1)}, bf16[256,16,128]{2,1,0:T(8,128)(2,1)}, u32[]{:S(2)}) copy-start(bf16[256,16,128]{2,1,0:T(8,128)(2,1)} %param.6) | copy-start | bytes 3145732
  1.5 10.4 %all-to-all-start = ((s32[8,16,256]{2,1,0:T(8,128)}), s32[8,16,256]{2,1,0:T(8,128)S(1)}, u32[]{:S(2)}, u32[]{:S(2)}) async-start(s32[8,16,256]{2,1,0:T(8,128)} %broadcast_in_dim.4), calls=%async_computation | async-start | bytes 262144 | tf_op jit(solution)/shard_map/all_to_all | solution.py:214
  12.0 66.3 %all-to-all-start.1 = ((bf16[16,784,128]{2,1,0:T(8,128)(2,1)}), bf16[16,784,128]{2,1,0:T(8,128)(2,1)S(1)}, u32[]{:S(2)}, u32[]{:S(2)}) async-start(bf16[16,784,128]{2,1,0:T(8,128)(2,1)} %pad_maximum_fusion), calls=%async_computation.1 | async-start | bytes 6422528 | tf_op jit(solution)/shard_map/all_to_all | solution.py:238
  17.9 72.5 %collective-permute-start = (s32[8,2,2048]{2,1,0:T(2,128)S(1)}, s32[8,2,2048]{2,1,0:T(2,128)S(1)}, u32[]{:S(2)}, u32[]{:S(2)}) collective-permute-start(s32[8,2,2048]{2,1,0:T(2,128)S(1)} %reshape.21), channel_id=1, source_target_pairs={{0,1},{1,0},{2,3},{3,2},{4,5},{5,4},{6,7},{7,6},{8,9},{9,8},{10,11... | collective-permute-start | bytes 393224 | tf_op jit(solution)/shard_map/ppermute | solution.py:237
  90.4 16.7 %copy-start.4 = (bf16[256,2048]{1,0:T(8,128)(2,1)S(1)}, bf16[256,2048]{1,0:T(8,128)(2,1)}, u32[]{:S(2)}) copy-start(bf16[256,2048]{1,0:T(8,128)(2,1)} %param.9) | copy-start | bytes 3145732
  91.6 41.8 %all-to-all-start.2 = ((bf16[8,512,128]{2,1,0:T(8,128)(2,1)}), bf16[8,512,128]{2,1,0:T(8,128)(2,1)S(1)}, u32[]{:S(2)}, u32[]{:S(2)}) async-start(bf16[8,512,128]{2,1,0:T(8,128)(2,1)} %broadcast_in_dim.5), calls=%async_computation.2 | async-start | bytes 2097152 | tf_op jit(solution)/shard_map/all_to_all | solution.py:247
  133.4 45.1 %all-to-all-start.3 = ((bf16[16,256,256]{2,1,0:T(8,128)(2,1)}), bf16[16,256,256]{2,1,0:T(8,128)(2,1)S(1)}, u32[]{:S(2)}, u32[]{:S(2)}) async-start(bf16[16,256,256]{2,1,0:T(8,128)(2,1)} %pad_maximum_fusion.1), calls=%async_computation.3 | async-start | bytes 4194304 | tf_op jit(solution)/shard_map/all_to_all | solution.py:254
  137.2 9.6 %copy-start.2 = (s32[8,1,2048]{0,2,1:T(8,128)S(1)}, s32[8,1,2048]{0,2,1:T(8,128)}, u32[]{:S(2)}) copy-start(s32[8,1,2048]{0,2,1:T(8,128)} %copy.29) | copy-start | bytes 196612
  137.2 9.6 %collective-permute-start.1 = (bf16[8,512,128]{2,1,0:T(8,128)(2,1)S(1)}, bf16[8,512,128]{2,1,0:T(8,128)(2,1)S(1)}, u32[]{:S(2)}, u32[]{:S(2)}) collective-permute-start(bf16[8,512,128]{2,1,0:T(8,128)(2,1)S(1)} %all-to-all-done.2.attended_ref), channel_id=1, source_target_pairs={{0,2},{2,0},{4,6},{6,4},{8,10},{10,8},{12,14},{14,12},{16,18},{18,... | collective-permute-start | bytes 3145736 | tf_op jit(solution)/shard_map/ppermute | solution.py:258
  137.6 25.3 %collective-permute-start.2 = (bf16[8,512,128]{2,1,0:T(8,128)(2,1)S(1)}, bf16[8,512,128]{2,1,0:T(8,128)(2,1)}, u32[]{:S(2)}, u32[]{:S(2)}) collective-permute-start(bf16[8,512,128]{2,1,0:T(8,128)(2,1)S(1)} %all-to-all-done.2.attended_ref), channel_id=1, source_target_pairs={{0,1},{1,0},{2,3},{3,2},{4,5},{5,4},{6,7},{7,6},{8,9},{9,8},{10,11... | collective-permute-start | bytes 3145736 | tf_op jit(solution)/shard_map/ppermute | solution.py:257
  139.1 1.2 copy-start.3
  162.9 9.1 %collective-permute-start.3 = (bf16[8,512,128]{2,1,0:T(8,128)(2,1)}, bf16[8,512,128]{2,1,0:T(8,128)(2,1)S(1)}, u32[]{:S(2)}, u32[]{:S(2)}) collective-permute-start(bf16[8,512,128]{2,1,0:T(8,128)(2,1)} %collective-permute-done.2.attended_ref), channel_id=1, source_target_pairs={{0,2},{2,0},{4,6},{6,4},{8,10},{10,8},{12,14},{14,12},{16,18},{18,... | collective-permute-start | bytes 3145736 | tf_op jit(solution)/shard_map/ppermute | solution.py:264
  163.0 1.2 copy-start.1
  164.2 7.8 %copy-start = (s32[8,1,2048]{0,2,1:T(8,128)S(1)}, s32[8,1,2048]{0,2,1:T(8,128)}, u32[]{:S(2)}) copy-start(s32[8,1,2048]{0,2,1:T(8,128)} %copy.31) | copy-start | bytes 196612

commit v5 on v4

--- a/solution.py
+++ b/solution.py
@@ -160,21 +160,25 @@
     )(ids, attended, *held)
 
 
-def project_kernel(heads_ref, features_ref, weight_ref, out_ref):
-    heads, _, e_width = features_ref.shape
+def project_kernel(places_ref, features_ref, early_ref, late_ref, out_ref):
+    heads = features_ref.shape[0]
+    each = heads // 4
+    plane_at, core = places_ref[0], places_ref[1]
     total = None
-    for slot in range(0, heads, 2):
-        left = jnp.concatenate([features_ref[slot], features_ref[slot + 1]], axis=1)
-        starts = [pl.multiple_of(heads_ref[slot + j] * e_width, e_width) for j in range(2)]
-        right = jnp.concatenate([weight_ref[pl.ds(at, e_width), :] for at in starts], axis=0)
-        term = jnp.dot(left, right, preferred_element_type=jnp.float32)
-        total = term if total is None else total + term
+    for plane in range(2):
+        first = (plane_at + plane - 2 * plane * plane_at) * each
+        for i in range(each):
+            slots = [(2 * plane + at) * each + i for at in (core, 1 - core)]
+            left = jnp.concatenate([features_ref[at] for at in slots], axis=1)
+            right = jnp.concatenate([early_ref[first + i], late_ref[first + i]], axis=0)
+            term = jnp.dot(left, right, preferred_element_type=jnp.float32)
+            total = term if total is None else total + term
     out_ref[...] = total.astype(jnp.bfloat16)
 
 
-def project(slot_heads, features, weight, tok_tile):
+def project(places, features, early, late, tok_tile):
     heads, tokens, e_width = features.shape
-    cols = weight.shape[1]
+    cols = early.shape[2]
     return pl.pallas_call(
         project_kernel,
         out_shape=jax.ShapeDtypeStruct((tokens, cols), jnp.bfloat16),
@@ -183,18 +187,23 @@
             grid=(tokens // tok_tile,),
             in_specs=[
                 pl.BlockSpec((heads, tok_tile, e_width), lambda i, _: (0, i, 0)),
-                pl.BlockSpec(weight.shape, lambda i, _: (0, 0)),
+                pl.BlockSpec(early.shape, lambda i, _: (0, 0, 0)),
+                pl.BlockSpec(late.shape, lambda i, _: (0, 0, 0)),
             ],
             out_specs=pl.BlockSpec((tok_tile, cols), lambda i, _: (i, 0)),
         ),
         compiler_params=pltpu.CompilerParams(vmem_limit_bytes=50 * 2**20),
         cost_estimate=pl.CostEstimate(
-            flops=2 * tokens * weight.size,
-            bytes_accessed=2 * (features.size + weight.size + tokens * cols),
+            flops=2 * tokens * heads * e_width * cols,
+            bytes_accessed=2 * (features.size + heads * e_width * cols + tokens * cols),
             transcendentals=0,
         ),
         name="project",
-    )(slot_heads, features, weight)
+    )(places, features, early, late)
+
+
+def by_slot(ids, core):
+    return [lax.dynamic_index_in_dim(ids, at, 1, keepdims=False).T for at in (core, 1 - core)]
 
 
 def by_head(queries, keys, values, cluster_ids, out_weight):
@@ -207,40 +216,47 @@
     head_at = lax.axis_index("head")
     core = lax.rem(seq_at, 2)
     swap_heads = [(0, 1), (1, 0)]
+    swap_halves = [(i, (i + half) % n_seq) for i in range(n_seq)]
     swap_cores = [(i, i ^ 1) for i in range(n_seq)]
 
+    groups = [list(range(half)), list(range(half, n_seq))]
     ids_t = cluster_ids.T
-    groups = [list(range(half)), list(range(half, n_seq))]
-    near_ids = lax.all_to_all(
-        jnp.broadcast_to(ids_t[None], (half,) + ids_t.shape),
+    high, low = (ids_t // 16).astype(jnp.bfloat16), (ids_t % 16).astype(jnp.bfloat16)
+
+    cut = rows // 4 // 16 * 16
+    ahead = out_weight[:cut].reshape(cut, half, cols_each).transpose(1, 0, 2)
+    coded = jnp.broadcast_to(jnp.concatenate([high, low], axis=0)[None], (half, 2 * head_count, tok_rows))
+    early = lax.all_to_all(
+        jnp.concatenate([ahead, coded], axis=1),
         "seq",
         split_axis=0,
         concat_axis=0,
         axis_index_groups=groups,
         tiled=True,
     )
-    chips = 2 * jnp.arange(half, dtype=jnp.int32)
-    slot_heads = jnp.concatenate(
-        [plane * head_count + chips + at for plane in (head_at, 1 - head_at) for at in (core, 1 - core)]
-    )
-
-    high, low = ids_t // 16, ids_t % 16
+
     id_rows = -(-2 * tok_rows // (16 * e_width)) * 16
-    coded = jnp.concatenate([high, low], axis=1).astype(jnp.bfloat16)
+    coded = jnp.concatenate([high, low], axis=1)
     coded = jnp.pad(coded, ((0, 0), (0, id_rows * e_width - 2 * tok_rows)))
     packed = jnp.concatenate(
         [x.transpose(1, 0, 2) for x in (queries, keys, values)] + [coded.reshape(head_count, id_rows, e_width)],
         axis=1,
     )
-    near_ids, packed = lax.optimization_barrier((near_ids, packed))
+    early, packed = lax.optimization_barrier((early, packed))
+    coded = early[:, cut:]
+    early = early[:, :cut]
+    moved = lax.all_to_all(packed, "seq", split_axis=0, concat_axis=0, tiled=True)
+    moved, early = lax.optimization_barrier((moved, early))
+    crossed = lax.ppermute(early, "seq", swap_halves)
+    own = attend(moved, tok_rows)
+    own, crossed, coded, behind = lax.optimization_barrier((own, crossed, coded, out_weight[cut:]))
+    coded = coded.astype(jnp.int32)
+    near_ids = coded[:, :head_count] * 16 + coded[:, head_count:]
     near_ids = near_ids.transpose(1, 0, 2).reshape(half, 2, half * tok_rows)
     far_ids = lax.ppermute(near_ids, "head", swap_heads)
-    moved = lax.all_to_all(packed, "seq", split_axis=0, concat_axis=0, tiled=True)
-    own = attend(moved, tok_rows)
-    own, far_ids = lax.optimization_barrier((own, far_ids))
-    slot_ids = [
-        lax.dynamic_index_in_dim(x, at, 1, keepdims=False).T for x in (near_ids, far_ids) for at in (core, 1 - core)
-    ]
+    slot_ids = by_slot(near_ids, core)
+    late = behind.reshape(rows - cut, half, cols_each).transpose(1, 0, 2)
+    late = jnp.concatenate([late, late], axis=0)
 
     same_core = [list(range(at, n_seq, 2)) for at in range(2)]
     spread = jnp.broadcast_to(own[None], (half,) + own.shape)
@@ -248,11 +264,9 @@
         spread, "seq", split_axis=0, concat_axis=0, axis_index_groups=same_core, tiled=True
     )
 
-    blocks = out_weight.reshape(rows, half, cols_each).transpose(1, 0, 2)
-    blocks = jnp.concatenate([blocks, blocks], axis=0)
-    first, blocks, slot_ids = lax.optimization_barrier((first, blocks, slot_ids))
-    weight = lax.all_to_all(blocks, "seq", split_axis=0, concat_axis=0, tiled=True)
-    weight = weight.reshape(n_seq * rows, cols_each)
+    first, late, slot_ids, far_ids = lax.optimization_barrier((first, late, slot_ids, far_ids))
+    slot_ids = slot_ids + by_slot(far_ids, core)
+    late = lax.all_to_all(late, "seq", split_axis=0, concat_axis=0, tiled=True)
 
     third = lax.ppermute(first, "head", swap_heads)
     second = lax.ppermute(first, "seq", swap_cores)
@@ -264,7 +278,12 @@
     fourth = lax.ppermute(third, "seq", swap_cores)
     features = expand(slot_ids[2], third, features, 2, pieces, tok_tile)
     features = expand(slot_ids[3], fourth, features, 3, pieces, tok_tile)
-    near = project(slot_heads, features, weight, 2 * tok_rows)
+    in_lower = seq_at < half
+    early = jnp.where(
+        in_lower, jnp.concatenate([early, crossed], axis=0), jnp.concatenate([crossed, early], axis=0)
+    )
+    places = jnp.stack([head_at, core]).astype(jnp.int32)
+    near = project(places, features, early, late, tok_tile)
     mixed = lax.all_to_all(
         near.reshape(half, tok_rows, cols_each),
         "seq",
@@ -282,9 +301,12 @@
     return (
         head_count == n_seq
         and lax.axis_size("head") == 2
-        and n_seq % 4 == 0
+        and n_seq >= 4
+        and n_seq & (n_seq - 1) == 0
         and e_width == 128
         and tok_rows % e_width == 0
+        and out_weight.shape[0] == 2 * e_width
+        and out_weight.shape[1] == n_seq // 2 * tok_rows
         and out_weight.shape[1] % (n_seq // 2 * 128) == 0
     )
 

time: 214 us -> 219 us (1.023)
  waiting for transfers between devices: 88 us -> 93.9 us
  blocking collectives: 24.4 us -> 18.6 us
    ppermute x0 -> x1, starting transfers between devices: none -> 13.8 us  [by_head(): crossed = lax.ppermute(early, 'seq', swap_halves)]
    all_to_all x1, starting transfers between devices: 15.6 us -> 3.69 us  [by_head(): lax.all_to_all(spread, 'seq', split_axis=0, concat_axis=0, axis_index_gro...]
    all_to_all x1, blocking collectives: 24.4 us -> 18.6 us  [by_head(): lax.all_to_all(near.reshape(half, tok_rows, cols_each), 'seq', split_axis...]
    all_to_all x2, waiting for transfers between devices: 0.56 us -> 4.82 us  [the longest x1 4.82 us: by_head(): lax.all_to_all(jnp.concatenate([ahead, coded], axis=1), 'seq', split_axis...]
  transfers between devices with their start and end apart: 8 -> 9, of which waited for: 4 -> 4; matrix products, arithmetic and copies ran while one was open for 6% -> 5% of each run, Pallas kernels for 18% -> 19%
where the time goes in v5:
time: 219 us; the launch traced here: 218 us
  waiting for transfers between devices  93.9 us (43%)
  Pallas kernels  49.5 us (23%)
  starting transfers between devices  34.9 us (16%)
  blocking collectives  18.6 us (8%)
  local copies, waits for them, and re-layouts  14.8 us (7%)
  other arithmetic  6.01 us (3%)
    all_to_all x1, waiting for transfers between devices, by_head(): lax.all_to_all(packed, 'seq', split_axis=0, concat_axis=0, tiled=True)  59.5 us
    pallas_call x4, Pallas kernels, expand(): pl.pallas_call(expand_kernel, out_shape=jax.ShapeDtypeStruct((pieces * he...  28.3 us
    all_to_all x1, waiting for transfers between devices, by_head(): lax.all_to_all(spread, 'seq', split_axis=0, concat_axis=0, axis_index_gro...  19.9 us
    all_to_all x1, blocking collectives, by_head(): lax.all_to_all(near.reshape(half, tok_rows, cols_each), 'seq', split_axis...  18.6 us
    ppermute x1, starting transfers between devices, by_head(): crossed = lax.ppermute(early, 'seq', swap_halves)  13.8 us
    pallas_call x1, Pallas kernels, attend(): pl.pallas_call(lambda *refs: attend_kernel(tok_rows, *refs), out_shape=ja...  12.1 us
    ppermute x1, waiting for transfers between devices, by_head(): third = lax.ppermute(first, 'head', swap_heads)  9.63 us
    pallas_call x1, Pallas kernels, project(): pl.pallas_call(project_kernel, out_shape=jax.ShapeDtypeStruct((tokens, co...  8.97 us
  transfers between devices with their start and end apart: 9, of which 4 were waited for; matrix products, arithmetic and copies ran while one was open for 5% of the time, Pallas kernels for 19%

profile of v5, /device:TPU:0, one launch (start us, length us, event | category | flops | bytes accessed | tf_op | source)
XLA Modules:
  0.0 218.0 jit_solution(17602737900796408864)
XLA Ops:
  0.0 0.0 copy-start.4
  0.0 0.0 copy-start.6
  0.0 0.0 copy-start.5
  0.0 0.9 fusion.5
  0.9 1.0 slice.18
  2.0 0.8 pad_maximum_fusion.2
  2.8 5.3 %all-to-all-start = ((bf16[8,96,256]{2,1,0:T(8,128)(2,1)}), bf16[8,96,256]{2,1,0:T(8,128)(2,1)S(1)}, u32[]{:S(2)}, u32[]{:S(2)}) async-start(bf16[8,96,256]{2,1,0:T(8,128)(2,1)} %pad_maximum_fusion.2), calls=%async_computation | async-start | bytes 786432 | tf_op jit(solution)/shard_map/all_to_all | solution.py:229
  8.0 0.0 copy-done.4
  8.1 0.3 copy.33
  8.3 0.0 copy-done.6
  8.3 0.0 copy-done.5
  8.4 0.5 copy_bitcast_fusion
  8.9 1.8 pad_maximum_fusion
  10.7 4.8 %all-to-all-done = bf16[8,96,256]{2,1,0:T(8,128)(2,1)S(1)} async-done(((bf16[8,96,256]{2,1,0:T(8,128)(2,1)}), bf16[8,96,256]{2,1,0:T(8,128)(2,1)S(1)}, u32[]{:S(2)}, u32[]{:S(2)}) %all-to-all-start) | async-done | bytes 393248 | tf_op jit(solution)/shard_map/all_to_all | solution.py:229
  15.5 0.7 copy-done.3
  16.3 4.9 %all-to-all-start.1 = ((bf16[16,784,128]{2,1,0:T(8,128)(2,1)}), bf16[16,784,128]{2,1,0:T(8,128)(2,1)S(1)}, u32[]{:S(2)}, u32[]{:S(2)}) async-start(bf16[16,784,128]{2,1,0:T(8,128)(2,1)} %pad_maximum_fusion), calls=%async_computation.1 | async-start | bytes 6422528 | tf_op jit(solution)/shard_map/all_to_all | solution.py:248
  21.1 1.0 slice.19
  22.1 59.5 %all-to-all-done.1.refs_0_ = bf16[16,784,128]{2,1,0:T(8,128)(2,1)S(1)} async-done(((bf16[16,784,128]{2,1,0:T(8,128)(2,1)}), bf16[16,784,128]{2,1,0:T(8,128)(2,1)S(1)}, u32[]{:S(2)}, u32[]{:S(2)}) %all-to-all-start.1) | async-done | bytes 3211296 | tf_op jit(solution)/shard_map/all_to_all | solution.py:248
  81.6 13.8 %collective-permute-start = (bf16[8,64,256]{2,1,0:T(8,128)(2,1)S(1)}, bf16[8,64,256]{2,1,0:T(8,128)(2,1)S(1)}, u32[]{:S(2)}, u32[]{:S(2)}) collective-permute-start(bf16[8,64,256]{2,1,0:T(8,128)(2,1)S(1)} %slice.19), channel_id=1, source_target_pairs={{0,16},{2,18},{4,20},{6,22},{8,24},{10,26},{12,28},{14,30},{16,0},... | collective-permute-start | bytes 786440 | tf_op jit(solution)/shard_map/ppermute | solution.py:250
  95.5 12.1 %attend.1 = bf16[512,128]{1,0:T(8,128)(2,1)S(1)} custom-call(bf16[16,784,128]{2,1,0:T(8,128)(2,1)S(1)} %all-to-all-done.1.refs_0_), custom_call_target="tpu_custom_call" | custom-call | flops 2147483648 | bytes 3211264 | tf_op jit(solution)/shard_map/attend/pallas_call | solution.py:104
  107.6 0.0 slice-start.1
  107.6 0.0 collective-permute-done
  107.7 0.0 copy-start.7
  107.7 0.7 copy-done.7
  108.3 1.1 broadcast_in_dim.5
  109.4 3.7 %all-to-all-start.2 = ((bf16[8,512,128]{2,1,0:T(8,128)(2,1)}), bf16[8,512,128]{2,1,0:T(8,128)(2,1)S(1)}, u32[]{:S(2)}, u32[]{:S(2)}) async-start(bf16[8,512,128]{2,1,0:T(8,128)(2,1)} %broadcast_in_dim.5), calls=%async_computation.2 | async-start | bytes 2097152 | tf_op jit(solution)/shard_map/all_to_all | solution.py:263
  113.1 0.0 slice-done.1
  113.2 0.1 copy.18
  113.3 0.1 reshape.23
  113.4 1.6 collective-permute-start.1
  115.0 0.1 constant_dynamic-slice_fusion.2
  115.1 1.3 copy.19
  116.4 1.3 copy.20
  117.8 0.0 slice-done
  117.8 0.1 copy.34
  117.8 1.3 pad_maximum_fusion.1
  119.2 0.0 collective-permute-done.1
  119.2 19.9 %all-to-all-done.2.attended_ref = bf16[8,512,128]{2,1,0:T(8,128)(2,1)S(1)} async-done(((bf16[8,512,128]{2,1,0:T(8,128)(2,1)}), bf16[8,512,128]{2,1,0:T(8,128)(2,1)S(1)}, u32[]{:S(2)}, u32[]{:S(2)}) %all-to-all-start.2) | async-done | bytes 1048608 | tf_op jit(solution)/shard_map/all_to_all | solution.py:263
  139.1 3.7 %all-to-all-start.3 = ((bf16[16,192,256]{2,1,0:T(8,128)(2,1)}), bf16[16,192,256]{2,1,0:T(8,128)(2,1)S(1)}, u32[]{:S(2)}, u32[]{:S(2)}) async-start(bf16[16,192,256]{2,1,0:T(8,128)(2,1)} %pad_maximum_fusion.1), calls=%async_computation.3 | async-start | bytes 3145728 | tf_op jit(solution)/shard_map/all_to_all | solution.py:269
  142.9 0.0 copy-start
  142.9 0.5 collective-permute-start.2
  143.3 1.5 collective-permute-start.3
  144.8 1.2 copy-done.1
  146.1 6.4 %expand.4.refs_0_ = bf16[32,2048,128]{2,1,0:T(8,128)(2,1)} custom-call(s32[2048,8]{1,0:T(8,128)S(1)} %bitcast.71, bf16[8,512,128]{2,1,0:T(8,128)(2,1)S(1)} %all-to-all-done.2.attended_ref), custom_call_target="tpu_custom_call" | custom-call | flops 4294967296 | bytes 5242880 | tf_op jit(solution)/shard_map/expand/pallas_call | solution.py:142
  152.5 0.0 copy-done.8
  152.5 0.0 collective-permute-done.2.attended_ref
  152.5 0.0 copy-done
  152.5 6.5 %expand.5.refs_0_ = bf16[32,2048,128]{2,1,0:T(8,128)(2,1)} custom-call(s32[2048,8]{1,0:T(8,128)S(1)} %bitcast.70, bf16[8,512,128]{2,1,0:T(8,128)(2,1)S(1)} %collective-permute-done.2.attended_ref, bf16[32,2048,128]{2,1,0:T(8,128)(2,1)} %expand.4.refs_0_), custom_call_target="tpu_custom_call", output_to_operand_aliasing={{}: (2, {})} | custom-call | flops 4294967296 | bytes 5242880 | tf_op jit(solution)/shard_map/expand/pallas_call | solution.py:142
  159.0 9.6 %collective-permute-done.3.attended_ref = bf16[8,512,128]{2,1,0:T(8,128)(2,1)} collective-permute-done((bf16[8,512,128]{2,1,0:T(8,128)(2,1)S(1)}, bf16[8,512,128]{2,1,0:T(8,128)(2,1)}, u32[]{:S(2)}, u32[]{:S(2)}) %collective-permute-start.3) | collective-permute-done | bytes 1048608 | tf_op jit(solution)/shard_map/ppermute | solution.py:271
  168.6 0.0 collective-permute-start.4
  168.6 0.1 pad_add_fusion.places_ref
  168.7 1.1 maximum_select_fusion.early_ref
  169.8 1.1 constant_dynamic-slice_fusion
  170.9 1.3 copy.22
  172.3 0.3 copy.21
  172.6 0.0 copy-start.2
  172.6 1.2 copy-done.2
  173.8 7.7 %expand.6.refs_0_ = bf16[32,2048,128]{2,1,0:T(8,128)(2,1)} custom-call(s32[2048,8]{1,0:T(8,128)S(1)} %bitcast.73, bf16[8,512,128]{2,1,0:T(8,128)(2,1)} %collective-permute-done.3.attended_ref, bf16[32,2048,128]{2,1,0:T(8,128)(2,1)} %expand.5.refs_0_), custom_call_target="tpu_custom_call", output_to_operand_aliasing={{}: (2, {})} | custom-call | flops 4294967296 | bytes 5242880 | tf_op jit(solution)/shard_map/expand/pallas_call | solution.py:142
  181.6 0.0 collective-permute-done.4.attended_ref
  181.6 7.7 %expand.7.features_ref = bf16[32,2048,128]{2,1,0:T(8,128)(2,1)} custom-call(s32[2048,8]{1,0:T(8,128)S(1)} %bitcast.72, bf16[8,512,128]{2,1,0:T(8,128)(2,1)} %collective-permute-done.4.attended_ref, bf16[32,2048,128]{2,1,0:T(8,128)(2,1)} %expand.6.refs_0_), custom_call_target="tpu_custom_call", output_to_operand_aliasing={{}: (2, {})} | custom-call | flops 4294967296 | bytes 5242880 | tf_op jit(solution)/shard_map/expand/pallas_call | solution.py:142
  189.3 0.0 all-to-all-done.3.late_ref
  189.3 9.0 %project.1 = bf16[2048,256]{1,0:T(8,128)(2,1)S(1)} custom-call(s32[2]{0:T(128)S(1)} %pad_add_fusion.places_ref, bf16[32,2048,128]{2,1,0:T(8,128)(2,1)} %expand.7.features_ref, bf16[16,64,256]{2,1,0:T(8,128)(2,1)S(1)} %maximum_select_fusion.early_ref, bf16[16,192,256]{2,1,0:T(8,128)(2,1)S(1)} %all-to-all-done.3.late_ref), custom_call_target="tpu_custom_call" | custom-call | flops 4294967296 | bytes 19922944 | tf_op jit(solution)/shard_map/project/pallas_call | solution.py:182
  198.3 18.6 %all_to_all.25 = bf16[8,256,256]{2,1,0:T(8,128)(2,1)S(1)} all-to-all(bf16[8,256,256]{2,1,0:T(8,128)(2,1)S(1)} %bitcast.74), channel_id=1, replica_groups={{0,2,4,6,8,10,12,14},{16,18,20,22,24,26,28,30},{1,3,5,7,9,11,13,15},{17..., dimensions={0} | all-to-all | bytes 2097152 | tf_op jit(solution)/shard_map/all_to_all | solution.py:287
  216.9 1.1 copy.26
  (11 shorter events, 0.1 us)
Async XLA Ops:
  0.0 8.1 %copy-start.4 = (bf16[256,16,128]{2,1,0:T(8,128)(2,1)S(1)}, bf16[256,16,128]{2,1,0:T(8,128)(2,1)}, u32[]{:S(2)}) copy-start(bf16[256,16,128]{2,1,0:T(8,128)(2,1)} %param.5) | copy-start | bytes 3145732
  0.0 8.3 %copy-start.6 = (bf16[256,16,128]{2,1,0:T(8,128)(2,1)S(1)}, bf16[256,16,128]{2,1,0:T(8,128)(2,1)}, u32[]{:S(2)}) copy-start(bf16[256,16,128]{2,1,0:T(8,128)(2,1)} %param.6) | copy-start | bytes 3145732
  0.0 8.3 %copy-start.5 = (bf16[256,16,128]{2,1,0:T(8,128)(2,1)S(1)}, bf16[256,16,128]{2,1,0:T(8,128)(2,1)}, u32[]{:S(2)}) copy-start(bf16[256,16,128]{2,1,0:T(8,128)(2,1)} %param.7) | copy-start | bytes 3145732
  2.8 12.7 %all-to-all-start = ((bf16[8,96,256]{2,1,0:T(8,128)(2,1)}), bf16[8,96,256]{2,1,0:T(8,128)(2,1)S(1)}, u32[]{:S(2)}, u32[]{:S(2)}) async-start(bf16[8,96,256]{2,1,0:T(8,128)(2,1)} %pad_maximum_fusion.2), calls=%async_computation | async-start | bytes 786432 | tf_op jit(solution)/shard_map/all_to_all | solution.py:229
  15.5 0.7 copy-start.3
  16.3 65.4 %all-to-all-start.1 = ((bf16[16,784,128]{2,1,0:T(8,128)(2,1)}), bf16[16,784,128]{2,1,0:T(8,128)(2,1)S(1)}, u32[]{:S(2)}, u32[]{:S(2)}) async-start(bf16[16,784,128]{2,1,0:T(8,128)(2,1)} %pad_maximum_fusion), calls=%async_computation.1 | async-start | bytes 6422528 | tf_op jit(solution)/shard_map/all_to_all | solution.py:248
  81.6 26.0 %collective-permute-start = (bf16[8,64,256]{2,1,0:T(8,128)(2,1)S(1)}, bf16[8,64,256]{2,1,0:T(8,128)(2,1)S(1)}, u32[]{:S(2)}, u32[]{:S(2)}) collective-permute-start(bf16[8,64,256]{2,1,0:T(8,128)(2,1)S(1)} %slice.19), channel_id=1, source_target_pairs={{0,16},{2,18},{4,20},{6,22},{8,24},{10,26},{12,28},{14,30},{16,0},... | collective-permute-start | bytes 786440 | tf_op jit(solution)/shard_map/ppermute | solution.py:250
  107.6 5.5 %slice-start.1 = ((bf16[8,96,256]{2,1,0:T(8,128)(2,1)}), bf16[8,32,256]{2,1,0:T(8,128)(2,1)S(1)}, s32[]{:S(2)}) async-start(bf16[8,96,256]{2,1,0:T(8,128)(2,1)} %copy-done.3), calls=%async_computation.6 | async-start | bytes 262144 | tf_op jit(solution)/shard_map/slice | solution.py:246
  107.7 0.7 copy-start.7
  109.4 8.3 %slice-start = ((bf16[256,2048]{1,0:T(8,128)(2,1)}), bf16[192,2048]{1,0:T(8,128)(2,1)S(1)}, s32[]{:S(2)}) async-start(bf16[256,2048]{1,0:T(8,128)(2,1)} %param.9), calls=%async_computation.5 | async-start | bytes 1572864 | tf_op jit(solution)/shard_map/slice | solution.py:252
  109.4 29.7 %all-to-all-start.2 = ((bf16[8,512,128]{2,1,0:T(8,128)(2,1)}), bf16[8,512,128]{2,1,0:T(8,128)(2,1)S(1)}, u32[]{:S(2)}, u32[]{:S(2)}) async-start(bf16[8,512,128]{2,1,0:T(8,128)(2,1)} %broadcast_in_dim.5), calls=%async_computation.2 | async-start | bytes 2097152 | tf_op jit(solution)/shard_map/all_to_all | solution.py:263
  113.4 5.8 %collective-permute-start.1 = (s32[8,2,2048]{2,1,0:T(2,128)S(1)}, s32[8,2,2048]{2,1,0:T(2,128)S(1)}, u32[]{:S(2)}, u32[]{:S(2)}) collective-permute-start(s32[8,2,2048]{2,1,0:T(2,128)S(1)} %reshape.23), channel_id=1, source_target_pairs={{0,1},{1,0},{2,3},{3,2},{4,5},{5,4},{6,7},{7,6},{8,9},{9,8},{10,11... | collective-permute-start | bytes 393224 | tf_op jit(solution)/shard_map/ppermute | solution.py:256
  119.2 33.3 %copy-start.8 = (s32[8,2,2048]{2,1,0:T(2,128)}, s32[8,2,2048]{2,1,0:T(2,128)S(1)}, u32[]{:S(2)}) copy-start(s32[8,2,2048]{2,1,0:T(2,128)S(1)} %collective-permute-done.1) | copy-start | bytes 393220
  139.1 50.2 %all-to-all-start.3 = ((bf16[16,192,256]{2,1,0:T(8,128)(2,1)}), bf16[16,192,256]{2,1,0:T(8,128)(2,1)S(1)}, u32[]{:S(2)}, u32[]{:S(2)}) async-start(bf16[16,192,256]{2,1,0:T(8,128)(2,1)} %pad_maximum_fusion.1), calls=%async_computation.3 | async-start | bytes 3145728 | tf_op jit(solution)/shard_map/all_to_all | solution.py:269
  142.9 9.6 %copy-start = (s32[8,1,2048]{0,2,1:T(8,128)S(1)}, s32[8,1,2048]{0,2,1:T(8,128)}, u32[]{:S(2)}) copy-start(s32[8,1,2048]{0,2,1:T(8,128)} %copy.20) | copy-start | bytes 196612
  142.9 9.6 %collective-permute-start.2 = (bf16[8,512,128]{2,1,0:T(8,128)(2,1)S(1)}, bf16[8,512,128]{2,1,0:T(8,128)(2,1)S(1)}, u32[]{:S(2)}, u32[]{:S(2)}) collective-permute-start(bf16[8,512,128]{2,1,0:T(8,128)(2,1)S(1)} %all-to-all-done.2.attended_ref), channel_id=1, source_target_pairs={{0,2},{2,0},{4,6},{6,4},{8,10},{10,8},{12,14},{14,12},{16,18},{18,... | collective-permute-start | bytes 3145736 | tf_op jit(solution)/shard_map/ppermute | solution.py:272
  143.3 25.3 %collective-permute-start.3 = (bf16[8,512,128]{2,1,0:T(8,128)(2,1)S(1)}, bf16[8,512,128]{2,1,0:T(8,128)(2,1)}, u32[]{:S(2)}, u32[]{:S(2)}) collective-permute-start(bf16[8,512,128]{2,1,0:T(8,128)(2,1)S(1)} %all-to-all-done.2.attended_ref), channel_id=1, source_target_pairs={{0,1},{1,0},{2,3},{3,2},{4,5},{5,4},{6,7},{7,6},{8,9},{9,8},{10,11... | collective-permute-start | bytes 3145736 | tf_op jit(solution)/shard_map/ppermute | solution.py:271
  144.8 1.2 copy-start.1
  168.6 12.9 %collective-permute-start.4 = (bf16[8,512,128]{2,1,0:T(8,128)(2,1)}, bf16[8,512,128]{2,1,0:T(8,128)(2,1)}, u32[]{:S(2)}, u32[]{:S(2)}) collective-permute-start(bf16[8,512,128]{2,1,0:T(8,128)(2,1)} %collective-permute-done.3.attended_ref), channel_id=1, source_target_pairs={{0,2},{2,0},{4,6},{6,4},{8,10},{10,8},{12,14},{14,12},{16,18},{18,... | collective-permute-start | bytes 3145736 | tf_op jit(solution)/shard_map/ppermute | solution.py:278
  172.6 1.2 copy-start.2

commit v6 on v5

--- a/solution.py
+++ b/solution.py
@@ -111,7 +111,7 @@
             pltpu.VMEM((n_src, C, tok_rows), jnp.float32),
             pltpu.VMEM((C, e_width), jnp.float32),
         ],
-        compiler_params=pltpu.CompilerParams(vmem_limit_bytes=40 * 2**20),
+        compiler_params=pltpu.CompilerParams(vmem_limit_bytes=24 * 2**20),
         cost_estimate=pl.CostEstimate(
             flops=8 * C * tokens * e_width, bytes_accessed=moved.size * 2, transcendentals=C * tokens
         ),
@@ -122,21 +122,20 @@
 def expand_kernel(ids_ref, attended_ref, *refs):
     out_ref = refs[-1]
     heads, clusters, e_width = attended_ref.shape
-    tok_tile = ids_ref.shape[0]
+    tok_tile = ids_ref.shape[2]
     labels = lax.broadcasted_iota(jnp.int32, (tok_tile, e_width), 1).astype(jnp.int16)
     one, zero = jnp.bfloat16(1.0), jnp.bfloat16(0.0)
+    columns = ids_ref[0].T
     for h in range(heads):
-        ids = jnp.broadcast_to(ids_ref[:, h : h + 1], (tok_tile, e_width)).astype(jnp.int16)
-        parts = [
-            jnp.where(ids == labels + jnp.int16(at), one, zero) for at in range(0, clusters, e_width)
-        ]
+        ids = jnp.broadcast_to(columns[:, h : h + 1], (tok_tile, e_width)).astype(jnp.int16)
+        parts = [jnp.where(ids == labels + jnp.int16(at), one, zero) for at in range(0, clusters, e_width)]
         onehot = jnp.concatenate(parts, axis=1)
         found = jnp.dot(onehot, attended_ref[h], preferred_element_type=jnp.float32)
         out_ref[h] = found.astype(jnp.bfloat16)
 
 
-def expand(ids, attended, store, piece, pieces, tok_tile):
-    tokens, heads = ids.shape
+def expand(ids, part, attended, store, piece, pieces, tok_tile):
+    _, heads, tokens = ids.shape
     _, clusters, e_width = attended.shape
     held = () if store is None else (store,)
     return pl.pallas_call(
@@ -144,7 +143,7 @@
         out_shape=jax.ShapeDtypeStruct((pieces * heads, tokens, e_width), jnp.bfloat16),
         grid=(tokens // tok_tile,),
         in_specs=[
-            pl.BlockSpec((tok_tile, heads), lambda i: (i, 0)),
+            pl.BlockSpec((1, heads, tok_tile), lambda i: (part, 0, i)),
             pl.BlockSpec((heads, clusters, e_width), lambda i: (0, 0, 0)),
         ]
         + [pl.BlockSpec(memory_space=pl.ANY) for _ in held],
@@ -153,32 +152,34 @@
         compiler_params=pltpu.CompilerParams(vmem_limit_bytes=50 * 2**20),
         cost_estimate=pl.CostEstimate(
             flops=4 * tokens * heads * clusters * e_width,
-            bytes_accessed=2 * (attended.size + heads * tokens * e_width),
+            bytes_accessed=2 * heads * (clusters + tokens) * e_width,
             transcendentals=0,
         ),
         name="expand",
     )(ids, attended, *held)
 
 
-def project_kernel(places_ref, features_ref, early_ref, late_ref, out_ref):
-    heads = features_ref.shape[0]
+def project_kernel(places_ref, features_ref, near_ref, *refs):
+    *far_refs, out_ref = refs
+    heads, _, e_width = features_ref.shape
     each = heads // 4
-    plane_at, core = places_ref[0], places_ref[1]
+    head_at, core, half_at = places_ref[0], places_ref[1], places_ref[2]
     total = None
-    for plane in range(2):
-        first = (plane_at + plane - 2 * plane * plane_at) * each
+    for plane, weight_refs in ((half_at, (near_ref,)), (1 - half_at, far_refs)):
+        base = jnp.where(plane == head_at, 0, 2 * each)
         for i in range(each):
-            slots = [(2 * plane + at) * each + i for at in (core, 1 - core)]
+            slots = [base + at * each + i for at in (core, 1 - core)]
             left = jnp.concatenate([features_ref[at] for at in slots], axis=1)
-            right = jnp.concatenate([early_ref[first + i], late_ref[first + i]], axis=0)
+            chip = jnp.bitwise_xor(half_at, i % 2) * (each // 2) + i // 2
+            right = jnp.concatenate([x[chip] for x in weight_refs], axis=0)[: 2 * e_width]
             term = jnp.dot(left, right, preferred_element_type=jnp.float32)
             total = term if total is None else total + term
     out_ref[...] = total.astype(jnp.bfloat16)
 
 
-def project(places, features, early, late, tok_tile):
+def project(places, features, near, far, tok_tile):
     heads, tokens, e_width = features.shape
-    cols = early.shape[2]
+    cols = near.shape[2]
     return pl.pallas_call(
         project_kernel,
         out_shape=jax.ShapeDtypeStruct((tokens, cols), jnp.bfloat16),
@@ -187,9 +188,9 @@
             grid=(tokens // tok_tile,),
             in_specs=[
                 pl.BlockSpec((heads, tok_tile, e_width), lambda i, _: (0, i, 0)),
-                pl.BlockSpec(early.shape, lambda i, _: (0, 0, 0)),
-                pl.BlockSpec(late.shape, lambda i, _: (0, 0, 0)),
-            ],
+                pl.BlockSpec(near.shape, lambda i, _: (0, 0, 0)),
+            ]
+            + [pl.BlockSpec(x.shape, lambda i, _: (0, 0, 0)) for x in far],
             out_specs=pl.BlockSpec((tok_tile, cols), lambda i, _: (i, 0)),
         ),
         compiler_params=pltpu.CompilerParams(vmem_limit_bytes=50 * 2**20),
@@ -199,11 +200,15 @@
             transcendentals=0,
         ),
         name="project",
-    )(places, features, early, late)
-
-
-def by_slot(ids, core):
-    return [lax.dynamic_index_in_dim(ids, at, 1, keepdims=False).T for at in (core, 1 - core)]
+    )(places, features, near, *far)
+
+
+def by_slot(ids, half_at, core):
+    sources, heads, tok_rows = ids.shape
+    ids = ids.reshape(sources, 2, heads // 4, 2, tok_rows).transpose(3, 2, 1, 0, 4)
+    ids = jnp.where(half_at == 0, ids, ids[:, :, ::-1])
+    ids = jnp.where(core == 0, ids, ids[::-1])
+    return ids.reshape(2, heads // 2, sources * tok_rows)
 
 
 def by_head(queries, keys, values, cluster_ids, out_weight):
@@ -214,27 +219,16 @@
     cols_each = cols // half
     seq_at = lax.axis_index("seq")
     head_at = lax.axis_index("head")
+    half_at = seq_at // half
     core = lax.rem(seq_at, 2)
     swap_heads = [(0, 1), (1, 0)]
     swap_halves = [(i, (i + half) % n_seq) for i in range(n_seq)]
     swap_cores = [(i, i ^ 1) for i in range(n_seq)]
-
-    groups = [list(range(half)), list(range(half, n_seq))]
+    halves = [list(range(half)), list(range(half, n_seq))]
+    same_core = [list(range(at + core_of, at + half, 2)) for at in (0, half) for core_of in range(2)]
+
     ids_t = cluster_ids.T
     high, low = (ids_t // 16).astype(jnp.bfloat16), (ids_t % 16).astype(jnp.bfloat16)
-
-    cut = rows // 4 // 16 * 16
-    ahead = out_weight[:cut].reshape(cut, half, cols_each).transpose(1, 0, 2)
-    coded = jnp.broadcast_to(jnp.concatenate([high, low], axis=0)[None], (half, 2 * head_count, tok_rows))
-    early = lax.all_to_all(
-        jnp.concatenate([ahead, coded], axis=1),
-        "seq",
-        split_axis=0,
-        concat_axis=0,
-        axis_index_groups=groups,
-        tiled=True,
-    )
-
     id_rows = -(-2 * tok_rows // (16 * e_width)) * 16
     coded = jnp.concatenate([high, low], axis=1)
     coded = jnp.pad(coded, ((0, 0), (0, id_rows * e_width - 2 * tok_rows)))
@@ -242,54 +236,55 @@
         [x.transpose(1, 0, 2) for x in (queries, keys, values)] + [coded.reshape(head_count, id_rows, e_width)],
         axis=1,
     )
-    early, packed = lax.optimization_barrier((early, packed))
-    coded = early[:, cut:]
-    early = early[:, :cut]
+    packed, out_weight, high, low = lax.optimization_barrier((packed, out_weight, high, low))
     moved = lax.all_to_all(packed, "seq", split_axis=0, concat_axis=0, tiled=True)
-    moved, early = lax.optimization_barrier((moved, early))
-    crossed = lax.ppermute(early, "seq", swap_halves)
+
+    blocks = out_weight.reshape(rows, half, cols_each).transpose(1, 0, 2)
+    coded = jnp.broadcast_to(jnp.concatenate([high, low], axis=0)[None], (half, 2 * head_count, tok_rows))
+    blocks = jnp.concatenate([blocks, coded], axis=1)
+    moved, blocks = lax.optimization_barrier((moved, blocks))
+    near = lax.all_to_all(blocks, "seq", split_axis=0, concat_axis=0, axis_index_groups=halves, tiled=True)
     own = attend(moved, tok_rows)
-    own, crossed, coded, behind = lax.optimization_barrier((own, crossed, coded, out_weight[cut:]))
-    coded = coded.astype(jnp.int32)
-    near_ids = coded[:, :head_count] * 16 + coded[:, head_count:]
-    near_ids = near_ids.transpose(1, 0, 2).reshape(half, 2, half * tok_rows)
-    far_ids = lax.ppermute(near_ids, "head", swap_heads)
-    slot_ids = by_slot(near_ids, core)
-    late = behind.reshape(rows - cut, half, cols_each).transpose(1, 0, 2)
-    late = jnp.concatenate([late, late], axis=0)
-
-    same_core = [list(range(at, n_seq, 2)) for at in range(2)]
-    spread = jnp.broadcast_to(own[None], (half,) + own.shape)
-    first = lax.all_to_all(
-        spread, "seq", split_axis=0, concat_axis=0, axis_index_groups=same_core, tiled=True
-    )
-
-    first, late, slot_ids, far_ids = lax.optimization_barrier((first, late, slot_ids, far_ids))
-    slot_ids = slot_ids + by_slot(far_ids, core)
-    late = lax.all_to_all(late, "seq", split_axis=0, concat_axis=0, tiled=True)
-
-    third = lax.ppermute(first, "head", swap_heads)
+    own, near = lax.optimization_barrier((own, near))
+
+    def spread(pair):
+        copies = jnp.broadcast_to(pair[None], (half // 2,) + pair.shape)
+        got = lax.all_to_all(
+            copies, "seq", split_axis=0, concat_axis=0, axis_index_groups=same_core, tiled=True
+        )
+        return got.reshape((half,) + own.shape)
+
+    pair = jnp.stack([own, lax.ppermute(own, "seq", swap_halves)])
+    far_pair = lax.ppermute(pair, "head", swap_heads)
+    cuts = [rows * share // 256 // 16 * 16 for share in (0, 112, 192, 256)]
+    far = [lax.ppermute(near[:, a:b], "seq", swap_halves) for a, b in zip(cuts, cuts[1:])]
+    first = spread(pair)
+
+    coded = near[:, rows:].astype(jnp.int32)
+    slot_ids = by_slot(coded[:, :head_count] * 16 + coded[:, head_count:], half_at, core)
+    far_ids = lax.ppermute(slot_ids, "head", swap_heads)
+    first, slot_ids, far_ids, far_pair, far[0] = lax.optimization_barrier(
+        (first, slot_ids, far_ids, far_pair, far[0])
+    )
     second = lax.ppermute(first, "seq", swap_cores)
-    pieces = len(slot_ids)
+    third = spread(far_pair)
+
+    pieces = 4
     tok_tile = 2 * tok_rows
-    features = expand(slot_ids[0], first, None, 0, pieces, tok_tile)
-    features = expand(slot_ids[1], second, features, 1, pieces, tok_tile)
-    features, third = lax.optimization_barrier((features, third))
+    features = expand(slot_ids, 0, first, None, 0, pieces, tok_tile)
+    features = expand(slot_ids, 1, second, features, 1, pieces, tok_tile)
+    features, third, far[1] = lax.optimization_barrier((features, third, far[1]))
     fourth = lax.ppermute(third, "seq", swap_cores)
-    features = expand(slot_ids[2], third, features, 2, pieces, tok_tile)
-    features = expand(slot_ids[3], fourth, features, 3, pieces, tok_tile)
-    in_lower = seq_at < half
-    early = jnp.where(
-        in_lower, jnp.concatenate([early, crossed], axis=0), jnp.concatenate([crossed, early], axis=0)
-    )
-    places = jnp.stack([head_at, core]).astype(jnp.int32)
-    near = project(places, features, early, late, tok_tile)
+    features = expand(far_ids, 0, third, features, 2, pieces, tok_tile)
+    features = expand(far_ids, 1, fourth, features, 3, pieces, tok_tile)
+    places = jnp.stack([head_at, core, half_at]).astype(jnp.int32)
+    near_out = project(places, features, near, far, tok_tile)
     mixed = lax.all_to_all(
-        near.reshape(half, tok_rows, cols_each),
+        near_out.reshape(half, tok_rows, cols_each),
         "seq",
         split_axis=0,
         concat_axis=0,
-        axis_index_groups=groups,
+        axis_index_groups=halves,
         tiled=True,
     )
     return mixed.transpose(1, 0, 2).reshape(tok_rows, cols)
@@ -301,7 +296,7 @@
     return (
         head_count == n_seq
         and lax.axis_size("head") == 2
-        and n_seq >= 4
+        and n_seq >= 8
         and n_seq & (n_seq - 1) == 0
         and e_width == 128
         and tok_rows % e_width == 0

time: 219 us -> 213 us (0.973)
  waiting for transfers between devices: 93.9 us -> 82.1 us
  starting transfers between devices: 34.9 us -> 40.5 us
  local copies, waits for them, and re-layouts: 14.8 us -> 18.1 us
    all_to_all x3, waiting for transfers between devices: 24.8 us -> 5.31 us  [the longest x2 3.49 us: spread(): lax.all_to_all(copies, 'seq', split_axis=0, concat_axis=0, axis_index_gro...]
    ppermute x3 -> x6, waiting for transfers between devices: 9.63 us -> 23.2 us  [the longest x3 9.48 us: by_head(): lax.ppermute(near[:, a:b], 'seq', swap_halves)]
    all_to_all x3, starting transfers between devices: 12.7 us -> 21.9 us  [the longest x1 14.7 us: by_head(): lax.all_to_all(blocks, 'seq', split_axis=0, concat_axis=0, axis_index_gro...]
    all_to_all x1, waiting for transfers between devices: 59.5 us -> 53.6 us  [by_head(): lax.all_to_all(packed, 'seq', split_axis=0, concat_axis=0, tiled=True)]
    ppermute x3 -> x6, starting transfers between devices: 16.9 us -> 11.1 us  [the longest x3 6.38 us: by_head(): lax.ppermute(near[:, a:b], 'seq', swap_halves)]
    dynamic_slice x6 -> x0, local copies, waits for them, and re-layouts: 5.58 us -> none  [by_slot(): lax.dynamic_index_in_dim(ids, at, 1, keepdims=False)]
    all_to_all x1, starting transfers between devices: 4.87 us -> 7.39 us  [by_head(): lax.all_to_all(packed, 'seq', split_axis=0, concat_axis=0, tiled=True)]
    optimization_barrier x0 -> x1, local copies, waits for them, and re-layouts: none -> 2.26 us  [by_head(): lax.optimization_barrier((packed, out_weight, high, low))]
  transfers between devices with their start and end apart: 9 -> 12, of which waited for: 4 -> 8; matrix products, arithmetic and copies ran while one was open for 5% -> 4% of each run, Pallas kernels for 19% -> 19%
where the time goes in v6:
time: 213 us
  waiting for transfers between devices  82.1 us (39%)
  Pallas kernels  49.5 us (23%)
  starting transfers between devices  40.5 us (19%)
  local copies, waits for them, and re-layouts  18.1 us (8%)
  blocking collectives  17.4 us (8%)
  other arithmetic  5.11 us (2%)
    all_to_all x1, waiting for transfers between devices, by_head(): lax.all_to_all(packed, 'seq', split_axis=0, concat_axis=0, tiled=True)  53.6 us
    pallas_call x4, Pallas kernels, expand(): pl.pallas_call(expand_kernel, out_shape=jax.ShapeDtypeStruct((pieces * he...  28.3 us
    all_to_all x1, blocking collectives, by_head(): lax.all_to_all(near_out.reshape(half, tok_rows, cols_each), 'seq', split_...  17.4 us
    all_to_all x1, starting transfers between devices, by_head(): lax.all_to_all(blocks, 'seq', split_axis=0, concat_axis=0, axis_index_gro...  14.7 us
    pallas_call x1, Pallas kernels, attend(): pl.pallas_call(lambda *refs: attend_kernel(tok_rows, *refs), out_shape=ja...  12.1 us
    ppermute x3, waiting for transfers between devices, by_head(): lax.ppermute(near[:, a:b], 'seq', swap_halves)  9.48 us
    pallas_call x1, Pallas kernels, project(): pl.pallas_call(project_kernel, out_shape=jax.ShapeDtypeStruct((tokens, co...  9.01 us
    ppermute x1, waiting for transfers between devices, by_head(): far_ids = lax.ppermute(slot_ids, 'head', swap_heads)  7.51 us
  transfers between devices with their start and end apart: 12, of which 8 were waited for; matrix products, arithmetic and copies ran while one was open for 4% of the time, Pallas kernels for 19%

profile of v6, /device:TPU:0, one launch (start us, length us, event | category | flops | bytes accessed | tf_op | source)
XLA Modules:
  0.0 212.8 jit_solution(7716714069381698701)
XLA Ops:
  0.0 0.7 fusion.4
  0.8 1.5 copy.26
  2.3 2.1 copy_bitcast_fusion
  4.4 1.8 pad_maximum_fusion
  6.1 7.4 %all-to-all-start = ((bf16[16,784,128]{2,1,0:T(8,128)(2,1)}), bf16[16,784,128]{2,1,0:T(8,128)(2,1)S(1)}, u32[]{:S(2)}, u32[]{:S(2)}) async-start(bf16[16,784,128]{2,1,0:T(8,128)(2,1)} %pad_maximum_fusion), calls=%async_computation | async-start | bytes 6422528 | tf_op jit(solution)/shard_map/all_to_all | solution.py:240
  13.5 2.3 %copy.17 = bf16[256,2048]{0,1:T(8,128)(2,1)} copy(bf16[256,2048]{1,0:T(8,128)(2,1)} %param.9) | data formatting | bytes 2097152 | tf_op jit(solution)/shard_map/optimization_barrier | solution.py:239
  15.8 2.3 %copy.18 = bf16[256,8,256]{2,0,1:T(8,128)(2,1)} copy(bf16[256,8,256]{0,2,1:T(8,128)(2,1)} %bitcast.61) | data formatting | bytes 2097152 | tf_op jit(solution)/shard_map/reshape | solution.py:242
  18.1 2.3 %pad_maximum_fusion.1 = bf16[8,288,256]{2,1,0:T(8,128)(2,1)} fusion(bf16[8,32,256]{2,1,0:T(8,128)(2,1)S(1)} %broadcast_in_dim.6, bf16[8,256,256]{2,1,0:T(8,128)(2,1)} %bitcast.59), kind=kLoop, calls=%fused_computation.1 | loop fusion | flops 2359296 | bytes 2359296 | tf_op jit(solution)/shard_map/concatenate | solution.py:244
  20.4 53.6 %all-to-all-done.refs_0_ = bf16[16,784,128]{2,1,0:T(8,128)(2,1)S(1)} async-done(((bf16[16,784,128]{2,1,0:T(8,128)(2,1)}), bf16[16,784,128]{2,1,0:T(8,128)(2,1)S(1)}, u32[]{:S(2)}, u32[]{:S(2)}) %all-to-all-start) | async-done | bytes 3211296 | tf_op jit(solution)/shard_map/all_to_all | solution.py:240
  74.0 0.0 copy-start
  74.0 1.6 copy-done
  75.7 14.7 %all-to-all-start.1 = ((bf16[8,288,256]{2,1,0:T(8,128)(2,1)}), bf16[8,288,256]{2,1,0:T(8,128)(2,1)S(1)}, u32[]{:S(2)}, u32[]{:S(2)}) async-start(bf16[8,288,256]{2,1,0:T(8,128)(2,1)} %pad_maximum_fusion.1), calls=%async_computation.1 | async-start | bytes 2359296 | tf_op jit(solution)/shard_map/all_to_all | solution.py:246
  90.4 0.0 copy-start.1
  90.4 1.9 copy-done.1
  92.3 12.1 %attend.1 = bf16[512,128]{1,0:T(8,128)(2,1)S(1)} custom-call(bf16[16,784,128]{2,1,0:T(8,128)(2,1)S(1)} %copy-done.1), custom_call_target="tpu_custom_call" | custom-call | flops 2147483648 | bytes 3211264 | tf_op jit(solution)/shard_map/attend/pallas_call | solution.py:104
  104.5 1.8 all-to-all-done.1.near_ref
  106.3 2.6 %collective-permute-start = (bf16[512,128]{1,0:T(8,128)(2,1)S(1)}, bf16[512,128]{1,0:T(8,128)(2,1)S(1)}, u32[]{:S(2)}, u32[]{:S(2)}) collective-permute-start(bf16[512,128]{1,0:T(8,128)(2,1)S(1)} %attend.1), channel_id=1, source_target_pairs={{0,16},{2,18},{4,20},{6,22},{8,24},{10,26},{12,28},{14,30},{16,0},... | collective-permute-start | bytes 393224 | tf_op jit(solution)/shard_map/ppermute | solution.py:257
  108.9 6.2 %collective-permute-done = bf16[512,128]{1,0:T(8,128)(2,1)S(1)} collective-permute-done((bf16[512,128]{1,0:T(8,128)(2,1)S(1)}, bf16[512,128]{1,0:T(8,128)(2,1)S(1)}, u32[]{:S(2)}, u32[]{:S(2)}) %collective-permute-start) | collective-permute-done | bytes 131104 | tf_op jit(solution)/shard_map/ppermute | solution.py:257
  115.1 1.1 broadcast_in_dim.7
  116.2 3.5 %all-to-all-start.2 = ((bf16[4,2,512,128]{3,2,1,0:T(8,128)(2,1)}), bf16[4,2,512,128]{3,2,1,0:T(8,128)(2,1)S(1)}, u32[]{:S(2)}, u32[]{:S(2)}) async-start(bf16[4,2,512,128]{3,2,1,0:T(8,128)(2,1)} %broadcast_in_dim.7), calls=%async_computation.2 | async-start | bytes 2097152 | tf_op jit(solution)/shard_map/all_to_all | solution.py:252
  119.7 0.8 slice.21
  120.6 0.1 reshape.30
  120.7 2.1 collective-permute-start.3
  122.8 0.4 rev.7
  123.2 1.6 collective-permute-start.2
  124.8 0.1 broadcast_select_fusion
  124.9 0.1 copy.19
  125.0 0.6 collective-permute-start.1
  125.6 7.5 %collective-permute-done.1.ids_ref = s32[2,8,2048]{2,1,0:T(8,128)S(1)} collective-permute-done((s32[2,8,2048]{2,1,0:T(8,128)S(1)}, s32[2,8,2048]{2,1,0:T(8,128)S(1)}, u32[]{:S(2)}, u32[]{:S(2)}) %collective-permute-start.1) | collective-permute-done | bytes 131104 | tf_op jit(solution)/shard_map/ppermute | solution.py:265
  133.1 0.0 collective-permute-done.2
  133.1 8.3 %collective-permute-done.3.refs_0_ = bf16[8,112,256]{2,1,0:T(8,128)(2,1)S(1)} collective-permute-done((bf16[8,112,256]{2,1,0:T(8,128)(2,1)}, bf16[8,112,256]{2,1,0:T(8,128)(2,1)S(1)}, u32[]{:S(2)}, u32[]{:S(2)}) %collective-permute-start.3) | collective-permute-done | bytes 458784 | tf_op jit(solution)/shard_map/ppermute | solution.py:260
  141.4 0.0 copy-start.2
  141.4 2.0 all-to-all-done.2
  143.4 2.1 broadcast_in_dim.8
  145.4 0.0 copy-done.2
  145.4 3.7 %all-to-all-start.3 = ((bf16[4,2,512,128]{3,2,1,0:T(8,128)(2,1)}), bf16[4,2,512,128]{3,2,1,0:T(8,128)(2,1)S(1)}, u32[]{:S(2)}, u32[]{:S(2)}) async-start(bf16[4,2,512,128]{3,2,1,0:T(8,128)(2,1)} %broadcast_in_dim.8), calls=%async_computation.3 | async-start | bytes 2097152 | tf_op jit(solution)/shard_map/all_to_all | solution.py:252
  149.1 0.0 collective-permute-start.4
  149.2 2.3 %collective-permute-start.5 = (bf16[8,80,256]{2,1,0:T(8,128)(2,1)S(1)}, bf16[8,80,256]{2,1,0:T(8,128)(2,1)S(1)}, u32[]{:S(2)}, u32[]{:S(2)}) collective-permute-start(bf16[8,80,256]{2,1,0:T(8,128)(2,1)S(1)} %slice.22), channel_id=1, source_target_pairs={{0,16},{2,18},{4,20},{6,22},{8,24},{10,26},{12,28},{14,30},{16,0},... | collective-permute-start | bytes 983048 | tf_op jit(solution)/shard_map/ppermute | solution.py:260
  151.5 7.1 %expand.4.refs_0_ = bf16[32,2048,128]{2,1,0:T(8,128)(2,1)} custom-call(s32[2,8,2048]{2,1,0:T(8,128)S(1)} %reshape.31.ids_ref, bf16[8,512,128]{2,1,0:T(8,128)(2,1)S(1)} %bitcast.53), custom_call_target="tpu_custom_call" | custom-call | flops 4294967296 | bytes 5242880 | tf_op jit(solution)/shard_map/expand/pallas_call | solution.py:141
  158.5 0.0 collective-permute-done.4.attended_ref
  158.5 7.1 %expand.5.refs_0_ = bf16[32,2048,128]{2,1,0:T(8,128)(2,1)} custom-call(s32[2,8,2048]{2,1,0:T(8,128)S(1)} %reshape.31.ids_ref, bf16[8,512,128]{2,1,0:T(8,128)(2,1)S(1)} %collective-permute-done.4.attended_ref, bf16[32,2048,128]{2,1,0:T(8,128)(2,1)} %expand.4.refs_0_), custom_call_target="tpu_custom_call", output_to_operand_aliasing={{}: (2, {})} | custom-call | flops 4294967296 | bytes 5242880 | tf_op jit(solution)/shard_map/expand/pallas_call | solution.py:141
  165.6 1.2 collective-permute-done.5.refs_1_
  166.8 0.0 copy-start.4
  166.8 0.7 copy-done.4
  167.5 1.5 all-to-all-done.3
  169.0 0.0 collective-permute-start.6
  169.0 0.1 pad_add_fusion.places_ref
  169.1 2.0 collective-permute-start.7
  171.1 7.1 %expand.6.refs_0_ = bf16[32,2048,128]{2,1,0:T(8,128)(2,1)} custom-call(s32[2,8,2048]{2,1,0:T(8,128)S(1)} %collective-permute-done.1.ids_ref, bf16[8,512,128]{2,1,0:T(8,128)(2,1)S(1)} %bitcast.55, bf16[32,2048,128]{2,1,0:T(8,128)(2,1)} %expand.5.refs_0_), custom_call_target="tpu_custom_call", output_to_operand_aliasing={{}: (2, {})} | custom-call | flops 4294967296 | bytes 5242880 | tf_op jit(solution)/shard_map/expand/pallas_call | solution.py:141
  178.2 0.0 copy-start.3
  178.2 0.0 copy-start.5
  178.2 0.0 collective-permute-done.6.attended_ref
  178.2 7.1 %expand.7.features_ref = bf16[32,2048,128]{2,1,0:T(8,128)(2,1)} custom-call(s32[2,8,2048]{2,1,0:T(8,128)S(1)} %collective-permute-done.1.ids_ref, bf16[8,512,128]{2,1,0:T(8,128)(2,1)S(1)} %collective-permute-done.6.attended_ref, bf16[32,2048,128]{2,1,0:T(8,128)(2,1)} %expand.6.refs_0_), custom_call_target="tpu_custom_call", output_to_operand_aliasing={{}: (2, {})} | custom-call | flops 4294967296 | bytes 5242880 | tf_op jit(solution)/shard_map/expand/pallas_call | solution.py:141
  185.3 0.0 collective-permute-done.7.refs_2_
  185.3 0.0 copy-done.3
  185.3 0.0 copy-done.5
  185.3 9.0 %project.1 = bf16[2048,256]{1,0:T(8,128)(2,1)S(1)} custom-call(s32[3]{0:T(128)S(1)} %pad_add_fusion.places_ref, bf16[32,2048,128]{2,1,0:T(8,128)(2,1)} %expand.7.features_ref, bf16[8,288,256]{2,1,0:T(8,128)(2,1)S(1)} %all-to-all-done.1.near_ref, bf16[8,112,256]{2,1,0:T(8,128)(2,1)S(1)} %copy-done.3, bf16[8,80,256]{2,1,0:T(8,128)(2,1)S(1)} %copy-done.5, ...), custom_call_target="tpu_custom_call" | custom-call | flops 4294967296 | bytes 19922944 | tf_op jit(solution)/shard_map/project/pallas_call | solution.py:183
  194.3 17.4 %all_to_all.25 = bf16[8,256,256]{2,1,0:T(8,128)(2,1)S(1)} all-to-all(bf16[8,256,256]{2,1,0:T(8,128)(2,1)S(1)} %bitcast.56), channel_id=1, replica_groups={{0,2,4,6,8,10,12,14},{16,18,20,22,24,26,28,30},{1,3,5,7,9,11,13,15},{17..., dimensions={0} | all-to-all | bytes 2097152 | tf_op jit(solution)/shard_map/all_to_all | solution.py:282
  211.7 1.1 copy.21
  (11 shorter events, 0.2 us)
Async XLA Ops:
  6.1 67.9 %all-to-all-start = ((bf16[16,784,128]{2,1,0:T(8,128)(2,1)}), bf16[16,784,128]{2,1,0:T(8,128)(2,1)S(1)}, u32[]{:S(2)}, u32[]{:S(2)}) async-start(bf16[16,784,128]{2,1,0:T(8,128)(2,1)} %pad_maximum_fusion), calls=%async_computation | async-start | bytes 6422528 | tf_op jit(solution)/shard_map/all_to_all | solution.py:240
  74.0 1.7 copy-start
  75.7 30.6 %all-to-all-start.1 = ((bf16[8,288,256]{2,1,0:T(8,128)(2,1)}), bf16[8,288,256]{2,1,0:T(8,128)(2,1)S(1)}, u32[]{:S(2)}, u32[]{:S(2)}) async-start(bf16[8,288,256]{2,1,0:T(8,128)(2,1)} %pad_maximum_fusion.1), calls=%async_computation.1 | async-start | bytes 2359296 | tf_op jit(solution)/shard_map/all_to_all | solution.py:246
  90.4 1.9 copy-start.1
  106.3 8.7 %collective-permute-start = (bf16[512,128]{1,0:T(8,128)(2,1)S(1)}, bf16[512,128]{1,0:T(8,128)(2,1)S(1)}, u32[]{:S(2)}, u32[]{:S(2)}) collective-permute-start(bf16[512,128]{1,0:T(8,128)(2,1)S(1)} %attend.1), channel_id=1, source_target_pairs={{0,16},{2,18},{4,20},{6,22},{8,24},{10,26},{12,28},{14,30},{16,0},... | collective-permute-start | bytes 393224 | tf_op jit(solution)/shard_map/ppermute | solution.py:257
  116.2 27.2 %all-to-all-start.2 = ((bf16[4,2,512,128]{3,2,1,0:T(8,128)(2,1)}), bf16[4,2,512,128]{3,2,1,0:T(8,128)(2,1)S(1)}, u32[]{:S(2)}, u32[]{:S(2)}) async-start(bf16[4,2,512,128]{3,2,1,0:T(8,128)(2,1)} %broadcast_in_dim.7), calls=%async_computation.2 | async-start | bytes 2097152 | tf_op jit(solution)/shard_map/all_to_all | solution.py:252
  120.7 20.7 %collective-permute-start.3 = (bf16[8,112,256]{2,1,0:T(8,128)(2,1)}, bf16[8,112,256]{2,1,0:T(8,128)(2,1)S(1)}, u32[]{:S(2)}, u32[]{:S(2)}) collective-permute-start(bf16[8,112,256]{2,1,0:T(8,128)(2,1)} %slice.21), channel_id=1, source_target_pairs={{0,16},{2,18},{4,20},{6,22},{8,24},{10,26},{12,28},{14,30},{16,0},... | collective-permute-start | bytes 1376264 | tf_op jit(solution)/shard_map/ppermute | solution.py:260
  123.2 9.9 %collective-permute-start.2 = (bf16[2,512,128]{2,1,0:T(8,128)(2,1)S(1)}, bf16[2,512,128]{2,1,0:T(8,128)(2,1)}, u32[]{:S(2)}, u32[]{:S(2)}) collective-permute-start(bf16[2,512,128]{2,1,0:T(8,128)(2,1)S(1)} %pad_maximum_fusion.2), channel_id=1, source_target_pairs={{0,1},{1,0},{2,3},{3,2},{4,5},{5,4},{6,7},{7,6},{8,9},{9,8},{10,11... | collective-permute-start | bytes 786440 | tf_op jit(solution)/shard_map/ppermute | solution.py:258
  125.0 8.1 %collective-permute-start.1 = (s32[2,8,2048]{2,1,0:T(8,128)S(1)}, s32[2,8,2048]{2,1,0:T(8,128)S(1)}, u32[]{:S(2)}, u32[]{:S(2)}) collective-permute-start(s32[2,8,2048]{2,1,0:T(8,128)S(1)} %reshape.31.ids_ref), channel_id=1, source_target_pairs={{0,1},{1,0},{2,3},{3,2},{4,5},{5,4},{6,7},{7,6},{8,9},{9,8},{10,11... | collective-permute-start | bytes 393224 | tf_op jit(solution)/shard_map/ppermute | solution.py:265
  141.4 4.1 %copy-start.2 = (bf16[8,112,256]{2,1,0:T(8,128)(2,1)}, bf16[8,112,256]{2,1,0:T(8,128)(2,1)S(1)}, u32[]{:S(2)}) copy-start(bf16[8,112,256]{2,1,0:T(8,128)(2,1)S(1)} %collective-permute-done.3.refs_0_) | copy-start | bytes 1376260
  145.4 23.6 %all-to-all-start.3 = ((bf16[4,2,512,128]{3,2,1,0:T(8,128)(2,1)}), bf16[4,2,512,128]{3,2,1,0:T(8,128)(2,1)S(1)}, u32[]{:S(2)}, u32[]{:S(2)}) async-start(bf16[4,2,512,128]{3,2,1,0:T(8,128)(2,1)} %broadcast_in_dim.8), calls=%async_computation.3 | async-start | bytes 2097152 | tf_op jit(solution)/shard_map/all_to_all | solution.py:252
  149.1 9.4 %collective-permute-start.4 = (bf16[8,512,128]{2,1,0:T(8,128)(2,1)S(1)}, bf16[8,512,128]{2,1,0:T(8,128)(2,1)S(1)}, u32[]{:S(2)}, u32[]{:S(2)}) collective-permute-start(bf16[8,512,128]{2,1,0:T(8,128)(2,1)S(1)} %bitcast.52), channel_id=1, source_target_pairs={{0,2},{2,0},{4,6},{6,4},{8,10},{10,8},{12,14},{14,12},{16,18},{18,... | collective-permute-start | bytes 3145736 | tf_op jit(solution)/shard_map/ppermute | solution.py:269
  149.2 17.7 %collective-permute-start.5 = (bf16[8,80,256]{2,1,0:T(8,128)(2,1)S(1)}, bf16[8,80,256]{2,1,0:T(8,128)(2,1)S(1)}, u32[]{:S(2)}, u32[]{:S(2)}) collective-permute-start(bf16[8,80,256]{2,1,0:T(8,128)(2,1)S(1)} %slice.22), channel_id=1, source_target_pairs={{0,16},{2,18},{4,20},{6,22},{8,24},{10,26},{12,28},{14,30},{16,0},... | collective-permute-start | bytes 983048 | tf_op jit(solution)/shard_map/ppermute | solution.py:260
  166.8 0.7 copy-start.4
  169.0 9.2 %collective-permute-start.6 = (bf16[8,512,128]{2,1,0:T(8,128)(2,1)S(1)}, bf16[8,512,128]{2,1,0:T(8,128)(2,1)S(1)}, u32[]{:S(2)}, u32[]{:S(2)}) collective-permute-start(bf16[8,512,128]{2,1,0:T(8,128)(2,1)S(1)} %bitcast.54), channel_id=1, source_target_pairs={{0,2},{2,0},{4,6},{6,4},{8,10},{10,8},{12,14},{14,12},{16,18},{18,... | collective-permute-start | bytes 3145736 | tf_op jit(solution)/shard_map/ppermute | solution.py:277
  169.1 16.2 %collective-permute-start.7 = (bf16[8,64,256]{2,1,0:T(8,128)(2,1)S(1)}, bf16[8,64,256]{2,1,0:T(8,128)(2,1)S(1)}, u32[]{:S(2)}, u32[]{:S(2)}) collective-permute-start(bf16[8,64,256]{2,1,0:T(8,128)(2,1)S(1)} %slice.23), channel_id=1, source_target_pairs={{0,16},{2,18},{4,20},{6,22},{8,24},{10,26},{12,28},{14,30},{16,0},... | collective-permute-start | bytes 786440 | tf_op jit(solution)/shard_map/ppermute | solution.py:260
  178.2 7.1 %copy-start.3 = (bf16[8,112,256]{2,1,0:T(8,128)(2,1)S(1)}, bf16[8,112,256]{2,1,0:T(8,128)(2,1)}, u32[]{:S(2)}) copy-start(bf16[8,112,256]{2,1,0:T(8,128)(2,1)} %copy-done.2) | copy-start | bytes 1376260
  178.2 7.1 %copy-start.5 = (bf16[8,80,256]{2,1,0:T(8,128)(2,1)S(1)}, bf16[8,80,256]{2,1,0:T(8,128)(2,1)}, u32[]{:S(2)}) copy-start(bf16[8,80,256]{2,1,0:T(8,128)(2,1)} %copy-done.4) | copy-start | bytes 983044

commit v7 on v6

--- a/solution.py
+++ b/solution.py
@@ -163,15 +163,16 @@
     *far_refs, out_ref = refs
     heads, _, e_width = features_ref.shape
     each = heads // 4
-    head_at, core, half_at = places_ref[0], places_ref[1], places_ref[2]
+    head_at, core, half_at, place = (places_ref[i] for i in range(4))
     total = None
     for plane, weight_refs in ((half_at, (near_ref,)), (1 - half_at, far_refs)):
         base = jnp.where(plane == head_at, 0, 2 * each)
-        for i in range(each):
-            slots = [base + at * each + i for at in (core, 1 - core)]
-            left = jnp.concatenate([features_ref[at] for at in slots], axis=1)
-            chip = jnp.bitwise_xor(half_at, i % 2) * (each // 2) + i // 2
-            right = jnp.concatenate([x[chip] for x in weight_refs], axis=0)[: 2 * e_width]
+        blocks = [(x, i) for x in weight_refs for i in range(x.shape[0])]
+        for k, (weight_ref, i) in enumerate(blocks):
+            chip = jnp.bitwise_xor(place, k)
+            slot = 2 * lax.rem(chip, each // 2) + jnp.bitwise_xor(half_at, lax.div(chip, each // 2))
+            left = jnp.concatenate([features_ref[base + at * each + slot] for at in (core, 1 - core)], axis=1)
+            right = weight_ref[i, : 2 * e_width, :]
             term = jnp.dot(left, right, preferred_element_type=jnp.float32)
             total = term if total is None else total + term
     out_ref[...] = total.astype(jnp.bfloat16)
@@ -221,6 +222,7 @@
     head_at = lax.axis_index("head")
     half_at = seq_at // half
     core = lax.rem(seq_at, 2)
+    place = lax.rem(seq_at, half)
     swap_heads = [(0, 1), (1, 0)]
     swap_halves = [(i, (i + half) % n_seq) for i in range(n_seq)]
     swap_cores = [(i, i ^ 1) for i in range(n_seq)]
@@ -240,15 +242,24 @@
     moved = lax.all_to_all(packed, "seq", split_axis=0, concat_axis=0, tiled=True)
 
     blocks = out_weight.reshape(rows, half, cols_each).transpose(1, 0, 2)
-    coded = jnp.broadcast_to(jnp.concatenate([high, low], axis=0)[None], (half, 2 * head_count, tok_rows))
-    blocks = jnp.concatenate([blocks, coded], axis=1)
-    moved, blocks = lax.optimization_barrier((moved, blocks))
-    near = lax.all_to_all(blocks, "seq", split_axis=0, concat_axis=0, axis_index_groups=halves, tiled=True)
+    coded = jnp.concatenate([high, low], axis=0)
+    near = []
+    for k in range(half):
+        block = lax.dynamic_index_in_dim(blocks, jnp.bitwise_xor(place, k), 0, keepdims=False)
+        block = jnp.concatenate([block, coded], axis=0)
+        near.append(lax.ppermute(block, "seq", [(i, i ^ k) for i in range(n_seq)]) if k else block)
+    near = jnp.stack(near)
+    moved, near = lax.optimization_barrier((moved, near))
+    cuts = [half * i // 4 for i in range(5)]
+    far = [lax.ppermute(near[a:b, :rows], "seq", swap_halves) for a, b in zip(cuts[:1], cuts[1:])]
     own = attend(moved, tok_rows)
-    own, near = lax.optimization_barrier((own, near))
-
-    def spread(pair):
-        copies = jnp.broadcast_to(pair[None], (half // 2,) + pair.shape)
+    own, near, far[0] = lax.optimization_barrier((own, near, far[0]))
+    far += [lax.ppermute(near[a:b, :rows], "seq", swap_halves) for a, b in zip(cuts[1:], cuts[2:])]
+
+    def copied(pair):
+        return jnp.broadcast_to(pair[None], (half // 2,) + pair.shape)
+
+    def spread(copies):
         got = lax.all_to_all(
             copies, "seq", split_axis=0, concat_axis=0, axis_index_groups=same_core, tiled=True
         )
@@ -256,28 +267,31 @@
 
     pair = jnp.stack([own, lax.ppermute(own, "seq", swap_halves)])
     far_pair = lax.ppermute(pair, "head", swap_heads)
-    cuts = [rows * share // 256 // 16 * 16 for share in (0, 112, 192, 256)]
-    far = [lax.ppermute(near[:, a:b], "seq", swap_halves) for a, b in zip(cuts, cuts[1:])]
-    first = spread(pair)
+    first = spread(copied(pair))
 
     coded = near[:, rows:].astype(jnp.int32)
-    slot_ids = by_slot(coded[:, :head_count] * 16 + coded[:, head_count:], half_at, core)
+    coded = coded[:, :head_count] * 16 + coded[:, head_count:]
+    coded = jnp.concatenate(
+        [lax.dynamic_slice_in_dim(coded, jnp.bitwise_xor(place, i), 1, axis=0) for i in range(half)], axis=0
+    )
+    slot_ids = by_slot(coded, half_at, core)
     far_ids = lax.ppermute(slot_ids, "head", swap_heads)
-    first, slot_ids, far_ids, far_pair, far[0] = lax.optimization_barrier(
-        (first, slot_ids, far_ids, far_pair, far[0])
+    far_copies = copied(far_pair)
+    first, slot_ids, far_ids, far_copies, far[1] = lax.optimization_barrier(
+        (first, slot_ids, far_ids, far_copies, far[1])
     )
     second = lax.ppermute(first, "seq", swap_cores)
-    third = spread(far_pair)
+    third = spread(far_copies)
 
     pieces = 4
     tok_tile = 2 * tok_rows
     features = expand(slot_ids, 0, first, None, 0, pieces, tok_tile)
     features = expand(slot_ids, 1, second, features, 1, pieces, tok_tile)
-    features, third, far[1] = lax.optimization_barrier((features, third, far[1]))
+    features, third, far[2] = lax.optimization_barrier((features, third, far[2]))
     fourth = lax.ppermute(third, "seq", swap_cores)
     features = expand(far_ids, 0, third, features, 2, pieces, tok_tile)
     features = expand(far_ids, 1, fourth, features, 3, pieces, tok_tile)
-    places = jnp.stack([head_at, core, half_at]).astype(jnp.int32)
+    places = jnp.stack([head_at, core, half_at, place]).astype(jnp.int32)
     near_out = project(places, features, near, far, tok_tile)
     mixed = lax.all_to_all(
         near_out.reshape(half, tok_rows, cols_each),

time: 213 us -> 200 us (0.939)
  local copies, waits for them, and re-layouts: 18.1 us -> 10.6 us
  starting transfers between devices: 40.5 us -> 35.9 us
    all_to_all x1, waiting for transfers between devices: 53.6 us -> 0.01 us  [by_head(): lax.all_to_all(packed, 'seq', split_axis=0, concat_axis=0, tiled=True)]
    ppermute x3 -> x11, waiting for transfers between devices: 9.48 us -> 62.3 us  [the longest x7 58.2 us: by_head(): lax.ppermute(block, 'seq', [(i, i ^ k) for i in range(n_seq)])]
    all_to_all x1 -> x0, starting transfers between devices: 14.7 us -> none  [by_head(): lax.all_to_all(blocks, 'seq', split_axis=0, concat_axis=0, axis_index_gro...]
    ppermute x3 -> x11, starting transfers between devices: 6.38 us -> 17.9 us  [the longest x4 11 us: by_head(): lax.ppermute(near[a:b, :rows], 'seq', swap_halves)]
    unnamed x14 -> x42, local copies, waits for them, and re-layouts: 5.78 us -> 2.82 us
    ppermute x1, starting transfers between devices: 2.59 us -> 0.1 us  [by_head(): pair = jnp.stack([own, lax.ppermute(own, 'seq', swap_halves)])]
    another operation x0 -> x2, local copies, waits for them, and re-layouts: none -> 2.46 us
    reshape x1 -> x0, local copies, waits for them, and re-layouts: 2.28 us -> none  [by_head(): blocks = out_weight.reshape(rows, half, cols_each).transpose(1, 0, 2)]
  transfers between devices with their start and end apart: 12 -> 19, of which waited for: 8 -> 11; matrix products, arithmetic and copies ran while one was open for 4% -> 2% of each run, Pallas kernels for 19% -> 21%
where the time goes in v7:
time: 200 us; the launch traced here: 199 us
  waiting for transfers between devices  80.1 us (40%)
  Pallas kernels  51.5 us (26%)
  starting transfers between devices  35.9 us (18%)
  blocking collectives  17.4 us (9%)
  local copies, waits for them, and re-layouts  10.6 us (5%)
  other arithmetic  3.1 us (2%)
    ppermute x7, waiting for transfers between devices, by_head(): lax.ppermute(block, 'seq', [(i, i ^ k) for i in range(n_seq)])  58.2 us
    pallas_call x4, Pallas kernels, expand(): pl.pallas_call(expand_kernel, out_shape=jax.ShapeDtypeStruct((pieces * he...  28.4 us
    all_to_all x1, blocking collectives, by_head(): lax.all_to_all(near_out.reshape(half, tok_rows, cols_each), 'seq', split_...  17.4 us
    pallas_call x1, Pallas kernels, attend(): pl.pallas_call(lambda *refs: attend_kernel(tok_rows, *refs), out_shape=ja...  14.1 us
    ppermute x4, starting transfers between devices, by_head(): lax.ppermute(near[a:b, :rows], 'seq', swap_halves)  11 us
    pallas_call x1, Pallas kernels, project(): pl.pallas_call(project_kernel, out_shape=jax.ShapeDtypeStruct((tokens, co...  8.99 us
    all_to_all x2, starting transfers between devices, spread(): lax.all_to_all(copies, 'seq', split_axis=0, concat_axis=0, axis_index_gro...  8.19 us
    ppermute x1, waiting for transfers between devices, by_head(): far_ids = lax.ppermute(slot_ids, 'head', swap_heads)  7.85 us
  transfers between devices with their start and end apart: 19, of which 11 were waited for; matrix products, arithmetic and copies ran while one was open for 2% of the time, Pallas kernels for 21%

profile of v7, /device:TPU:0, one launch (start us, length us, event | category | flops | bytes accessed | tf_op | source)
XLA Modules:
  0.0 199.0 jit_solution(17915080050978643978)
XLA Ops:
  0.0 0.9 fusion.6
  0.9 1.5 copy.44
  2.4 0.5 copy_bitcast_fusion
  3.0 1.8 pad_maximum_fusion
  4.8 7.6 %all-to-all-start = ((bf16[16,784,128]{2,1,0:T(8,128)(2,1)}), bf16[16,784,128]{2,1,0:T(8,128)(2,1)}, u32[]{:S(2)}, u32[]{:S(2)}) async-start(bf16[16,784,128]{2,1,0:T(8,128)(2,1)} %pad_maximum_fusion), calls=%async_computation | async-start | bytes 6422528 | tf_op jit(solution)/shard_map/all_to_all | solution.py:242
  12.5 0.3 copy.32
  12.8 2.4 %constant_dynamic-slice_fusion = (bf16[256,1,256]{2,1,0:T(2,128)(2,1)S(1)}, bf16[256,1,256]{2,1,0:T(2,128)(2,1)S(1)}, bf16[256,1,256]{2,1,0:T(2,128)(2,1)S(1)}, ...) fusion(bf16[256,8,256]{2,1,0:T(8,128)(2,1)S(1)} %bitcast.101, ...), kind=kLoop, calls=%fused_computation.68 | loop fusion | bytes 2097184 | tf_op jit(solution)/shard_map/dynamic-slice.7
  15.4 0.1 pad_maximum_fusion.1
  15.5 2.6 %collective-permute-start.6 = (bf16[288,256]{1,0:T(8,128)(2,1)S(1)}, bf16[288,256]{1,0:T(8,128)(2,1)S(1)}, u32[]{:S(2)}, u32[]{:S(2)}) collective-permute-start(bf16[288,256]{1,0:T(8,128)(2,1)S(1)} %get-tuple-element.50), channel_id=1, source_target_pairs={{0,14},{2,12},{4,10},{6,8},{8,6},{10,4},{12,2},{14,0},{16,30},{18,... | collective-permute-start | bytes 442376 | tf_op jit(solution)/shard_map/ppermute | solution.py:250
  18.1 0.4 collective-permute-start
  18.4 0.6 collective-permute-start.1
  19.0 0.9 collective-permute-start.2
  19.9 0.6 collective-permute-start.3
  20.6 0.0 collective-permute-done
  20.6 1.5 collective-permute-start.4
  22.1 15.2 %collective-permute-done.1 = bf16[288,256]{1,0:T(8,128)(2,1)S(1)} collective-permute-done((bf16[288,256]{1,0:T(8,128)(2,1)S(1)}, bf16[288,256]{1,0:T(8,128)(2,1)S(1)}, u32[]{:S(2)}, u32[]{:S(2)}) %collective-permute-start.1) | collective-permute-done | bytes 147488 | tf_op jit(solution)/shard_map/ppermute | solution.py:250
  37.3 0.5 collective-permute-start.5
  37.8 7.0 %collective-permute-done.2 = bf16[288,256]{1,0:T(8,128)(2,1)S(1)} collective-permute-done((bf16[288,256]{1,0:T(8,128)(2,1)S(1)}, bf16[288,256]{1,0:T(8,128)(2,1)S(1)}, u32[]{:S(2)}, u32[]{:S(2)}) %collective-permute-start.2) | collective-permute-done | bytes 147488 | tf_op jit(solution)/shard_map/ppermute | solution.py:250
  44.8 27.9 %collective-permute-done.3 = bf16[288,256]{1,0:T(8,128)(2,1)S(1)} collective-permute-done((bf16[288,256]{1,0:T(8,128)(2,1)S(1)}, bf16[288,256]{1,0:T(8,128)(2,1)S(1)}, u32[]{:S(2)}, u32[]{:S(2)}) %collective-permute-start.3) | collective-permute-done | bytes 147488 | tf_op jit(solution)/shard_map/ppermute | solution.py:250
  72.7 3.1 %collective-permute-done.4 = bf16[288,256]{1,0:T(8,128)(2,1)S(1)} collective-permute-done((bf16[288,256]{1,0:T(8,128)(2,1)S(1)}, bf16[288,256]{1,0:T(8,128)(2,1)S(1)}, u32[]{:S(2)}, u32[]{:S(2)}) %collective-permute-start.4) | collective-permute-done | bytes 147488 | tf_op jit(solution)/shard_map/ppermute | solution.py:250
  75.9 5.0 %collective-permute-done.5 = bf16[288,256]{1,0:T(8,128)(2,1)S(1)} collective-permute-done((bf16[288,256]{1,0:T(8,128)(2,1)S(1)}, bf16[288,256]{1,0:T(8,128)(2,1)S(1)}, u32[]{:S(2)}, u32[]{:S(2)}) %collective-permute-start.5) | collective-permute-done | bytes 147488 | tf_op jit(solution)/shard_map/ppermute | solution.py:250
  80.8 0.0 collective-permute-done.6
  80.9 0.0 all-to-all-done.refs_0_
  80.9 6.9 %collective-permute-start.7 = (bf16[2,256,256]{2,1,0:T(8,128)(2,1)S(1)}, bf16[2,256,256]{2,1,0:T(8,128)(2,1)S(1)}, u32[]{:S(2)}, u32[]{:S(2)}) collective-permute-start(bf16[2,256,256]{2,1,0:T(8,128)(2,1)S(1)} %slice.21), channel_id=1, source_target_pairs={{0,16},{2,18},{4,20},{6,22},{8,24},{10,26},{12,28},{14,30},{16,0},... | collective-permute-start | bytes 786440 | tf_op jit(solution)/shard_map/ppermute | solution.py:254
  87.9 14.1 %attend.1 = bf16[512,128]{1,0:T(8,128)(2,1)S(1)} custom-call(bf16[16,784,128]{2,1,0:T(8,128)(2,1)} %all-to-all-done.refs_0_), custom_call_target="tpu_custom_call" | custom-call | flops 2147483648 | bytes 3211264 | tf_op jit(solution)/shard_map/attend/pallas_call | solution.py:104
  101.9 0.0 collective-permute-done.7.refs_0_
  101.9 0.0 copy-start
  102.0 0.1 collective-permute-start.8
  102.1 6.4 %collective-permute-done.8 = bf16[512,128]{1,0:T(8,128)(2,1)S(1)} collective-permute-done((bf16[512,128]{1,0:T(8,128)(2,1)S(1)}, bf16[512,128]{1,0:T(8,128)(2,1)S(1)}, u32[]{:S(2)}, u32[]{:S(2)}) %collective-permute-start.8) | collective-permute-done | bytes 131104 | tf_op jit(solution)/shard_map/ppermute | solution.py:268
  108.5 1.1 broadcast_in_dim.4
  109.7 4.1 %all-to-all-start.1 = ((bf16[4,2,512,128]{3,2,1,0:T(8,128)(2,1)}), bf16[4,2,512,128]{3,2,1,0:T(8,128)(2,1)S(1)}, u32[]{:S(2)}, u32[]{:S(2)}) async-start(bf16[4,2,512,128]{3,2,1,0:T(8,128)(2,1)} %broadcast_in_dim.4), calls=%async_computation.1 | async-start | bytes 2097152 | tf_op jit(solution)/shard_map/all_to_all | solution.py:263
  113.9 0.1 reshape.45
  114.0 0.4 rev.7
  114.4 0.9 fusion.11
  115.3 1.2 collective-permute-start.11
  116.5 1.5 collective-permute-start.10
  118.0 0.1 broadcast_select_fusion
  118.1 0.1 copy.20
  118.2 0.6 collective-permute-start.9
  118.8 7.8 %collective-permute-done.9.ids_ref = s32[2,8,2048]{2,1,0:T(8,128)S(1)} collective-permute-done((s32[2,8,2048]{2,1,0:T(8,128)S(1)}, s32[2,8,2048]{2,1,0:T(8,128)S(1)}, u32[]{:S(2)}, u32[]{:S(2)}) %collective-permute-start.9) | collective-permute-done | bytes 131104 | tf_op jit(solution)/shard_map/ppermute | solution.py:278
  126.6 3.4 %collective-permute-done.11.refs_1_ = bf16[2,256,256]{2,1,0:T(8,128)(2,1)S(1)} collective-permute-done((bf16[2,256,256]{2,1,0:T(8,128)(2,1)}, bf16[2,256,256]{2,1,0:T(8,128)(2,1)S(1)}, u32[]{:S(2)}, u32[]{:S(2)}) %collective-permute-start.11) | collective-permute-done | bytes 262176 | tf_op jit(solution)/shard_map/ppermute | solution.py:257
  130.1 0.0 collective-permute-done.10
  130.1 2.1 %all-to-all-done.1 = bf16[4,2,512,128]{3,2,1,0:T(8,128)(2,1)S(1)} async-done(((bf16[4,2,512,128]{3,2,1,0:T(8,128)(2,1)}), bf16[4,2,512,128]{3,2,1,0:T(8,128)(2,1)S(1)}, u32[]{:S(2)}, u32[]{:S(2)}) %all-to-all-start.1) | async-done | bytes 1048608 | tf_op jit(solution)/shard_map/all_to_all | solution.py:263
  132.2 1.1 broadcast_in_dim.5
  133.3 4.1 %all-to-all-start.2 = ((bf16[4,2,512,128]{3,2,1,0:T(8,128)(2,1)}), bf16[4,2,512,128]{3,2,1,0:T(8,128)(2,1)S(1)}, u32[]{:S(2)}, u32[]{:S(2)}) async-start(bf16[4,2,512,128]{3,2,1,0:T(8,128)(2,1)} %broadcast_in_dim.5), calls=%async_computation.2 | async-start | bytes 2097152 | tf_op jit(solution)/shard_map/all_to_all | solution.py:263
  137.4 0.0 collective-permute-start.12
  137.4 1.0 collective-permute-start.13
  138.3 7.1 %expand.4.refs_0_ = bf16[32,2048,128]{2,1,0:T(8,128)(2,1)} custom-call(s32[2,8,2048]{2,1,0:T(8,128)S(1)} %reshape.46.ids_ref, bf16[8,512,128]{2,1,0:T(8,128)(2,1)S(1)} %bitcast.96), custom_call_target="tpu_custom_call" | custom-call | flops 4294967296 | bytes 5242880 | tf_op jit(solution)/shard_map/expand/pallas_call | solution.py:141
  145.4 0.0 collective-permute-done.12.attended_ref
  145.4 7.1 %expand.5.refs_0_ = bf16[32,2048,128]{2,1,0:T(8,128)(2,1)} custom-call(s32[2,8,2048]{2,1,0:T(8,128)S(1)} %reshape.46.ids_ref, bf16[8,512,128]{2,1,0:T(8,128)(2,1)S(1)} %collective-permute-done.12.attended_ref, bf16[32,2048,128]{2,1,0:T(8,128)(2,1)} %expand.4.refs_0_), custom_call_target="tpu_custom_call", output_to_operand_aliasing={{}: (2, {})} | custom-call | flops 4294967296 | bytes 5242880 | tf_op jit(solution)/shard_map/expand/pallas_call | solution.py:141
  152.6 0.7 collective-permute-done.13.refs_2_
  153.2 0.7 copy-done.4
  153.9 1.4 all-to-all-done.2
  155.4 0.0 collective-permute-start.14
  155.4 0.1 pad_add_fusion.places_ref
  155.4 1.9 collective-permute-start.15
  157.3 7.1 %expand.6.refs_0_ = bf16[32,2048,128]{2,1,0:T(8,128)(2,1)} custom-call(s32[2,8,2048]{2,1,0:T(8,128)S(1)} %collective-permute-done.9.ids_ref, bf16[8,512,128]{2,1,0:T(8,128)(2,1)S(1)} %bitcast.98, bf16[32,2048,128]{2,1,0:T(8,128)(2,1)} %expand.5.refs_0_), custom_call_target="tpu_custom_call", output_to_operand_aliasing={{}: (2, {})} | custom-call | flops 4294967296 | bytes 5242880 | tf_op jit(solution)/shard_map/expand/pallas_call | solution.py:141
  164.4 0.0 collective-permute-done.14.attended_ref
  164.4 7.1 %expand.7.features_ref = bf16[32,2048,128]{2,1,0:T(8,128)(2,1)} custom-call(s32[2,8,2048]{2,1,0:T(8,128)S(1)} %collective-permute-done.9.ids_ref, bf16[8,512,128]{2,1,0:T(8,128)(2,1)S(1)} %collective-permute-done.14.attended_ref, bf16[32,2048,128]{2,1,0:T(8,128)(2,1)} %expand.6.refs_0_), custom_call_target="tpu_custom_call", output_to_operand_aliasing={{}: (2, {})} | custom-call | flops 4294967296 | bytes 5242880 | tf_op jit(solution)/shard_map/expand/pallas_call | solution.py:141
  171.5 0.0 collective-permute-done.15.refs_3_
  171.5 0.0 copy-done.3
  171.5 9.0 %project.1 = bf16[2048,256]{1,0:T(8,128)(2,1)S(1)} custom-call(s32[4]{0:T(128)S(1)} %pad_add_fusion.places_ref, bf16[32,2048,128]{2,1,0:T(8,128)(2,1)} %expand.7.features_ref, bf16[8,288,256]{2,1,0:T(8,128)(2,1)S(1)} %bitcast_dynamic-update-slice_fusion.near_ref, bf16[2,256,256]{2,1,0:T(8,128)(2,1)S(1)} %copy-done.1, bf16[2,256,256]{2,1,0:T(8,128)(2,1)S(1)} %copy-done.3, ...), custom_call_target="tpu_custom_call" | custom-call | flops 4294967296 | bytes 19922944 | tf_op jit(solution)/shard_map/project/pallas_call | solution.py:184
  180.5 17.4 %all_to_all.20 = bf16[8,256,256]{2,1,0:T(8,128)(2,1)S(1)} all-to-all(bf16[8,256,256]{2,1,0:T(8,128)(2,1)S(1)} %bitcast.99), channel_id=1, replica_groups={{0,2,4,6,8,10,12,14},{16,18,20,22,24,26,28,30},{1,3,5,7,9,11,13,15},{17..., dimensions={0} | all-to-all | bytes 2097152 | tf_op jit(solution)/shard_map/all_to_all | solution.py:296
  197.9 1.1 copy.30
  (48 shorter events, 0.5 us)
Async XLA Ops:
  0.0 2.4 %copy-start.7 = (bf16[256,16,128]{2,1,0:T(8,128)(2,1)S(1)}, bf16[256,16,128]{2,1,0:T(8,128)(2,1)}, u32[]{:S(2)}) copy-start(bf16[256,16,128]{2,1,0:T(8,128)(2,1)} %param.7) | copy-start | bytes 3145732
  0.0 2.4 %copy-start.8 = (bf16[256,16,128]{2,1,0:T(8,128)(2,1)S(1)}, bf16[256,16,128]{2,1,0:T(8,128)(2,1)}, u32[]{:S(2)}) copy-start(bf16[256,16,128]{2,1,0:T(8,128)(2,1)} %param.6) | copy-start | bytes 3145732
  4.8 7.6 %copy-start.6 = (bf16[256,2048]{1,0:T(8,128)(2,1)S(1)}, bf16[256,2048]{1,0:T(8,128)(2,1)}, u32[]{:S(2)}) copy-start(bf16[256,2048]{1,0:T(8,128)(2,1)} %param.9) | copy-start | bytes 3145732
  4.8 76.0 %all-to-all-start = ((bf16[16,784,128]{2,1,0:T(8,128)(2,1)}), bf16[16,784,128]{2,1,0:T(8,128)(2,1)}, u32[]{:S(2)}, u32[]{:S(2)}) async-start(bf16[16,784,128]{2,1,0:T(8,128)(2,1)} %pad_maximum_fusion), calls=%async_computation | async-start | bytes 6422528 | tf_op jit(solution)/shard_map/all_to_all | solution.py:242
  15.5 65.3 %collective-permute-start.6 = (bf16[288,256]{1,0:T(8,128)(2,1)S(1)}, bf16[288,256]{1,0:T(8,128)(2,1)S(1)}, u32[]{:S(2)}, u32[]{:S(2)}) collective-permute-start(bf16[288,256]{1,0:T(8,128)(2,1)S(1)} %get-tuple-element.50), channel_id=1, source_target_pairs={{0,14},{2,12},{4,10},{6,8},{8,6},{10,4},{12,2},{14,0},{16,30},{18,... | collective-permute-start | bytes 442376 | tf_op jit(solution)/shard_map/ppermute | solution.py:250
  18.1 2.5 %collective-permute-start = (bf16[288,256]{1,0:T(8,128)(2,1)S(1)}, bf16[288,256]{1,0:T(8,128)(2,1)S(1)}, u32[]{:S(2)}, u32[]{:S(2)}) collective-permute-start(bf16[288,256]{1,0:T(8,128)(2,1)S(1)} %get-tuple-element.51), channel_id=1, source_target_pairs={{0,2},{2,0},{4,6},{6,4},{8,10},{10,8},{12,14},{14,12},{16,18},{18,... | collective-permute-start | bytes 442376 | tf_op jit(solution)/shard_map/ppermute | solution.py:250
  18.4 18.9 %collective-permute-start.1 = (bf16[288,256]{1,0:T(8,128)(2,1)S(1)}, bf16[288,256]{1,0:T(8,128)(2,1)S(1)}, u32[]{:S(2)}, u32[]{:S(2)}) collective-permute-start(bf16[288,256]{1,0:T(8,128)(2,1)S(1)} %get-tuple-element.52), channel_id=1, source_target_pairs={{0,4},{2,6},{4,0},{6,2},{8,12},{10,14},{12,8},{14,10},{16,20},{18,... | collective-permute-start | bytes 442376 | tf_op jit(solution)/shard_map/ppermute | solution.py:250
  19.0 25.8 %collective-permute-start.2 = (bf16[288,256]{1,0:T(8,128)(2,1)S(1)}, bf16[288,256]{1,0:T(8,128)(2,1)S(1)}, u32[]{:S(2)}, u32[]{:S(2)}) collective-permute-start(bf16[288,256]{1,0:T(8,128)(2,1)S(1)} %get-tuple-element.53), channel_id=1, source_target_pairs={{0,6},{2,4},{4,2},{6,0},{8,14},{10,12},{12,10},{14,8},{16,22},{18,... | collective-permute-start | bytes 442376 | tf_op jit(solution)/shard_map/ppermute | solution.py:250
  19.9 52.8 %collective-permute-start.3 = (bf16[288,256]{1,0:T(8,128)(2,1)S(1)}, bf16[288,256]{1,0:T(8,128)(2,1)S(1)}, u32[]{:S(2)}, u32[]{:S(2)}) collective-permute-start(bf16[288,256]{1,0:T(8,128)(2,1)S(1)} %get-tuple-element.54), channel_id=1, source_target_pairs={{0,8},{2,10},{4,12},{6,14},{8,0},{10,2},{12,4},{14,6},{16,24},{18,... | collective-permute-start | bytes 442376 | tf_op jit(solution)/shard_map/ppermute | solution.py:250
  20.6 55.3 %collective-permute-start.4 = (bf16[288,256]{1,0:T(8,128)(2,1)S(1)}, bf16[288,256]{1,0:T(8,128)(2,1)S(1)}, u32[]{:S(2)}, u32[]{:S(2)}) collective-permute-start(bf16[288,256]{1,0:T(8,128)(2,1)S(1)} %get-tuple-element.55), channel_id=1, source_target_pairs={{0,10},{2,8},{4,14},{6,12},{8,2},{10,0},{12,6},{14,4},{16,26},{18,... | collective-permute-start | bytes 442376 | tf_op jit(solution)/shard_map/ppermute | solution.py:250
  37.3 43.5 %collective-permute-start.5 = (bf16[288,256]{1,0:T(8,128)(2,1)S(1)}, bf16[288,256]{1,0:T(8,128)(2,1)S(1)}, u32[]{:S(2)}, u32[]{:S(2)}) collective-permute-start(bf16[288,256]{1,0:T(8,128)(2,1)S(1)} %pad_maximum_fusion.2), channel_id=1, source_target_pairs={{0,12},{2,14},{4,8},{6,10},{8,4},{10,6},{12,0},{14,2},{16,28},{18,... | collective-permute-start | bytes 442376 | tf_op jit(solution)/shard_map/ppermute | solution.py:250
  80.9 21.0 %collective-permute-start.7 = (bf16[2,256,256]{2,1,0:T(8,128)(2,1)S(1)}, bf16[2,256,256]{2,1,0:T(8,128)(2,1)S(1)}, u32[]{:S(2)}, u32[]{:S(2)}) collective-permute-start(bf16[2,256,256]{2,1,0:T(8,128)(2,1)S(1)} %slice.21), channel_id=1, source_target_pairs={{0,16},{2,18},{4,20},{6,22},{8,24},{10,26},{12,28},{14,30},{16,0},... | collective-permute-start | bytes 786440 | tf_op jit(solution)/shard_map/ppermute | solution.py:254
  101.9 7.7 %copy-start = (bf16[2,256,256]{2,1,0:T(8,128)(2,1)}, bf16[2,256,256]{2,1,0:T(8,128)(2,1)S(1)}, u32[]{:S(2)}) copy-start(bf16[2,256,256]{2,1,0:T(8,128)(2,1)S(1)} %collective-permute-done.7.refs_0_) | copy-start | bytes 786436
  102.0 6.6 %collective-permute-start.8 = (bf16[512,128]{1,0:T(8,128)(2,1)S(1)}, bf16[512,128]{1,0:T(8,128)(2,1)S(1)}, u32[]{:S(2)}, u32[]{:S(2)}) collective-permute-start(bf16[512,128]{1,0:T(8,128)(2,1)S(1)} %attend.1), channel_id=1, source_target_pairs={{0,16},{2,18},{4,20},{6,22},{8,24},{10,26},{12,28},{14,30},{16,0},... | collective-permute-start | bytes 393224 | tf_op jit(solution)/shard_map/ppermute | solution.py:268
  109.7 22.5 %all-to-all-start.1 = ((bf16[4,2,512,128]{3,2,1,0:T(8,128)(2,1)}), bf16[4,2,512,128]{3,2,1,0:T(8,128)(2,1)S(1)}, u32[]{:S(2)}, u32[]{:S(2)}) async-start(bf16[4,2,512,128]{3,2,1,0:T(8,128)(2,1)} %broadcast_in_dim.4), calls=%async_computation.1 | async-start | bytes 2097152 | tf_op jit(solution)/shard_map/all_to_all | solution.py:263
  115.3 14.8 %collective-permute-start.11 = (bf16[2,256,256]{2,1,0:T(8,128)(2,1)}, bf16[2,256,256]{2,1,0:T(8,128)(2,1)S(1)}, u32[]{:S(2)}, u32[]{:S(2)}) collective-permute-start(bf16[2,256,256]{2,1,0:T(8,128)(2,1)} %get-tuple-element.41), channel_id=1, source_target_pairs={{0,16},{2,18},{4,20},{6,22},{8,24},{10,26},{12,28},{14,30},{16,0},... | collective-permute-start | bytes 786440 | tf_op jit(solution)/shard_map/ppermute | solution.py:257
  116.5 13.6 %collective-permute-start.10 = (bf16[2,512,128]{2,1,0:T(8,128)(2,1)S(1)}, bf16[2,512,128]{2,1,0:T(8,128)(2,1)S(1)}, u32[]{:S(2)}, u32[]{:S(2)}) collective-permute-start(bf16[2,512,128]{2,1,0:T(8,128)(2,1)S(1)} %pad_maximum_fusion.17), channel_id=1, source_target_pairs={{0,1},{1,0},{2,3},{3,2},{4,5},{5,4},{6,7},{7,6},{8,9},{9,8},{10,11... | collective-permute-start | bytes 786440 | tf_op jit(solution)/shard_map/ppermute | solution.py:269
  118.2 8.5 %collective-permute-start.9 = (s32[2,8,2048]{2,1,0:T(8,128)S(1)}, s32[2,8,2048]{2,1,0:T(8,128)S(1)}, u32[]{:S(2)}, u32[]{:S(2)}) collective-permute-start(s32[2,8,2048]{2,1,0:T(8,128)S(1)} %reshape.46.ids_ref), channel_id=1, source_target_pairs={{0,1},{1,0},{2,3},{3,2},{4,5},{5,4},{6,7},{7,6},{8,9},{9,8},{10,11... | collective-permute-start | bytes 393224 | tf_op jit(solution)/shard_map/ppermute | solution.py:278
  130.1 3.2 %copy-start.2 = (bf16[2,256,256]{2,1,0:T(8,128)(2,1)}, bf16[2,256,256]{2,1,0:T(8,128)(2,1)S(1)}, u32[]{:S(2)}) copy-start(bf16[2,256,256]{2,1,0:T(8,128)(2,1)S(1)} %collective-permute-done.11.refs_1_) | copy-start | bytes 786436
  133.3 22.1 %all-to-all-start.2 = ((bf16[4,2,512,128]{3,2,1,0:T(8,128)(2,1)}), bf16[4,2,512,128]{3,2,1,0:T(8,128)(2,1)S(1)}, u32[]{:S(2)}, u32[]{:S(2)}) async-start(bf16[4,2,512,128]{3,2,1,0:T(8,128)(2,1)} %broadcast_in_dim.5), calls=%async_computation.2 | async-start | bytes 2097152 | tf_op jit(solution)/shard_map/all_to_all | solution.py:263
  137.4 8.1 %collective-permute-start.12 = (bf16[8,512,128]{2,1,0:T(8,128)(2,1)S(1)}, bf16[8,512,128]{2,1,0:T(8,128)(2,1)S(1)}, u32[]{:S(2)}, u32[]{:S(2)}) collective-permute-start(bf16[8,512,128]{2,1,0:T(8,128)(2,1)S(1)} %bitcast.95), channel_id=1, source_target_pairs={{0,2},{2,0},{4,6},{6,4},{8,10},{10,8},{12,14},{14,12},{16,18},{18,... | collective-permute-start | bytes 3145736 | tf_op jit(solution)/shard_map/ppermute | solution.py:283
  137.4 15.8 %collective-permute-start.13 = (bf16[2,256,256]{2,1,0:T(8,128)(2,1)}, bf16[2,256,256]{2,1,0:T(8,128)(2,1)S(1)}, u32[]{:S(2)}, u32[]{:S(2)}) collective-permute-start(bf16[2,256,256]{2,1,0:T(8,128)(2,1)} %get-tuple-element.40), channel_id=1, source_target_pairs={{0,16},{2,18},{4,20},{6,22},{8,24},{10,26},{12,28},{14,30},{16,0},... | collective-permute-start | bytes 786440 | tf_op jit(solution)/shard_map/ppermute | solution.py:257
  153.2 0.7 copy-start.4
  155.4 9.0 %collective-permute-start.14 = (bf16[8,512,128]{2,1,0:T(8,128)(2,1)S(1)}, bf16[8,512,128]{2,1,0:T(8,128)(2,1)S(1)}, u32[]{:S(2)}, u32[]{:S(2)}) collective-permute-start(bf16[8,512,128]{2,1,0:T(8,128)(2,1)S(1)} %bitcast.97), channel_id=1, source_target_pairs={{0,2},{2,0},{4,6},{6,4},{8,10},{10,8},{12,14},{14,12},{16,18},{18,... | collective-permute-start | bytes 3145736 | tf_op jit(solution)/shard_map/ppermute | solution.py:291
  155.4 16.1 %collective-permute-start.15 = (bf16[2,256,256]{2,1,0:T(8,128)(2,1)}, bf16[2,256,256]{2,1,0:T(8,128)(2,1)S(1)}, u32[]{:S(2)}, u32[]{:S(2)}) collective-permute-start(bf16[2,256,256]{2,1,0:T(8,128)(2,1)} %get-tuple-element.39), channel_id=1, source_target_pairs={{0,16},{2,18},{4,20},{6,22},{8,24},{10,26},{12,28},{14,30},{16,0},... | collective-permute-start | bytes 786440 | tf_op jit(solution)/shard_map/ppermute | solution.py:257
  164.4 7.1 %copy-start.1 = (bf16[2,256,256]{2,1,0:T(8,128)(2,1)S(1)}, bf16[2,256,256]{2,1,0:T(8,128)(2,1)}, u32[]{:S(2)}) copy-start(bf16[2,256,256]{2,1,0:T(8,128)(2,1)} %copy-done) | copy-start | bytes 786436
  164.4 7.1 %copy-start.3 = (bf16[2,256,256]{2,1,0:T(8,128)(2,1)S(1)}, bf16[2,256,256]{2,1,0:T(8,128)(2,1)}, u32[]{:S(2)}) copy-start(bf16[2,256,256]{2,1,0:T(8,128)(2,1)} %copy-done.2) | copy-start | bytes 786436
  164.4 7.1 %copy-start.5 = (bf16[2,256,256]{2,1,0:T(8,128)(2,1)S(1)}, bf16[2,256,256]{2,1,0:T(8,128)(2,1)}, u32[]{:S(2)}) copy-start(bf16[2,256,256]{2,1,0:T(8,128)(2,1)} %copy-done.4) | copy-start | bytes 786436

commit v8 on v7

--- a/solution.py
+++ b/solution.py
@@ -60,7 +60,7 @@
 
     sums_ref[...] = jnp.zeros_like(sums_ref)
 
-    @pl.loop(0, n_src)
+    @pl.loop(0, n_src, unroll=4)
     def _(src):
         coded = moved_ref[src, 3 * tok_rows :, :].astype(jnp.float32).astype(jnp.int32)
         parts = []
@@ -81,7 +81,7 @@
             top = jnp.maximum(top, scores[:, i * lanes : (i + 1) * lanes])
         return top
 
-    top = lax.fori_loop(0, n_src, score, jnp.full((C, lanes), -jnp.inf, jnp.float32))
+    top = lax.fori_loop(0, n_src, score, jnp.full((C, lanes), -jnp.inf, jnp.float32), unroll=4)
     top = jnp.broadcast_to(jnp.max(top, axis=1, keepdims=True), (C, tok_rows))
 
     acc_ref[...] = jnp.zeros_like(acc_ref)
@@ -94,7 +94,7 @@
         acc_ref[...] += jnp.dot(weights.astype(jnp.bfloat16), values, preferred_element_type=jnp.float32)
         return total
 
-    total = lax.fori_loop(0, n_src, weigh, jnp.zeros((C, lanes), jnp.float32))
+    total = lax.fori_loop(0, n_src, weigh, jnp.zeros((C, lanes), jnp.float32), unroll=4)
     out_ref[...] = (acc_ref[...] / jnp.sum(total, axis=1, keepdims=True)).astype(jnp.bfloat16)
 
 
@@ -119,17 +119,21 @@
     )(moved)
 
 
+def one_hot(column, clusters, lanes):
+    shape = (column.shape[0], lanes)
+    labels = lax.broadcasted_iota(jnp.int32, shape, 1).astype(jnp.int16)
+    ids = jnp.broadcast_to(column, shape).astype(jnp.int16)
+    one, zero = jnp.bfloat16(1.0), jnp.bfloat16(0.0)
+    parts = [jnp.where(ids == labels + jnp.int16(at), one, zero) for at in range(0, clusters, lanes)]
+    return jnp.concatenate(parts, axis=1)
+
+
 def expand_kernel(ids_ref, attended_ref, *refs):
     out_ref = refs[-1]
     heads, clusters, e_width = attended_ref.shape
-    tok_tile = ids_ref.shape[2]
-    labels = lax.broadcasted_iota(jnp.int32, (tok_tile, e_width), 1).astype(jnp.int16)
-    one, zero = jnp.bfloat16(1.0), jnp.bfloat16(0.0)
     columns = ids_ref[0].T
     for h in range(heads):
-        ids = jnp.broadcast_to(columns[:, h : h + 1], (tok_tile, e_width)).astype(jnp.int16)
-        parts = [jnp.where(ids == labels + jnp.int16(at), one, zero) for at in range(0, clusters, e_width)]
-        onehot = jnp.concatenate(parts, axis=1)
+        onehot = one_hot(columns[:, h : h + 1], clusters, e_width)
         found = jnp.dot(onehot, attended_ref[h], preferred_element_type=jnp.float32)
         out_ref[h] = found.astype(jnp.bfloat16)
 
@@ -159,23 +163,35 @@
     )(ids, attended, *held)
 
 
+def slot_of(place, k, half_at, chips):
+    chip = jnp.bitwise_xor(place, k)
+    return 2 * lax.rem(chip, chips // 2) + jnp.bitwise_xor(half_at, lax.div(chip, chips // 2))
+
+
 def project_kernel(places_ref, features_ref, near_ref, *refs):
     *far_refs, out_ref = refs
     heads, _, e_width = features_ref.shape
-    each = heads // 4
+    chips = heads // 2
     head_at, core, half_at, place = (places_ref[i] for i in range(4))
-    total = None
-    for plane, weight_refs in ((half_at, (near_ref,)), (1 - half_at, far_refs)):
-        base = jnp.where(plane == head_at, 0, 2 * each)
+
+    def add_up(weight_refs):
+        total = None
         blocks = [(x, i) for x in weight_refs for i in range(x.shape[0])]
         for k, (weight_ref, i) in enumerate(blocks):
-            chip = jnp.bitwise_xor(place, k)
-            slot = 2 * lax.rem(chip, each // 2) + jnp.bitwise_xor(half_at, lax.div(chip, each // 2))
-            left = jnp.concatenate([features_ref[base + at * each + slot] for at in (core, 1 - core)], axis=1)
+            slot = slot_of(place, k, half_at, chips)
+            left = jnp.concatenate([features_ref[at * chips + slot] for at in (core, 1 - core)], axis=1)
             right = weight_ref[i, : 2 * e_width, :]
             term = jnp.dot(left, right, preferred_element_type=jnp.float32)
             total = term if total is None else total + term
-    out_ref[...] = total.astype(jnp.bfloat16)
+        out_ref[...] = total
+
+    @pl.when(half_at == head_at)
+    def _():
+        add_up((near_ref,))
+
+    @pl.when(half_at != head_at)
+    def _():
+        add_up(far_refs)
 
 
 def project(places, features, near, far, tok_tile):
@@ -183,7 +199,7 @@
     cols = near.shape[2]
     return pl.pallas_call(
         project_kernel,
-        out_shape=jax.ShapeDtypeStruct((tokens, cols), jnp.bfloat16),
+        out_shape=jax.ShapeDtypeStruct((tokens, cols), jnp.float32),
         grid_spec=pltpu.PrefetchScalarGridSpec(
             num_scalar_prefetch=1,
             grid=(tokens // tok_tile,),
@@ -197,11 +213,77 @@
         compiler_params=pltpu.CompilerParams(vmem_limit_bytes=50 * 2**20),
         cost_estimate=pl.CostEstimate(
             flops=2 * tokens * heads * e_width * cols,
-            bytes_accessed=2 * (features.size + heads * e_width * cols + tokens * cols),
+            bytes_accessed=2 * (features.size + heads * e_width * cols + 2 * tokens * cols),
             transcendentals=0,
         ),
         name="project",
     )(places, features, near, *far)
+
+
+def lookup_kernel(places_ref, ids_ref, same_ref, other_ref, sum_ref, near_ref, *refs):
+    *far_refs, out_ref, table_ref = refs
+    chips, clusters, e_width = same_ref.shape
+    head_at, core, half_at, place = (places_ref[i] for i in range(4))
+
+    def make_table(weight_refs):
+        blocks = [(x, i) for x in weight_refs for i in range(x.shape[0])]
+        for k, (weight_ref, i) in enumerate(blocks):
+            slot = slot_of(place, k, half_at, chips)
+            for part, (attended_ref, at) in enumerate(((same_ref, core), (other_ref, 1 - core))):
+                right = weight_ref[i, pl.ds(pl.multiple_of(at * e_width, e_width), e_width), :]
+                product = jnp.dot(attended_ref[slot], right, preferred_element_type=jnp.float32)
+                table_ref[part * chips + slot] = product.astype(jnp.bfloat16)
+
+    first = pl.program_id(0) == 0
+
+    @pl.when(jnp.logical_and(first, half_at != head_at))
+    def _():
+        make_table((near_ref,))
+
+    @pl.when(jnp.logical_and(first, half_at == head_at))
+    def _():
+        make_table(far_refs)
+
+    total = sum_ref[...]
+    for part in range(2):
+        columns = ids_ref[part].T
+        for h in range(0, chips, 2):
+            onehot = jnp.concatenate(
+                [one_hot(columns[:, i : i + 1], clusters, e_width) for i in (h, h + 1)], axis=1
+            )
+            right = jnp.concatenate([table_ref[part * chips + i] for i in (h, h + 1)], axis=0)
+            total += jnp.dot(onehot, right, preferred_element_type=jnp.float32)
+    out_ref[...] = total.astype(jnp.bfloat16)
+
+
+def lookup(places, ids, same, other, sums, near, far, tok_tile):
+    chips, clusters, e_width = same.shape
+    tokens, cols = sums.shape
+    return pl.pallas_call(
+        lookup_kernel,
+        out_shape=jax.ShapeDtypeStruct((tokens, cols), jnp.bfloat16),
+        grid_spec=pltpu.PrefetchScalarGridSpec(
+            num_scalar_prefetch=1,
+            grid=(tokens // tok_tile,),
+            in_specs=[
+                pl.BlockSpec((2, chips, tok_tile), lambda i, _: (0, 0, i)),
+                pl.BlockSpec(same.shape, lambda i, _: (0, 0, 0)),
+                pl.BlockSpec(other.shape, lambda i, _: (0, 0, 0)),
+                pl.BlockSpec((tok_tile, cols), lambda i, _: (i, 0)),
+                pl.BlockSpec(near.shape, lambda i, _: (0, 0, 0)),
+            ]
+            + [pl.BlockSpec(x.shape, lambda i, _: (0, 0, 0)) for x in far],
+            out_specs=pl.BlockSpec((tok_tile, cols), lambda i, _: (i, 0)),
+            scratch_shapes=[pltpu.VMEM((2 * chips, clusters, cols), jnp.bfloat16)],
+        ),
+        compiler_params=pltpu.CompilerParams(vmem_limit_bytes=50 * 2**20),
+        cost_estimate=pl.CostEstimate(
+            flops=4 * tokens * chips * clusters * cols,
+            bytes_accessed=4 * (same.size + near.size + 2 * tokens * cols),
+            transcendentals=0,
+        ),
+        name="lookup",
+    )(places, ids, same, other, sums, near, *far)
 
 
 def by_slot(ids, half_at, core):
@@ -250,7 +332,7 @@
         near.append(lax.ppermute(block, "seq", [(i, i ^ k) for i in range(n_seq)]) if k else block)
     near = jnp.stack(near)
     moved, near = lax.optimization_barrier((moved, near))
-    cuts = [half * i // 4 for i in range(5)]
+    cuts = [half * i // 8 for i in (0, 3, 5, 8)]
     far = [lax.ppermute(near[a:b, :rows], "seq", swap_halves) for a, b in zip(cuts[:1], cuts[1:])]
     own = attend(moved, tok_rows)
     own, near, far[0] = lax.optimization_barrier((own, near, far[0]))
@@ -283,16 +365,14 @@
     second = lax.ppermute(first, "seq", swap_cores)
     third = spread(far_copies)
 
-    pieces = 4
     tok_tile = 2 * tok_rows
-    features = expand(slot_ids, 0, first, None, 0, pieces, tok_tile)
-    features = expand(slot_ids, 1, second, features, 1, pieces, tok_tile)
+    features = expand(slot_ids, 0, first, None, 0, 2, tok_tile)
+    features = expand(slot_ids, 1, second, features, 1, 2, tok_tile)
     features, third, far[2] = lax.optimization_barrier((features, third, far[2]))
     fourth = lax.ppermute(third, "seq", swap_cores)
-    features = expand(far_ids, 0, third, features, 2, pieces, tok_tile)
-    features = expand(far_ids, 1, fourth, features, 3, pieces, tok_tile)
     places = jnp.stack([head_at, core, half_at, place]).astype(jnp.int32)
-    near_out = project(places, features, near, far, tok_tile)
+    sums = project(places, features, near, far, tok_tile)
+    near_out = lookup(places, far_ids, third, fourth, sums, near, far, tok_tile)
     mixed = lax.all_to_all(
         near_out.reshape(half, tok_rows, cols_each),
         "seq",

time: 200 us -> 207 us (1.035)
  waiting for transfers between devices: 80.1 us -> 95.1 us
  Pallas kernels: 51.5 us -> 43.8 us
  starting transfers between devices: 35.9 us -> 33.5 us
    pallas_call x0 -> x1, Pallas kernels: none -> 14.4 us  [lookup(): pl.pallas_call(lookup_kernel, out_shape=jax.ShapeDtypeStruct((tokens, col...]
    pallas_call x4 -> x2, Pallas kernels: 28.4 us -> 14.2 us  [expand(): pl.pallas_call(expand_kernel, out_shape=jax.ShapeDtypeStruct((pieces * he...]
    ppermute x4 -> x3, waiting for transfers between devices: 4.09 us -> 18 us  [by_head(): lax.ppermute(near[a:b, :rows], 'seq', swap_halves)]
    pallas_call x1, Pallas kernels: 14.1 us -> 8.02 us  [attend(): pl.pallas_call(lambda *refs: attend_kernel(tok_rows, *refs), out_shape=ja...]
    ppermute x4 -> x3, starting transfers between devices: 11 us -> 9.99 us  [by_head(): lax.ppermute(near[a:b, :rows], 'seq', swap_halves)]
  transfers between devices with their start and end apart: 19 -> 18, of which waited for: 11 -> 13; matrix products, arithmetic and copies ran while one was open for 2% -> 2% of each run, Pallas kernels for 21% -> 14%
where the time goes in v8:
time: 207 us; the launch traced here: 206 us
  waiting for transfers between devices  95.1 us (46%)
  Pallas kernels  43.8 us (21%)
  starting transfers between devices  33.5 us (16%)
  blocking collectives  18.9 us (9%)
  local copies, waits for them, and re-layouts  11.5 us (6%)
  other arithmetic  3.08 us (1%)
    ppermute x7, waiting for transfers between devices, by_head(): lax.ppermute(block, 'seq', [(i, i ^ k) for i in range(n_seq)])  58.1 us
    all_to_all x1, blocking collectives, by_head(): lax.all_to_all(near_out.reshape(half, tok_rows, cols_each), 'seq', split_...  18.9 us
    ppermute x3, waiting for transfers between devices, by_head(): lax.ppermute(near[a:b, :rows], 'seq', swap_halves)  18 us
    pallas_call x1, Pallas kernels, lookup(): pl.pallas_call(lookup_kernel, out_shape=jax.ShapeDtypeStruct((tokens, col...  14.4 us
    pallas_call x2, Pallas kernels, expand(): pl.pallas_call(expand_kernel, out_shape=jax.ShapeDtypeStruct((pieces * he...  14.2 us
    ppermute x3, starting transfers between devices, by_head(): lax.ppermute(near[a:b, :rows], 'seq', swap_halves)  9.99 us
    ppermute x1, waiting for transfers between devices, by_head(): pair = jnp.stack([own, lax.ppermute(own, 'seq', swap_halves)])  8.07 us
    pallas_call x1, Pallas kernels, attend(): pl.pallas_call(lambda *refs: attend_kernel(tok_rows, *refs), out_shape=ja...  8.02 us
  transfers between devices with their start and end apart: 18, of which 13 were waited for; matrix products, arithmetic and copies ran while one was open for 2% of the time, Pallas kernels for 14%

profile of v8, /device:TPU:0, one launch (start us, length us, event | category | flops | bytes accessed | tf_op | source)
XLA Modules:
  0.0 206.4 jit_solution(8338741048521355835)
XLA Ops:
  0.0 0.9 fusion.6
  0.9 1.5 copy.42
  2.4 0.0 copy-done.8
  2.4 0.5 copy_bitcast_fusion
  3.0 1.8 pad_maximum_fusion
  4.8 7.6 %all-to-all-start = ((bf16[16,784,128]{2,1,0:T(8,128)(2,1)}), bf16[16,784,128]{2,1,0:T(8,128)(2,1)}, u32[]{:S(2)}, u32[]{:S(2)}) async-start(bf16[16,784,128]{2,1,0:T(8,128)(2,1)} %pad_maximum_fusion), calls=%async_computation | async-start | bytes 6422528 | tf_op jit(solution)/shard_map/all_to_all | solution.py:324
  12.5 0.3 copy.30
  12.8 2.4 %constant_dynamic-slice_fusion = (bf16[256,1,256]{2,1,0:T(2,128)(2,1)S(1)}, bf16[256,1,256]{2,1,0:T(2,128)(2,1)S(1)}, bf16[256,1,256]{2,1,0:T(2,128)(2,1)S(1)}, ...) fusion(bf16[256,8,256]{2,1,0:T(8,128)(2,1)S(1)} %bitcast.101, ...), kind=kLoop, calls=%fused_computation.68 | loop fusion | bytes 2097184 | tf_op jit(solution)/shard_map/dynamic-slice.7
  15.4 0.1 pad_maximum_fusion.1
  15.5 0.4 collective-permute-start
  15.9 1.7 collective-permute-start.1
  17.6 0.0 collective-permute-start.2
  17.6 1.7 collective-permute-start.3
  19.3 0.1 collective-permute-start.4
  19.5 0.0 collective-permute-done
  19.5 2.6 %collective-permute-start.5 = (bf16[288,256]{1,0:T(8,128)(2,1)S(1)}, bf16[288,256]{1,0:T(8,128)(2,1)S(1)}, u32[]{:S(2)}, u32[]{:S(2)}) collective-permute-start(bf16[288,256]{1,0:T(8,128)(2,1)S(1)} %pad_maximum_fusion.2), channel_id=1, source_target_pairs={{0,12},{2,14},{4,8},{6,10},{8,4},{10,6},{12,0},{14,2},{16,28},{18,... | collective-permute-start | bytes 442376 | tf_op jit(solution)/shard_map/ppermute | solution.py:332
  22.1 15.2 %collective-permute-done.1 = bf16[288,256]{1,0:T(8,128)(2,1)S(1)} collective-permute-done((bf16[288,256]{1,0:T(8,128)(2,1)S(1)}, bf16[288,256]{1,0:T(8,128)(2,1)S(1)}, u32[]{:S(2)}, u32[]{:S(2)}) %collective-permute-start.1) | collective-permute-done | bytes 147488 | tf_op jit(solution)/shard_map/ppermute | solution.py:332
  37.3 0.0 collective-permute-start.6
  37.3 7.4 %collective-permute-done.2 = bf16[288,256]{1,0:T(8,128)(2,1)S(1)} collective-permute-done((bf16[288,256]{1,0:T(8,128)(2,1)S(1)}, bf16[288,256]{1,0:T(8,128)(2,1)S(1)}, u32[]{:S(2)}, u32[]{:S(2)}) %collective-permute-start.2) | collective-permute-done | bytes 147488 | tf_op jit(solution)/shard_map/ppermute | solution.py:332
  44.8 23.8 %collective-permute-done.3 = bf16[288,256]{1,0:T(8,128)(2,1)S(1)} collective-permute-done((bf16[288,256]{1,0:T(8,128)(2,1)S(1)}, bf16[288,256]{1,0:T(8,128)(2,1)S(1)}, u32[]{:S(2)}, u32[]{:S(2)}) %collective-permute-start.3) | collective-permute-done | bytes 147488 | tf_op jit(solution)/shard_map/ppermute | solution.py:332
  68.6 3.1 %collective-permute-done.4 = bf16[288,256]{1,0:T(8,128)(2,1)S(1)} collective-permute-done((bf16[288,256]{1,0:T(8,128)(2,1)S(1)}, bf16[288,256]{1,0:T(8,128)(2,1)S(1)}, u32[]{:S(2)}, u32[]{:S(2)}) %collective-permute-start.4) | collective-permute-done | bytes 147488 | tf_op jit(solution)/shard_map/ppermute | solution.py:332
  71.8 6.2 %collective-permute-done.5 = bf16[288,256]{1,0:T(8,128)(2,1)S(1)} collective-permute-done((bf16[288,256]{1,0:T(8,128)(2,1)S(1)}, bf16[288,256]{1,0:T(8,128)(2,1)S(1)}, u32[]{:S(2)}, u32[]{:S(2)}) %collective-permute-start.5) | collective-permute-done | bytes 147488 | tf_op jit(solution)/shard_map/ppermute | solution.py:332
  78.1 2.3 %collective-permute-done.6 = bf16[288,256]{1,0:T(8,128)(2,1)S(1)} collective-permute-done((bf16[288,256]{1,0:T(8,128)(2,1)S(1)}, bf16[288,256]{1,0:T(8,128)(2,1)S(1)}, u32[]{:S(2)}, u32[]{:S(2)}) %collective-permute-start.6) | collective-permute-done | bytes 147488 | tf_op jit(solution)/shard_map/ppermute | solution.py:332
  80.4 0.0 all-to-all-done.refs_0_
  80.4 7.4 %collective-permute-start.7 = (bf16[3,256,256]{2,1,0:T(8,128)(2,1)S(1)}, bf16[3,256,256]{2,1,0:T(8,128)(2,1)S(1)}, u32[]{:S(2)}, u32[]{:S(2)}) collective-permute-start(bf16[3,256,256]{2,1,0:T(8,128)(2,1)S(1)} %slice.18), channel_id=1, source_target_pairs={{0,16},{2,18},{4,20},{6,22},{8,24},{10,26},{12,28},{14,30},{16,0},... | collective-permute-start | bytes 1179656 | tf_op jit(solution)/shard_map/ppermute | solution.py:336
  87.9 8.0 %attend.1 = bf16[512,128]{1,0:T(8,128)(2,1)S(1)} custom-call(bf16[16,784,128]{2,1,0:T(8,128)(2,1)} %all-to-all-done.refs_0_), custom_call_target="tpu_custom_call" | custom-call | flops 2147483648 | bytes 3211264 | tf_op jit(solution)/shard_map/attend/pallas_call | solution.py:104
  95.9 9.3 %collective-permute-done.7.refs_0_ = bf16[3,256,256]{2,1,0:T(8,128)(2,1)S(1)} collective-permute-done((bf16[3,256,256]{2,1,0:T(8,128)(2,1)S(1)}, bf16[3,256,256]{2,1,0:T(8,128)(2,1)S(1)}, u32[]{:S(2)}, u32[]{:S(2)}) %collective-permute-start.7) | collective-permute-done | bytes 393248 | tf_op jit(solution)/shard_map/ppermute | solution.py:336
  105.1 0.0 collective-permute-start.8
  105.2 8.1 %collective-permute-done.8 = bf16[512,128]{1,0:T(8,128)(2,1)S(1)} collective-permute-done((bf16[512,128]{1,0:T(8,128)(2,1)S(1)}, bf16[512,128]{1,0:T(8,128)(2,1)S(1)}, u32[]{:S(2)}, u32[]{:S(2)}) %collective-permute-start.8) | collective-permute-done | bytes 131104 | tf_op jit(solution)/shard_map/ppermute | solution.py:350
  113.3 1.1 broadcast_in_dim.4
  114.4 3.5 %all-to-all-start.1 = ((bf16[4,2,512,128]{3,2,1,0:T(8,128)(2,1)}), bf16[4,2,512,128]{3,2,1,0:T(8,128)(2,1)S(1)}, u32[]{:S(2)}, u32[]{:S(2)}) async-start(bf16[4,2,512,128]{3,2,1,0:T(8,128)(2,1)} %broadcast_in_dim.4), calls=%async_computation.1 | async-start | bytes 2097152 | tf_op jit(solution)/shard_map/all_to_all | solution.py:345
  117.9 0.7 slice.22
  118.8 0.1 reshape.45
  118.9 0.4 rev.7
  119.3 1.3 collective-permute-start.11
  120.6 1.5 collective-permute-start.10
  122.1 0.1 broadcast_select_fusion
  122.1 0.1 copy.18
  122.3 0.6 collective-permute-start.9
  122.9 7.5 %collective-permute-done.9.ids_ref = s32[2,8,2048]{2,1,0:T(8,128)S(1)} collective-permute-done((s32[2,8,2048]{2,1,0:T(8,128)S(1)}, s32[2,8,2048]{2,1,0:T(8,128)S(1)}, u32[]{:S(2)}, u32[]{:S(2)}) %collective-permute-start.9) | collective-permute-done | bytes 131104 | tf_op jit(solution)/shard_map/ppermute | solution.py:360
  130.4 5.0 %collective-permute-done.11.refs_1_ = bf16[2,256,256]{2,1,0:T(8,128)(2,1)S(1)} collective-permute-done((bf16[2,256,256]{2,1,0:T(8,128)(2,1)}, bf16[2,256,256]{2,1,0:T(8,128)(2,1)S(1)}, u32[]{:S(2)}, u32[]{:S(2)}) %collective-permute-start.11) | collective-permute-done | bytes 262176 | tf_op jit(solution)/shard_map/ppermute | solution.py:339
  135.4 0.0 collective-permute-done.10
  135.4 2.1 %all-to-all-done.1 = bf16[4,2,512,128]{3,2,1,0:T(8,128)(2,1)S(1)} async-done(((bf16[4,2,512,128]{3,2,1,0:T(8,128)(2,1)}), bf16[4,2,512,128]{3,2,1,0:T(8,128)(2,1)S(1)}, u32[]{:S(2)}, u32[]{:S(2)}) %all-to-all-start.1) | async-done | bytes 1048608 | tf_op jit(solution)/shard_map/all_to_all | solution.py:345
  137.5 1.1 broadcast_in_dim.5
  138.6 0.0 copy-done.5
  138.6 3.7 %all-to-all-start.2 = ((bf16[4,2,512,128]{3,2,1,0:T(8,128)(2,1)}), bf16[4,2,512,128]{3,2,1,0:T(8,128)(2,1)S(1)}, u32[]{:S(2)}, u32[]{:S(2)}) async-start(bf16[4,2,512,128]{3,2,1,0:T(8,128)(2,1)} %broadcast_in_dim.5), calls=%async_computation.2 | async-start | bytes 2097152 | tf_op jit(solution)/shard_map/all_to_all | solution.py:345
  142.3 0.1 collective-permute-start.12
  142.4 1.3 collective-permute-start.13
  143.7 7.1 %expand.2.refs_0_ = bf16[16,2048,128]{2,1,0:T(8,128)(2,1)} custom-call(s32[2,8,2048]{2,1,0:T(8,128)S(1)} %reshape.46.ids_ref, bf16[8,512,128]{2,1,0:T(8,128)(2,1)S(1)} %bitcast.96), custom_call_target="tpu_custom_call" | custom-call | flops 4294967296 | bytes 5242880 | tf_op jit(solution)/shard_map/expand/pallas_call | solution.py:145
  150.8 0.0 collective-permute-done.12.attended_ref
  150.8 7.1 %expand.3.features_ref = bf16[16,2048,128]{2,1,0:T(8,128)(2,1)} custom-call(s32[2,8,2048]{2,1,0:T(8,128)S(1)} %reshape.46.ids_ref, bf16[8,512,128]{2,1,0:T(8,128)(2,1)S(1)} %collective-permute-done.12.attended_ref, bf16[16,2048,128]{2,1,0:T(8,128)(2,1)} %expand.2.refs_0_), custom_call_target="tpu_custom_call", output_to_operand_aliasing={{}: (2, {})} | custom-call | flops 4294967296 | bytes 5242880 | tf_op jit(solution)/shard_map/expand/pallas_call | solution.py:145
  157.9 3.7 %collective-permute-done.13.refs_2_ = bf16[3,256,256]{2,1,0:T(8,128)(2,1)S(1)} collective-permute-done((bf16[3,256,256]{2,1,0:T(8,128)(2,1)S(1)}, bf16[3,256,256]{2,1,0:T(8,128)(2,1)S(1)}, u32[]{:S(2)}, u32[]{:S(2)}) %collective-permute-start.13) | collective-permute-done | bytes 393248 | tf_op jit(solution)/shard_map/ppermute | solution.py:339
  161.7 0.8 copy-done.3
  162.5 1.2 all-to-all-done.2
  163.7 0.0 collective-permute-start.14
  163.7 0.1 pad_add_fusion.places_ref
  163.8 0.0 copy-done.6
  163.8 0.0 copy-start.4
  163.8 1.0 copy-done.4
  164.8 7.1 %project.1.sum_ref = f32[2048,256]{1,0:T(8,128)} custom-call(s32[4]{0:T(128)S(1)} %pad_add_fusion.places_ref, bf16[16,2048,128]{2,1,0:T(8,128)(2,1)} %expand.3.features_ref, bf16[8,288,256]{2,1,0:T(8,128)(2,1)S(1)} %bitcast_dynamic-update-slice_fusion.near_ref, bf16[3,256,256]{2,1,0:T(8,128)(2,1)S(1)} %copy-done.2, bf16[2,256,256]{2,1,0:T(8,128)(2,1)S(1)} %copy-done.6, ...), custom_call_target="tpu_custom_call" | custom-call | flops 2147483648 | bytes 11534336 | tf_op jit(solution)/shard_map/project/pallas_call | solution.py:200
  171.9 0.0 collective-permute-done.14.other_ref
  171.9 14.4 %lookup.1 = bf16[2048,256]{1,0:T(8,128)(2,1)S(1)} custom-call(s32[4]{0:T(128)S(1)} %pad_add_fusion.places_ref, s32[2,8,2048]{2,1,0:T(8,128)S(1)} %collective-permute-done.9.ids_ref, bf16[8,512,128]{2,1,0:T(8,128)(2,1)S(1)} %bitcast.98, bf16[8,512,128]{2,1,0:T(8,128)(2,1)} %collective-permute-done.14.other_ref, f32[2048,256]{1,0:T(8,128)} %project.1.sum_ref, ...), custom_call_target="tpu_custom_call" | custom-call | flops 8589934592 | bytes 8650752 | tf_op jit(solution)/shard_map/lookup/pallas_call | solution.py:262
  186.3 18.9 %all_to_all.20 = bf16[8,256,256]{2,1,0:T(8,128)(2,1)S(1)} all-to-all(bf16[8,256,256]{2,1,0:T(8,128)(2,1)S(1)} %bitcast.99), channel_id=1, replica_groups={{0,2,4,6,8,10,12,14},{16,18,20,22,24,26,28,30},{1,3,5,7,9,11,13,15},{17..., dimensions={0} | all-to-all | bytes 2097152 | tf_op jit(solution)/shard_map/all_to_all | solution.py:376
  205.3 1.1 copy.28
  (48 shorter events, 0.5 us)
Async XLA Ops:
  0.0 2.4 %copy-start.8 = (bf16[256,16,128]{2,1,0:T(8,128)(2,1)S(1)}, bf16[256,16,128]{2,1,0:T(8,128)(2,1)}, u32[]{:S(2)}) copy-start(bf16[256,16,128]{2,1,0:T(8,128)(2,1)} %param.7) | copy-start | bytes 3145732
  0.0 2.4 %copy-start.9 = (bf16[256,16,128]{2,1,0:T(8,128)(2,1)S(1)}, bf16[256,16,128]{2,1,0:T(8,128)(2,1)}, u32[]{:S(2)}) copy-start(bf16[256,16,128]{2,1,0:T(8,128)(2,1)} %param.6) | copy-start | bytes 3145732
  4.8 7.6 %copy-start.7 = (bf16[256,2048]{1,0:T(8,128)(2,1)S(1)}, bf16[256,2048]{1,0:T(8,128)(2,1)}, u32[]{:S(2)}) copy-start(bf16[256,2048]{1,0:T(8,128)(2,1)} %param.9) | copy-start | bytes 3145732
  4.8 75.5 %all-to-all-start = ((bf16[16,784,128]{2,1,0:T(8,128)(2,1)}), bf16[16,784,128]{2,1,0:T(8,128)(2,1)}, u32[]{:S(2)}, u32[]{:S(2)}) async-start(bf16[16,784,128]{2,1,0:T(8,128)(2,1)} %pad_maximum_fusion), calls=%async_computation | async-start | bytes 6422528 | tf_op jit(solution)/shard_map/all_to_all | solution.py:324
  15.5 4.0 %collective-permute-start = (bf16[288,256]{1,0:T(8,128)(2,1)S(1)}, bf16[288,256]{1,0:T(8,128)(2,1)S(1)}, u32[]{:S(2)}, u32[]{:S(2)}) collective-permute-start(bf16[288,256]{1,0:T(8,128)(2,1)S(1)} %get-tuple-element.48), channel_id=1, source_target_pairs={{0,2},{2,0},{4,6},{6,4},{8,10},{10,8},{12,14},{14,12},{16,18},{18,... | collective-permute-start | bytes 442376 | tf_op jit(solution)/shard_map/ppermute | solution.py:332
  15.9 21.4 %collective-permute-start.1 = (bf16[288,256]{1,0:T(8,128)(2,1)S(1)}, bf16[288,256]{1,0:T(8,128)(2,1)S(1)}, u32[]{:S(2)}, u32[]{:S(2)}) collective-permute-start(bf16[288,256]{1,0:T(8,128)(2,1)S(1)} %get-tuple-element.49), channel_id=1, source_target_pairs={{0,4},{2,6},{4,0},{6,2},{8,12},{10,14},{12,8},{14,10},{16,20},{18,... | collective-permute-start | bytes 442376 | tf_op jit(solution)/shard_map/ppermute | solution.py:332
  17.6 27.2 %collective-permute-start.2 = (bf16[288,256]{1,0:T(8,128)(2,1)S(1)}, bf16[288,256]{1,0:T(8,128)(2,1)S(1)}, u32[]{:S(2)}, u32[]{:S(2)}) collective-permute-start(bf16[288,256]{1,0:T(8,128)(2,1)S(1)} %get-tuple-element.50), channel_id=1, source_target_pairs={{0,6},{2,4},{4,2},{6,0},{8,14},{10,12},{12,10},{14,8},{16,22},{18,... | collective-permute-start | bytes 442376 | tf_op jit(solution)/shard_map/ppermute | solution.py:332
  17.6 51.1 %collective-permute-start.3 = (bf16[288,256]{1,0:T(8,128)(2,1)S(1)}, bf16[288,256]{1,0:T(8,128)(2,1)S(1)}, u32[]{:S(2)}, u32[]{:S(2)}) collective-permute-start(bf16[288,256]{1,0:T(8,128)(2,1)S(1)} %get-tuple-element.51), channel_id=1, source_target_pairs={{0,8},{2,10},{4,12},{6,14},{8,0},{10,2},{12,4},{14,6},{16,24},{18,... | collective-permute-start | bytes 442376 | tf_op jit(solution)/shard_map/ppermute | solution.py:332
  19.3 52.5 %collective-permute-start.4 = (bf16[288,256]{1,0:T(8,128)(2,1)S(1)}, bf16[288,256]{1,0:T(8,128)(2,1)S(1)}, u32[]{:S(2)}, u32[]{:S(2)}) collective-permute-start(bf16[288,256]{1,0:T(8,128)(2,1)S(1)} %get-tuple-element.52), channel_id=1, source_target_pairs={{0,10},{2,8},{4,14},{6,12},{8,2},{10,0},{12,6},{14,4},{16,26},{18,... | collective-permute-start | bytes 442376 | tf_op jit(solution)/shard_map/ppermute | solution.py:332
  19.5 58.6 %collective-permute-start.5 = (bf16[288,256]{1,0:T(8,128)(2,1)S(1)}, bf16[288,256]{1,0:T(8,128)(2,1)S(1)}, u32[]{:S(2)}, u32[]{:S(2)}) collective-permute-start(bf16[288,256]{1,0:T(8,128)(2,1)S(1)} %pad_maximum_fusion.2), channel_id=1, source_target_pairs={{0,12},{2,14},{4,8},{6,10},{8,4},{10,6},{12,0},{14,2},{16,28},{18,... | collective-permute-start | bytes 442376 | tf_op jit(solution)/shard_map/ppermute | solution.py:332
  37.3 43.0 %collective-permute-start.6 = (bf16[288,256]{1,0:T(8,128)(2,1)S(1)}, bf16[288,256]{1,0:T(8,128)(2,1)S(1)}, u32[]{:S(2)}, u32[]{:S(2)}) collective-permute-start(bf16[288,256]{1,0:T(8,128)(2,1)S(1)} %get-tuple-element.47), channel_id=1, source_target_pairs={{0,14},{2,12},{4,10},{6,8},{8,6},{10,4},{12,2},{14,0},{16,30},{18,... | collective-permute-start | bytes 442376 | tf_op jit(solution)/shard_map/ppermute | solution.py:332
  80.4 83.4 %copy-start = (bf16[8,288,256]{2,1,0:T(8,128)(2,1)}, bf16[8,288,256]{2,1,0:T(8,128)(2,1)S(1)}, u32[]{:S(2)}) copy-start(bf16[8,288,256]{2,1,0:T(8,128)(2,1)S(1)} %bitcast_dynamic-update-slice_fusion.near_ref) | copy-start | bytes 3538948
  80.4 24.7 %collective-permute-start.7 = (bf16[3,256,256]{2,1,0:T(8,128)(2,1)S(1)}, bf16[3,256,256]{2,1,0:T(8,128)(2,1)S(1)}, u32[]{:S(2)}, u32[]{:S(2)}) collective-permute-start(bf16[3,256,256]{2,1,0:T(8,128)(2,1)S(1)} %slice.18), channel_id=1, source_target_pairs={{0,16},{2,18},{4,20},{6,22},{8,24},{10,26},{12,28},{14,30},{16,0},... | collective-permute-start | bytes 1179656 | tf_op jit(solution)/shard_map/ppermute | solution.py:336
  105.1 9.2 %copy-start.1 = (bf16[3,256,256]{2,1,0:T(8,128)(2,1)}, bf16[3,256,256]{2,1,0:T(8,128)(2,1)S(1)}, u32[]{:S(2)}) copy-start(bf16[3,256,256]{2,1,0:T(8,128)(2,1)S(1)} %collective-permute-done.7.refs_0_) | copy-start | bytes 1179652
  105.1 8.1 %collective-permute-start.8 = (bf16[512,128]{1,0:T(8,128)(2,1)S(1)}, bf16[512,128]{1,0:T(8,128)(2,1)S(1)}, u32[]{:S(2)}, u32[]{:S(2)}) collective-permute-start(bf16[512,128]{1,0:T(8,128)(2,1)S(1)} %attend.1), channel_id=1, source_target_pairs={{0,16},{2,18},{4,20},{6,22},{8,24},{10,26},{12,28},{14,30},{16,0},... | collective-permute-start | bytes 393224 | tf_op jit(solution)/shard_map/ppermute | solution.py:350
  114.4 23.1 %all-to-all-start.1 = ((bf16[4,2,512,128]{3,2,1,0:T(8,128)(2,1)}), bf16[4,2,512,128]{3,2,1,0:T(8,128)(2,1)S(1)}, u32[]{:S(2)}, u32[]{:S(2)}) async-start(bf16[4,2,512,128]{3,2,1,0:T(8,128)(2,1)} %broadcast_in_dim.4), calls=%async_computation.1 | async-start | bytes 2097152 | tf_op jit(solution)/shard_map/all_to_all | solution.py:345
  119.3 16.1 %collective-permute-start.11 = (bf16[2,256,256]{2,1,0:T(8,128)(2,1)}, bf16[2,256,256]{2,1,0:T(8,128)(2,1)S(1)}, u32[]{:S(2)}, u32[]{:S(2)}) collective-permute-start(bf16[2,256,256]{2,1,0:T(8,128)(2,1)} %slice.22), channel_id=1, source_target_pairs={{0,16},{2,18},{4,20},{6,22},{8,24},{10,26},{12,28},{14,30},{16,0},... | collective-permute-start | bytes 786440 | tf_op jit(solution)/shard_map/ppermute | solution.py:339
  120.6 14.9 %collective-permute-start.10 = (bf16[2,512,128]{2,1,0:T(8,128)(2,1)S(1)}, bf16[2,512,128]{2,1,0:T(8,128)(2,1)S(1)}, u32[]{:S(2)}, u32[]{:S(2)}) collective-permute-start(bf16[2,512,128]{2,1,0:T(8,128)(2,1)S(1)} %pad_maximum_fusion.17), channel_id=1, source_target_pairs={{0,1},{1,0},{2,3},{3,2},{4,5},{5,4},{6,7},{7,6},{8,9},{9,8},{10,11... | collective-permute-start | bytes 786440 | tf_op jit(solution)/shard_map/ppermute | solution.py:351
  122.3 8.1 %collective-permute-start.9 = (s32[2,8,2048]{2,1,0:T(8,128)S(1)}, s32[2,8,2048]{2,1,0:T(8,128)S(1)}, u32[]{:S(2)}, u32[]{:S(2)}) collective-permute-start(s32[2,8,2048]{2,1,0:T(8,128)S(1)} %reshape.46.ids_ref), channel_id=1, source_target_pairs={{0,1},{1,0},{2,3},{3,2},{4,5},{5,4},{6,7},{7,6},{8,9},{9,8},{10,11... | collective-permute-start | bytes 393224 | tf_op jit(solution)/shard_map/ppermute | solution.py:360
  135.4 3.2 %copy-start.5 = (bf16[2,256,256]{2,1,0:T(8,128)(2,1)}, bf16[2,256,256]{2,1,0:T(8,128)(2,1)S(1)}, u32[]{:S(2)}) copy-start(bf16[2,256,256]{2,1,0:T(8,128)(2,1)S(1)} %collective-permute-done.11.refs_1_) | copy-start | bytes 786436
  138.6 25.1 %all-to-all-start.2 = ((bf16[4,2,512,128]{3,2,1,0:T(8,128)(2,1)}), bf16[4,2,512,128]{3,2,1,0:T(8,128)(2,1)S(1)}, u32[]{:S(2)}, u32[]{:S(2)}) async-start(bf16[4,2,512,128]{3,2,1,0:T(8,128)(2,1)} %broadcast_in_dim.5), calls=%async_computation.2 | async-start | bytes 2097152 | tf_op jit(solution)/shard_map/all_to_all | solution.py:345
  142.3 8.5 %collective-permute-start.12 = (bf16[8,512,128]{2,1,0:T(8,128)(2,1)S(1)}, bf16[8,512,128]{2,1,0:T(8,128)(2,1)S(1)}, u32[]{:S(2)}, u32[]{:S(2)}) collective-permute-start(bf16[8,512,128]{2,1,0:T(8,128)(2,1)S(1)} %bitcast.95), channel_id=1, source_target_pairs={{0,2},{2,0},{4,6},{6,4},{8,10},{10,8},{12,14},{14,12},{16,18},{18,... | collective-permute-start | bytes 3145736 | tf_op jit(solution)/shard_map/ppermute | solution.py:365
  142.4 19.3 %collective-permute-start.13 = (bf16[3,256,256]{2,1,0:T(8,128)(2,1)S(1)}, bf16[3,256,256]{2,1,0:T(8,128)(2,1)S(1)}, u32[]{:S(2)}, u32[]{:S(2)}) collective-permute-start(bf16[3,256,256]{2,1,0:T(8,128)(2,1)S(1)} %slice.23), channel_id=1, source_target_pairs={{0,16},{2,18},{4,20},{6,22},{8,24},{10,26},{12,28},{14,30},{16,0},... | collective-permute-start | bytes 1179656 | tf_op jit(solution)/shard_map/ppermute | solution.py:339
  150.8 12.9 %copy-start.2 = (bf16[3,256,256]{2,1,0:T(8,128)(2,1)S(1)}, bf16[3,256,256]{2,1,0:T(8,128)(2,1)}, u32[]{:S(2)}) copy-start(bf16[3,256,256]{2,1,0:T(8,128)(2,1)} %copy-done.1) | copy-start | bytes 1179652
  150.8 12.9 %copy-start.6 = (bf16[2,256,256]{2,1,0:T(8,128)(2,1)S(1)}, bf16[2,256,256]{2,1,0:T(8,128)(2,1)}, u32[]{:S(2)}) copy-start(bf16[2,256,256]{2,1,0:T(8,128)(2,1)} %copy-done.5) | copy-start | bytes 786436
  161.7 0.8 copy-start.3
  163.7 8.2 %collective-permute-start.14 = (bf16[8,512,128]{2,1,0:T(8,128)(2,1)S(1)}, bf16[8,512,128]{2,1,0:T(8,128)(2,1)}, u32[]{:S(2)}, u32[]{:S(2)}) collective-permute-start(bf16[8,512,128]{2,1,0:T(8,128)(2,1)S(1)} %bitcast.97), channel_id=1, source_target_pairs={{0,2},{2,0},{4,6},{6,4},{8,10},{10,8},{12,14},{14,12},{16,18},{18,... | collective-permute-start | bytes 3145736 | tf_op jit(solution)/shard_map/ppermute | solution.py:372
  163.8 1.0 copy-start.4

commit v9 on v7

--- a/solution.py
+++ b/solution.py
@@ -60,7 +60,7 @@
 
     sums_ref[...] = jnp.zeros_like(sums_ref)
 
-    @pl.loop(0, n_src)
+    @pl.loop(0, n_src, unroll=4)
     def _(src):
         coded = moved_ref[src, 3 * tok_rows :, :].astype(jnp.float32).astype(jnp.int32)
         parts = []
@@ -81,7 +81,7 @@
             top = jnp.maximum(top, scores[:, i * lanes : (i + 1) * lanes])
         return top
 
-    top = lax.fori_loop(0, n_src, score, jnp.full((C, lanes), -jnp.inf, jnp.float32))
+    top = lax.fori_loop(0, n_src, score, jnp.full((C, lanes), -jnp.inf, jnp.float32), unroll=4)
     top = jnp.broadcast_to(jnp.max(top, axis=1, keepdims=True), (C, tok_rows))
 
     acc_ref[...] = jnp.zeros_like(acc_ref)
@@ -94,7 +94,7 @@
         acc_ref[...] += jnp.dot(weights.astype(jnp.bfloat16), values, preferred_element_type=jnp.float32)
         return total
 
-    total = lax.fori_loop(0, n_src, weigh, jnp.zeros((C, lanes), jnp.float32))
+    total = lax.fori_loop(0, n_src, weigh, jnp.zeros((C, lanes), jnp.float32), unroll=4)
     out_ref[...] = (acc_ref[...] / jnp.sum(total, axis=1, keepdims=True)).astype(jnp.bfloat16)
 
 
@@ -250,7 +250,7 @@
         near.append(lax.ppermute(block, "seq", [(i, i ^ k) for i in range(n_seq)]) if k else block)
     near = jnp.stack(near)
     moved, near = lax.optimization_barrier((moved, near))
-    cuts = [half * i // 4 for i in range(5)]
+    cuts = [half * i // 8 for i in (0, 1, 2, 4, 6, 8)]
     far = [lax.ppermute(near[a:b, :rows], "seq", swap_halves) for a, b in zip(cuts[:1], cuts[1:])]
     own = attend(moved, tok_rows)
     own, near, far[0] = lax.optimization_barrier((own, near, far[0]))
@@ -265,7 +265,8 @@
         )
         return got.reshape((half,) + own.shape)
 
-    pair = jnp.stack([own, lax.ppermute(own, "seq", swap_halves)])
+    crossed, far[1] = lax.optimization_barrier((lax.ppermute(own, "seq", swap_halves), far[1]))
+    pair = jnp.stack([own, crossed])
     far_pair = lax.ppermute(pair, "head", swap_heads)
     first = spread(copied(pair))
 
@@ -277,8 +278,8 @@
     slot_ids = by_slot(coded, half_at, core)
     far_ids = lax.ppermute(slot_ids, "head", swap_heads)
     far_copies = copied(far_pair)
-    first, slot_ids, far_ids, far_copies, far[1] = lax.optimization_barrier(
-        (first, slot_ids, far_ids, far_copies, far[1])
+    first, slot_ids, far_ids, far_copies, far[2] = lax.optimization_barrier(
+        (first, slot_ids, far_ids, far_copies, far[2])
     )
     second = lax.ppermute(first, "seq", swap_cores)
     third = spread(far_copies)
@@ -287,7 +288,7 @@
     tok_tile = 2 * tok_rows
     features = expand(slot_ids, 0, first, None, 0, pieces, tok_tile)
     features = expand(slot_ids, 1, second, features, 1, pieces, tok_tile)
-    features, third, far[2] = lax.optimization_barrier((features, third, far[2]))
+    features, third, far[3] = lax.optimization_barrier((features, third, far[3]))
     fourth = lax.ppermute(third, "seq", swap_cores)
     features = expand(far_ids, 0, third, features, 2, pieces, tok_tile)
     features = expand(far_ids, 1, fourth, features, 3, pieces, tok_tile)

time: 200 us -> 200 us (level)
  Pallas kernels: 51.5 us -> 45.4 us
  waiting for transfers between devices: 80.1 us -> 83.2 us
  starting transfers between devices: 35.9 us -> 38.7 us
    ppermute x4 -> x5, waiting for transfers between devices: 4.09 us -> 10.9 us  [by_head(): lax.ppermute(near[a:b, :rows], 'seq', swap_halves)]
    pallas_call x1, Pallas kernels: 14.1 us -> 8.02 us  [attend(): pl.pallas_call(lambda *refs: attend_kernel(tok_rows, *refs), out_shape=ja...]
    ppermute x1, waiting for transfers between devices: 6.38 us -> 2.07 us  [by_head(): lax.ppermute(own, 'seq', swap_halves)]
    ppermute x1, starting transfers between devices: 0.1 us -> 2.91 us  [by_head(): lax.ppermute(own, 'seq', swap_halves)]
    unnamed x42 -> x46, local copies, waits for them, and re-layouts: 2.82 us -> 4.11 us
    ppermute x4 -> x5, starting transfers between devices: 11 us -> 11.3 us  [by_head(): lax.ppermute(near[a:b, :rows], 'seq', swap_halves)]
  transfers between devices with their start and end apart: 19 -> 20, of which waited for: 11 -> 12; matrix products, arithmetic and copies ran while one was open for 2% -> 2% of each run, Pallas kernels for 21% -> 18%
where the time goes in v9:
time: 200 us
  waiting for transfers between devices  83.2 us (42%)
  Pallas kernels  45.4 us (23%)
  starting transfers between devices  38.7 us (19%)
  blocking collectives  17.4 us (9%)
  local copies, waits for them, and re-layouts  11.7 us (6%)
  other arithmetic  3.08 us (2%)
    ppermute x7, waiting for transfers between devices, by_head(): lax.ppermute(block, 'seq', [(i, i ^ k) for i in range(n_seq)])  58.5 us
    pallas_call x4, Pallas kernels, expand(): pl.pallas_call(expand_kernel, out_shape=jax.ShapeDtypeStruct((pieces * he...  28.4 us
    all_to_all x1, blocking collectives, by_head(): lax.all_to_all(near_out.reshape(half, tok_rows, cols_each), 'seq', split_...  17.4 us
    ppermute x5, starting transfers between devices, by_head(): lax.ppermute(near[a:b, :rows], 'seq', swap_halves)  11.3 us
    ppermute x5, waiting for transfers between devices, by_head(): lax.ppermute(near[a:b, :rows], 'seq', swap_halves)  10.9 us
    pallas_call x1, Pallas kernels, project(): pl.pallas_call(project_kernel, out_shape=jax.ShapeDtypeStruct((tokens, co...  8.99 us
    ppermute x1, waiting for transfers between devices, by_head(): far_ids = lax.ppermute(slot_ids, 'head', swap_heads)  8.19 us
    pallas_call x1, Pallas kernels, attend(): pl.pallas_call(lambda *refs: attend_kernel(tok_rows, *refs), out_shape=ja...  8.02 us
  transfers between devices with their start and end apart: 20, of which 12 were waited for; matrix products, arithmetic and copies ran while one was open for 2% of the time, Pallas kernels for 18%

profile of v9, /device:TPU:0, one launch (start us, length us, event | category | flops | bytes accessed | tf_op | source)
XLA Modules:
  0.0 200.0 jit_solution(3323117114414573431)
XLA Ops:
  0.0 0.9 fusion.6
  0.9 1.5 copy.44
  2.4 0.5 copy_bitcast_fusion
  3.0 1.8 pad_maximum_fusion
  4.8 7.6 %all-to-all-start = ((bf16[16,784,128]{2,1,0:T(8,128)(2,1)}), bf16[16,784,128]{2,1,0:T(8,128)(2,1)}, u32[]{:S(2)}, u32[]{:S(2)}) async-start(bf16[16,784,128]{2,1,0:T(8,128)(2,1)} %pad_maximum_fusion), calls=%async_computation | async-start | bytes 6422528 | tf_op jit(solution)/shard_map/all_to_all | solution.py:242
  12.5 0.3 copy.32
  12.8 2.2 %constant_dynamic-slice_fusion = (bf16[256,1,256]{2,1,0:T(2,128)(2,1)S(1)}, bf16[256,1,256]{2,1,0:T(2,128)(2,1)S(1)}, bf16[256,1,256]{2,1,0:T(2,128)(2,1)S(1)}, ...) fusion(bf16[256,8,256]{2,1,0:T(8,128)(2,1)S(1)} %bitcast.101, ...), kind=kLoop, calls=%fused_computation.68 | loop fusion | bytes 2097184 | tf_op jit(solution)/shard_map/dynamic-slice.7
  15.1 0.1 pad_maximum_fusion.1
  15.2 2.6 %collective-permute-start.6 = (bf16[288,256]{1,0:T(8,128)(2,1)S(1)}, bf16[288,256]{1,0:T(8,128)(2,1)S(1)}, u32[]{:S(2)}, u32[]{:S(2)}) collective-permute-start(bf16[288,256]{1,0:T(8,128)(2,1)S(1)} %get-tuple-element.54), channel_id=1, source_target_pairs={{0,14},{2,12},{4,10},{6,8},{8,6},{10,4},{12,2},{14,0},{16,30},{18,... | collective-permute-start | bytes 442376 | tf_op jit(solution)/shard_map/ppermute | solution.py:250
  17.8 0.4 collective-permute-start
  18.1 0.6 collective-permute-start.1
  18.7 0.9 collective-permute-start.2
  19.6 0.6 collective-permute-start.3
  20.3 0.0 collective-permute-done
  20.3 1.5 collective-permute-start.4
  21.8 15.5 %collective-permute-done.1 = bf16[288,256]{1,0:T(8,128)(2,1)S(1)} collective-permute-done((bf16[288,256]{1,0:T(8,128)(2,1)S(1)}, bf16[288,256]{1,0:T(8,128)(2,1)S(1)}, u32[]{:S(2)}, u32[]{:S(2)}) %collective-permute-start.1) | collective-permute-done | bytes 147488 | tf_op jit(solution)/shard_map/ppermute | solution.py:250
  37.3 0.5 collective-permute-start.5
  37.8 7.0 %collective-permute-done.2 = bf16[288,256]{1,0:T(8,128)(2,1)S(1)} collective-permute-done((bf16[288,256]{1,0:T(8,128)(2,1)S(1)}, bf16[288,256]{1,0:T(8,128)(2,1)S(1)}, u32[]{:S(2)}, u32[]{:S(2)}) %collective-permute-start.2) | collective-permute-done | bytes 147488 | tf_op jit(solution)/shard_map/ppermute | solution.py:250
  44.8 27.9 %collective-permute-done.3 = bf16[288,256]{1,0:T(8,128)(2,1)S(1)} collective-permute-done((bf16[288,256]{1,0:T(8,128)(2,1)S(1)}, bf16[288,256]{1,0:T(8,128)(2,1)S(1)}, u32[]{:S(2)}, u32[]{:S(2)}) %collective-permute-start.3) | collective-permute-done | bytes 147488 | tf_op jit(solution)/shard_map/ppermute | solution.py:250
  72.7 3.1 %collective-permute-done.4 = bf16[288,256]{1,0:T(8,128)(2,1)S(1)} collective-permute-done((bf16[288,256]{1,0:T(8,128)(2,1)S(1)}, bf16[288,256]{1,0:T(8,128)(2,1)S(1)}, u32[]{:S(2)}, u32[]{:S(2)}) %collective-permute-start.4) | collective-permute-done | bytes 147488 | tf_op jit(solution)/shard_map/ppermute | solution.py:250
  75.8 5.0 %collective-permute-done.5 = bf16[288,256]{1,0:T(8,128)(2,1)S(1)} collective-permute-done((bf16[288,256]{1,0:T(8,128)(2,1)S(1)}, bf16[288,256]{1,0:T(8,128)(2,1)S(1)}, u32[]{:S(2)}, u32[]{:S(2)}) %collective-permute-start.5) | collective-permute-done | bytes 147488 | tf_op jit(solution)/shard_map/ppermute | solution.py:250
  80.8 0.0 collective-permute-done.6
  80.9 0.0 all-to-all-done.refs_0_
  80.9 6.9 %collective-permute-start.7 = (bf16[1,256,256]{2,1,0:T(8,128)(2,1)S(1)}, bf16[1,256,256]{2,1,0:T(8,128)(2,1)S(1)}, u32[]{:S(2)}, u32[]{:S(2)}) collective-permute-start(bf16[1,256,256]{2,1,0:T(8,128)(2,1)S(1)} %slice.24), channel_id=1, source_target_pairs={{0,16},{2,18},{4,20},{6,22},{8,24},{10,26},{12,28},{14,30},{16,0},... | collective-permute-start | bytes 393224 | tf_op jit(solution)/shard_map/ppermute | solution.py:254
  87.8 8.0 %attend.1 = bf16[512,128]{1,0:T(8,128)(2,1)S(1)} custom-call(bf16[16,784,128]{2,1,0:T(8,128)(2,1)} %all-to-all-done.refs_0_), custom_call_target="tpu_custom_call" | custom-call | flops 2147483648 | bytes 3211264 | tf_op jit(solution)/shard_map/attend/pallas_call | solution.py:104
  95.9 0.7 copy-done.4
  96.6 0.1 collective-permute-start.9
  96.7 2.9 %collective-permute-start.8 = (bf16[512,128]{1,0:T(8,128)(2,1)S(1)}, bf16[512,128]{1,0:T(8,128)(2,1)S(1)}, u32[]{:S(2)}, u32[]{:S(2)}) collective-permute-start(bf16[512,128]{1,0:T(8,128)(2,1)S(1)} %attend.1), channel_id=1, source_target_pairs={{0,16},{2,18},{4,20},{6,22},{8,24},{10,26},{12,28},{14,30},{16,0},... | collective-permute-start | bytes 393224 | tf_op jit(solution)/shard_map/ppermute | solution.py:268
  99.6 6.4 %collective-permute-done.9.refs_1_ = bf16[1,256,256]{2,1,0:T(8,128)(2,1)S(1)} collective-permute-done((bf16[1,256,256]{2,1,0:T(8,128)(2,1)S(1)}, bf16[1,256,256]{2,1,0:T(8,128)(2,1)S(1)}, u32[]{:S(2)}, u32[]{:S(2)}) %collective-permute-start.9) | collective-permute-done | bytes 131104 | tf_op jit(solution)/shard_map/ppermute | solution.py:257
  106.0 0.6 copy-done.6
  106.7 2.1 %collective-permute-done.8 = bf16[512,128]{1,0:T(8,128)(2,1)S(1)} collective-permute-done((bf16[512,128]{1,0:T(8,128)(2,1)S(1)}, bf16[512,128]{1,0:T(8,128)(2,1)S(1)}, u32[]{:S(2)}, u32[]{:S(2)}) %collective-permute-start.8) | collective-permute-done | bytes 131104 | tf_op jit(solution)/shard_map/ppermute | solution.py:268
  108.8 1.1 broadcast_in_dim.4
  109.9 4.1 %all-to-all-start.1 = ((bf16[4,2,512,128]{3,2,1,0:T(8,128)(2,1)}), bf16[4,2,512,128]{3,2,1,0:T(8,128)(2,1)S(1)}, u32[]{:S(2)}, u32[]{:S(2)}) async-start(bf16[4,2,512,128]{3,2,1,0:T(8,128)(2,1)} %broadcast_in_dim.4), calls=%async_computation.1 | async-start | bytes 2097152 | tf_op jit(solution)/shard_map/all_to_all | solution.py:263
  114.1 0.1 reshape.45
  114.2 0.4 rev.7
  114.6 0.9 fusion.11
  115.6 1.2 collective-permute-start.12
  116.8 1.5 collective-permute-start.11
  118.3 0.1 broadcast_select_fusion
  118.3 0.1 copy.20
  118.4 0.6 collective-permute-start.10
  119.0 8.2 %collective-permute-done.10.ids_ref = s32[2,8,2048]{2,1,0:T(8,128)S(1)} collective-permute-done((s32[2,8,2048]{2,1,0:T(8,128)S(1)}, s32[2,8,2048]{2,1,0:T(8,128)S(1)}, u32[]{:S(2)}, u32[]{:S(2)}) %collective-permute-start.10) | collective-permute-done | bytes 131104 | tf_op jit(solution)/shard_map/ppermute | solution.py:279
  127.2 3.8 %collective-permute-done.12.refs_2_ = bf16[2,256,256]{2,1,0:T(8,128)(2,1)S(1)} collective-permute-done((bf16[2,256,256]{2,1,0:T(8,128)(2,1)}, bf16[2,256,256]{2,1,0:T(8,128)(2,1)S(1)}, u32[]{:S(2)}, u32[]{:S(2)}) %collective-permute-start.12) | collective-permute-done | bytes 262176 | tf_op jit(solution)/shard_map/ppermute | solution.py:257
  131.0 0.0 collective-permute-done.11
  131.0 2.1 %all-to-all-done.1 = bf16[4,2,512,128]{3,2,1,0:T(8,128)(2,1)S(1)} async-done(((bf16[4,2,512,128]{3,2,1,0:T(8,128)(2,1)}), bf16[4,2,512,128]{3,2,1,0:T(8,128)(2,1)S(1)}, u32[]{:S(2)}, u32[]{:S(2)}) %all-to-all-start.1) | async-done | bytes 1048608 | tf_op jit(solution)/shard_map/all_to_all | solution.py:263
  133.1 1.1 broadcast_in_dim.5
  134.2 3.7 %all-to-all-start.2 = ((bf16[4,2,512,128]{3,2,1,0:T(8,128)(2,1)}), bf16[4,2,512,128]{3,2,1,0:T(8,128)(2,1)S(1)}, u32[]{:S(2)}, u32[]{:S(2)}) async-start(bf16[4,2,512,128]{3,2,1,0:T(8,128)(2,1)} %broadcast_in_dim.5), calls=%async_computation.2 | async-start | bytes 2097152 | tf_op jit(solution)/shard_map/all_to_all | solution.py:263
  137.9 0.0 collective-permute-start.13
  138.0 1.3 collective-permute-start.14
  139.3 7.1 %expand.4.refs_0_ = bf16[32,2048,128]{2,1,0:T(8,128)(2,1)} custom-call(s32[2,8,2048]{2,1,0:T(8,128)S(1)} %reshape.46.ids_ref, bf16[8,512,128]{2,1,0:T(8,128)(2,1)S(1)} %bitcast.96), custom_call_target="tpu_custom_call" | custom-call | flops 4294967296 | bytes 5242880 | tf_op jit(solution)/shard_map/expand/pallas_call | solution.py:141
  146.4 0.0 collective-permute-done.13.attended_ref
  146.4 7.1 %expand.5.refs_0_ = bf16[32,2048,128]{2,1,0:T(8,128)(2,1)} custom-call(s32[2,8,2048]{2,1,0:T(8,128)S(1)} %reshape.46.ids_ref, bf16[8,512,128]{2,1,0:T(8,128)(2,1)S(1)} %collective-permute-done.13.attended_ref, bf16[32,2048,128]{2,1,0:T(8,128)(2,1)} %expand.4.refs_0_), custom_call_target="tpu_custom_call", output_to_operand_aliasing={{}: (2, {})} | custom-call | flops 4294967296 | bytes 5242880 | tf_op jit(solution)/shard_map/expand/pallas_call | solution.py:141
  153.5 0.7 collective-permute-done.14.refs_3_
  154.2 0.7 copy-done.2
  154.9 1.4 all-to-all-done.2
  156.3 0.0 collective-permute-start.15
  156.3 0.1 pad_add_fusion.places_ref
  156.4 1.8 collective-permute-start.16
  158.2 7.1 %expand.6.refs_0_ = bf16[32,2048,128]{2,1,0:T(8,128)(2,1)} custom-call(s32[2,8,2048]{2,1,0:T(8,128)S(1)} %collective-permute-done.10.ids_ref, bf16[8,512,128]{2,1,0:T(8,128)(2,1)S(1)} %bitcast.98, bf16[32,2048,128]{2,1,0:T(8,128)(2,1)} %expand.5.refs_0_), custom_call_target="tpu_custom_call", output_to_operand_aliasing={{}: (2, {})} | custom-call | flops 4294967296 | bytes 5242880 | tf_op jit(solution)/shard_map/expand/pallas_call | solution.py:141
  165.3 0.0 collective-permute-done.15.attended_ref
  165.4 7.1 %expand.7.features_ref = bf16[32,2048,128]{2,1,0:T(8,128)(2,1)} custom-call(s32[2,8,2048]{2,1,0:T(8,128)S(1)} %collective-permute-done.10.ids_ref, bf16[8,512,128]{2,1,0:T(8,128)(2,1)S(1)} %collective-permute-done.15.attended_ref, bf16[32,2048,128]{2,1,0:T(8,128)(2,1)} %expand.6.refs_0_), custom_call_target="tpu_custom_call", output_to_operand_aliasing={{}: (2, {})} | custom-call | flops 4294967296 | bytes 5242880 | tf_op jit(solution)/shard_map/expand/pallas_call | solution.py:141
  172.5 9.0 %project.1 = bf16[2048,256]{1,0:T(8,128)(2,1)S(1)} custom-call(s32[4]{0:T(128)S(1)} %pad_add_fusion.places_ref, bf16[32,2048,128]{2,1,0:T(8,128)(2,1)} %expand.7.features_ref, bf16[8,288,256]{2,1,0:T(8,128)(2,1)S(1)} %bitcast_dynamic-update-slice_fusion.near_ref, bf16[1,256,256]{2,1,0:T(8,128)(2,1)S(1)} %copy-done.5, bf16[1,256,256]{2,1,0:T(8,128)(2,1)S(1)} %copy-done.7, ...), custom_call_target="tpu_custom_call" | custom-call | flops 4294967296 | bytes 19922944 | tf_op jit(solution)/shard_map/project/pallas_call | solution.py:184
  181.5 17.4 %all_to_all.20 = bf16[8,256,256]{2,1,0:T(8,128)(2,1)S(1)} all-to-all(bf16[8,256,256]{2,1,0:T(8,128)(2,1)S(1)} %bitcast.99), channel_id=1, replica_groups={{0,2,4,6,8,10,12,14},{16,18,20,22,24,26,28,30},{1,3,5,7,9,11,13,15},{17..., dimensions={0} | all-to-all | bytes 2097152 | tf_op jit(solution)/shard_map/all_to_all | solution.py:297
  198.9 1.1 copy.30
  (55 shorter events, 0.5 us)
Async XLA Ops:
  0.0 2.4 %copy-start.9 = (bf16[256,16,128]{2,1,0:T(8,128)(2,1)S(1)}, bf16[256,16,128]{2,1,0:T(8,128)(2,1)}, u32[]{:S(2)}) copy-start(bf16[256,16,128]{2,1,0:T(8,128)(2,1)} %param.7) | copy-start | bytes 3145732
  0.0 2.4 %copy-start.10 = (bf16[256,16,128]{2,1,0:T(8,128)(2,1)S(1)}, bf16[256,16,128]{2,1,0:T(8,128)(2,1)}, u32[]{:S(2)}) copy-start(bf16[256,16,128]{2,1,0:T(8,128)(2,1)} %param.6) | copy-start | bytes 3145732
  4.8 7.6 %copy-start.8 = (bf16[256,2048]{1,0:T(8,128)(2,1)S(1)}, bf16[256,2048]{1,0:T(8,128)(2,1)}, u32[]{:S(2)}) copy-start(bf16[256,2048]{1,0:T(8,128)(2,1)} %param.9) | copy-start | bytes 3145732
  4.8 76.0 %all-to-all-start = ((bf16[16,784,128]{2,1,0:T(8,128)(2,1)}), bf16[16,784,128]{2,1,0:T(8,128)(2,1)}, u32[]{:S(2)}, u32[]{:S(2)}) async-start(bf16[16,784,128]{2,1,0:T(8,128)(2,1)} %pad_maximum_fusion), calls=%async_computation | async-start | bytes 6422528 | tf_op jit(solution)/shard_map/all_to_all | solution.py:242
  15.2 65.6 %collective-permute-start.6 = (bf16[288,256]{1,0:T(8,128)(2,1)S(1)}, bf16[288,256]{1,0:T(8,128)(2,1)S(1)}, u32[]{:S(2)}, u32[]{:S(2)}) collective-permute-start(bf16[288,256]{1,0:T(8,128)(2,1)S(1)} %get-tuple-element.54), channel_id=1, source_target_pairs={{0,14},{2,12},{4,10},{6,8},{8,6},{10,4},{12,2},{14,0},{16,30},{18,... | collective-permute-start | bytes 442376 | tf_op jit(solution)/shard_map/ppermute | solution.py:250
  17.8 2.5 %collective-permute-start = (bf16[288,256]{1,0:T(8,128)(2,1)S(1)}, bf16[288,256]{1,0:T(8,128)(2,1)S(1)}, u32[]{:S(2)}, u32[]{:S(2)}) collective-permute-start(bf16[288,256]{1,0:T(8,128)(2,1)S(1)} %get-tuple-element.55), channel_id=1, source_target_pairs={{0,2},{2,0},{4,6},{6,4},{8,10},{10,8},{12,14},{14,12},{16,18},{18,... | collective-permute-start | bytes 442376 | tf_op jit(solution)/shard_map/ppermute | solution.py:250
  18.1 19.2 %collective-permute-start.1 = (bf16[288,256]{1,0:T(8,128)(2,1)S(1)}, bf16[288,256]{1,0:T(8,128)(2,1)S(1)}, u32[]{:S(2)}, u32[]{:S(2)}) collective-permute-start(bf16[288,256]{1,0:T(8,128)(2,1)S(1)} %get-tuple-element.56), channel_id=1, source_target_pairs={{0,4},{2,6},{4,0},{6,2},{8,12},{10,14},{12,8},{14,10},{16,20},{18,... | collective-permute-start | bytes 442376 | tf_op jit(solution)/shard_map/ppermute | solution.py:250
  18.7 26.1 %collective-permute-start.2 = (bf16[288,256]{1,0:T(8,128)(2,1)S(1)}, bf16[288,256]{1,0:T(8,128)(2,1)S(1)}, u32[]{:S(2)}, u32[]{:S(2)}) collective-permute-start(bf16[288,256]{1,0:T(8,128)(2,1)S(1)} %get-tuple-element.57), channel_id=1, source_target_pairs={{0,6},{2,4},{4,2},{6,0},{8,14},{10,12},{12,10},{14,8},{16,22},{18,... | collective-permute-start | bytes 442376 | tf_op jit(solution)/shard_map/ppermute | solution.py:250
  19.6 53.0 %collective-permute-start.3 = (bf16[288,256]{1,0:T(8,128)(2,1)S(1)}, bf16[288,256]{1,0:T(8,128)(2,1)S(1)}, u32[]{:S(2)}, u32[]{:S(2)}) collective-permute-start(bf16[288,256]{1,0:T(8,128)(2,1)S(1)} %get-tuple-element.58), channel_id=1, source_target_pairs={{0,8},{2,10},{4,12},{6,14},{8,0},{10,2},{12,4},{14,6},{16,24},{18,... | collective-permute-start | bytes 442376 | tf_op jit(solution)/shard_map/ppermute | solution.py:250
  20.3 55.5 %collective-permute-start.4 = (bf16[288,256]{1,0:T(8,128)(2,1)S(1)}, bf16[288,256]{1,0:T(8,128)(2,1)S(1)}, u32[]{:S(2)}, u32[]{:S(2)}) collective-permute-start(bf16[288,256]{1,0:T(8,128)(2,1)S(1)} %get-tuple-element.59), channel_id=1, source_target_pairs={{0,10},{2,8},{4,14},{6,12},{8,2},{10,0},{12,6},{14,4},{16,26},{18,... | collective-permute-start | bytes 442376 | tf_op jit(solution)/shard_map/ppermute | solution.py:250
  37.3 43.5 %collective-permute-start.5 = (bf16[288,256]{1,0:T(8,128)(2,1)S(1)}, bf16[288,256]{1,0:T(8,128)(2,1)S(1)}, u32[]{:S(2)}, u32[]{:S(2)}) collective-permute-start(bf16[288,256]{1,0:T(8,128)(2,1)S(1)} %pad_maximum_fusion.2), channel_id=1, source_target_pairs={{0,12},{2,14},{4,8},{6,10},{8,4},{10,6},{12,0},{14,2},{16,28},{18,... | collective-permute-start | bytes 442376 | tf_op jit(solution)/shard_map/ppermute | solution.py:250
  80.9 15.0 %collective-permute-start.7 = (bf16[1,256,256]{2,1,0:T(8,128)(2,1)S(1)}, bf16[1,256,256]{2,1,0:T(8,128)(2,1)S(1)}, u32[]{:S(2)}, u32[]{:S(2)}) collective-permute-start(bf16[1,256,256]{2,1,0:T(8,128)(2,1)S(1)} %slice.24), channel_id=1, source_target_pairs={{0,16},{2,18},{4,20},{6,22},{8,24},{10,26},{12,28},{14,30},{16,0},... | collective-permute-start | bytes 393224 | tf_op jit(solution)/shard_map/ppermute | solution.py:254
  95.9 0.7 copy-start.4
  96.6 9.4 %collective-permute-start.9 = (bf16[1,256,256]{2,1,0:T(8,128)(2,1)S(1)}, bf16[1,256,256]{2,1,0:T(8,128)(2,1)S(1)}, u32[]{:S(2)}, u32[]{:S(2)}) collective-permute-start(bf16[1,256,256]{2,1,0:T(8,128)(2,1)S(1)} %slice.25), channel_id=1, source_target_pairs={{0,16},{2,18},{4,20},{6,22},{8,24},{10,26},{12,28},{14,30},{16,0},... | collective-permute-start | bytes 393224 | tf_op jit(solution)/shard_map/ppermute | solution.py:257
  96.7 12.1 %collective-permute-start.8 = (bf16[512,128]{1,0:T(8,128)(2,1)S(1)}, bf16[512,128]{1,0:T(8,128)(2,1)S(1)}, u32[]{:S(2)}, u32[]{:S(2)}) collective-permute-start(bf16[512,128]{1,0:T(8,128)(2,1)S(1)} %attend.1), channel_id=1, source_target_pairs={{0,16},{2,18},{4,20},{6,22},{8,24},{10,26},{12,28},{14,30},{16,0},... | collective-permute-start | bytes 393224 | tf_op jit(solution)/shard_map/ppermute | solution.py:268
  106.0 0.6 copy-start.6
  109.9 23.2 %all-to-all-start.1 = ((bf16[4,2,512,128]{3,2,1,0:T(8,128)(2,1)}), bf16[4,2,512,128]{3,2,1,0:T(8,128)(2,1)S(1)}, u32[]{:S(2)}, u32[]{:S(2)}) async-start(bf16[4,2,512,128]{3,2,1,0:T(8,128)(2,1)} %broadcast_in_dim.4), calls=%async_computation.1 | async-start | bytes 2097152 | tf_op jit(solution)/shard_map/all_to_all | solution.py:263
  115.6 15.5 %collective-permute-start.12 = (bf16[2,256,256]{2,1,0:T(8,128)(2,1)}, bf16[2,256,256]{2,1,0:T(8,128)(2,1)S(1)}, u32[]{:S(2)}, u32[]{:S(2)}) collective-permute-start(bf16[2,256,256]{2,1,0:T(8,128)(2,1)} %get-tuple-element.45), channel_id=1, source_target_pairs={{0,16},{2,18},{4,20},{6,22},{8,24},{10,26},{12,28},{14,30},{16,0},... | collective-permute-start | bytes 786440 | tf_op jit(solution)/shard_map/ppermute | solution.py:257
  116.8 14.3 %collective-permute-start.11 = (bf16[2,512,128]{2,1,0:T(8,128)(2,1)S(1)}, bf16[2,512,128]{2,1,0:T(8,128)(2,1)S(1)}, u32[]{:S(2)}, u32[]{:S(2)}) collective-permute-start(bf16[2,512,128]{2,1,0:T(8,128)(2,1)S(1)} %pad_maximum_fusion.17), channel_id=1, source_target_pairs={{0,1},{1,0},{2,3},{3,2},{4,5},{5,4},{6,7},{7,6},{8,9},{9,8},{10,11... | collective-permute-start | bytes 786440 | tf_op jit(solution)/shard_map/ppermute | solution.py:270
  118.4 8.8 %collective-permute-start.10 = (s32[2,8,2048]{2,1,0:T(8,128)S(1)}, s32[2,8,2048]{2,1,0:T(8,128)S(1)}, u32[]{:S(2)}, u32[]{:S(2)}) collective-permute-start(s32[2,8,2048]{2,1,0:T(8,128)S(1)} %reshape.46.ids_ref), channel_id=1, source_target_pairs={{0,1},{1,0},{2,3},{3,2},{4,5},{5,4},{6,7},{7,6},{8,9},{9,8},{10,11... | collective-permute-start | bytes 393224 | tf_op jit(solution)/shard_map/ppermute | solution.py:279
  131.0 3.2 %copy-start = (bf16[2,256,256]{2,1,0:T(8,128)(2,1)}, bf16[2,256,256]{2,1,0:T(8,128)(2,1)S(1)}, u32[]{:S(2)}) copy-start(bf16[2,256,256]{2,1,0:T(8,128)(2,1)S(1)} %collective-permute-done.12.refs_2_) | copy-start | bytes 786436
  134.2 22.1 %all-to-all-start.2 = ((bf16[4,2,512,128]{3,2,1,0:T(8,128)(2,1)}), bf16[4,2,512,128]{3,2,1,0:T(8,128)(2,1)S(1)}, u32[]{:S(2)}, u32[]{:S(2)}) async-start(bf16[4,2,512,128]{3,2,1,0:T(8,128)(2,1)} %broadcast_in_dim.5), calls=%async_computation.2 | async-start | bytes 2097152 | tf_op jit(solution)/shard_map/all_to_all | solution.py:263
  137.9 8.4 %collective-permute-start.13 = (bf16[8,512,128]{2,1,0:T(8,128)(2,1)S(1)}, bf16[8,512,128]{2,1,0:T(8,128)(2,1)S(1)}, u32[]{:S(2)}, u32[]{:S(2)}) collective-permute-start(bf16[8,512,128]{2,1,0:T(8,128)(2,1)S(1)} %bitcast.95), channel_id=1, source_target_pairs={{0,2},{2,0},{4,6},{6,4},{8,10},{10,8},{12,14},{14,12},{16,18},{18,... | collective-permute-start | bytes 3145736 | tf_op jit(solution)/shard_map/ppermute | solution.py:284
  138.0 16.2 %collective-permute-start.14 = (bf16[2,256,256]{2,1,0:T(8,128)(2,1)}, bf16[2,256,256]{2,1,0:T(8,128)(2,1)S(1)}, u32[]{:S(2)}, u32[]{:S(2)}) collective-permute-start(bf16[2,256,256]{2,1,0:T(8,128)(2,1)} %get-tuple-element.44), channel_id=1, source_target_pairs={{0,16},{2,18},{4,20},{6,22},{8,24},{10,26},{12,28},{14,30},{16,0},... | collective-permute-start | bytes 786440 | tf_op jit(solution)/shard_map/ppermute | solution.py:257
  154.2 0.7 copy-start.2
  156.3 9.0 %collective-permute-start.15 = (bf16[8,512,128]{2,1,0:T(8,128)(2,1)S(1)}, bf16[8,512,128]{2,1,0:T(8,128)(2,1)S(1)}, u32[]{:S(2)}, u32[]{:S(2)}) collective-permute-start(bf16[8,512,128]{2,1,0:T(8,128)(2,1)S(1)} %bitcast.97), channel_id=1, source_target_pairs={{0,2},{2,0},{4,6},{6,4},{8,10},{10,8},{12,14},{14,12},{16,18},{18,... | collective-permute-start | bytes 3145736 | tf_op jit(solution)/shard_map/ppermute | solution.py:292
  156.4 16.1 %collective-permute-start.16 = (bf16[2,256,256]{2,1,0:T(8,128)(2,1)}, bf16[2,256,256]{2,1,0:T(8,128)(2,1)S(1)}, u32[]{:S(2)}, u32[]{:S(2)}) collective-permute-start(bf16[2,256,256]{2,1,0:T(8,128)(2,1)} %get-tuple-element.43), channel_id=1, source_target_pairs={{0,16},{2,18},{4,20},{6,22},{8,24},{10,26},{12,28},{14,30},{16,0},... | collective-permute-start | bytes 786440 | tf_op jit(solution)/shard_map/ppermute | solution.py:257
  165.3 7.1 %copy-start.1 = (bf16[2,256,256]{2,1,0:T(8,128)(2,1)S(1)}, bf16[2,256,256]{2,1,0:T(8,128)(2,1)}, u32[]{:S(2)}) copy-start(bf16[2,256,256]{2,1,0:T(8,128)(2,1)} %copy-done) | copy-start | bytes 786436
  165.3 7.1 %copy-start.3 = (bf16[2,256,256]{2,1,0:T(8,128)(2,1)S(1)}, bf16[2,256,256]{2,1,0:T(8,128)(2,1)}, u32[]{:S(2)}) copy-start(bf16[2,256,256]{2,1,0:T(8,128)(2,1)} %copy-done.2) | copy-start | bytes 786436
  165.3 7.1 %copy-start.5 = (bf16[1,256,256]{2,1,0:T(8,128)(2,1)S(1)}, bf16[1,256,256]{2,1,0:T(8,128)(2,1)}, u32[]{:S(2)}) copy-start(bf16[1,256,256]{2,1,0:T(8,128)(2,1)} %copy-done.4) | copy-start | bytes 393220
  165.3 7.1 %copy-start.7 = (bf16[1,256,256]{2,1,0:T(8,128)(2,1)S(1)}, bf16[1,256,256]{2,1,0:T(8,128)(2,1)}, u32[]{:S(2)}) copy-start(bf16[1,256,256]{2,1,0:T(8,128)(2,1)} %copy-done.6) | copy-start | bytes 393220

commit v10 on v7

--- a/solution.py
+++ b/solution.py
@@ -60,7 +60,7 @@
 
     sums_ref[...] = jnp.zeros_like(sums_ref)
 
-    @pl.loop(0, n_src)
+    @pl.loop(0, n_src, unroll=4)
     def _(src):
         coded = moved_ref[src, 3 * tok_rows :, :].astype(jnp.float32).astype(jnp.int32)
         parts = []
@@ -81,7 +81,7 @@
             top = jnp.maximum(top, scores[:, i * lanes : (i + 1) * lanes])
         return top
 
-    top = lax.fori_loop(0, n_src, score, jnp.full((C, lanes), -jnp.inf, jnp.float32))
+    top = lax.fori_loop(0, n_src, score, jnp.full((C, lanes), -jnp.inf, jnp.float32), unroll=4)
     top = jnp.broadcast_to(jnp.max(top, axis=1, keepdims=True), (C, tok_rows))
 
     acc_ref[...] = jnp.zeros_like(acc_ref)
@@ -94,7 +94,7 @@
         acc_ref[...] += jnp.dot(weights.astype(jnp.bfloat16), values, preferred_element_type=jnp.float32)
         return total
 
-    total = lax.fori_loop(0, n_src, weigh, jnp.zeros((C, lanes), jnp.float32))
+    total = lax.fori_loop(0, n_src, weigh, jnp.zeros((C, lanes), jnp.float32), unroll=4)
     out_ref[...] = (acc_ref[...] / jnp.sum(total, axis=1, keepdims=True)).astype(jnp.bfloat16)
 
 
@@ -250,7 +250,7 @@
         near.append(lax.ppermute(block, "seq", [(i, i ^ k) for i in range(n_seq)]) if k else block)
     near = jnp.stack(near)
     moved, near = lax.optimization_barrier((moved, near))
-    cuts = [half * i // 4 for i in range(5)]
+    cuts = [half * i // 8 for i in (0, 1, 3, 6, 8)]
     far = [lax.ppermute(near[a:b, :rows], "seq", swap_halves) for a, b in zip(cuts[:1], cuts[1:])]
     own = attend(moved, tok_rows)
     own, near, far[0] = lax.optimization_barrier((own, near, far[0]))

time: 200 us -> 198 us (0.990)
  Pallas kernels: 51.5 us -> 45.4 us
  waiting for transfers between devices: 80.1 us -> 82.9 us
    pallas_call x1, Pallas kernels: 14.1 us -> 8.02 us  [attend(): pl.pallas_call(lambda *refs: attend_kernel(tok_rows, *refs), out_shape=ja...]
    ppermute x4, waiting for transfers between devices: 4.09 us -> 6.81 us  [by_head(): lax.ppermute(near[a:b, :rows], 'seq', swap_halves)]
  transfers between devices with their start and end apart: 19 -> 19, of which waited for: 11 -> 11; matrix products, arithmetic and copies ran while one was open for 2% -> 2% of each run, Pallas kernels for 21% -> 18%
where the time goes in v10:
time: 198 us
  waiting for transfers between devices  82.9 us (42%)
  Pallas kernels  45.4 us (23%)
  starting transfers between devices  36.1 us (18%)
  blocking collectives  18.6 us (9%)
  local copies, waits for them, and re-layouts  11 us (6%)
  other arithmetic  3.09 us (2%)
    ppermute x7, waiting for transfers between devices, by_head(): lax.ppermute(block, 'seq', [(i, i ^ k) for i in range(n_seq)])  58.3 us
    pallas_call x4, Pallas kernels, expand(): pl.pallas_call(expand_kernel, out_shape=jax.ShapeDtypeStruct((pieces * he...  28.4 us
    all_to_all x1, blocking collectives, by_head(): lax.all_to_all(near_out.reshape(half, tok_rows, cols_each), 'seq', split_...  18.6 us
    ppermute x4, starting transfers between devices, by_head(): lax.ppermute(near[a:b, :rows], 'seq', swap_halves)  11.7 us
    pallas_call x1, Pallas kernels, project(): pl.pallas_call(project_kernel, out_shape=jax.ShapeDtypeStruct((tokens, co...  8.98 us
    all_to_all x2, starting transfers between devices, spread(): lax.all_to_all(copies, 'seq', split_axis=0, concat_axis=0, axis_index_gro...  8.09 us
    pallas_call x1, Pallas kernels, attend(): pl.pallas_call(lambda *refs: attend_kernel(tok_rows, *refs), out_shape=ja...  8.02 us
    ppermute x1, waiting for transfers between devices, by_head(): far_ids = lax.ppermute(slot_ids, 'head', swap_heads)  7.78 us
  transfers between devices with their start and end apart: 19, of which 11 were waited for; matrix products, arithmetic and copies ran while one was open for 2% of the time, Pallas kernels for 18%

profile of v10, /device:TPU:0, one launch (start us, length us, event | category | flops | bytes accessed | tf_op | source)
XLA Modules:
  0.0 197.6 jit_solution(7317490677554900770)
XLA Ops:
  0.0 0.9 fusion.6
  0.9 1.5 copy.44
  2.4 0.5 copy_bitcast_fusion
  3.0 1.8 pad_maximum_fusion
  4.8 7.6 %all-to-all-start = ((bf16[16,784,128]{2,1,0:T(8,128)(2,1)}), bf16[16,784,128]{2,1,0:T(8,128)(2,1)}, u32[]{:S(2)}, u32[]{:S(2)}) async-start(bf16[16,784,128]{2,1,0:T(8,128)(2,1)} %pad_maximum_fusion), calls=%async_computation | async-start | bytes 6422528 | tf_op jit(solution)/shard_map/all_to_all | solution.py:242
  12.5 0.3 copy.32
  12.8 2.2 %constant_dynamic-slice_fusion = (bf16[256,1,256]{2,1,0:T(2,128)(2,1)S(1)}, bf16[256,1,256]{2,1,0:T(2,128)(2,1)S(1)}, bf16[256,1,256]{2,1,0:T(2,128)(2,1)S(1)}, ...) fusion(bf16[256,8,256]{2,1,0:T(8,128)(2,1)S(1)} %bitcast.101, ...), kind=kLoop, calls=%fused_computation.68 | loop fusion | bytes 2097184 | tf_op jit(solution)/shard_map/dynamic-slice.7
  15.2 0.1 pad_maximum_fusion.1
  15.2 0.4 collective-permute-start
  15.7 2.6 %collective-permute-start.5 = (bf16[288,256]{1,0:T(8,128)(2,1)S(1)}, bf16[288,256]{1,0:T(8,128)(2,1)S(1)}, u32[]{:S(2)}, u32[]{:S(2)}) collective-permute-start(bf16[288,256]{1,0:T(8,128)(2,1)S(1)} %pad_maximum_fusion.2), channel_id=1, source_target_pairs={{0,12},{2,14},{4,8},{6,10},{8,4},{10,6},{12,0},{14,2},{16,28},{18,... | collective-permute-start | bytes 442376 | tf_op jit(solution)/shard_map/ppermute | solution.py:250
  18.3 0.6 collective-permute-start.1
  18.9 0.9 collective-permute-start.2
  19.7 0.6 collective-permute-start.3
  20.3 0.0 collective-permute-done
  20.4 1.6 collective-permute-start.4
  21.9 15.4 %collective-permute-done.1 = bf16[288,256]{1,0:T(8,128)(2,1)S(1)} collective-permute-done((bf16[288,256]{1,0:T(8,128)(2,1)S(1)}, bf16[288,256]{1,0:T(8,128)(2,1)S(1)}, u32[]{:S(2)}, u32[]{:S(2)}) %collective-permute-start.1) | collective-permute-done | bytes 147488 | tf_op jit(solution)/shard_map/ppermute | solution.py:250
  37.3 0.0 collective-permute-start.6
  37.4 7.4 %collective-permute-done.2 = bf16[288,256]{1,0:T(8,128)(2,1)S(1)} collective-permute-done((bf16[288,256]{1,0:T(8,128)(2,1)S(1)}, bf16[288,256]{1,0:T(8,128)(2,1)S(1)}, u32[]{:S(2)}, u32[]{:S(2)}) %collective-permute-start.2) | collective-permute-done | bytes 147488 | tf_op jit(solution)/shard_map/ppermute | solution.py:250
  44.8 27.9 %collective-permute-done.3 = bf16[288,256]{1,0:T(8,128)(2,1)S(1)} collective-permute-done((bf16[288,256]{1,0:T(8,128)(2,1)S(1)}, bf16[288,256]{1,0:T(8,128)(2,1)S(1)}, u32[]{:S(2)}, u32[]{:S(2)}) %collective-permute-start.3) | collective-permute-done | bytes 147488 | tf_op jit(solution)/shard_map/ppermute | solution.py:250
  72.7 3.1 %collective-permute-done.4 = bf16[288,256]{1,0:T(8,128)(2,1)S(1)} collective-permute-done((bf16[288,256]{1,0:T(8,128)(2,1)S(1)}, bf16[288,256]{1,0:T(8,128)(2,1)S(1)}, u32[]{:S(2)}, u32[]{:S(2)}) %collective-permute-start.4) | collective-permute-done | bytes 147488 | tf_op jit(solution)/shard_map/ppermute | solution.py:250
  75.9 0.0 collective-permute-done.5
  75.9 4.5 %collective-permute-done.6 = bf16[288,256]{1,0:T(8,128)(2,1)S(1)} collective-permute-done((bf16[288,256]{1,0:T(8,128)(2,1)S(1)}, bf16[288,256]{1,0:T(8,128)(2,1)S(1)}, u32[]{:S(2)}, u32[]{:S(2)}) %collective-permute-start.6) | collective-permute-done | bytes 147488 | tf_op jit(solution)/shard_map/ppermute | solution.py:250
  80.4 0.0 all-to-all-done.refs_0_
  80.4 7.5 %collective-permute-start.7 = (bf16[1,256,256]{2,1,0:T(8,128)(2,1)S(1)}, bf16[1,256,256]{2,1,0:T(8,128)(2,1)S(1)}, u32[]{:S(2)}, u32[]{:S(2)}) collective-permute-start(bf16[1,256,256]{2,1,0:T(8,128)(2,1)S(1)} %slice.21), channel_id=1, source_target_pairs={{0,16},{2,18},{4,20},{6,22},{8,24},{10,26},{12,28},{14,30},{16,0},... | collective-permute-start | bytes 393224 | tf_op jit(solution)/shard_map/ppermute | solution.py:254
  87.9 8.0 %attend.1 = bf16[512,128]{1,0:T(8,128)(2,1)S(1)} custom-call(bf16[16,784,128]{2,1,0:T(8,128)(2,1)} %all-to-all-done.refs_0_), custom_call_target="tpu_custom_call" | custom-call | flops 2147483648 | bytes 3211264 | tf_op jit(solution)/shard_map/attend/pallas_call | solution.py:104
  95.9 0.0 collective-permute-done.7.refs_0_
  95.9 0.6 copy-done.4
  96.6 0.1 collective-permute-start.8
  96.7 6.4 %collective-permute-done.8 = bf16[512,128]{1,0:T(8,128)(2,1)S(1)} collective-permute-done((bf16[512,128]{1,0:T(8,128)(2,1)S(1)}, bf16[512,128]{1,0:T(8,128)(2,1)S(1)}, u32[]{:S(2)}, u32[]{:S(2)}) %collective-permute-start.8) | collective-permute-done | bytes 131104 | tf_op jit(solution)/shard_map/ppermute | solution.py:268
  103.1 1.1 broadcast_in_dim.4
  104.3 4.1 %all-to-all-start.1 = ((bf16[4,2,512,128]{3,2,1,0:T(8,128)(2,1)}), bf16[4,2,512,128]{3,2,1,0:T(8,128)(2,1)S(1)}, u32[]{:S(2)}, u32[]{:S(2)}) async-start(bf16[4,2,512,128]{3,2,1,0:T(8,128)(2,1)} %broadcast_in_dim.4), calls=%async_computation.1 | async-start | bytes 2097152 | tf_op jit(solution)/shard_map/all_to_all | solution.py:263
  108.5 0.1 reshape.45
  108.6 0.4 rev.7
  109.0 0.8 fusion.11
  109.8 1.2 collective-permute-start.11
  111.0 1.5 collective-permute-start.10
  112.5 0.1 broadcast_select_fusion
  112.6 0.1 copy.20
  112.7 0.6 collective-permute-start.9
  113.3 7.8 %collective-permute-done.9.ids_ref = s32[2,8,2048]{2,1,0:T(8,128)S(1)} collective-permute-done((s32[2,8,2048]{2,1,0:T(8,128)S(1)}, s32[2,8,2048]{2,1,0:T(8,128)S(1)}, u32[]{:S(2)}, u32[]{:S(2)}) %collective-permute-start.9) | collective-permute-done | bytes 131104 | tf_op jit(solution)/shard_map/ppermute | solution.py:278
  121.1 3.6 %collective-permute-done.11.refs_1_ = bf16[2,256,256]{2,1,0:T(8,128)(2,1)S(1)} collective-permute-done((bf16[2,256,256]{2,1,0:T(8,128)(2,1)}, bf16[2,256,256]{2,1,0:T(8,128)(2,1)S(1)}, u32[]{:S(2)}, u32[]{:S(2)}) %collective-permute-start.11) | collective-permute-done | bytes 262176 | tf_op jit(solution)/shard_map/ppermute | solution.py:257
  124.7 0.0 collective-permute-done.10
  124.7 2.1 %all-to-all-done.1 = bf16[4,2,512,128]{3,2,1,0:T(8,128)(2,1)S(1)} async-done(((bf16[4,2,512,128]{3,2,1,0:T(8,128)(2,1)}), bf16[4,2,512,128]{3,2,1,0:T(8,128)(2,1)S(1)}, u32[]{:S(2)}, u32[]{:S(2)}) %all-to-all-start.1) | async-done | bytes 1048608 | tf_op jit(solution)/shard_map/all_to_all | solution.py:263
  126.8 1.1 broadcast_in_dim.5
  127.9 0.0 copy-done.2
  127.9 4.0 %all-to-all-start.2 = ((bf16[4,2,512,128]{3,2,1,0:T(8,128)(2,1)}), bf16[4,2,512,128]{3,2,1,0:T(8,128)(2,1)S(1)}, u32[]{:S(2)}, u32[]{:S(2)}) async-start(bf16[4,2,512,128]{3,2,1,0:T(8,128)(2,1)} %broadcast_in_dim.5), calls=%async_computation.2 | async-start | bytes 2097152 | tf_op jit(solution)/shard_map/all_to_all | solution.py:263
  131.9 0.0 collective-permute-start.12
  131.9 1.1 collective-permute-start.13
  133.0 7.1 %expand.4.refs_0_ = bf16[32,2048,128]{2,1,0:T(8,128)(2,1)} custom-call(s32[2,8,2048]{2,1,0:T(8,128)S(1)} %reshape.46.ids_ref, bf16[8,512,128]{2,1,0:T(8,128)(2,1)S(1)} %bitcast.96), custom_call_target="tpu_custom_call" | custom-call | flops 4294967296 | bytes 5242880 | tf_op jit(solution)/shard_map/expand/pallas_call | solution.py:141
  140.1 0.0 collective-permute-done.12.attended_ref
  140.1 7.1 %expand.5.refs_0_ = bf16[32,2048,128]{2,1,0:T(8,128)(2,1)} custom-call(s32[2,8,2048]{2,1,0:T(8,128)S(1)} %reshape.46.ids_ref, bf16[8,512,128]{2,1,0:T(8,128)(2,1)S(1)} %collective-permute-done.12.attended_ref, bf16[32,2048,128]{2,1,0:T(8,128)(2,1)} %expand.4.refs_0_), custom_call_target="tpu_custom_call", output_to_operand_aliasing={{}: (2, {})} | custom-call | flops 4294967296 | bytes 5242880 | tf_op jit(solution)/shard_map/expand/pallas_call | solution.py:141
  147.2 3.2 %collective-permute-done.13.refs_2_ = bf16[3,256,256]{2,1,0:T(8,128)(2,1)S(1)} collective-permute-done((bf16[3,256,256]{2,1,0:T(8,128)(2,1)S(1)}, bf16[3,256,256]{2,1,0:T(8,128)(2,1)S(1)}, u32[]{:S(2)}, u32[]{:S(2)}) %collective-permute-start.13) | collective-permute-done | bytes 393248 | tf_op jit(solution)/shard_map/ppermute | solution.py:257
  150.4 0.7 copy-done
  151.2 1.5 all-to-all-done.2
  152.6 0.0 collective-permute-start.14
  152.6 0.1 pad_add_fusion.places_ref
  152.7 2.0 %collective-permute-start.15 = (bf16[2,256,256]{2,1,0:T(8,128)(2,1)}, bf16[2,256,256]{2,1,0:T(8,128)(2,1)S(1)}, u32[]{:S(2)}, u32[]{:S(2)}) collective-permute-start(bf16[2,256,256]{2,1,0:T(8,128)(2,1)} %get-tuple-element.39), channel_id=1, source_target_pairs={{0,16},{2,18},{4,20},{6,22},{8,24},{10,26},{12,28},{14,30},{16,0},... | collective-permute-start | bytes 786440 | tf_op jit(solution)/shard_map/ppermute | solution.py:257
  154.7 7.1 %expand.6.refs_0_ = bf16[32,2048,128]{2,1,0:T(8,128)(2,1)} custom-call(s32[2,8,2048]{2,1,0:T(8,128)S(1)} %collective-permute-done.9.ids_ref, bf16[8,512,128]{2,1,0:T(8,128)(2,1)S(1)} %bitcast.98, bf16[32,2048,128]{2,1,0:T(8,128)(2,1)} %expand.5.refs_0_), custom_call_target="tpu_custom_call", output_to_operand_aliasing={{}: (2, {})} | custom-call | flops 4294967296 | bytes 5242880 | tf_op jit(solution)/shard_map/expand/pallas_call | solution.py:141
  161.8 0.0 collective-permute-done.14.attended_ref
  161.8 7.1 %expand.7.features_ref = bf16[32,2048,128]{2,1,0:T(8,128)(2,1)} custom-call(s32[2,8,2048]{2,1,0:T(8,128)S(1)} %collective-permute-done.9.ids_ref, bf16[8,512,128]{2,1,0:T(8,128)(2,1)S(1)} %collective-permute-done.14.attended_ref, bf16[32,2048,128]{2,1,0:T(8,128)(2,1)} %expand.6.refs_0_), custom_call_target="tpu_custom_call", output_to_operand_aliasing={{}: (2, {})} | custom-call | flops 4294967296 | bytes 5242880 | tf_op jit(solution)/shard_map/expand/pallas_call | solution.py:141
  168.9 0.0 collective-permute-done.15.refs_3_
  168.9 9.0 %project.1 = bf16[2048,256]{1,0:T(8,128)(2,1)S(1)} custom-call(s32[4]{0:T(128)S(1)} %pad_add_fusion.places_ref, bf16[32,2048,128]{2,1,0:T(8,128)(2,1)} %expand.7.features_ref, bf16[8,288,256]{2,1,0:T(8,128)(2,1)S(1)} %bitcast_dynamic-update-slice_fusion.near_ref, bf16[1,256,256]{2,1,0:T(8,128)(2,1)S(1)} %copy-done.5, bf16[2,256,256]{2,1,0:T(8,128)(2,1)S(1)} %copy-done.3, ...), custom_call_target="tpu_custom_call" | custom-call | flops 4294967296 | bytes 19922944 | tf_op jit(solution)/shard_map/project/pallas_call | solution.py:184
  177.9 18.6 %all_to_all.20 = bf16[8,256,256]{2,1,0:T(8,128)(2,1)S(1)} all-to-all(bf16[8,256,256]{2,1,0:T(8,128)(2,1)S(1)} %bitcast.99), channel_id=1, replica_groups={{0,2,4,6,8,10,12,14},{16,18,20,22,24,26,28,30},{1,3,5,7,9,11,13,15},{17..., dimensions={0} | all-to-all | bytes 2097152 | tf_op jit(solution)/shard_map/all_to_all | solution.py:296
  196.5 1.1 copy.30
  (49 shorter events, 0.5 us)
Async XLA Ops:
  0.0 2.4 %copy-start.8 = (bf16[256,16,128]{2,1,0:T(8,128)(2,1)S(1)}, bf16[256,16,128]{2,1,0:T(8,128)(2,1)}, u32[]{:S(2)}) copy-start(bf16[256,16,128]{2,1,0:T(8,128)(2,1)} %param.6) | copy-start | bytes 3145732
  0.0 2.4 %copy-start.7 = (bf16[256,16,128]{2,1,0:T(8,128)(2,1)S(1)}, bf16[256,16,128]{2,1,0:T(8,128)(2,1)}, u32[]{:S(2)}) copy-start(bf16[256,16,128]{2,1,0:T(8,128)(2,1)} %param.7) | copy-start | bytes 3145732
  4.8 7.6 %copy-start.6 = (bf16[256,2048]{1,0:T(8,128)(2,1)S(1)}, bf16[256,2048]{1,0:T(8,128)(2,1)}, u32[]{:S(2)}) copy-start(bf16[256,2048]{1,0:T(8,128)(2,1)} %param.9) | copy-start | bytes 3145732
  4.8 75.5 %all-to-all-start = ((bf16[16,784,128]{2,1,0:T(8,128)(2,1)}), bf16[16,784,128]{2,1,0:T(8,128)(2,1)}, u32[]{:S(2)}, u32[]{:S(2)}) async-start(bf16[16,784,128]{2,1,0:T(8,128)(2,1)} %pad_maximum_fusion), calls=%async_computation | async-start | bytes 6422528 | tf_op jit(solution)/shard_map/all_to_all | solution.py:242
  15.2 5.1 %collective-permute-start = (bf16[288,256]{1,0:T(8,128)(2,1)S(1)}, bf16[288,256]{1,0:T(8,128)(2,1)S(1)}, u32[]{:S(2)}, u32[]{:S(2)}) collective-permute-start(bf16[288,256]{1,0:T(8,128)(2,1)S(1)} %get-tuple-element.50), channel_id=1, source_target_pairs={{0,2},{2,0},{4,6},{6,4},{8,10},{10,8},{12,14},{14,12},{16,18},{18,... | collective-permute-start | bytes 442376 | tf_op jit(solution)/shard_map/ppermute | solution.py:250
  15.7 60.2 %collective-permute-start.5 = (bf16[288,256]{1,0:T(8,128)(2,1)S(1)}, bf16[288,256]{1,0:T(8,128)(2,1)S(1)}, u32[]{:S(2)}, u32[]{:S(2)}) collective-permute-start(bf16[288,256]{1,0:T(8,128)(2,1)S(1)} %pad_maximum_fusion.2), channel_id=1, source_target_pairs={{0,12},{2,14},{4,8},{6,10},{8,4},{10,6},{12,0},{14,2},{16,28},{18,... | collective-permute-start | bytes 442376 | tf_op jit(solution)/shard_map/ppermute | solution.py:250
  18.3 19.0 %collective-permute-start.1 = (bf16[288,256]{1,0:T(8,128)(2,1)S(1)}, bf16[288,256]{1,0:T(8,128)(2,1)S(1)}, u32[]{:S(2)}, u32[]{:S(2)}) collective-permute-start(bf16[288,256]{1,0:T(8,128)(2,1)S(1)} %get-tuple-element.51), channel_id=1, source_target_pairs={{0,4},{2,6},{4,0},{6,2},{8,12},{10,14},{12,8},{14,10},{16,20},{18,... | collective-permute-start | bytes 442376 | tf_op jit(solution)/shard_map/ppermute | solution.py:250
  18.9 25.9 %collective-permute-start.2 = (bf16[288,256]{1,0:T(8,128)(2,1)S(1)}, bf16[288,256]{1,0:T(8,128)(2,1)S(1)}, u32[]{:S(2)}, u32[]{:S(2)}) collective-permute-start(bf16[288,256]{1,0:T(8,128)(2,1)S(1)} %get-tuple-element.52), channel_id=1, source_target_pairs={{0,6},{2,4},{4,2},{6,0},{8,14},{10,12},{12,10},{14,8},{16,22},{18,... | collective-permute-start | bytes 442376 | tf_op jit(solution)/shard_map/ppermute | solution.py:250
  19.7 53.0 %collective-permute-start.3 = (bf16[288,256]{1,0:T(8,128)(2,1)S(1)}, bf16[288,256]{1,0:T(8,128)(2,1)S(1)}, u32[]{:S(2)}, u32[]{:S(2)}) collective-permute-start(bf16[288,256]{1,0:T(8,128)(2,1)S(1)} %get-tuple-element.53), channel_id=1, source_target_pairs={{0,8},{2,10},{4,12},{6,14},{8,0},{10,2},{12,4},{14,6},{16,24},{18,... | collective-permute-start | bytes 442376 | tf_op jit(solution)/shard_map/ppermute | solution.py:250
  20.4 55.5 %collective-permute-start.4 = (bf16[288,256]{1,0:T(8,128)(2,1)S(1)}, bf16[288,256]{1,0:T(8,128)(2,1)S(1)}, u32[]{:S(2)}, u32[]{:S(2)}) collective-permute-start(bf16[288,256]{1,0:T(8,128)(2,1)S(1)} %get-tuple-element.54), channel_id=1, source_target_pairs={{0,10},{2,8},{4,14},{6,12},{8,2},{10,0},{12,6},{14,4},{16,26},{18,... | collective-permute-start | bytes 442376 | tf_op jit(solution)/shard_map/ppermute | solution.py:250
  37.3 43.0 %collective-permute-start.6 = (bf16[288,256]{1,0:T(8,128)(2,1)S(1)}, bf16[288,256]{1,0:T(8,128)(2,1)S(1)}, u32[]{:S(2)}, u32[]{:S(2)}) collective-permute-start(bf16[288,256]{1,0:T(8,128)(2,1)S(1)} %get-tuple-element.49), channel_id=1, source_target_pairs={{0,14},{2,12},{4,10},{6,8},{8,6},{10,4},{12,2},{14,0},{16,30},{18,... | collective-permute-start | bytes 442376 | tf_op jit(solution)/shard_map/ppermute | solution.py:250
  80.4 15.5 %collective-permute-start.7 = (bf16[1,256,256]{2,1,0:T(8,128)(2,1)S(1)}, bf16[1,256,256]{2,1,0:T(8,128)(2,1)S(1)}, u32[]{:S(2)}, u32[]{:S(2)}) collective-permute-start(bf16[1,256,256]{2,1,0:T(8,128)(2,1)S(1)} %slice.21), channel_id=1, source_target_pairs={{0,16},{2,18},{4,20},{6,22},{8,24},{10,26},{12,28},{14,30},{16,0},... | collective-permute-start | bytes 393224 | tf_op jit(solution)/shard_map/ppermute | solution.py:254
  95.9 0.7 copy-start.4
  96.6 6.5 %collective-permute-start.8 = (bf16[512,128]{1,0:T(8,128)(2,1)S(1)}, bf16[512,128]{1,0:T(8,128)(2,1)S(1)}, u32[]{:S(2)}, u32[]{:S(2)}) collective-permute-start(bf16[512,128]{1,0:T(8,128)(2,1)S(1)} %attend.1), channel_id=1, source_target_pairs={{0,16},{2,18},{4,20},{6,22},{8,24},{10,26},{12,28},{14,30},{16,0},... | collective-permute-start | bytes 393224 | tf_op jit(solution)/shard_map/ppermute | solution.py:268
  104.3 22.6 %all-to-all-start.1 = ((bf16[4,2,512,128]{3,2,1,0:T(8,128)(2,1)}), bf16[4,2,512,128]{3,2,1,0:T(8,128)(2,1)S(1)}, u32[]{:S(2)}, u32[]{:S(2)}) async-start(bf16[4,2,512,128]{3,2,1,0:T(8,128)(2,1)} %broadcast_in_dim.4), calls=%async_computation.1 | async-start | bytes 2097152 | tf_op jit(solution)/shard_map/all_to_all | solution.py:263
  109.8 14.9 %collective-permute-start.11 = (bf16[2,256,256]{2,1,0:T(8,128)(2,1)}, bf16[2,256,256]{2,1,0:T(8,128)(2,1)S(1)}, u32[]{:S(2)}, u32[]{:S(2)}) collective-permute-start(bf16[2,256,256]{2,1,0:T(8,128)(2,1)} %get-tuple-element.40), channel_id=1, source_target_pairs={{0,16},{2,18},{4,20},{6,22},{8,24},{10,26},{12,28},{14,30},{16,0},... | collective-permute-start | bytes 786440 | tf_op jit(solution)/shard_map/ppermute | solution.py:257
  111.0 13.7 %collective-permute-start.10 = (bf16[2,512,128]{2,1,0:T(8,128)(2,1)S(1)}, bf16[2,512,128]{2,1,0:T(8,128)(2,1)S(1)}, u32[]{:S(2)}, u32[]{:S(2)}) collective-permute-start(bf16[2,512,128]{2,1,0:T(8,128)(2,1)S(1)} %pad_maximum_fusion.17), channel_id=1, source_target_pairs={{0,1},{1,0},{2,3},{3,2},{4,5},{5,4},{6,7},{7,6},{8,9},{9,8},{10,11... | collective-permute-start | bytes 786440 | tf_op jit(solution)/shard_map/ppermute | solution.py:269
  112.7 8.4 %collective-permute-start.9 = (s32[2,8,2048]{2,1,0:T(8,128)S(1)}, s32[2,8,2048]{2,1,0:T(8,128)S(1)}, u32[]{:S(2)}, u32[]{:S(2)}) collective-permute-start(s32[2,8,2048]{2,1,0:T(8,128)S(1)} %reshape.46.ids_ref), channel_id=1, source_target_pairs={{0,1},{1,0},{2,3},{3,2},{4,5},{5,4},{6,7},{7,6},{8,9},{9,8},{10,11... | collective-permute-start | bytes 393224 | tf_op jit(solution)/shard_map/ppermute | solution.py:278
  124.7 3.2 %copy-start.2 = (bf16[2,256,256]{2,1,0:T(8,128)(2,1)}, bf16[2,256,256]{2,1,0:T(8,128)(2,1)S(1)}, u32[]{:S(2)}) copy-start(bf16[2,256,256]{2,1,0:T(8,128)(2,1)S(1)} %collective-permute-done.11.refs_1_) | copy-start | bytes 786436
  127.9 24.7 %all-to-all-start.2 = ((bf16[4,2,512,128]{3,2,1,0:T(8,128)(2,1)}), bf16[4,2,512,128]{3,2,1,0:T(8,128)(2,1)S(1)}, u32[]{:S(2)}, u32[]{:S(2)}) async-start(bf16[4,2,512,128]{3,2,1,0:T(8,128)(2,1)} %broadcast_in_dim.5), calls=%async_computation.2 | async-start | bytes 2097152 | tf_op jit(solution)/shard_map/all_to_all | solution.py:263
  131.9 8.2 %collective-permute-start.12 = (bf16[8,512,128]{2,1,0:T(8,128)(2,1)S(1)}, bf16[8,512,128]{2,1,0:T(8,128)(2,1)S(1)}, u32[]{:S(2)}, u32[]{:S(2)}) collective-permute-start(bf16[8,512,128]{2,1,0:T(8,128)(2,1)S(1)} %bitcast.95), channel_id=1, source_target_pairs={{0,2},{2,0},{4,6},{6,4},{8,10},{10,8},{12,14},{14,12},{16,18},{18,... | collective-permute-start | bytes 3145736 | tf_op jit(solution)/shard_map/ppermute | solution.py:283
  131.9 18.5 %collective-permute-start.13 = (bf16[3,256,256]{2,1,0:T(8,128)(2,1)S(1)}, bf16[3,256,256]{2,1,0:T(8,128)(2,1)S(1)}, u32[]{:S(2)}, u32[]{:S(2)}) collective-permute-start(bf16[3,256,256]{2,1,0:T(8,128)(2,1)S(1)} %slice.26), channel_id=1, source_target_pairs={{0,16},{2,18},{4,20},{6,22},{8,24},{10,26},{12,28},{14,30},{16,0},... | collective-permute-start | bytes 1179656 | tf_op jit(solution)/shard_map/ppermute | solution.py:257
  150.4 0.7 copy-start
  152.6 9.2 %collective-permute-start.14 = (bf16[8,512,128]{2,1,0:T(8,128)(2,1)S(1)}, bf16[8,512,128]{2,1,0:T(8,128)(2,1)S(1)}, u32[]{:S(2)}, u32[]{:S(2)}) collective-permute-start(bf16[8,512,128]{2,1,0:T(8,128)(2,1)S(1)} %bitcast.97), channel_id=1, source_target_pairs={{0,2},{2,0},{4,6},{6,4},{8,10},{10,8},{12,14},{14,12},{16,18},{18,... | collective-permute-start | bytes 3145736 | tf_op jit(solution)/shard_map/ppermute | solution.py:291
  152.7 16.2 %collective-permute-start.15 = (bf16[2,256,256]{2,1,0:T(8,128)(2,1)}, bf16[2,256,256]{2,1,0:T(8,128)(2,1)S(1)}, u32[]{:S(2)}, u32[]{:S(2)}) collective-permute-start(bf16[2,256,256]{2,1,0:T(8,128)(2,1)} %get-tuple-element.39), channel_id=1, source_target_pairs={{0,16},{2,18},{4,20},{6,22},{8,24},{10,26},{12,28},{14,30},{16,0},... | collective-permute-start | bytes 786440 | tf_op jit(solution)/shard_map/ppermute | solution.py:257
  161.8 7.1 %copy-start.1 = (bf16[3,256,256]{2,1,0:T(8,128)(2,1)S(1)}, bf16[3,256,256]{2,1,0:T(8,128)(2,1)}, u32[]{:S(2)}) copy-start(bf16[3,256,256]{2,1,0:T(8,128)(2,1)} %copy-done) | copy-start | bytes 1179652
  161.8 7.1 %copy-start.3 = (bf16[2,256,256]{2,1,0:T(8,128)(2,1)S(1)}, bf16[2,256,256]{2,1,0:T(8,128)(2,1)}, u32[]{:S(2)}) copy-start(bf16[2,256,256]{2,1,0:T(8,128)(2,1)} %copy-done.2) | copy-start | bytes 786436
  161.8 7.1 %copy-start.5 = (bf16[1,256,256]{2,1,0:T(8,128)(2,1)S(1)}, bf16[1,256,256]{2,1,0:T(8,128)(2,1)}, u32[]{:S(2)}) copy-start(bf16[1,256,256]{2,1,0:T(8,128)(2,1)} %copy-done.4) | copy-start | bytes 393220

commit v11 on v10

--- a/solution.py
+++ b/solution.py
@@ -60,7 +60,7 @@
 
     sums_ref[...] = jnp.zeros_like(sums_ref)
 
-    @pl.loop(0, n_src, unroll=4)
+    @pl.loop(0, n_src, unroll=8)
     def _(src):
         coded = moved_ref[src, 3 * tok_rows :, :].astype(jnp.float32).astype(jnp.int32)
         parts = []
@@ -81,7 +81,7 @@
             top = jnp.maximum(top, scores[:, i * lanes : (i + 1) * lanes])
         return top
 
-    top = lax.fori_loop(0, n_src, score, jnp.full((C, lanes), -jnp.inf, jnp.float32), unroll=4)
+    top = lax.fori_loop(0, n_src, score, jnp.full((C, lanes), -jnp.inf, jnp.float32), unroll=8)
     top = jnp.broadcast_to(jnp.max(top, axis=1, keepdims=True), (C, tok_rows))
 
     acc_ref[...] = jnp.zeros_like(acc_ref)
@@ -94,7 +94,7 @@
         acc_ref[...] += jnp.dot(weights.astype(jnp.bfloat16), values, preferred_element_type=jnp.float32)
         return total
 
-    total = lax.fori_loop(0, n_src, weigh, jnp.zeros((C, lanes), jnp.float32), unroll=4)
+    total = lax.fori_loop(0, n_src, weigh, jnp.zeros((C, lanes), jnp.float32), unroll=8)
     out_ref[...] = (acc_ref[...] / jnp.sum(total, axis=1, keepdims=True)).astype(jnp.bfloat16)
 
 
@@ -250,11 +250,10 @@
         near.append(lax.ppermute(block, "seq", [(i, i ^ k) for i in range(n_seq)]) if k else block)
     near = jnp.stack(near)
     moved, near = lax.optimization_barrier((moved, near))
-    cuts = [half * i // 8 for i in (0, 1, 3, 6, 8)]
-    far = [lax.ppermute(near[a:b, :rows], "seq", swap_halves) for a, b in zip(cuts[:1], cuts[1:])]
+    cuts = [half * i // 8 for i in (0, 3, 6, 8)]
     own = attend(moved, tok_rows)
-    own, near, far[0] = lax.optimization_barrier((own, near, far[0]))
-    far += [lax.ppermute(near[a:b, :rows], "seq", swap_halves) for a, b in zip(cuts[1:], cuts[2:])]
+    own, near = lax.optimization_barrier((own, near))
+    far = [lax.ppermute(near[a:b, :rows], "seq", swap_halves) for a, b in zip(cuts, cuts[1:])]
 
     def copied(pair):
         return jnp.broadcast_to(pair[None], (half // 2,) + pair.shape)
@@ -266,7 +265,6 @@
         return got.reshape((half,) + own.shape)
 
     pair = jnp.stack([own, lax.ppermute(own, "seq", swap_halves)])
-    far_pair = lax.ppermute(pair, "head", swap_heads)
     first = spread(copied(pair))
 
     coded = near[:, rows:].astype(jnp.int32)
@@ -276,18 +274,15 @@
     )
     slot_ids = by_slot(coded, half_at, core)
     far_ids = lax.ppermute(slot_ids, "head", swap_heads)
-    far_copies = copied(far_pair)
-    first, slot_ids, far_ids, far_copies, far[1] = lax.optimization_barrier(
-        (first, slot_ids, far_ids, far_copies, far[1])
-    )
+    first, slot_ids, far_ids, far[0] = lax.optimization_barrier((first, slot_ids, far_ids, far[0]))
     second = lax.ppermute(first, "seq", swap_cores)
-    third = spread(far_copies)
+    third = lax.ppermute(first, "head", swap_heads)
 
     pieces = 4
     tok_tile = 2 * tok_rows
     features = expand(slot_ids, 0, first, None, 0, pieces, tok_tile)
     features = expand(slot_ids, 1, second, features, 1, pieces, tok_tile)
-    features, third, far[2] = lax.optimization_barrier((features, third, far[2]))
+    features, third, far[1] = lax.optimization_barrier((features, third, far[1]))
     fourth = lax.ppermute(third, "seq", swap_cores)
     features = expand(far_ids, 0, third, features, 2, pieces, tok_tile)
     features = expand(far_ids, 1, fourth, features, 3, pieces, tok_tile)

time: 198 us -> 199 us (level)
  waiting for transfers between devices: 82.9 us -> 86.4 us
    ppermute x4 -> x3, waiting for transfers between devices: 6.81 us -> 14.6 us  [by_head(): lax.ppermute(near[a:b, :rows], 'seq', swap_halves)]
    ppermute x1, starting transfers between devices: 0.08 us -> 7.46 us  [by_head(): pair = jnp.stack([own, lax.ppermute(own, 'seq', swap_halves)])]
    ppermute x4 -> x3, starting transfers between devices: 11.7 us -> 6.89 us  [by_head(): lax.ppermute(near[a:b, :rows], 'seq', swap_halves)]
    all_to_all x2 -> x1, starting transfers between devices: 8.09 us -> 3.7 us  [spread(): lax.all_to_all(copies, 'seq', split_axis=0, concat_axis=0, axis_index_gro...]
    ppermute x1, waiting for transfers between devices: 7.78 us -> 3.47 us  [by_head(): far_ids = lax.ppermute(slot_ids, 'head', swap_heads)]
    ppermute x1, waiting for transfers between devices: 0.01 us -> 2.54 us  [by_head(): third = lax.ppermute(first, 'head', swap_heads)]
    all_to_all x2 -> x1, waiting for transfers between devices: 3.55 us -> 1.39 us  [spread(): lax.all_to_all(copies, 'seq', split_axis=0, concat_axis=0, axis_index_gro...]
  transfers between devices with their start and end apart: 19 -> 17, of which waited for: 11 -> 12; matrix products, arithmetic and copies ran while one was open for 2% -> 2% of each run, Pallas kernels for 18% -> 14%
where the time goes in v11:
time: 199 us
  waiting for transfers between devices  86.4 us (43%)
  Pallas kernels  44.6 us (22%)
  starting transfers between devices  35.2 us (18%)
  blocking collectives  19.4 us (10%)
  local copies, waits for them, and re-layouts  9.97 us (5%)
  other arithmetic  3.09 us (2%)
    ppermute x7, waiting for transfers between devices, by_head(): lax.ppermute(block, 'seq', [(i, i ^ k) for i in range(n_seq)])  58.4 us
    pallas_call x4, Pallas kernels, expand(): pl.pallas_call(expand_kernel, out_shape=jax.ShapeDtypeStruct((pieces * he...  28.6 us
    all_to_all x1, blocking collectives, by_head(): lax.all_to_all(near_out.reshape(half, tok_rows, cols_each), 'seq', split_...  19.4 us
    ppermute x3, waiting for transfers between devices, by_head(): lax.ppermute(near[a:b, :rows], 'seq', swap_halves)  14.6 us
    pallas_call x1, Pallas kernels, project(): pl.pallas_call(project_kernel, out_shape=jax.ShapeDtypeStruct((tokens, co...  8.99 us
    all_to_all x1, starting transfers between devices, by_head(): lax.all_to_all(packed, 'seq', split_axis=0, concat_axis=0, tiled=True)  7.56 us
    ppermute x1, starting transfers between devices, by_head(): pair = jnp.stack([own, lax.ppermute(own, 'seq', swap_halves)])  7.46 us
    pallas_call x1, Pallas kernels, attend(): pl.pallas_call(lambda *refs: attend_kernel(tok_rows, *refs), out_shape=ja...  7.02 us
  transfers between devices with their start and end apart: 17, of which 12 were waited for; matrix products, arithmetic and copies ran while one was open for 2% of the time, Pallas kernels for 14%

profile of v11, /device:TPU:0, one launch (start us, length us, event | category | flops | bytes accessed | tf_op | source)
XLA Modules:
  0.0 199.1 jit_solution(6681353646827207056)
XLA Ops:
  0.0 0.0 copy-start.5
  0.0 0.9 fusion.6
  0.9 1.5 copy.44
  2.4 0.0 copy-done.5
  2.4 0.0 copy-done.6
  2.4 0.5 copy_bitcast_fusion
  3.0 1.8 pad_maximum_fusion
  4.8 7.6 %all-to-all-start = ((bf16[16,784,128]{2,1,0:T(8,128)(2,1)}), bf16[16,784,128]{2,1,0:T(8,128)(2,1)}, u32[]{:S(2)}, u32[]{:S(2)}) async-start(bf16[16,784,128]{2,1,0:T(8,128)(2,1)} %pad_maximum_fusion), calls=%async_computation | async-start | bytes 6422528 | tf_op jit(solution)/shard_map/all_to_all | solution.py:242
  12.4 0.0 copy-done.4
  12.5 0.3 copy.32
  12.8 2.2 %constant_dynamic-slice_fusion = (bf16[256,1,256]{2,1,0:T(2,128)(2,1)S(1)}, bf16[256,1,256]{2,1,0:T(2,128)(2,1)S(1)}, bf16[256,1,256]{2,1,0:T(2,128)(2,1)S(1)}, ...) fusion(bf16[256,8,256]{2,1,0:T(8,128)(2,1)S(1)} %bitcast.99, ...), kind=kLoop, calls=%fused_computation.68 | loop fusion | bytes 2097184 | tf_op jit(solution)/shard_map/dynamic-slice.7
  15.1 0.1 pad_maximum_fusion.1
  15.2 0.4 collective-permute-start
  15.6 1.7 collective-permute-start.1
  17.3 0.0 collective-permute-start.2
  17.3 1.7 collective-permute-start.3
  19.0 0.1 collective-permute-start.4
  19.2 0.0 collective-permute-done
  19.2 2.6 %collective-permute-start.5 = (bf16[288,256]{1,0:T(8,128)(2,1)S(1)}, bf16[288,256]{1,0:T(8,128)(2,1)S(1)}, u32[]{:S(2)}, u32[]{:S(2)}) collective-permute-start(bf16[288,256]{1,0:T(8,128)(2,1)S(1)} %pad_maximum_fusion.2), channel_id=1, source_target_pairs={{0,12},{2,14},{4,8},{6,10},{8,4},{10,6},{12,0},{14,2},{16,28},{18,... | collective-permute-start | bytes 442376 | tf_op jit(solution)/shard_map/ppermute | solution.py:250
  21.9 15.4 %collective-permute-done.1 = bf16[288,256]{1,0:T(8,128)(2,1)S(1)} collective-permute-done((bf16[288,256]{1,0:T(8,128)(2,1)S(1)}, bf16[288,256]{1,0:T(8,128)(2,1)S(1)}, u32[]{:S(2)}, u32[]{:S(2)}) %collective-permute-start.1) | collective-permute-done | bytes 147488 | tf_op jit(solution)/shard_map/ppermute | solution.py:250
  37.3 0.0 collective-permute-start.6
  37.3 7.4 %collective-permute-done.2 = bf16[288,256]{1,0:T(8,128)(2,1)S(1)} collective-permute-done((bf16[288,256]{1,0:T(8,128)(2,1)S(1)}, bf16[288,256]{1,0:T(8,128)(2,1)S(1)}, u32[]{:S(2)}, u32[]{:S(2)}) %collective-permute-start.2) | collective-permute-done | bytes 147488 | tf_op jit(solution)/shard_map/ppermute | solution.py:250
  44.8 23.8 %collective-permute-done.3 = bf16[288,256]{1,0:T(8,128)(2,1)S(1)} collective-permute-done((bf16[288,256]{1,0:T(8,128)(2,1)S(1)}, bf16[288,256]{1,0:T(8,128)(2,1)S(1)}, u32[]{:S(2)}, u32[]{:S(2)}) %collective-permute-start.3) | collective-permute-done | bytes 147488 | tf_op jit(solution)/shard_map/ppermute | solution.py:250
  68.7 3.1 %collective-permute-done.4 = bf16[288,256]{1,0:T(8,128)(2,1)S(1)} collective-permute-done((bf16[288,256]{1,0:T(8,128)(2,1)S(1)}, bf16[288,256]{1,0:T(8,128)(2,1)S(1)}, u32[]{:S(2)}, u32[]{:S(2)}) %collective-permute-start.4) | collective-permute-done | bytes 147488 | tf_op jit(solution)/shard_map/ppermute | solution.py:250
  71.8 6.2 %collective-permute-done.5 = bf16[288,256]{1,0:T(8,128)(2,1)S(1)} collective-permute-done((bf16[288,256]{1,0:T(8,128)(2,1)S(1)}, bf16[288,256]{1,0:T(8,128)(2,1)S(1)}, u32[]{:S(2)}, u32[]{:S(2)}) %collective-permute-start.5) | collective-permute-done | bytes 147488 | tf_op jit(solution)/shard_map/ppermute | solution.py:250
  78.1 2.3 %collective-permute-done.6 = bf16[288,256]{1,0:T(8,128)(2,1)S(1)} collective-permute-done((bf16[288,256]{1,0:T(8,128)(2,1)S(1)}, bf16[288,256]{1,0:T(8,128)(2,1)S(1)}, u32[]{:S(2)}, u32[]{:S(2)}) %collective-permute-start.6) | collective-permute-done | bytes 147488 | tf_op jit(solution)/shard_map/ppermute | solution.py:250
  80.4 0.0 all-to-all-done.refs_0_
  80.4 7.0 %attend.1 = bf16[512,128]{1,0:T(8,128)(2,1)S(1)} custom-call(bf16[16,784,128]{2,1,0:T(8,128)(2,1)} %all-to-all-done.refs_0_), custom_call_target="tpu_custom_call" | custom-call | flops 2147483648 | bytes 3211264 | tf_op jit(solution)/shard_map/attend/pallas_call | solution.py:104
  87.4 7.5 %collective-permute-start.7 = (bf16[512,128]{1,0:T(8,128)(2,1)S(1)}, bf16[512,128]{1,0:T(8,128)(2,1)S(1)}, u32[]{:S(2)}, u32[]{:S(2)}) collective-permute-start(bf16[512,128]{1,0:T(8,128)(2,1)S(1)} %attend.1), channel_id=1, source_target_pairs={{0,16},{2,18},{4,20},{6,22},{8,24},{10,26},{12,28},{14,30},{16,0},... | collective-permute-start | bytes 393224 | tf_op jit(solution)/shard_map/ppermute | solution.py:267
  94.9 6.0 %collective-permute-done.7 = bf16[512,128]{1,0:T(8,128)(2,1)S(1)} collective-permute-done((bf16[512,128]{1,0:T(8,128)(2,1)S(1)}, bf16[512,128]{1,0:T(8,128)(2,1)S(1)}, u32[]{:S(2)}, u32[]{:S(2)}) %collective-permute-start.7) | collective-permute-done | bytes 131104 | tf_op jit(solution)/shard_map/ppermute | solution.py:267
  100.9 1.1 broadcast_in_dim.2
  102.0 3.7 %all-to-all-start.1 = ((bf16[4,2,512,128]{3,2,1,0:T(8,128)(2,1)}), bf16[4,2,512,128]{3,2,1,0:T(8,128)(2,1)S(1)}, u32[]{:S(2)}, u32[]{:S(2)}) async-start(bf16[4,2,512,128]{3,2,1,0:T(8,128)(2,1)} %broadcast_in_dim.2), calls=%async_computation.1 | async-start | bytes 2097152 | tf_op jit(solution)/shard_map/all_to_all | solution.py:262
  105.9 0.1 reshape.41
  106.0 0.8 fusion.11
  106.8 2.7 %collective-permute-start.9 = (bf16[3,256,256]{2,1,0:T(8,128)(2,1)S(1)}, bf16[3,256,256]{2,1,0:T(8,128)(2,1)S(1)}, u32[]{:S(2)}, u32[]{:S(2)}) collective-permute-start(bf16[3,256,256]{2,1,0:T(8,128)(2,1)S(1)} %get-tuple-element.36), channel_id=1, source_target_pairs={{0,16},{2,18},{4,20},{6,22},{8,24},{10,26},{12,28},{14,30},{16,0},... | collective-permute-start | bytes 1179656 | tf_op jit(solution)/shard_map/ppermute | solution.py:256
  109.6 0.4 rev.7
  110.0 0.1 broadcast_select_fusion
  110.0 0.1 copy.20
  110.2 1.6 collective-permute-start.8
  111.7 3.5 %collective-permute-done.8.ids_ref = s32[2,8,2048]{2,1,0:T(8,128)S(1)} collective-permute-done((s32[2,8,2048]{2,1,0:T(8,128)S(1)}, s32[2,8,2048]{2,1,0:T(8,128)S(1)}, u32[]{:S(2)}, u32[]{:S(2)}) %collective-permute-start.8) | collective-permute-done | bytes 131104 | tf_op jit(solution)/shard_map/ppermute | solution.py:276
  115.2 10.1 %collective-permute-done.9.refs_0_ = bf16[3,256,256]{2,1,0:T(8,128)(2,1)S(1)} collective-permute-done((bf16[3,256,256]{2,1,0:T(8,128)(2,1)S(1)}, bf16[3,256,256]{2,1,0:T(8,128)(2,1)S(1)}, u32[]{:S(2)}, u32[]{:S(2)}) %collective-permute-start.9) | collective-permute-done | bytes 393248 | tf_op jit(solution)/shard_map/ppermute | solution.py:256
  125.3 0.8 copy-done
  126.0 1.4 all-to-all-done.1
  127.4 0.0 collective-permute-start.10
  127.4 1.5 collective-permute-start.11
  128.9 2.0 %collective-permute-start.12 = (bf16[3,256,256]{2,1,0:T(8,128)(2,1)}, bf16[3,256,256]{2,1,0:T(8,128)(2,1)S(1)}, u32[]{:S(2)}, u32[]{:S(2)}) collective-permute-start(bf16[3,256,256]{2,1,0:T(8,128)(2,1)} %get-tuple-element.35), channel_id=1, source_target_pairs={{0,16},{2,18},{4,20},{6,22},{8,24},{10,26},{12,28},{14,30},{16,0},... | collective-permute-start | bytes 1179656 | tf_op jit(solution)/shard_map/ppermute | solution.py:256
  131.0 7.1 %expand.4.refs_0_ = bf16[32,2048,128]{2,1,0:T(8,128)(2,1)} custom-call(s32[2,8,2048]{2,1,0:T(8,128)S(1)} %reshape.42.ids_ref, bf16[8,512,128]{2,1,0:T(8,128)(2,1)S(1)} %bitcast.96), custom_call_target="tpu_custom_call" | custom-call | flops 4294967296 | bytes 5242880 | tf_op jit(solution)/shard_map/expand/pallas_call | solution.py:141
  138.1 0.0 collective-permute-done.10.attended_ref
  138.1 7.1 %expand.5.refs_0_ = bf16[32,2048,128]{2,1,0:T(8,128)(2,1)} custom-call(s32[2,8,2048]{2,1,0:T(8,128)S(1)} %reshape.42.ids_ref, bf16[8,512,128]{2,1,0:T(8,128)(2,1)S(1)} %collective-permute-done.10.attended_ref, bf16[32,2048,128]{2,1,0:T(8,128)(2,1)} %expand.4.refs_0_), custom_call_target="tpu_custom_call", output_to_operand_aliasing={{}: (2, {})} | custom-call | flops 4294967296 | bytes 5242880 | tf_op jit(solution)/shard_map/expand/pallas_call | solution.py:141
  145.2 4.5 %collective-permute-done.12.refs_1_ = bf16[3,256,256]{2,1,0:T(8,128)(2,1)S(1)} collective-permute-done((bf16[3,256,256]{2,1,0:T(8,128)(2,1)}, bf16[3,256,256]{2,1,0:T(8,128)(2,1)S(1)}, u32[]{:S(2)}, u32[]{:S(2)}) %collective-permute-start.12) | collective-permute-done | bytes 393248 | tf_op jit(solution)/shard_map/ppermute | solution.py:256
  149.7 0.7 copy-done.2
  150.5 2.5 %collective-permute-done.11.attended_ref = bf16[8,512,128]{2,1,0:T(8,128)(2,1)S(1)} collective-permute-done((bf16[8,512,128]{2,1,0:T(8,128)(2,1)S(1)}, bf16[8,512,128]{2,1,0:T(8,128)(2,1)S(1)}, u32[]{:S(2)}, u32[]{:S(2)}) %collective-permute-start.11) | collective-permute-done | bytes 1048608 | tf_op jit(solution)/shard_map/ppermute | solution.py:279
  153.0 0.0 collective-permute-start.13
  153.0 0.1 pad_add_fusion.places_ref
  153.1 2.1 %collective-permute-start.14 = (bf16[2,256,256]{2,1,0:T(8,128)(2,1)S(1)}, bf16[2,256,256]{2,1,0:T(8,128)(2,1)S(1)}, u32[]{:S(2)}, u32[]{:S(2)}) collective-permute-start(bf16[2,256,256]{2,1,0:T(8,128)(2,1)S(1)} %slice.23), channel_id=1, source_target_pairs={{0,16},{2,18},{4,20},{6,22},{8,24},{10,26},{12,28},{14,30},{16,0},... | collective-permute-start | bytes 786440 | tf_op jit(solution)/shard_map/ppermute | solution.py:256
  155.2 7.2 %expand.6.refs_0_ = bf16[32,2048,128]{2,1,0:T(8,128)(2,1)} custom-call(s32[2,8,2048]{2,1,0:T(8,128)S(1)} %collective-permute-done.8.ids_ref, bf16[8,512,128]{2,1,0:T(8,128)(2,1)S(1)} %collective-permute-done.11.attended_ref, bf16[32,2048,128]{2,1,0:T(8,128)(2,1)} %expand.5.refs_0_), custom_call_target="tpu_custom_call", output_to_operand_aliasing={{}: (2, {})} | custom-call | flops 4294967296 | bytes 5242880 | tf_op jit(solution)/shard_map/expand/pallas_call | solution.py:141
  162.4 0.0 collective-permute-done.13.attended_ref
  162.4 7.2 %expand.7.features_ref = bf16[32,2048,128]{2,1,0:T(8,128)(2,1)} custom-call(s32[2,8,2048]{2,1,0:T(8,128)S(1)} %collective-permute-done.8.ids_ref, bf16[8,512,128]{2,1,0:T(8,128)(2,1)S(1)} %collective-permute-done.13.attended_ref, bf16[32,2048,128]{2,1,0:T(8,128)(2,1)} %expand.6.refs_0_), custom_call_target="tpu_custom_call", output_to_operand_aliasing={{}: (2, {})} | custom-call | flops 4294967296 | bytes 5242880 | tf_op jit(solution)/shard_map/expand/pallas_call | solution.py:141
  169.6 0.0 collective-permute-done.14.refs_2_
  169.6 0.0 copy-done.1
  169.6 0.0 copy-done.3
  169.6 9.0 %project.1 = bf16[2048,256]{1,0:T(8,128)(2,1)S(1)} custom-call(s32[4]{0:T(128)S(1)} %pad_add_fusion.places_ref, bf16[32,2048,128]{2,1,0:T(8,128)(2,1)} %expand.7.features_ref, bf16[8,288,256]{2,1,0:T(8,128)(2,1)S(1)} %bitcast_dynamic-update-slice_fusion.near_ref, bf16[3,256,256]{2,1,0:T(8,128)(2,1)S(1)} %copy-done.1, bf16[3,256,256]{2,1,0:T(8,128)(2,1)S(1)} %copy-done.3, ...), custom_call_target="tpu_custom_call" | custom-call | flops 4294967296 | bytes 19922944 | tf_op jit(solution)/shard_map/project/pallas_call | solution.py:184
  178.6 19.4 %all_to_all.15 = bf16[8,256,256]{2,1,0:T(8,128)(2,1)S(1)} all-to-all(bf16[8,256,256]{2,1,0:T(8,128)(2,1)S(1)} %bitcast.97), channel_id=1, replica_groups={{0,2,4,6,8,10,12,14},{16,18,20,22,24,26,28,30},{1,3,5,7,9,11,13,15},{17..., dimensions={0} | all-to-all | bytes 2097152 | tf_op jit(solution)/shard_map/all_to_all | solution.py:291
  198.0 1.1 copy.30
  (39 shorter events, 0.5 us)
Async XLA Ops:
  0.0 2.4 %copy-start.5 = (bf16[256,16,128]{2,1,0:T(8,128)(2,1)S(1)}, bf16[256,16,128]{2,1,0:T(8,128)(2,1)}, u32[]{:S(2)}) copy-start(bf16[256,16,128]{2,1,0:T(8,128)(2,1)} %param.7) | copy-start | bytes 3145732
  0.0 2.4 %copy-start.6 = (bf16[256,16,128]{2,1,0:T(8,128)(2,1)S(1)}, bf16[256,16,128]{2,1,0:T(8,128)(2,1)}, u32[]{:S(2)}) copy-start(bf16[256,16,128]{2,1,0:T(8,128)(2,1)} %param.6) | copy-start | bytes 3145732
  4.8 7.6 %copy-start.4 = (bf16[256,2048]{1,0:T(8,128)(2,1)S(1)}, bf16[256,2048]{1,0:T(8,128)(2,1)}, u32[]{:S(2)}) copy-start(bf16[256,2048]{1,0:T(8,128)(2,1)} %param.9) | copy-start | bytes 3145732
  4.8 75.5 %all-to-all-start = ((bf16[16,784,128]{2,1,0:T(8,128)(2,1)}), bf16[16,784,128]{2,1,0:T(8,128)(2,1)}, u32[]{:S(2)}, u32[]{:S(2)}) async-start(bf16[16,784,128]{2,1,0:T(8,128)(2,1)} %pad_maximum_fusion), calls=%async_computation | async-start | bytes 6422528 | tf_op jit(solution)/shard_map/all_to_all | solution.py:242
  15.2 4.0 %collective-permute-start = (bf16[288,256]{1,0:T(8,128)(2,1)S(1)}, bf16[288,256]{1,0:T(8,128)(2,1)S(1)}, u32[]{:S(2)}, u32[]{:S(2)}) collective-permute-start(bf16[288,256]{1,0:T(8,128)(2,1)S(1)} %get-tuple-element.46), channel_id=1, source_target_pairs={{0,2},{2,0},{4,6},{6,4},{8,10},{10,8},{12,14},{14,12},{16,18},{18,... | collective-permute-start | bytes 442376 | tf_op jit(solution)/shard_map/ppermute | solution.py:250
  15.6 21.7 %collective-permute-start.1 = (bf16[288,256]{1,0:T(8,128)(2,1)S(1)}, bf16[288,256]{1,0:T(8,128)(2,1)S(1)}, u32[]{:S(2)}, u32[]{:S(2)}) collective-permute-start(bf16[288,256]{1,0:T(8,128)(2,1)S(1)} %get-tuple-element.47), channel_id=1, source_target_pairs={{0,4},{2,6},{4,0},{6,2},{8,12},{10,14},{12,8},{14,10},{16,20},{18,... | collective-permute-start | bytes 442376 | tf_op jit(solution)/shard_map/ppermute | solution.py:250
  17.3 27.5 %collective-permute-start.2 = (bf16[288,256]{1,0:T(8,128)(2,1)S(1)}, bf16[288,256]{1,0:T(8,128)(2,1)S(1)}, u32[]{:S(2)}, u32[]{:S(2)}) collective-permute-start(bf16[288,256]{1,0:T(8,128)(2,1)S(1)} %get-tuple-element.48), channel_id=1, source_target_pairs={{0,6},{2,4},{4,2},{6,0},{8,14},{10,12},{12,10},{14,8},{16,22},{18,... | collective-permute-start | bytes 442376 | tf_op jit(solution)/shard_map/ppermute | solution.py:250
  17.3 51.3 %collective-permute-start.3 = (bf16[288,256]{1,0:T(8,128)(2,1)S(1)}, bf16[288,256]{1,0:T(8,128)(2,1)S(1)}, u32[]{:S(2)}, u32[]{:S(2)}) collective-permute-start(bf16[288,256]{1,0:T(8,128)(2,1)S(1)} %get-tuple-element.49), channel_id=1, source_target_pairs={{0,8},{2,10},{4,12},{6,14},{8,0},{10,2},{12,4},{14,6},{16,24},{18,... | collective-permute-start | bytes 442376 | tf_op jit(solution)/shard_map/ppermute | solution.py:250
  19.0 52.8 %collective-permute-start.4 = (bf16[288,256]{1,0:T(8,128)(2,1)S(1)}, bf16[288,256]{1,0:T(8,128)(2,1)S(1)}, u32[]{:S(2)}, u32[]{:S(2)}) collective-permute-start(bf16[288,256]{1,0:T(8,128)(2,1)S(1)} %get-tuple-element.50), channel_id=1, source_target_pairs={{0,10},{2,8},{4,14},{6,12},{8,2},{10,0},{12,6},{14,4},{16,26},{18,... | collective-permute-start | bytes 442376 | tf_op jit(solution)/shard_map/ppermute | solution.py:250
  19.2 58.8 %collective-permute-start.5 = (bf16[288,256]{1,0:T(8,128)(2,1)S(1)}, bf16[288,256]{1,0:T(8,128)(2,1)S(1)}, u32[]{:S(2)}, u32[]{:S(2)}) collective-permute-start(bf16[288,256]{1,0:T(8,128)(2,1)S(1)} %pad_maximum_fusion.2), channel_id=1, source_target_pairs={{0,12},{2,14},{4,8},{6,10},{8,4},{10,6},{12,0},{14,2},{16,28},{18,... | collective-permute-start | bytes 442376 | tf_op jit(solution)/shard_map/ppermute | solution.py:250
  37.3 43.0 %collective-permute-start.6 = (bf16[288,256]{1,0:T(8,128)(2,1)S(1)}, bf16[288,256]{1,0:T(8,128)(2,1)S(1)}, u32[]{:S(2)}, u32[]{:S(2)}) collective-permute-start(bf16[288,256]{1,0:T(8,128)(2,1)S(1)} %get-tuple-element.45), channel_id=1, source_target_pairs={{0,14},{2,12},{4,10},{6,8},{8,6},{10,4},{12,2},{14,0},{16,30},{18,... | collective-permute-start | bytes 442376 | tf_op jit(solution)/shard_map/ppermute | solution.py:250
  87.4 13.5 %collective-permute-start.7 = (bf16[512,128]{1,0:T(8,128)(2,1)S(1)}, bf16[512,128]{1,0:T(8,128)(2,1)S(1)}, u32[]{:S(2)}, u32[]{:S(2)}) collective-permute-start(bf16[512,128]{1,0:T(8,128)(2,1)S(1)} %attend.1), channel_id=1, source_target_pairs={{0,16},{2,18},{4,20},{6,22},{8,24},{10,26},{12,28},{14,30},{16,0},... | collective-permute-start | bytes 393224 | tf_op jit(solution)/shard_map/ppermute | solution.py:267
  102.0 25.4 %all-to-all-start.1 = ((bf16[4,2,512,128]{3,2,1,0:T(8,128)(2,1)}), bf16[4,2,512,128]{3,2,1,0:T(8,128)(2,1)S(1)}, u32[]{:S(2)}, u32[]{:S(2)}) async-start(bf16[4,2,512,128]{3,2,1,0:T(8,128)(2,1)} %broadcast_in_dim.2), calls=%async_computation.1 | async-start | bytes 2097152 | tf_op jit(solution)/shard_map/all_to_all | solution.py:262
  106.8 18.5 %collective-permute-start.9 = (bf16[3,256,256]{2,1,0:T(8,128)(2,1)S(1)}, bf16[3,256,256]{2,1,0:T(8,128)(2,1)S(1)}, u32[]{:S(2)}, u32[]{:S(2)}) collective-permute-start(bf16[3,256,256]{2,1,0:T(8,128)(2,1)S(1)} %get-tuple-element.36), channel_id=1, source_target_pairs={{0,16},{2,18},{4,20},{6,22},{8,24},{10,26},{12,28},{14,30},{16,0},... | collective-permute-start | bytes 1179656 | tf_op jit(solution)/shard_map/ppermute | solution.py:256
  110.2 5.0 %collective-permute-start.8 = (s32[2,8,2048]{2,1,0:T(8,128)S(1)}, s32[2,8,2048]{2,1,0:T(8,128)S(1)}, u32[]{:S(2)}, u32[]{:S(2)}) collective-permute-start(s32[2,8,2048]{2,1,0:T(8,128)S(1)} %reshape.42.ids_ref), channel_id=1, source_target_pairs={{0,1},{1,0},{2,3},{3,2},{4,5},{5,4},{6,7},{7,6},{8,9},{9,8},{10,11... | collective-permute-start | bytes 393224 | tf_op jit(solution)/shard_map/ppermute | solution.py:276
  125.3 0.8 copy-start
  127.4 10.7 %collective-permute-start.10 = (bf16[8,512,128]{2,1,0:T(8,128)(2,1)S(1)}, bf16[8,512,128]{2,1,0:T(8,128)(2,1)S(1)}, u32[]{:S(2)}, u32[]{:S(2)}) collective-permute-start(bf16[8,512,128]{2,1,0:T(8,128)(2,1)S(1)} %bitcast.94), channel_id=1, source_target_pairs={{0,2},{2,0},{4,6},{6,4},{8,10},{10,8},{12,14},{14,12},{16,18},{18,... | collective-permute-start | bytes 3145736 | tf_op jit(solution)/shard_map/ppermute | solution.py:278
  127.4 25.6 %collective-permute-start.11 = (bf16[8,512,128]{2,1,0:T(8,128)(2,1)S(1)}, bf16[8,512,128]{2,1,0:T(8,128)(2,1)S(1)}, u32[]{:S(2)}, u32[]{:S(2)}) collective-permute-start(bf16[8,512,128]{2,1,0:T(8,128)(2,1)S(1)} %bitcast.95), channel_id=1, source_target_pairs={{0,1},{1,0},{2,3},{3,2},{4,5},{5,4},{6,7},{7,6},{8,9},{9,8},{10,11... | collective-permute-start | bytes 3145736 | tf_op jit(solution)/shard_map/ppermute | solution.py:279
  128.9 20.8 %collective-permute-start.12 = (bf16[3,256,256]{2,1,0:T(8,128)(2,1)}, bf16[3,256,256]{2,1,0:T(8,128)(2,1)S(1)}, u32[]{:S(2)}, u32[]{:S(2)}) collective-permute-start(bf16[3,256,256]{2,1,0:T(8,128)(2,1)} %get-tuple-element.35), channel_id=1, source_target_pairs={{0,16},{2,18},{4,20},{6,22},{8,24},{10,26},{12,28},{14,30},{16,0},... | collective-permute-start | bytes 1179656 | tf_op jit(solution)/shard_map/ppermute | solution.py:256
  149.7 0.7 copy-start.2
  153.0 9.4 %collective-permute-start.13 = (bf16[8,512,128]{2,1,0:T(8,128)(2,1)S(1)}, bf16[8,512,128]{2,1,0:T(8,128)(2,1)S(1)}, u32[]{:S(2)}, u32[]{:S(2)}) collective-permute-start(bf16[8,512,128]{2,1,0:T(8,128)(2,1)S(1)} %collective-permute-done.11.attended_ref), channel_id=1, source_target_pairs={{0,2},{2,0},{4,6},{6,4},{8,10},{10,8},{12,14},{14,12},{16,18},{18,... | collective-permute-start | bytes 3145736 | tf_op jit(solution)/shard_map/ppermute | solution.py:286
  153.1 16.5 %collective-permute-start.14 = (bf16[2,256,256]{2,1,0:T(8,128)(2,1)S(1)}, bf16[2,256,256]{2,1,0:T(8,128)(2,1)S(1)}, u32[]{:S(2)}, u32[]{:S(2)}) collective-permute-start(bf16[2,256,256]{2,1,0:T(8,128)(2,1)S(1)} %slice.23), channel_id=1, source_target_pairs={{0,16},{2,18},{4,20},{6,22},{8,24},{10,26},{12,28},{14,30},{16,0},... | collective-permute-start | bytes 786440 | tf_op jit(solution)/shard_map/ppermute | solution.py:256
  162.4 7.2 %copy-start.1 = (bf16[3,256,256]{2,1,0:T(8,128)(2,1)S(1)}, bf16[3,256,256]{2,1,0:T(8,128)(2,1)}, u32[]{:S(2)}) copy-start(bf16[3,256,256]{2,1,0:T(8,128)(2,1)} %copy-done) | copy-start | bytes 1179652
  162.4 7.2 %copy-start.3 = (bf16[3,256,256]{2,1,0:T(8,128)(2,1)S(1)}, bf16[3,256,256]{2,1,0:T(8,128)(2,1)}, u32[]{:S(2)}) copy-start(bf16[3,256,256]{2,1,0:T(8,128)(2,1)} %copy-done.2) | copy-start | bytes 1179652

commit v12 on v10

--- a/solution.py
+++ b/solution.py
@@ -60,7 +60,7 @@
 
     sums_ref[...] = jnp.zeros_like(sums_ref)
 
-    @pl.loop(0, n_src, unroll=4)
+    @pl.loop(0, n_src, unroll=8)
     def _(src):
         coded = moved_ref[src, 3 * tok_rows :, :].astype(jnp.float32).astype(jnp.int32)
         parts = []
@@ -81,7 +81,7 @@
             top = jnp.maximum(top, scores[:, i * lanes : (i + 1) * lanes])
         return top
 
-    top = lax.fori_loop(0, n_src, score, jnp.full((C, lanes), -jnp.inf, jnp.float32), unroll=4)
+    top = lax.fori_loop(0, n_src, score, jnp.full((C, lanes), -jnp.inf, jnp.float32), unroll=8)
     top = jnp.broadcast_to(jnp.max(top, axis=1, keepdims=True), (C, tok_rows))
 
     acc_ref[...] = jnp.zeros_like(acc_ref)
@@ -94,7 +94,7 @@
         acc_ref[...] += jnp.dot(weights.astype(jnp.bfloat16), values, preferred_element_type=jnp.float32)
         return total
 
-    total = lax.fori_loop(0, n_src, weigh, jnp.zeros((C, lanes), jnp.float32), unroll=4)
+    total = lax.fori_loop(0, n_src, weigh, jnp.zeros((C, lanes), jnp.float32), unroll=8)
     out_ref[...] = (acc_ref[...] / jnp.sum(total, axis=1, keepdims=True)).astype(jnp.bfloat16)
 
 
@@ -119,7 +119,7 @@
     )(moved)
 
 
-def expand_kernel(ids_ref, attended_ref, *refs):
+def expand_kernel(offset, order, ids_ref, attended_ref, *refs):
     out_ref = refs[-1]
     heads, clusters, e_width = attended_ref.shape
     tok_tile = ids_ref.shape[2]
@@ -127,27 +127,27 @@
     one, zero = jnp.bfloat16(1.0), jnp.bfloat16(0.0)
     columns = ids_ref[0].T
     for h in range(heads):
-        ids = jnp.broadcast_to(columns[:, h : h + 1], (tok_tile, e_width)).astype(jnp.int16)
+        ids = jnp.broadcast_to(columns[:, offset + h : offset + h + 1], (tok_tile, e_width)).astype(jnp.int16)
         parts = [jnp.where(ids == labels + jnp.int16(at), one, zero) for at in range(0, clusters, e_width)]
         onehot = jnp.concatenate(parts, axis=1)
-        found = jnp.dot(onehot, attended_ref[h], preferred_element_type=jnp.float32)
+        found = jnp.dot(onehot, attended_ref[order[h]], preferred_element_type=jnp.float32)
         out_ref[h] = found.astype(jnp.bfloat16)
 
 
-def expand(ids, part, attended, store, piece, pieces, tok_tile):
-    _, heads, tokens = ids.shape
-    _, clusters, e_width = attended.shape
+def expand(ids, part, offset, attended, order, store, slot, slots, tok_tile):
+    _, rows, tokens = ids.shape
+    heads, clusters, e_width = attended.shape
     held = () if store is None else (store,)
     return pl.pallas_call(
-        expand_kernel,
-        out_shape=jax.ShapeDtypeStruct((pieces * heads, tokens, e_width), jnp.bfloat16),
+        lambda *refs: expand_kernel(offset, order, *refs),
+        out_shape=jax.ShapeDtypeStruct((slots, tokens, e_width), jnp.bfloat16),
         grid=(tokens // tok_tile,),
         in_specs=[
-            pl.BlockSpec((1, heads, tok_tile), lambda i: (part, 0, i)),
+            pl.BlockSpec((1, rows, tok_tile), lambda i: (part, 0, i)),
             pl.BlockSpec((heads, clusters, e_width), lambda i: (0, 0, 0)),
         ]
         + [pl.BlockSpec(memory_space=pl.ANY) for _ in held],
-        out_specs=pl.BlockSpec((heads, tok_tile, e_width), lambda i: (piece, i, 0)),
+        out_specs=pl.BlockSpec((heads, tok_tile, e_width), lambda i: (slot // heads, i, 0)),
         input_output_aliases={2: 0} if held else {},
         compiler_params=pltpu.CompilerParams(vmem_limit_bytes=50 * 2**20),
         cost_estimate=pl.CostEstimate(
@@ -170,7 +170,7 @@
         blocks = [(x, i) for x in weight_refs for i in range(x.shape[0])]
         for k, (weight_ref, i) in enumerate(blocks):
             chip = jnp.bitwise_xor(place, k)
-            slot = 2 * lax.rem(chip, each // 2) + jnp.bitwise_xor(half_at, lax.div(chip, each // 2))
+            slot = lax.rem(chip, each // 2) + each // 2 * jnp.bitwise_xor(half_at, lax.div(chip, each // 2))
             left = jnp.concatenate([features_ref[base + at * each + slot] for at in (core, 1 - core)], axis=1)
             right = weight_ref[i, : 2 * e_width, :]
             term = jnp.dot(left, right, preferred_element_type=jnp.float32)
@@ -206,8 +206,8 @@
 
 def by_slot(ids, half_at, core):
     sources, heads, tok_rows = ids.shape
-    ids = ids.reshape(sources, 2, heads // 4, 2, tok_rows).transpose(3, 2, 1, 0, 4)
-    ids = jnp.where(half_at == 0, ids, ids[:, :, ::-1])
+    ids = ids.reshape(sources, 2, heads // 4, 2, tok_rows).transpose(3, 1, 2, 0, 4)
+    ids = jnp.where(half_at == 0, ids, ids[:, ::-1])
     ids = jnp.where(core == 0, ids, ids[::-1])
     return ids.reshape(2, heads // 2, sources * tok_rows)
 
@@ -263,11 +263,12 @@
         got = lax.all_to_all(
             copies, "seq", split_axis=0, concat_axis=0, axis_index_groups=same_core, tiled=True
         )
-        return got.reshape((half,) + own.shape)
-
-    pair = jnp.stack([own, lax.ppermute(own, "seq", swap_halves)])
+        return got.reshape((-1,) + own.shape)
+
+    crossed = lax.ppermute(own, "seq", swap_halves)
+    pair = jnp.stack([own, crossed])
     far_pair = lax.ppermute(pair, "head", swap_heads)
-    first = spread(copied(pair))
+    first = spread(copied(own))
 
     coded = near[:, rows:].astype(jnp.int32)
     coded = coded[:, :head_count] * 16 + coded[:, head_count:]
@@ -276,21 +277,29 @@
     )
     slot_ids = by_slot(coded, half_at, core)
     far_ids = lax.ppermute(slot_ids, "head", swap_heads)
+    first, slot_ids, crossed = lax.optimization_barrier((first, slot_ids, crossed))
+    other_first = spread(copied(crossed))
+    second = lax.ppermute(first, "seq", swap_cores)
+
+    share = half // 2
+    slots = 4 * half
+    tok_tile = 2 * tok_rows
+    alone = list(range(share))
+    paired = [2 * (i % share) + i // share for i in range(half)]
+    features = expand(slot_ids, 0, 0, first, alone, None, 0, slots, tok_tile)
+    features = expand(slot_ids, 1, 0, second, alone, features, half, slots, tok_tile)
     far_copies = copied(far_pair)
-    first, slot_ids, far_ids, far_copies, far[1] = lax.optimization_barrier(
-        (first, slot_ids, far_ids, far_copies, far[1])
-    )
-    second = lax.ppermute(first, "seq", swap_cores)
+    features, other_first, far_ids, far_copies, far[1] = lax.optimization_barrier(
+        (features, other_first, far_ids, far_copies, far[1])
+    )
+    other_second = lax.ppermute(other_first, "seq", swap_cores)
     third = spread(far_copies)
-
-    pieces = 4
-    tok_tile = 2 * tok_rows
-    features = expand(slot_ids, 0, first, None, 0, pieces, tok_tile)
-    features = expand(slot_ids, 1, second, features, 1, pieces, tok_tile)
+    features = expand(slot_ids, 0, share, other_first, alone, features, share, slots, tok_tile)
+    features = expand(slot_ids, 1, share, other_second, alone, features, half + share, slots, tok_tile)
     features, third, far[2] = lax.optimization_barrier((features, third, far[2]))
     fourth = lax.ppermute(third, "seq", swap_cores)
-    features = expand(far_ids, 0, third, features, 2, pieces, tok_tile)
-    features = expand(far_ids, 1, fourth, features, 3, pieces, tok_tile)
+    features = expand(far_ids, 0, 0, third, paired, features, 2 * half, slots, tok_tile)
+    features = expand(far_ids, 1, 0, fourth, paired, features, 3 * half, slots, tok_tile)
     places = jnp.stack([head_at, core, half_at, place]).astype(jnp.int32)
     near_out = project(places, features, near, far, tok_tile)
     mixed = lax.all_to_all(

time: 198 us -> 203 us (1.025)
  starting transfers between devices: 36.1 us -> 40.3 us
  Pallas kernels: 45.4 us -> 49 us
  waiting for transfers between devices: 82.9 us -> 79.5 us
    ppermute x1, waiting for transfers between devices: 7.78 us -> 0.01 us  [by_head(): far_ids = lax.ppermute(slot_ids, 'head', swap_heads)]
    ppermute x1 -> x2, waiting for transfers between devices: 6.41 us -> 0.01 us  [the longest x1 0.01 us: by_head(): crossed = lax.ppermute(own, 'seq', swap_halves)]
    ppermute x4, waiting for transfers between devices: 6.81 us -> 12.8 us  [by_head(): lax.ppermute(near[a:b, :rows], 'seq', swap_halves)]
    all_to_all x2 -> x3, waiting for transfers between devices: 3.55 us -> 8.4 us  [spread(): lax.all_to_all(copies, 'seq', split_axis=0, concat_axis=0, axis_index_gro...]
    pallas_call x4 -> x6, Pallas kernels: 28.4 us -> 33 us  [expand(): pl.pallas_call(lambda *refs: expand_kernel(offset, order, *refs), out_sha...]
    all_to_all x2 -> x3, starting transfers between devices: 8.09 us -> 12.2 us  [spread(): lax.all_to_all(copies, 'seq', split_axis=0, concat_axis=0, axis_index_gro...]
  transfers between devices with their start and end apart: 19 -> 21, of which waited for: 11 -> 9; matrix products, arithmetic and copies ran while one was open for 2% -> 3% of each run, Pallas kernels for 18% -> 20%
where the time goes in v12:
time: 203 us
  waiting for transfers between devices  79.5 us (39%)
  Pallas kernels  49 us (24%)
  starting transfers between devices  40.3 us (20%)
  blocking collectives  17.5 us (9%)
  local copies, waits for them, and re-layouts  11.9 us (6%)
  other arithmetic  4 us (2%)
    ppermute x7, waiting for transfers between devices, by_head(): lax.ppermute(block, 'seq', [(i, i ^ k) for i in range(n_seq)])  58.3 us
    pallas_call x6, Pallas kernels, expand(): pl.pallas_call(lambda *refs: expand_kernel(offset, order, *refs), out_sha...  33 us
    all_to_all x1, blocking collectives, by_head(): lax.all_to_all(near_out.reshape(half, tok_rows, cols_each), 'seq', split_...  17.5 us
    ppermute x4, waiting for transfers between devices, by_head(): lax.ppermute(near[a:b, :rows], 'seq', swap_halves)  12.8 us
    all_to_all x3, starting transfers between devices, spread(): lax.all_to_all(copies, 'seq', split_axis=0, concat_axis=0, axis_index_gro...  12.2 us
    ppermute x4, starting transfers between devices, by_head(): lax.ppermute(near[a:b, :rows], 'seq', swap_halves)  11.7 us
    pallas_call x1, Pallas kernels, project(): pl.pallas_call(project_kernel, out_shape=jax.ShapeDtypeStruct((tokens, co...  8.98 us
    all_to_all x3, waiting for transfers between devices, spread(): lax.all_to_all(copies, 'seq', split_axis=0, concat_axis=0, axis_index_gro...  8.4 us
  transfers between devices with their start and end apart: 21, of which 9 were waited for; matrix products, arithmetic and copies ran while one was open for 3% of the time, Pallas kernels for 20%

profile of v12, /device:TPU:0, one launch (start us, length us, event | category | flops | bytes accessed | tf_op | source)
XLA Modules:
  0.0 202.8 jit_solution(11916800381257101835)
XLA Ops:
  0.0 0.9 fusion.6
  0.9 1.5 copy.46
  2.4 0.5 copy_bitcast_fusion
  3.0 1.8 pad_maximum_fusion
  4.8 7.6 %all-to-all-start = ((bf16[16,784,128]{2,1,0:T(8,128)(2,1)}), bf16[16,784,128]{2,1,0:T(8,128)(2,1)}, u32[]{:S(2)}, u32[]{:S(2)}) async-start(bf16[16,784,128]{2,1,0:T(8,128)(2,1)} %pad_maximum_fusion), calls=%async_computation | async-start | bytes 6422528 | tf_op jit(solution)/shard_map/all_to_all | solution.py:242
  12.5 0.3 copy.34
  12.8 2.2 %constant_dynamic-slice_fusion = (bf16[256,1,256]{2,1,0:T(2,128)(2,1)S(1)}, bf16[256,1,256]{2,1,0:T(2,128)(2,1)S(1)}, bf16[256,1,256]{2,1,0:T(2,128)(2,1)S(1)}, ...) fusion(bf16[256,8,256]{2,1,0:T(8,128)(2,1)S(1)} %bitcast.98, ...), kind=kLoop, calls=%fused_computation.68 | loop fusion | bytes 2097184 | tf_op jit(solution)/shard_map/dynamic-slice.7
  15.1 0.1 pad_maximum_fusion.1
  15.2 0.4 collective-permute-start
  15.6 2.6 %collective-permute-start.5 = (bf16[288,256]{1,0:T(8,128)(2,1)S(1)}, bf16[288,256]{1,0:T(8,128)(2,1)S(1)}, u32[]{:S(2)}, u32[]{:S(2)}) collective-permute-start(bf16[288,256]{1,0:T(8,128)(2,1)S(1)} %pad_maximum_fusion.2), channel_id=1, source_target_pairs={{0,12},{2,14},{4,8},{6,10},{8,4},{10,6},{12,0},{14,2},{16,28},{18,... | collective-permute-start | bytes 442376 | tf_op jit(solution)/shard_map/ppermute | solution.py:250
  18.3 0.6 collective-permute-start.1
  18.9 0.9 collective-permute-start.2
  19.7 0.6 collective-permute-start.3
  20.3 0.0 collective-permute-done
  20.3 1.6 collective-permute-start.4
  21.9 15.4 %collective-permute-done.1 = bf16[288,256]{1,0:T(8,128)(2,1)S(1)} collective-permute-done((bf16[288,256]{1,0:T(8,128)(2,1)S(1)}, bf16[288,256]{1,0:T(8,128)(2,1)S(1)}, u32[]{:S(2)}, u32[]{:S(2)}) %collective-permute-start.1) | collective-permute-done | bytes 147488 | tf_op jit(solution)/shard_map/ppermute | solution.py:250
  37.3 0.0 collective-permute-start.6
  37.3 7.4 %collective-permute-done.2 = bf16[288,256]{1,0:T(8,128)(2,1)S(1)} collective-permute-done((bf16[288,256]{1,0:T(8,128)(2,1)S(1)}, bf16[288,256]{1,0:T(8,128)(2,1)S(1)}, u32[]{:S(2)}, u32[]{:S(2)}) %collective-permute-start.2) | collective-permute-done | bytes 147488 | tf_op jit(solution)/shard_map/ppermute | solution.py:250
  44.8 27.9 %collective-permute-done.3 = bf16[288,256]{1,0:T(8,128)(2,1)S(1)} collective-permute-done((bf16[288,256]{1,0:T(8,128)(2,1)S(1)}, bf16[288,256]{1,0:T(8,128)(2,1)S(1)}, u32[]{:S(2)}, u32[]{:S(2)}) %collective-permute-start.3) | collective-permute-done | bytes 147488 | tf_op jit(solution)/shard_map/ppermute | solution.py:250
  72.7 3.1 %collective-permute-done.4 = bf16[288,256]{1,0:T(8,128)(2,1)S(1)} collective-permute-done((bf16[288,256]{1,0:T(8,128)(2,1)S(1)}, bf16[288,256]{1,0:T(8,128)(2,1)S(1)}, u32[]{:S(2)}, u32[]{:S(2)}) %collective-permute-start.4) | collective-permute-done | bytes 147488 | tf_op jit(solution)/shard_map/ppermute | solution.py:250
  75.9 0.0 collective-permute-done.5
  75.9 4.5 %collective-permute-done.6 = bf16[288,256]{1,0:T(8,128)(2,1)S(1)} collective-permute-done((bf16[288,256]{1,0:T(8,128)(2,1)S(1)}, bf16[288,256]{1,0:T(8,128)(2,1)S(1)}, u32[]{:S(2)}, u32[]{:S(2)}) %collective-permute-start.6) | collective-permute-done | bytes 147488 | tf_op jit(solution)/shard_map/ppermute | solution.py:250
  80.4 7.5 %collective-permute-start.7 = (bf16[1,256,256]{2,1,0:T(8,128)(2,1)S(1)}, bf16[1,256,256]{2,1,0:T(8,128)(2,1)S(1)}, u32[]{:S(2)}, u32[]{:S(2)}) collective-permute-start(bf16[1,256,256]{2,1,0:T(8,128)(2,1)S(1)} %slice.21), channel_id=1, source_target_pairs={{0,16},{2,18},{4,20},{6,22},{8,24},{10,26},{12,28},{14,30},{16,0},... | collective-permute-start | bytes 393224 | tf_op jit(solution)/shard_map/ppermute | solution.py:254
  87.8 7.0 %attend.1 = bf16[512,128]{1,0:T(8,128)(2,1)S(1)} custom-call(bf16[16,784,128]{2,1,0:T(8,128)(2,1)} %all-to-all-done.refs_0_), custom_call_target="tpu_custom_call" | custom-call | flops 2147483648 | bytes 3211264 | tf_op jit(solution)/shard_map/attend/pallas_call | solution.py:104
  95.0 0.1 collective-permute-start.8
  95.1 0.9 broadcast_in_dim.8
  96.0 5.0 %all-to-all-start.1 = ((bf16[4,512,128]{2,1,0:T(8,128)(2,1)}), bf16[4,512,128]{2,1,0:T(8,128)(2,1)S(1)}, u32[]{:S(2)}, u32[]{:S(2)}) async-start(bf16[4,512,128]{2,1,0:T(8,128)(2,1)} %broadcast_in_dim.8), calls=%async_computation.1 | async-start | bytes 1048576 | tf_op jit(solution)/shard_map/all_to_all | solution.py:263
  101.0 0.1 reshape.42
  101.2 0.4 rev.7
  101.6 0.1 broadcast_select_fusion
  101.6 0.1 copy.22
  101.8 0.0 collective-permute-done.8
  101.8 7.1 %all-to-all-done.1.refs_1_ = bf16[4,512,128]{2,1,0:T(8,128)(2,1)S(1)} async-done(((bf16[4,512,128]{2,1,0:T(8,128)(2,1)}), bf16[4,512,128]{2,1,0:T(8,128)(2,1)S(1)}, u32[]{:S(2)}, u32[]{:S(2)}) %all-to-all-start.1) | async-done | bytes 524320 | tf_op jit(solution)/shard_map/all_to_all | solution.py:263
  108.9 0.9 broadcast_in_dim.9
  109.8 3.5 %all-to-all-start.2 = ((bf16[4,512,128]{2,1,0:T(8,128)(2,1)}), bf16[4,512,128]{2,1,0:T(8,128)(2,1)S(1)}, u32[]{:S(2)}, u32[]{:S(2)}) async-start(bf16[4,512,128]{2,1,0:T(8,128)(2,1)} %broadcast_in_dim.9), calls=%async_computation.2 | async-start | bytes 1048576 | tf_op jit(solution)/shard_map/all_to_all | solution.py:263
  113.3 1.6 collective-permute-start.10
  114.8 0.0 collective-permute-start.9
  114.8 0.7 fusion.11
  115.6 0.9 collective-permute-start.12
  116.5 0.9 pad_maximum_fusion.17
  117.4 0.6 collective-permute-start.11
  118.0 4.7 %expand.6.refs_2_ = bf16[32,2048,128]{2,1,0:T(8,128)(2,1)} custom-call(s32[2,8,2048]{2,1,0:T(8,128)S(1)} %reshape.43.refs_0_, bf16[4,512,128]{2,1,0:T(8,128)(2,1)S(1)} %all-to-all-done.1.refs_1_), custom_call_target="tpu_custom_call" | custom-call | flops 2147483648 | bytes 2621440 | tf_op jit(solution)/shard_map/expand/pallas_call | solution.py:141
  122.7 0.0 collective-permute-done.9.refs_1_
  122.7 4.7 %expand.7.refs_2_ = bf16[32,2048,128]{2,1,0:T(8,128)(2,1)} custom-call(s32[2,8,2048]{2,1,0:T(8,128)S(1)} %reshape.43.refs_0_, bf16[4,512,128]{2,1,0:T(8,128)(2,1)S(1)} %collective-permute-done.9.refs_1_, bf16[32,2048,128]{2,1,0:T(8,128)(2,1)} %expand.6.refs_2_), custom_call_target="tpu_custom_call", output_to_operand_aliasing={{}: (2, {})} | custom-call | flops 2147483648 | bytes 2621440 | tf_op jit(solution)/shard_map/expand/pallas_call | solution.py:141
  127.4 3.5 %collective-permute-done.12.refs_1_ = bf16[2,256,256]{2,1,0:T(8,128)(2,1)S(1)} collective-permute-done((bf16[2,256,256]{2,1,0:T(8,128)(2,1)S(1)}, bf16[2,256,256]{2,1,0:T(8,128)(2,1)S(1)}, u32[]{:S(2)}, u32[]{:S(2)}) %collective-permute-start.12) | collective-permute-done | bytes 262176 | tf_op jit(solution)/shard_map/ppermute | solution.py:257
  130.9 0.0 collective-permute-done.11
  130.9 0.0 all-to-all-done.2.refs_1_
  130.9 2.1 %broadcast_in_dim.11 = bf16[4,2,512,128]{3,2,1,0:T(8,128)(2,1)} broadcast(bf16[2,512,128]{2,1,0:T(8,128)(2,1)} %collective-permute-done.11), dimensions={1,2,3} | broadcast | bytes 1310720 | tf_op jit(solution)/shard_map/broadcast_in_dim | solution.py:260
  133.0 3.7 %all-to-all-start.3 = ((bf16[4,2,512,128]{3,2,1,0:T(8,128)(2,1)}), bf16[4,2,512,128]{3,2,1,0:T(8,128)(2,1)S(1)}, u32[]{:S(2)}, u32[]{:S(2)}) async-start(bf16[4,2,512,128]{3,2,1,0:T(8,128)(2,1)} %broadcast_in_dim.11), calls=%async_computation.3 | async-start | bytes 2097152 | tf_op jit(solution)/shard_map/all_to_all | solution.py:263
  136.7 0.1 collective-permute-start.13
  136.8 1.2 collective-permute-start.14
  138.1 4.7 %expand.8.refs_2_ = bf16[32,2048,128]{2,1,0:T(8,128)(2,1)} custom-call(s32[2,8,2048]{2,1,0:T(8,128)S(1)} %reshape.43.refs_0_, bf16[4,512,128]{2,1,0:T(8,128)(2,1)S(1)} %all-to-all-done.2.refs_1_, bf16[32,2048,128]{2,1,0:T(8,128)(2,1)} %expand.7.refs_2_), custom_call_target="tpu_custom_call", output_to_operand_aliasing={{}: (2, {})} | custom-call | flops 2147483648 | bytes 2621440 | tf_op jit(solution)/shard_map/expand/pallas_call | solution.py:141
  142.7 4.7 %expand.9.refs_2_ = bf16[32,2048,128]{2,1,0:T(8,128)(2,1)} custom-call(s32[2,8,2048]{2,1,0:T(8,128)S(1)} %reshape.43.refs_0_, bf16[4,512,128]{2,1,0:T(8,128)(2,1)S(1)} %collective-permute-done.13.refs_1_, bf16[32,2048,128]{2,1,0:T(8,128)(2,1)} %expand.8.refs_2_), custom_call_target="tpu_custom_call", output_to_operand_aliasing={{}: (2, {})} | custom-call | flops 2147483648 | bytes 2621440 | tf_op jit(solution)/shard_map/expand/pallas_call | solution.py:141
  147.5 9.3 %collective-permute-done.14.refs_2_ = bf16[3,256,256]{2,1,0:T(8,128)(2,1)S(1)} collective-permute-done((bf16[3,256,256]{2,1,0:T(8,128)(2,1)S(1)}, bf16[3,256,256]{2,1,0:T(8,128)(2,1)S(1)}, u32[]{:S(2)}, u32[]{:S(2)}) %collective-permute-start.14) | collective-permute-done | bytes 393248 | tf_op jit(solution)/shard_map/ppermute | solution.py:257
  156.8 0.7 copy-done
  157.5 1.2 all-to-all-done.3
  158.8 0.1 pad_add_fusion.places_ref
  158.8 2.1 %collective-permute-start.16 = (bf16[2,256,256]{2,1,0:T(8,128)(2,1)}, bf16[2,256,256]{2,1,0:T(8,128)(2,1)S(1)}, u32[]{:S(2)}, u32[]{:S(2)}) collective-permute-start(bf16[2,256,256]{2,1,0:T(8,128)(2,1)} %get-tuple-element.45), channel_id=1, source_target_pairs={{0,16},{2,18},{4,20},{6,22},{8,24},{10,26},{12,28},{14,30},{16,0},... | collective-permute-start | bytes 786440 | tf_op jit(solution)/shard_map/ppermute | solution.py:257
  161.0 7.1 %expand.10.refs_2_ = bf16[32,2048,128]{2,1,0:T(8,128)(2,1)} custom-call(s32[2,8,2048]{2,1,0:T(8,128)S(1)} %collective-permute-done.10.refs_0_, bf16[8,512,128]{2,1,0:T(8,128)(2,1)S(1)} %bitcast.95, bf16[32,2048,128]{2,1,0:T(8,128)(2,1)} %expand.9.refs_2_), custom_call_target="tpu_custom_call", output_to_operand_aliasing={{}: (2, {})} | custom-call | flops 4294967296 | bytes 5242880 | tf_op jit(solution)/shard_map/expand/pallas_call | solution.py:141
  168.1 0.0 collective-permute-done.15.refs_1_
  168.1 7.1 %expand.11.features_ref = bf16[32,2048,128]{2,1,0:T(8,128)(2,1)} custom-call(s32[2,8,2048]{2,1,0:T(8,128)S(1)} %collective-permute-done.10.refs_0_, bf16[8,512,128]{2,1,0:T(8,128)(2,1)S(1)} %collective-permute-done.15.refs_1_, bf16[32,2048,128]{2,1,0:T(8,128)(2,1)} %expand.10.refs_2_), custom_call_target="tpu_custom_call", output_to_operand_aliasing={{}: (2, {})} | custom-call | flops 4294967296 | bytes 5242880 | tf_op jit(solution)/shard_map/expand/pallas_call | solution.py:141
  175.2 9.0 %project.1 = bf16[2048,256]{1,0:T(8,128)(2,1)S(1)} custom-call(s32[4]{0:T(128)S(1)} %pad_add_fusion.places_ref, bf16[32,2048,128]{2,1,0:T(8,128)(2,1)} %expand.11.features_ref, bf16[8,288,256]{2,1,0:T(8,128)(2,1)S(1)} %bitcast_dynamic-update-slice_fusion.near_ref, bf16[1,256,256]{2,1,0:T(8,128)(2,1)S(1)} %collective-permute-done.7.refs_0_, ...), custom_call_target="tpu_custom_call" | custom-call | flops 4294967296 | bytes 19922944 | tf_op jit(solution)/shard_map/project/pallas_call | solution.py:184
  184.1 17.5 %all_to_all.25 = bf16[8,256,256]{2,1,0:T(8,128)(2,1)S(1)} all-to-all(bf16[8,256,256]{2,1,0:T(8,128)(2,1)S(1)} %bitcast.96), channel_id=1, replica_groups={{0,2,4,6,8,10,12,14},{16,18,20,22,24,26,28,30},{1,3,5,7,9,11,13,15},{17..., dimensions={0} | all-to-all | bytes 2097152 | tf_op jit(solution)/shard_map/all_to_all | solution.py:305
  201.7 1.1 copy.32
  (54 shorter events, 0.5 us)
Async XLA Ops:
  0.0 2.4 %copy-start.6 = (bf16[256,16,128]{2,1,0:T(8,128)(2,1)S(1)}, bf16[256,16,128]{2,1,0:T(8,128)(2,1)}, u32[]{:S(2)}) copy-start(bf16[256,16,128]{2,1,0:T(8,128)(2,1)} %param.6) | copy-start | bytes 3145732
  0.0 2.4 %copy-start.5 = (bf16[256,16,128]{2,1,0:T(8,128)(2,1)S(1)}, bf16[256,16,128]{2,1,0:T(8,128)(2,1)}, u32[]{:S(2)}) copy-start(bf16[256,16,128]{2,1,0:T(8,128)(2,1)} %param.7) | copy-start | bytes 3145732
  4.8 7.6 %copy-start.4 = (bf16[256,2048]{1,0:T(8,128)(2,1)S(1)}, bf16[256,2048]{1,0:T(8,128)(2,1)}, u32[]{:S(2)}) copy-start(bf16[256,2048]{1,0:T(8,128)(2,1)} %param.9) | copy-start | bytes 3145732
  4.8 75.5 %all-to-all-start = ((bf16[16,784,128]{2,1,0:T(8,128)(2,1)}), bf16[16,784,128]{2,1,0:T(8,128)(2,1)}, u32[]{:S(2)}, u32[]{:S(2)}) async-start(bf16[16,784,128]{2,1,0:T(8,128)(2,1)} %pad_maximum_fusion), calls=%async_computation | async-start | bytes 6422528 | tf_op jit(solution)/shard_map/all_to_all | solution.py:242
  15.2 5.1 %collective-permute-start = (bf16[288,256]{1,0:T(8,128)(2,1)S(1)}, bf16[288,256]{1,0:T(8,128)(2,1)S(1)}, u32[]{:S(2)}, u32[]{:S(2)}) collective-permute-start(bf16[288,256]{1,0:T(8,128)(2,1)S(1)} %get-tuple-element.56), channel_id=1, source_target_pairs={{0,2},{2,0},{4,6},{6,4},{8,10},{10,8},{12,14},{14,12},{16,18},{18,... | collective-permute-start | bytes 442376 | tf_op jit(solution)/shard_map/ppermute | solution.py:250
  15.6 60.2 %collective-permute-start.5 = (bf16[288,256]{1,0:T(8,128)(2,1)S(1)}, bf16[288,256]{1,0:T(8,128)(2,1)S(1)}, u32[]{:S(2)}, u32[]{:S(2)}) collective-permute-start(bf16[288,256]{1,0:T(8,128)(2,1)S(1)} %pad_maximum_fusion.2), channel_id=1, source_target_pairs={{0,12},{2,14},{4,8},{6,10},{8,4},{10,6},{12,0},{14,2},{16,28},{18,... | collective-permute-start | bytes 442376 | tf_op jit(solution)/shard_map/ppermute | solution.py:250
  18.3 19.0 %collective-permute-start.1 = (bf16[288,256]{1,0:T(8,128)(2,1)S(1)}, bf16[288,256]{1,0:T(8,128)(2,1)S(1)}, u32[]{:S(2)}, u32[]{:S(2)}) collective-permute-start(bf16[288,256]{1,0:T(8,128)(2,1)S(1)} %get-tuple-element.57), channel_id=1, source_target_pairs={{0,4},{2,6},{4,0},{6,2},{8,12},{10,14},{12,8},{14,10},{16,20},{18,... | collective-permute-start | bytes 442376 | tf_op jit(solution)/shard_map/ppermute | solution.py:250
  18.9 25.9 %collective-permute-start.2 = (bf16[288,256]{1,0:T(8,128)(2,1)S(1)}, bf16[288,256]{1,0:T(8,128)(2,1)S(1)}, u32[]{:S(2)}, u32[]{:S(2)}) collective-permute-start(bf16[288,256]{1,0:T(8,128)(2,1)S(1)} %get-tuple-element.58), channel_id=1, source_target_pairs={{0,6},{2,4},{4,2},{6,0},{8,14},{10,12},{12,10},{14,8},{16,22},{18,... | collective-permute-start | bytes 442376 | tf_op jit(solution)/shard_map/ppermute | solution.py:250
  19.7 53.0 %collective-permute-start.3 = (bf16[288,256]{1,0:T(8,128)(2,1)S(1)}, bf16[288,256]{1,0:T(8,128)(2,1)S(1)}, u32[]{:S(2)}, u32[]{:S(2)}) collective-permute-start(bf16[288,256]{1,0:T(8,128)(2,1)S(1)} %get-tuple-element.59), channel_id=1, source_target_pairs={{0,8},{2,10},{4,12},{6,14},{8,0},{10,2},{12,4},{14,6},{16,24},{18,... | collective-permute-start | bytes 442376 | tf_op jit(solution)/shard_map/ppermute | solution.py:250
  20.3 55.5 %collective-permute-start.4 = (bf16[288,256]{1,0:T(8,128)(2,1)S(1)}, bf16[288,256]{1,0:T(8,128)(2,1)S(1)}, u32[]{:S(2)}, u32[]{:S(2)}) collective-permute-start(bf16[288,256]{1,0:T(8,128)(2,1)S(1)} %get-tuple-element.60), channel_id=1, source_target_pairs={{0,10},{2,8},{4,14},{6,12},{8,2},{10,0},{12,6},{14,4},{16,26},{18,... | collective-permute-start | bytes 442376 | tf_op jit(solution)/shard_map/ppermute | solution.py:250
  37.3 43.0 %collective-permute-start.6 = (bf16[288,256]{1,0:T(8,128)(2,1)S(1)}, bf16[288,256]{1,0:T(8,128)(2,1)S(1)}, u32[]{:S(2)}, u32[]{:S(2)}) collective-permute-start(bf16[288,256]{1,0:T(8,128)(2,1)S(1)} %get-tuple-element.55), channel_id=1, source_target_pairs={{0,14},{2,12},{4,10},{6,8},{8,6},{10,4},{12,2},{14,0},{16,30},{18,... | collective-permute-start | bytes 442376 | tf_op jit(solution)/shard_map/ppermute | solution.py:250
  80.4 14.5 %collective-permute-start.7 = (bf16[1,256,256]{2,1,0:T(8,128)(2,1)S(1)}, bf16[1,256,256]{2,1,0:T(8,128)(2,1)S(1)}, u32[]{:S(2)}, u32[]{:S(2)}) collective-permute-start(bf16[1,256,256]{2,1,0:T(8,128)(2,1)S(1)} %slice.21), channel_id=1, source_target_pairs={{0,16},{2,18},{4,20},{6,22},{8,24},{10,26},{12,28},{14,30},{16,0},... | collective-permute-start | bytes 393224 | tf_op jit(solution)/shard_map/ppermute | solution.py:254
  95.0 6.7 %collective-permute-start.8 = (bf16[512,128]{1,0:T(8,128)(2,1)S(1)}, bf16[512,128]{1,0:T(8,128)(2,1)S(1)}, u32[]{:S(2)}, u32[]{:S(2)}) collective-permute-start(bf16[512,128]{1,0:T(8,128)(2,1)S(1)} %attend.1), channel_id=1, source_target_pairs={{0,16},{2,18},{4,20},{6,22},{8,24},{10,26},{12,28},{14,30},{16,0},... | collective-permute-start | bytes 393224 | tf_op jit(solution)/shard_map/ppermute | solution.py:268
  96.0 12.9 %all-to-all-start.1 = ((bf16[4,512,128]{2,1,0:T(8,128)(2,1)}), bf16[4,512,128]{2,1,0:T(8,128)(2,1)S(1)}, u32[]{:S(2)}, u32[]{:S(2)}) async-start(bf16[4,512,128]{2,1,0:T(8,128)(2,1)} %broadcast_in_dim.8), calls=%async_computation.1 | async-start | bytes 1048576 | tf_op jit(solution)/shard_map/all_to_all | solution.py:263
  101.8 11.5 %copy-start.7 = (bf16[512,128]{1,0:T(8,128)(2,1)}, bf16[512,128]{1,0:T(8,128)(2,1)S(1)}, u32[]{:S(2)}) copy-start(bf16[512,128]{1,0:T(8,128)(2,1)S(1)} %collective-permute-done.8) | copy-start | bytes 393220
  109.8 21.1 %all-to-all-start.2 = ((bf16[4,512,128]{2,1,0:T(8,128)(2,1)}), bf16[4,512,128]{2,1,0:T(8,128)(2,1)S(1)}, u32[]{:S(2)}, u32[]{:S(2)}) async-start(bf16[4,512,128]{2,1,0:T(8,128)(2,1)} %broadcast_in_dim.9), calls=%async_computation.2 | async-start | bytes 1048576 | tf_op jit(solution)/shard_map/all_to_all | solution.py:263
  113.3 14.1 %collective-permute-start.10 = (s32[2,8,2048]{2,1,0:T(8,128)S(1)}, s32[2,8,2048]{2,1,0:T(8,128)S(1)}, u32[]{:S(2)}, u32[]{:S(2)}) collective-permute-start(s32[2,8,2048]{2,1,0:T(8,128)S(1)} %reshape.43.refs_0_), channel_id=1, source_target_pairs={{0,1},{1,0},{2,3},{3,2},{4,5},{5,4},{6,7},{7,6},{8,9},{9,8},{10,11... | collective-permute-start | bytes 393224 | tf_op jit(solution)/shard_map/ppermute | solution.py:279
  114.8 7.8 %collective-permute-start.9 = (bf16[4,512,128]{2,1,0:T(8,128)(2,1)S(1)}, bf16[4,512,128]{2,1,0:T(8,128)(2,1)S(1)}, u32[]{:S(2)}, u32[]{:S(2)}) collective-permute-start(bf16[4,512,128]{2,1,0:T(8,128)(2,1)S(1)} %all-to-all-done.1.refs_1_), channel_id=1, source_target_pairs={{0,2},{2,0},{4,6},{6,4},{8,10},{10,8},{12,14},{14,12},{16,18},{18,... | collective-permute-start | bytes 1572872 | tf_op jit(solution)/shard_map/ppermute | solution.py:282
  115.6 15.3 %collective-permute-start.12 = (bf16[2,256,256]{2,1,0:T(8,128)(2,1)S(1)}, bf16[2,256,256]{2,1,0:T(8,128)(2,1)S(1)}, u32[]{:S(2)}, u32[]{:S(2)}) collective-permute-start(bf16[2,256,256]{2,1,0:T(8,128)(2,1)S(1)} %get-tuple-element.46), channel_id=1, source_target_pairs={{0,16},{2,18},{4,20},{6,22},{8,24},{10,26},{12,28},{14,30},{16,0},... | collective-permute-start | bytes 786440 | tf_op jit(solution)/shard_map/ppermute | solution.py:257
  117.4 13.5 %collective-permute-start.11 = (bf16[2,512,128]{2,1,0:T(8,128)(2,1)S(1)}, bf16[2,512,128]{2,1,0:T(8,128)(2,1)}, u32[]{:S(2)}, u32[]{:S(2)}) collective-permute-start(bf16[2,512,128]{2,1,0:T(8,128)(2,1)S(1)} %pad_maximum_fusion.17), channel_id=1, source_target_pairs={{0,1},{1,0},{2,3},{3,2},{4,5},{5,4},{6,7},{7,6},{8,9},{9,8},{10,11... | collective-permute-start | bytes 786440 | tf_op jit(solution)/shard_map/ppermute | solution.py:270
  130.9 2.2 %copy-start.2 = (bf16[2,256,256]{2,1,0:T(8,128)(2,1)}, bf16[2,256,256]{2,1,0:T(8,128)(2,1)S(1)}, u32[]{:S(2)}) copy-start(bf16[2,256,256]{2,1,0:T(8,128)(2,1)S(1)} %collective-permute-done.12.refs_1_) | copy-start | bytes 786436
  133.0 25.7 %all-to-all-start.3 = ((bf16[4,2,512,128]{3,2,1,0:T(8,128)(2,1)}), bf16[4,2,512,128]{3,2,1,0:T(8,128)(2,1)S(1)}, u32[]{:S(2)}, u32[]{:S(2)}) async-start(bf16[4,2,512,128]{3,2,1,0:T(8,128)(2,1)} %broadcast_in_dim.11), calls=%async_computation.3 | async-start | bytes 2097152 | tf_op jit(solution)/shard_map/all_to_all | solution.py:263
  136.7 6.0 %collective-permute-start.13 = (bf16[4,512,128]{2,1,0:T(8,128)(2,1)S(1)}, bf16[4,512,128]{2,1,0:T(8,128)(2,1)S(1)}, u32[]{:S(2)}, u32[]{:S(2)}) collective-permute-start(bf16[4,512,128]{2,1,0:T(8,128)(2,1)S(1)} %all-to-all-done.2.refs_1_), channel_id=1, source_target_pairs={{0,2},{2,0},{4,6},{6,4},{8,10},{10,8},{12,14},{14,12},{16,18},{18,... | collective-permute-start | bytes 1572872 | tf_op jit(solution)/shard_map/ppermute | solution.py:295
  136.8 19.9 %collective-permute-start.14 = (bf16[3,256,256]{2,1,0:T(8,128)(2,1)S(1)}, bf16[3,256,256]{2,1,0:T(8,128)(2,1)S(1)}, u32[]{:S(2)}, u32[]{:S(2)}) collective-permute-start(bf16[3,256,256]{2,1,0:T(8,128)(2,1)S(1)} %slice.26), channel_id=1, source_target_pairs={{0,16},{2,18},{4,20},{6,22},{8,24},{10,26},{12,28},{14,30},{16,0},... | collective-permute-start | bytes 1179656 | tf_op jit(solution)/shard_map/ppermute | solution.py:257
  156.8 0.7 copy-start
  158.8 9.3 %collective-permute-start.15 = (bf16[8,512,128]{2,1,0:T(8,128)(2,1)S(1)}, bf16[8,512,128]{2,1,0:T(8,128)(2,1)S(1)}, u32[]{:S(2)}, u32[]{:S(2)}) collective-permute-start(bf16[8,512,128]{2,1,0:T(8,128)(2,1)S(1)} %bitcast.94), channel_id=1, source_target_pairs={{0,2},{2,0},{4,6},{6,4},{8,10},{10,8},{12,14},{14,12},{16,18},{18,... | collective-permute-start | bytes 3145736 | tf_op jit(solution)/shard_map/ppermute | solution.py:300
  158.8 16.3 %collective-permute-start.16 = (bf16[2,256,256]{2,1,0:T(8,128)(2,1)}, bf16[2,256,256]{2,1,0:T(8,128)(2,1)S(1)}, u32[]{:S(2)}, u32[]{:S(2)}) collective-permute-start(bf16[2,256,256]{2,1,0:T(8,128)(2,1)} %get-tuple-element.45), channel_id=1, source_target_pairs={{0,16},{2,18},{4,20},{6,22},{8,24},{10,26},{12,28},{14,30},{16,0},... | collective-permute-start | bytes 786440 | tf_op jit(solution)/shard_map/ppermute | solution.py:257
  168.1 7.1 %copy-start.1 = (bf16[3,256,256]{2,1,0:T(8,128)(2,1)S(1)}, bf16[3,256,256]{2,1,0:T(8,128)(2,1)}, u32[]{:S(2)}) copy-start(bf16[3,256,256]{2,1,0:T(8,128)(2,1)} %copy-done) | copy-start | bytes 1179652
  168.1 7.1 %copy-start.3 = (bf16[2,256,256]{2,1,0:T(8,128)(2,1)S(1)}, bf16[2,256,256]{2,1,0:T(8,128)(2,1)}, u32[]{:S(2)}) copy-start(bf16[2,256,256]{2,1,0:T(8,128)(2,1)} %copy-done.2) | copy-start | bytes 786436

commit v13 on v10

--- a/solution.py
+++ b/solution.py
@@ -60,7 +60,7 @@
 
     sums_ref[...] = jnp.zeros_like(sums_ref)
 
-    @pl.loop(0, n_src, unroll=4)
+    @pl.loop(0, n_src, unroll=8)
     def _(src):
         coded = moved_ref[src, 3 * tok_rows :, :].astype(jnp.float32).astype(jnp.int32)
         parts = []
@@ -81,7 +81,7 @@
             top = jnp.maximum(top, scores[:, i * lanes : (i + 1) * lanes])
         return top
 
-    top = lax.fori_loop(0, n_src, score, jnp.full((C, lanes), -jnp.inf, jnp.float32), unroll=4)
+    top = lax.fori_loop(0, n_src, score, jnp.full((C, lanes), -jnp.inf, jnp.float32), unroll=8)
     top = jnp.broadcast_to(jnp.max(top, axis=1, keepdims=True), (C, tok_rows))
 
     acc_ref[...] = jnp.zeros_like(acc_ref)
@@ -94,7 +94,7 @@
         acc_ref[...] += jnp.dot(weights.astype(jnp.bfloat16), values, preferred_element_type=jnp.float32)
         return total
 
-    total = lax.fori_loop(0, n_src, weigh, jnp.zeros((C, lanes), jnp.float32), unroll=4)
+    total = lax.fori_loop(0, n_src, weigh, jnp.zeros((C, lanes), jnp.float32), unroll=8)
     out_ref[...] = (acc_ref[...] / jnp.sum(total, axis=1, keepdims=True)).astype(jnp.bfloat16)
 
 
@@ -285,12 +285,12 @@
 
     pieces = 4
     tok_tile = 2 * tok_rows
-    features = expand(slot_ids, 0, first, None, 0, pieces, tok_tile)
-    features = expand(slot_ids, 1, second, features, 1, pieces, tok_tile)
+    features = expand(slot_ids, 0, first, None, 0, pieces, 2 * tok_tile)
+    features = expand(slot_ids, 1, second, features, 1, pieces, 2 * tok_tile)
     features, third, far[2] = lax.optimization_barrier((features, third, far[2]))
     fourth = lax.ppermute(third, "seq", swap_cores)
-    features = expand(far_ids, 0, third, features, 2, pieces, tok_tile)
-    features = expand(far_ids, 1, fourth, features, 3, pieces, tok_tile)
+    features = expand(far_ids, 0, third, features, 2, pieces, 2 * tok_tile)
+    features = expand(far_ids, 1, fourth, features, 3, pieces, 2 * tok_tile)
     places = jnp.stack([head_at, core, half_at, place]).astype(jnp.int32)
     near_out = project(places, features, near, far, tok_tile)
     mixed = lax.all_to_all(

time: 198 us -> 197 us (level)
  Pallas kernels: 45.4 us -> 43.3 us
where the time goes in v13:
time: 197 us; the launch traced here: 196 us
  waiting for transfers between devices  83.5 us (42%)
  Pallas kernels  43.3 us (22%)
  starting transfers between devices  36.1 us (18%)
  blocking collectives  18.6 us (9%)
  local copies, waits for them, and re-layouts  11 us (6%)
  other arithmetic  3.09 us (2%)
    ppermute x7, waiting for transfers between devices, by_head(): lax.ppermute(block, 'seq', [(i, i ^ k) for i in range(n_seq)])  58.3 us
    pallas_call x4, Pallas kernels, expand(): pl.pallas_call(expand_kernel, out_shape=jax.ShapeDtypeStruct((pieces * he...  27.3 us
    all_to_all x1, blocking collectives, by_head(): lax.all_to_all(near_out.reshape(half, tok_rows, cols_each), 'seq', split_...  18.6 us
    ppermute x4, starting transfers between devices, by_head(): lax.ppermute(near[a:b, :rows], 'seq', swap_halves)  11.7 us
    pallas_call x1, Pallas kernels, project(): pl.pallas_call(project_kernel, out_shape=jax.ShapeDtypeStruct((tokens, co...  8.98 us
    all_to_all x2, starting transfers between devices, spread(): lax.all_to_all(copies, 'seq', split_axis=0, concat_axis=0, axis_index_gro...  8.09 us
    ppermute x1, waiting for transfers between devices, by_head(): far_ids = lax.ppermute(slot_ids, 'head', swap_heads)  7.78 us
    all_to_all x1, starting transfers between devices, by_head(): lax.all_to_all(packed, 'seq', split_axis=0, concat_axis=0, tiled=True)  7.56 us
  transfers between devices with their start and end apart: 19, of which 11 were waited for; matrix products, arithmetic and copies ran while one was open for 2% of the time, Pallas kernels for 18%

profile of v13, /device:TPU:0, one launch (start us, length us, event | category | flops | bytes accessed | tf_op | source)
XLA Modules:
  0.0 196.1 jit_solution(7010240646937809039)
XLA Ops:
  0.0 0.9 fusion.6
  0.9 1.5 copy.44
  2.4 0.5 copy_bitcast_fusion
  3.0 1.8 pad_maximum_fusion
  4.8 7.6 %all-to-all-start = ((bf16[16,784,128]{2,1,0:T(8,128)(2,1)}), bf16[16,784,128]{2,1,0:T(8,128)(2,1)}, u32[]{:S(2)}, u32[]{:S(2)}) async-start(bf16[16,784,128]{2,1,0:T(8,128)(2,1)} %pad_maximum_fusion), calls=%async_computation | async-start | bytes 6422528 | tf_op jit(solution)/shard_map/all_to_all | solution.py:242
  12.5 0.3 copy.32
  12.8 2.2 %constant_dynamic-slice_fusion = (bf16[256,1,256]{2,1,0:T(2,128)(2,1)S(1)}, bf16[256,1,256]{2,1,0:T(2,128)(2,1)S(1)}, bf16[256,1,256]{2,1,0:T(2,128)(2,1)S(1)}, ...) fusion(bf16[256,8,256]{2,1,0:T(8,128)(2,1)S(1)} %bitcast.101, ...), kind=kLoop, calls=%fused_computation.68 | loop fusion | bytes 2097184 | tf_op jit(solution)/shard_map/dynamic-slice.7
  15.2 0.1 pad_maximum_fusion.1
  15.2 0.4 collective-permute-start
  15.7 2.6 %collective-permute-start.5 = (bf16[288,256]{1,0:T(8,128)(2,1)S(1)}, bf16[288,256]{1,0:T(8,128)(2,1)S(1)}, u32[]{:S(2)}, u32[]{:S(2)}) collective-permute-start(bf16[288,256]{1,0:T(8,128)(2,1)S(1)} %pad_maximum_fusion.2), channel_id=1, source_target_pairs={{0,12},{2,14},{4,8},{6,10},{8,4},{10,6},{12,0},{14,2},{16,28},{18,... | collective-permute-start | bytes 442376 | tf_op jit(solution)/shard_map/ppermute | solution.py:250
  18.3 0.6 collective-permute-start.1
  18.9 0.9 collective-permute-start.2
  19.7 0.6 collective-permute-start.3
  20.3 0.0 collective-permute-done
  20.4 1.6 collective-permute-start.4
  21.9 15.4 %collective-permute-done.1 = bf16[288,256]{1,0:T(8,128)(2,1)S(1)} collective-permute-done((bf16[288,256]{1,0:T(8,128)(2,1)S(1)}, bf16[288,256]{1,0:T(8,128)(2,1)S(1)}, u32[]{:S(2)}, u32[]{:S(2)}) %collective-permute-start.1) | collective-permute-done | bytes 147488 | tf_op jit(solution)/shard_map/ppermute | solution.py:250
  37.3 0.0 collective-permute-start.6
  37.4 7.4 %collective-permute-done.2 = bf16[288,256]{1,0:T(8,128)(2,1)S(1)} collective-permute-done((bf16[288,256]{1,0:T(8,128)(2,1)S(1)}, bf16[288,256]{1,0:T(8,128)(2,1)S(1)}, u32[]{:S(2)}, u32[]{:S(2)}) %collective-permute-start.2) | collective-permute-done | bytes 147488 | tf_op jit(solution)/shard_map/ppermute | solution.py:250
  44.8 27.9 %collective-permute-done.3 = bf16[288,256]{1,0:T(8,128)(2,1)S(1)} collective-permute-done((bf16[288,256]{1,0:T(8,128)(2,1)S(1)}, bf16[288,256]{1,0:T(8,128)(2,1)S(1)}, u32[]{:S(2)}, u32[]{:S(2)}) %collective-permute-start.3) | collective-permute-done | bytes 147488 | tf_op jit(solution)/shard_map/ppermute | solution.py:250
  72.7 3.1 %collective-permute-done.4 = bf16[288,256]{1,0:T(8,128)(2,1)S(1)} collective-permute-done((bf16[288,256]{1,0:T(8,128)(2,1)S(1)}, bf16[288,256]{1,0:T(8,128)(2,1)S(1)}, u32[]{:S(2)}, u32[]{:S(2)}) %collective-permute-start.4) | collective-permute-done | bytes 147488 | tf_op jit(solution)/shard_map/ppermute | solution.py:250
  75.9 0.0 collective-permute-done.5
  75.9 4.5 %collective-permute-done.6 = bf16[288,256]{1,0:T(8,128)(2,1)S(1)} collective-permute-done((bf16[288,256]{1,0:T(8,128)(2,1)S(1)}, bf16[288,256]{1,0:T(8,128)(2,1)S(1)}, u32[]{:S(2)}, u32[]{:S(2)}) %collective-permute-start.6) | collective-permute-done | bytes 147488 | tf_op jit(solution)/shard_map/ppermute | solution.py:250
  80.4 0.0 all-to-all-done.refs_0_
  80.4 7.5 %collective-permute-start.7 = (bf16[1,256,256]{2,1,0:T(8,128)(2,1)S(1)}, bf16[1,256,256]{2,1,0:T(8,128)(2,1)S(1)}, u32[]{:S(2)}, u32[]{:S(2)}) collective-permute-start(bf16[1,256,256]{2,1,0:T(8,128)(2,1)S(1)} %slice.21), channel_id=1, source_target_pairs={{0,16},{2,18},{4,20},{6,22},{8,24},{10,26},{12,28},{14,30},{16,0},... | collective-permute-start | bytes 393224 | tf_op jit(solution)/shard_map/ppermute | solution.py:254
  87.9 7.0 %attend.1 = bf16[512,128]{1,0:T(8,128)(2,1)S(1)} custom-call(bf16[16,784,128]{2,1,0:T(8,128)(2,1)} %all-to-all-done.refs_0_), custom_call_target="tpu_custom_call" | custom-call | flops 2147483648 | bytes 3211264 | tf_op jit(solution)/shard_map/attend/pallas_call | solution.py:104
  94.9 0.0 collective-permute-done.7.refs_0_
  94.9 0.6 copy-done.4
  95.6 0.1 collective-permute-start.8
  95.7 6.4 %collective-permute-done.8 = bf16[512,128]{1,0:T(8,128)(2,1)S(1)} collective-permute-done((bf16[512,128]{1,0:T(8,128)(2,1)S(1)}, bf16[512,128]{1,0:T(8,128)(2,1)S(1)}, u32[]{:S(2)}, u32[]{:S(2)}) %collective-permute-start.8) | collective-permute-done | bytes 131104 | tf_op jit(solution)/shard_map/ppermute | solution.py:268
  102.1 1.1 broadcast_in_dim.4
  103.2 4.1 %all-to-all-start.1 = ((bf16[4,2,512,128]{3,2,1,0:T(8,128)(2,1)}), bf16[4,2,512,128]{3,2,1,0:T(8,128)(2,1)S(1)}, u32[]{:S(2)}, u32[]{:S(2)}) async-start(bf16[4,2,512,128]{3,2,1,0:T(8,128)(2,1)} %broadcast_in_dim.4), calls=%async_computation.1 | async-start | bytes 2097152 | tf_op jit(solution)/shard_map/all_to_all | solution.py:263
  107.5 0.1 reshape.45
  107.6 0.4 rev.7
  108.0 0.8 fusion.11
  108.8 1.2 collective-permute-start.11
  110.0 1.5 collective-permute-start.10
  111.5 0.1 broadcast_select_fusion
  111.6 0.1 copy.20
  111.7 0.6 collective-permute-start.9
  112.3 7.8 %collective-permute-done.9.ids_ref = s32[2,8,2048]{2,1,0:T(8,128)S(1)} collective-permute-done((s32[2,8,2048]{2,1,0:T(8,128)S(1)}, s32[2,8,2048]{2,1,0:T(8,128)S(1)}, u32[]{:S(2)}, u32[]{:S(2)}) %collective-permute-start.9) | collective-permute-done | bytes 131104 | tf_op jit(solution)/shard_map/ppermute | solution.py:278
  120.1 3.6 %collective-permute-done.11.refs_1_ = bf16[2,256,256]{2,1,0:T(8,128)(2,1)S(1)} collective-permute-done((bf16[2,256,256]{2,1,0:T(8,128)(2,1)}, bf16[2,256,256]{2,1,0:T(8,128)(2,1)S(1)}, u32[]{:S(2)}, u32[]{:S(2)}) %collective-permute-start.11) | collective-permute-done | bytes 262176 | tf_op jit(solution)/shard_map/ppermute | solution.py:257
  123.7 0.0 collective-permute-done.10
  123.7 2.1 %all-to-all-done.1 = bf16[4,2,512,128]{3,2,1,0:T(8,128)(2,1)S(1)} async-done(((bf16[4,2,512,128]{3,2,1,0:T(8,128)(2,1)}), bf16[4,2,512,128]{3,2,1,0:T(8,128)(2,1)S(1)}, u32[]{:S(2)}, u32[]{:S(2)}) %all-to-all-start.1) | async-done | bytes 1048608 | tf_op jit(solution)/shard_map/all_to_all | solution.py:263
  125.8 1.1 broadcast_in_dim.5
  126.9 4.0 %all-to-all-start.2 = ((bf16[4,2,512,128]{3,2,1,0:T(8,128)(2,1)}), bf16[4,2,512,128]{3,2,1,0:T(8,128)(2,1)S(1)}, u32[]{:S(2)}, u32[]{:S(2)}) async-start(bf16[4,2,512,128]{3,2,1,0:T(8,128)(2,1)} %broadcast_in_dim.5), calls=%async_computation.2 | async-start | bytes 2097152 | tf_op jit(solution)/shard_map/all_to_all | solution.py:263
  130.9 0.0 collective-permute-start.12
  130.9 1.1 collective-permute-start.13
  132.0 6.8 %expand.4.refs_0_ = bf16[32,2048,128]{2,1,0:T(8,128)(2,1)} custom-call(s32[2,8,2048]{2,1,0:T(8,128)S(1)} %reshape.46.ids_ref, bf16[8,512,128]{2,1,0:T(8,128)(2,1)S(1)} %bitcast.96), custom_call_target="tpu_custom_call" | custom-call | flops 4294967296 | bytes 5242880 | tf_op jit(solution)/shard_map/expand/pallas_call | solution.py:141
  138.8 0.0 collective-permute-done.12.attended_ref
  138.8 6.8 %expand.5.refs_0_ = bf16[32,2048,128]{2,1,0:T(8,128)(2,1)} custom-call(s32[2,8,2048]{2,1,0:T(8,128)S(1)} %reshape.46.ids_ref, bf16[8,512,128]{2,1,0:T(8,128)(2,1)S(1)} %collective-permute-done.12.attended_ref, bf16[32,2048,128]{2,1,0:T(8,128)(2,1)} %expand.4.refs_0_), custom_call_target="tpu_custom_call", output_to_operand_aliasing={{}: (2, {})} | custom-call | flops 4294967296 | bytes 5242880 | tf_op jit(solution)/shard_map/expand/pallas_call | solution.py:141
  145.7 3.7 %collective-permute-done.13.refs_2_ = bf16[3,256,256]{2,1,0:T(8,128)(2,1)S(1)} collective-permute-done((bf16[3,256,256]{2,1,0:T(8,128)(2,1)S(1)}, bf16[3,256,256]{2,1,0:T(8,128)(2,1)S(1)}, u32[]{:S(2)}, u32[]{:S(2)}) %collective-permute-start.13) | collective-permute-done | bytes 393248 | tf_op jit(solution)/shard_map/ppermute | solution.py:257
  149.4 0.7 copy-done
  150.2 1.5 all-to-all-done.2
  151.6 0.0 collective-permute-start.14
  151.6 0.1 pad_add_fusion.places_ref
  151.7 2.0 %collective-permute-start.15 = (bf16[2,256,256]{2,1,0:T(8,128)(2,1)}, bf16[2,256,256]{2,1,0:T(8,128)(2,1)S(1)}, u32[]{:S(2)}, u32[]{:S(2)}) collective-permute-start(bf16[2,256,256]{2,1,0:T(8,128)(2,1)} %get-tuple-element.39), channel_id=1, source_target_pairs={{0,16},{2,18},{4,20},{6,22},{8,24},{10,26},{12,28},{14,30},{16,0},... | collective-permute-start | bytes 786440 | tf_op jit(solution)/shard_map/ppermute | solution.py:257
  153.7 6.8 %expand.6.refs_0_ = bf16[32,2048,128]{2,1,0:T(8,128)(2,1)} custom-call(s32[2,8,2048]{2,1,0:T(8,128)S(1)} %collective-permute-done.9.ids_ref, bf16[8,512,128]{2,1,0:T(8,128)(2,1)S(1)} %bitcast.98, bf16[32,2048,128]{2,1,0:T(8,128)(2,1)} %expand.5.refs_0_), custom_call_target="tpu_custom_call", output_to_operand_aliasing={{}: (2, {})} | custom-call | flops 4294967296 | bytes 5242880 | tf_op jit(solution)/shard_map/expand/pallas_call | solution.py:141
  160.5 0.0 collective-permute-done.14.attended_ref
  160.5 6.8 %expand.7.features_ref = bf16[32,2048,128]{2,1,0:T(8,128)(2,1)} custom-call(s32[2,8,2048]{2,1,0:T(8,128)S(1)} %collective-permute-done.9.ids_ref, bf16[8,512,128]{2,1,0:T(8,128)(2,1)S(1)} %collective-permute-done.14.attended_ref, bf16[32,2048,128]{2,1,0:T(8,128)(2,1)} %expand.6.refs_0_), custom_call_target="tpu_custom_call", output_to_operand_aliasing={{}: (2, {})} | custom-call | flops 4294967296 | bytes 5242880 | tf_op jit(solution)/shard_map/expand/pallas_call | solution.py:141
  167.4 0.0 collective-permute-done.15.refs_3_
  167.4 0.0 copy-done.3
  167.4 9.0 %project.1 = bf16[2048,256]{1,0:T(8,128)(2,1)S(1)} custom-call(s32[4]{0:T(128)S(1)} %pad_add_fusion.places_ref, bf16[32,2048,128]{2,1,0:T(8,128)(2,1)} %expand.7.features_ref, bf16[8,288,256]{2,1,0:T(8,128)(2,1)S(1)} %bitcast_dynamic-update-slice_fusion.near_ref, bf16[1,256,256]{2,1,0:T(8,128)(2,1)S(1)} %copy-done.5, bf16[2,256,256]{2,1,0:T(8,128)(2,1)S(1)} %copy-done.3, ...), custom_call_target="tpu_custom_call" | custom-call | flops 4294967296 | bytes 19922944 | tf_op jit(solution)/shard_map/project/pallas_call | solution.py:184
  176.4 18.6 %all_to_all.20 = bf16[8,256,256]{2,1,0:T(8,128)(2,1)S(1)} all-to-all(bf16[8,256,256]{2,1,0:T(8,128)(2,1)S(1)} %bitcast.99), channel_id=1, replica_groups={{0,2,4,6,8,10,12,14},{16,18,20,22,24,26,28,30},{1,3,5,7,9,11,13,15},{17..., dimensions={0} | all-to-all | bytes 2097152 | tf_op jit(solution)/shard_map/all_to_all | solution.py:296
  195.0 1.1 copy.30
  (49 shorter events, 0.5 us)
Async XLA Ops:
  0.0 2.4 %copy-start.8 = (bf16[256,16,128]{2,1,0:T(8,128)(2,1)S(1)}, bf16[256,16,128]{2,1,0:T(8,128)(2,1)}, u32[]{:S(2)}) copy-start(bf16[256,16,128]{2,1,0:T(8,128)(2,1)} %param.6) | copy-start | bytes 3145732
  0.0 2.4 %copy-start.7 = (bf16[256,16,128]{2,1,0:T(8,128)(2,1)S(1)}, bf16[256,16,128]{2,1,0:T(8,128)(2,1)}, u32[]{:S(2)}) copy-start(bf16[256,16,128]{2,1,0:T(8,128)(2,1)} %param.7) | copy-start | bytes 3145732
  4.8 7.6 %copy-start.6 = (bf16[256,2048]{1,0:T(8,128)(2,1)S(1)}, bf16[256,2048]{1,0:T(8,128)(2,1)}, u32[]{:S(2)}) copy-start(bf16[256,2048]{1,0:T(8,128)(2,1)} %param.9) | copy-start | bytes 3145732
  4.8 75.5 %all-to-all-start = ((bf16[16,784,128]{2,1,0:T(8,128)(2,1)}), bf16[16,784,128]{2,1,0:T(8,128)(2,1)}, u32[]{:S(2)}, u32[]{:S(2)}) async-start(bf16[16,784,128]{2,1,0:T(8,128)(2,1)} %pad_maximum_fusion), calls=%async_computation | async-start | bytes 6422528 | tf_op jit(solution)/shard_map/all_to_all | solution.py:242
  15.2 5.1 %collective-permute-start = (bf16[288,256]{1,0:T(8,128)(2,1)S(1)}, bf16[288,256]{1,0:T(8,128)(2,1)S(1)}, u32[]{:S(2)}, u32[]{:S(2)}) collective-permute-start(bf16[288,256]{1,0:T(8,128)(2,1)S(1)} %get-tuple-element.50), channel_id=1, source_target_pairs={{0,2},{2,0},{4,6},{6,4},{8,10},{10,8},{12,14},{14,12},{16,18},{18,... | collective-permute-start | bytes 442376 | tf_op jit(solution)/shard_map/ppermute | solution.py:250
  15.7 60.2 %collective-permute-start.5 = (bf16[288,256]{1,0:T(8,128)(2,1)S(1)}, bf16[288,256]{1,0:T(8,128)(2,1)S(1)}, u32[]{:S(2)}, u32[]{:S(2)}) collective-permute-start(bf16[288,256]{1,0:T(8,128)(2,1)S(1)} %pad_maximum_fusion.2), channel_id=1, source_target_pairs={{0,12},{2,14},{4,8},{6,10},{8,4},{10,6},{12,0},{14,2},{16,28},{18,... | collective-permute-start | bytes 442376 | tf_op jit(solution)/shard_map/ppermute | solution.py:250
  18.3 19.0 %collective-permute-start.1 = (bf16[288,256]{1,0:T(8,128)(2,1)S(1)}, bf16[288,256]{1,0:T(8,128)(2,1)S(1)}, u32[]{:S(2)}, u32[]{:S(2)}) collective-permute-start(bf16[288,256]{1,0:T(8,128)(2,1)S(1)} %get-tuple-element.51), channel_id=1, source_target_pairs={{0,4},{2,6},{4,0},{6,2},{8,12},{10,14},{12,8},{14,10},{16,20},{18,... | collective-permute-start | bytes 442376 | tf_op jit(solution)/shard_map/ppermute | solution.py:250
  18.9 25.9 %collective-permute-start.2 = (bf16[288,256]{1,0:T(8,128)(2,1)S(1)}, bf16[288,256]{1,0:T(8,128)(2,1)S(1)}, u32[]{:S(2)}, u32[]{:S(2)}) collective-permute-start(bf16[288,256]{1,0:T(8,128)(2,1)S(1)} %get-tuple-element.52), channel_id=1, source_target_pairs={{0,6},{2,4},{4,2},{6,0},{8,14},{10,12},{12,10},{14,8},{16,22},{18,... | collective-permute-start | bytes 442376 | tf_op jit(solution)/shard_map/ppermute | solution.py:250
  19.7 53.0 %collective-permute-start.3 = (bf16[288,256]{1,0:T(8,128)(2,1)S(1)}, bf16[288,256]{1,0:T(8,128)(2,1)S(1)}, u32[]{:S(2)}, u32[]{:S(2)}) collective-permute-start(bf16[288,256]{1,0:T(8,128)(2,1)S(1)} %get-tuple-element.53), channel_id=1, source_target_pairs={{0,8},{2,10},{4,12},{6,14},{8,0},{10,2},{12,4},{14,6},{16,24},{18,... | collective-permute-start | bytes 442376 | tf_op jit(solution)/shard_map/ppermute | solution.py:250
  20.4 55.5 %collective-permute-start.4 = (bf16[288,256]{1,0:T(8,128)(2,1)S(1)}, bf16[288,256]{1,0:T(8,128)(2,1)S(1)}, u32[]{:S(2)}, u32[]{:S(2)}) collective-permute-start(bf16[288,256]{1,0:T(8,128)(2,1)S(1)} %get-tuple-element.54), channel_id=1, source_target_pairs={{0,10},{2,8},{4,14},{6,12},{8,2},{10,0},{12,6},{14,4},{16,26},{18,... | collective-permute-start | bytes 442376 | tf_op jit(solution)/shard_map/ppermute | solution.py:250
  37.3 43.0 %collective-permute-start.6 = (bf16[288,256]{1,0:T(8,128)(2,1)S(1)}, bf16[288,256]{1,0:T(8,128)(2,1)S(1)}, u32[]{:S(2)}, u32[]{:S(2)}) collective-permute-start(bf16[288,256]{1,0:T(8,128)(2,1)S(1)} %get-tuple-element.49), channel_id=1, source_target_pairs={{0,14},{2,12},{4,10},{6,8},{8,6},{10,4},{12,2},{14,0},{16,30},{18,... | collective-permute-start | bytes 442376 | tf_op jit(solution)/shard_map/ppermute | solution.py:250
  80.4 14.5 %collective-permute-start.7 = (bf16[1,256,256]{2,1,0:T(8,128)(2,1)S(1)}, bf16[1,256,256]{2,1,0:T(8,128)(2,1)S(1)}, u32[]{:S(2)}, u32[]{:S(2)}) collective-permute-start(bf16[1,256,256]{2,1,0:T(8,128)(2,1)S(1)} %slice.21), channel_id=1, source_target_pairs={{0,16},{2,18},{4,20},{6,22},{8,24},{10,26},{12,28},{14,30},{16,0},... | collective-permute-start | bytes 393224 | tf_op jit(solution)/shard_map/ppermute | solution.py:254
  94.9 0.7 copy-start.4
  95.6 6.5 %collective-permute-start.8 = (bf16[512,128]{1,0:T(8,128)(2,1)S(1)}, bf16[512,128]{1,0:T(8,128)(2,1)S(1)}, u32[]{:S(2)}, u32[]{:S(2)}) collective-permute-start(bf16[512,128]{1,0:T(8,128)(2,1)S(1)} %attend.1), channel_id=1, source_target_pairs={{0,16},{2,18},{4,20},{6,22},{8,24},{10,26},{12,28},{14,30},{16,0},... | collective-permute-start | bytes 393224 | tf_op jit(solution)/shard_map/ppermute | solution.py:268
  103.2 22.6 %all-to-all-start.1 = ((bf16[4,2,512,128]{3,2,1,0:T(8,128)(2,1)}), bf16[4,2,512,128]{3,2,1,0:T(8,128)(2,1)S(1)}, u32[]{:S(2)}, u32[]{:S(2)}) async-start(bf16[4,2,512,128]{3,2,1,0:T(8,128)(2,1)} %broadcast_in_dim.4), calls=%async_computation.1 | async-start | bytes 2097152 | tf_op jit(solution)/shard_map/all_to_all | solution.py:263
  108.8 14.9 %collective-permute-start.11 = (bf16[2,256,256]{2,1,0:T(8,128)(2,1)}, bf16[2,256,256]{2,1,0:T(8,128)(2,1)S(1)}, u32[]{:S(2)}, u32[]{:S(2)}) collective-permute-start(bf16[2,256,256]{2,1,0:T(8,128)(2,1)} %get-tuple-element.40), channel_id=1, source_target_pairs={{0,16},{2,18},{4,20},{6,22},{8,24},{10,26},{12,28},{14,30},{16,0},... | collective-permute-start | bytes 786440 | tf_op jit(solution)/shard_map/ppermute | solution.py:257
  110.0 13.7 %collective-permute-start.10 = (bf16[2,512,128]{2,1,0:T(8,128)(2,1)S(1)}, bf16[2,512,128]{2,1,0:T(8,128)(2,1)S(1)}, u32[]{:S(2)}, u32[]{:S(2)}) collective-permute-start(bf16[2,512,128]{2,1,0:T(8,128)(2,1)S(1)} %pad_maximum_fusion.17), channel_id=1, source_target_pairs={{0,1},{1,0},{2,3},{3,2},{4,5},{5,4},{6,7},{7,6},{8,9},{9,8},{10,11... | collective-permute-start | bytes 786440 | tf_op jit(solution)/shard_map/ppermute | solution.py:269
  111.7 8.4 %collective-permute-start.9 = (s32[2,8,2048]{2,1,0:T(8,128)S(1)}, s32[2,8,2048]{2,1,0:T(8,128)S(1)}, u32[]{:S(2)}, u32[]{:S(2)}) collective-permute-start(s32[2,8,2048]{2,1,0:T(8,128)S(1)} %reshape.46.ids_ref), channel_id=1, source_target_pairs={{0,1},{1,0},{2,3},{3,2},{4,5},{5,4},{6,7},{7,6},{8,9},{9,8},{10,11... | collective-permute-start | bytes 393224 | tf_op jit(solution)/shard_map/ppermute | solution.py:278
  123.7 3.2 %copy-start.2 = (bf16[2,256,256]{2,1,0:T(8,128)(2,1)}, bf16[2,256,256]{2,1,0:T(8,128)(2,1)S(1)}, u32[]{:S(2)}) copy-start(bf16[2,256,256]{2,1,0:T(8,128)(2,1)S(1)} %collective-permute-done.11.refs_1_) | copy-start | bytes 786436
  126.9 24.7 %all-to-all-start.2 = ((bf16[4,2,512,128]{3,2,1,0:T(8,128)(2,1)}), bf16[4,2,512,128]{3,2,1,0:T(8,128)(2,1)S(1)}, u32[]{:S(2)}, u32[]{:S(2)}) async-start(bf16[4,2,512,128]{3,2,1,0:T(8,128)(2,1)} %broadcast_in_dim.5), calls=%async_computation.2 | async-start | bytes 2097152 | tf_op jit(solution)/shard_map/all_to_all | solution.py:263
  130.9 8.0 %collective-permute-start.12 = (bf16[8,512,128]{2,1,0:T(8,128)(2,1)S(1)}, bf16[8,512,128]{2,1,0:T(8,128)(2,1)S(1)}, u32[]{:S(2)}, u32[]{:S(2)}) collective-permute-start(bf16[8,512,128]{2,1,0:T(8,128)(2,1)S(1)} %bitcast.95), channel_id=1, source_target_pairs={{0,2},{2,0},{4,6},{6,4},{8,10},{10,8},{12,14},{14,12},{16,18},{18,... | collective-permute-start | bytes 3145736 | tf_op jit(solution)/shard_map/ppermute | solution.py:283
  130.9 18.5 %collective-permute-start.13 = (bf16[3,256,256]{2,1,0:T(8,128)(2,1)S(1)}, bf16[3,256,256]{2,1,0:T(8,128)(2,1)S(1)}, u32[]{:S(2)}, u32[]{:S(2)}) collective-permute-start(bf16[3,256,256]{2,1,0:T(8,128)(2,1)S(1)} %slice.26), channel_id=1, source_target_pairs={{0,16},{2,18},{4,20},{6,22},{8,24},{10,26},{12,28},{14,30},{16,0},... | collective-permute-start | bytes 1179656 | tf_op jit(solution)/shard_map/ppermute | solution.py:257
  149.4 0.7 copy-start
  151.6 8.9 %collective-permute-start.14 = (bf16[8,512,128]{2,1,0:T(8,128)(2,1)S(1)}, bf16[8,512,128]{2,1,0:T(8,128)(2,1)S(1)}, u32[]{:S(2)}, u32[]{:S(2)}) collective-permute-start(bf16[8,512,128]{2,1,0:T(8,128)(2,1)S(1)} %bitcast.97), channel_id=1, source_target_pairs={{0,2},{2,0},{4,6},{6,4},{8,10},{10,8},{12,14},{14,12},{16,18},{18,... | collective-permute-start | bytes 3145736 | tf_op jit(solution)/shard_map/ppermute | solution.py:291
  151.7 15.7 %collective-permute-start.15 = (bf16[2,256,256]{2,1,0:T(8,128)(2,1)}, bf16[2,256,256]{2,1,0:T(8,128)(2,1)S(1)}, u32[]{:S(2)}, u32[]{:S(2)}) collective-permute-start(bf16[2,256,256]{2,1,0:T(8,128)(2,1)} %get-tuple-element.39), channel_id=1, source_target_pairs={{0,16},{2,18},{4,20},{6,22},{8,24},{10,26},{12,28},{14,30},{16,0},... | collective-permute-start | bytes 786440 | tf_op jit(solution)/shard_map/ppermute | solution.py:257
  160.5 6.9 %copy-start.1 = (bf16[3,256,256]{2,1,0:T(8,128)(2,1)S(1)}, bf16[3,256,256]{2,1,0:T(8,128)(2,1)}, u32[]{:S(2)}) copy-start(bf16[3,256,256]{2,1,0:T(8,128)(2,1)} %copy-done) | copy-start | bytes 1179652
  160.5 6.9 %copy-start.3 = (bf16[2,256,256]{2,1,0:T(8,128)(2,1)S(1)}, bf16[2,256,256]{2,1,0:T(8,128)(2,1)}, u32[]{:S(2)}) copy-start(bf16[2,256,256]{2,1,0:T(8,128)(2,1)} %copy-done.2) | copy-start | bytes 786436
  160.5 6.9 %copy-start.5 = (bf16[1,256,256]{2,1,0:T(8,128)(2,1)S(1)}, bf16[1,256,256]{2,1,0:T(8,128)(2,1)}, u32[]{:S(2)}) copy-start(bf16[1,256,256]{2,1,0:T(8,128)(2,1)} %copy-done.4) | copy-start | bytes 393220

commit v14 on v13

--- a/solution.py
+++ b/solution.py
@@ -50,7 +50,15 @@
     return expand_and_project(ids, attended, weight)
 
 
-def attend_kernel(tok_rows, moved_ref, out_ref, sums_ref, scores_ref, acc_ref):
+def attend_kernel(tok_rows, source_ref, out_ref, sums_ref, scores_ref, acc_ref, moved_ref, sems):
+    rows = source_ref.shape[1]
+    spans = [(0, tok_rows), (3 * tok_rows, rows), (tok_rows, 2 * tok_rows), (2 * tok_rows, 3 * tok_rows)]
+    loads = [
+        pltpu.make_async_copy(source_ref.at[:, a:b], moved_ref.at[:, a:b], sems.at[i])
+        for i, (a, b) in enumerate(spans)
+    ]
+    for load in loads:
+        load.start()
     n_src, _, e_width = moved_ref.shape
     lanes = e_width
     blocks = tok_rows // lanes
@@ -59,8 +67,10 @@
     ones = jnp.ones((tok_rows, e_width), jnp.bfloat16)
 
     sums_ref[...] = jnp.zeros_like(sums_ref)
-
-    @pl.loop(0, n_src, unroll=8)
+    loads[0].wait()
+    loads[1].wait()
+
+    @pl.loop(0, n_src, unroll=16)
     def _(src):
         coded = moved_ref[src, 3 * tok_rows :, :].astype(jnp.float32).astype(jnp.int32)
         parts = []
@@ -73,6 +83,8 @@
 
     centroid = (sums_ref[:, :e_width] / jnp.maximum(sums_ref[:, e_width:], 1.0)).astype(jnp.bfloat16)
 
+    loads[2].wait()
+
     def score(src, top):
         keys = moved_ref[src, tok_rows : 2 * tok_rows, :]
         scores = lax.dot_general(centroid, keys, (((1,), (1,)), ((), ())), preferred_element_type=jnp.float32)
@@ -81,10 +93,11 @@
             top = jnp.maximum(top, scores[:, i * lanes : (i + 1) * lanes])
         return top
 
-    top = lax.fori_loop(0, n_src, score, jnp.full((C, lanes), -jnp.inf, jnp.float32), unroll=8)
+    top = lax.fori_loop(0, n_src, score, jnp.full((C, lanes), -jnp.inf, jnp.float32), unroll=16)
     top = jnp.broadcast_to(jnp.max(top, axis=1, keepdims=True), (C, tok_rows))
 
     acc_ref[...] = jnp.zeros_like(acc_ref)
+    loads[3].wait()
 
     def weigh(src, total):
         weights = jnp.exp((scores_ref[src] - top) * scale)
@@ -94,7 +107,7 @@
         acc_ref[...] += jnp.dot(weights.astype(jnp.bfloat16), values, preferred_element_type=jnp.float32)
         return total
 
-    total = lax.fori_loop(0, n_src, weigh, jnp.zeros((C, lanes), jnp.float32), unroll=8)
+    total = lax.fori_loop(0, n_src, weigh, jnp.zeros((C, lanes), jnp.float32), unroll=16)
     out_ref[...] = (acc_ref[...] / jnp.sum(total, axis=1, keepdims=True)).astype(jnp.bfloat16)
 
 
@@ -104,12 +117,14 @@
     return pl.pallas_call(
         lambda *refs: attend_kernel(tok_rows, *refs),
         out_shape=jax.ShapeDtypeStruct((C, e_width), jnp.bfloat16),
-        in_specs=[pl.BlockSpec(memory_space=pltpu.VMEM)],
+        in_specs=[pl.BlockSpec(memory_space=pl.ANY)],
         out_specs=pl.BlockSpec(memory_space=pltpu.VMEM),
         scratch_shapes=[
             pltpu.VMEM((C, 2 * e_width), jnp.float32),
             pltpu.VMEM((n_src, C, tok_rows), jnp.float32),
             pltpu.VMEM((C, e_width), jnp.float32),
+            pltpu.VMEM(moved.shape, moved.dtype),
+            pltpu.SemaphoreType.DMA((4,)),
         ],
         compiler_params=pltpu.CompilerParams(vmem_limit_bytes=24 * 2**20),
         cost_estimate=pl.CostEstimate(

time: 197 us -> 197 us (level)
  no operation moved by 1% of the time
where the time goes in v14:
time: 197 us; the launch traced here: 196 us
  waiting for transfers between devices  83.5 us (42%)
  Pallas kernels  43.6 us (22%)
  starting transfers between devices  36.1 us (18%)
  blocking collectives  18.6 us (9%)
  local copies, waits for them, and re-layouts  11 us (6%)
  other arithmetic  3.09 us (2%)
    ppermute x7, waiting for transfers between devices, by_head(): lax.ppermute(block, 'seq', [(i, i ^ k) for i in range(n_seq)])  58.3 us
    pallas_call x4, Pallas kernels, expand(): pl.pallas_call(expand_kernel, out_shape=jax.ShapeDtypeStruct((pieces * he...  27.3 us
    all_to_all x1, blocking collectives, by_head(): lax.all_to_all(near_out.reshape(half, tok_rows, cols_each), 'seq', split_...  18.6 us
    ppermute x4, starting transfers between devices, by_head(): lax.ppermute(near[a:b, :rows], 'seq', swap_halves)  11.7 us
    pallas_call x1, Pallas kernels, project(): pl.pallas_call(project_kernel, out_shape=jax.ShapeDtypeStruct((tokens, co...  8.98 us
    all_to_all x2, starting transfers between devices, spread(): lax.all_to_all(copies, 'seq', split_axis=0, concat_axis=0, axis_index_gro...  8.09 us
    ppermute x1, waiting for transfers between devices, by_head(): far_ids = lax.ppermute(slot_ids, 'head', swap_heads)  7.78 us
    all_to_all x1, starting transfers between devices, by_head(): lax.all_to_all(packed, 'seq', split_axis=0, concat_axis=0, tiled=True)  7.56 us
  transfers between devices with their start and end apart: 19, of which 11 were waited for; matrix products, arithmetic and copies ran while one was open for 2% of the time, Pallas kernels for 18%

profile of v14, /device:TPU:0, one launch (start us, length us, event | category | flops | bytes accessed | tf_op | source)
XLA Modules:
  0.0 196.3 jit_solution(9360569076051638278)
XLA Ops:
  0.0 0.9 fusion.6
  0.9 1.5 copy.44
  2.4 0.5 copy_bitcast_fusion
  3.0 1.8 pad_maximum_fusion
  4.8 7.6 %all-to-all-start = ((bf16[16,784,128]{2,1,0:T(8,128)(2,1)}), bf16[16,784,128]{2,1,0:T(8,128)(2,1)}, u32[]{:S(2)}, u32[]{:S(2)}) async-start(bf16[16,784,128]{2,1,0:T(8,128)(2,1)} %pad_maximum_fusion), calls=%async_computation | async-start | bytes 6422528 | tf_op jit(solution)/shard_map/all_to_all | solution.py:257
  12.5 0.3 copy.32
  12.8 2.2 %constant_dynamic-slice_fusion = (bf16[256,1,256]{2,1,0:T(2,128)(2,1)S(1)}, bf16[256,1,256]{2,1,0:T(2,128)(2,1)S(1)}, bf16[256,1,256]{2,1,0:T(2,128)(2,1)S(1)}, ...) fusion(bf16[256,8,256]{2,1,0:T(8,128)(2,1)S(1)} %bitcast.101, ...), kind=kLoop, calls=%fused_computation.68 | loop fusion | bytes 2097184 | tf_op jit(solution)/shard_map/dynamic-slice.7
  15.2 0.1 pad_maximum_fusion.1
  15.2 0.4 collective-permute-start
  15.7 2.6 %collective-permute-start.5 = (bf16[288,256]{1,0:T(8,128)(2,1)S(1)}, bf16[288,256]{1,0:T(8,128)(2,1)S(1)}, u32[]{:S(2)}, u32[]{:S(2)}) collective-permute-start(bf16[288,256]{1,0:T(8,128)(2,1)S(1)} %pad_maximum_fusion.2), channel_id=1, source_target_pairs={{0,12},{2,14},{4,8},{6,10},{8,4},{10,6},{12,0},{14,2},{16,28},{18,... | collective-permute-start | bytes 442376 | tf_op jit(solution)/shard_map/ppermute | solution.py:265
  18.3 0.6 collective-permute-start.1
  18.9 0.9 collective-permute-start.2
  19.7 0.6 collective-permute-start.3
  20.3 0.0 collective-permute-done
  20.4 1.6 collective-permute-start.4
  21.9 15.4 %collective-permute-done.1 = bf16[288,256]{1,0:T(8,128)(2,1)S(1)} collective-permute-done((bf16[288,256]{1,0:T(8,128)(2,1)S(1)}, bf16[288,256]{1,0:T(8,128)(2,1)S(1)}, u32[]{:S(2)}, u32[]{:S(2)}) %collective-permute-start.1) | collective-permute-done | bytes 147488 | tf_op jit(solution)/shard_map/ppermute | solution.py:265
  37.3 0.0 collective-permute-start.6
  37.4 7.4 %collective-permute-done.2 = bf16[288,256]{1,0:T(8,128)(2,1)S(1)} collective-permute-done((bf16[288,256]{1,0:T(8,128)(2,1)S(1)}, bf16[288,256]{1,0:T(8,128)(2,1)S(1)}, u32[]{:S(2)}, u32[]{:S(2)}) %collective-permute-start.2) | collective-permute-done | bytes 147488 | tf_op jit(solution)/shard_map/ppermute | solution.py:265
  44.8 27.9 %collective-permute-done.3 = bf16[288,256]{1,0:T(8,128)(2,1)S(1)} collective-permute-done((bf16[288,256]{1,0:T(8,128)(2,1)S(1)}, bf16[288,256]{1,0:T(8,128)(2,1)S(1)}, u32[]{:S(2)}, u32[]{:S(2)}) %collective-permute-start.3) | collective-permute-done | bytes 147488 | tf_op jit(solution)/shard_map/ppermute | solution.py:265
  72.7 3.1 %collective-permute-done.4 = bf16[288,256]{1,0:T(8,128)(2,1)S(1)} collective-permute-done((bf16[288,256]{1,0:T(8,128)(2,1)S(1)}, bf16[288,256]{1,0:T(8,128)(2,1)S(1)}, u32[]{:S(2)}, u32[]{:S(2)}) %collective-permute-start.4) | collective-permute-done | bytes 147488 | tf_op jit(solution)/shard_map/ppermute | solution.py:265
  75.9 0.0 collective-permute-done.5
  75.9 4.5 %collective-permute-done.6 = bf16[288,256]{1,0:T(8,128)(2,1)S(1)} collective-permute-done((bf16[288,256]{1,0:T(8,128)(2,1)S(1)}, bf16[288,256]{1,0:T(8,128)(2,1)S(1)}, u32[]{:S(2)}, u32[]{:S(2)}) %collective-permute-start.6) | collective-permute-done | bytes 147488 | tf_op jit(solution)/shard_map/ppermute | solution.py:265
  80.4 0.0 all-to-all-done.refs_0_
  80.4 7.5 %collective-permute-start.7 = (bf16[1,256,256]{2,1,0:T(8,128)(2,1)S(1)}, bf16[1,256,256]{2,1,0:T(8,128)(2,1)S(1)}, u32[]{:S(2)}, u32[]{:S(2)}) collective-permute-start(bf16[1,256,256]{2,1,0:T(8,128)(2,1)S(1)} %slice.21), channel_id=1, source_target_pairs={{0,16},{2,18},{4,20},{6,22},{8,24},{10,26},{12,28},{14,30},{16,0},... | collective-permute-start | bytes 393224 | tf_op jit(solution)/shard_map/ppermute | solution.py:269
  87.9 7.3 %attend.1 = bf16[512,128]{1,0:T(8,128)(2,1)S(1)} custom-call(bf16[16,784,128]{2,1,0:T(8,128)(2,1)} %all-to-all-done.refs_0_), custom_call_target="tpu_custom_call" | custom-call | flops 2147483648 | bytes 3211264 | tf_op jit(solution)/shard_map/attend/pallas_call | solution.py:117
  95.1 0.0 collective-permute-done.7.refs_0_
  95.1 0.6 copy-done.4
  95.8 0.1 collective-permute-start.8
  95.9 6.4 %collective-permute-done.8 = bf16[512,128]{1,0:T(8,128)(2,1)S(1)} collective-permute-done((bf16[512,128]{1,0:T(8,128)(2,1)S(1)}, bf16[512,128]{1,0:T(8,128)(2,1)S(1)}, u32[]{:S(2)}, u32[]{:S(2)}) %collective-permute-start.8) | collective-permute-done | bytes 131104 | tf_op jit(solution)/shard_map/ppermute | solution.py:283
  102.4 1.1 broadcast_in_dim.4
  103.5 4.1 %all-to-all-start.1 = ((bf16[4,2,512,128]{3,2,1,0:T(8,128)(2,1)}), bf16[4,2,512,128]{3,2,1,0:T(8,128)(2,1)S(1)}, u32[]{:S(2)}, u32[]{:S(2)}) async-start(bf16[4,2,512,128]{3,2,1,0:T(8,128)(2,1)} %broadcast_in_dim.4), calls=%async_computation.1 | async-start | bytes 2097152 | tf_op jit(solution)/shard_map/all_to_all | solution.py:278
  107.7 0.1 reshape.45
  107.8 0.4 rev.7
  108.2 0.8 fusion.11
  109.1 1.2 collective-permute-start.11
  110.3 1.5 collective-permute-start.10
  111.8 0.1 broadcast_select_fusion
  111.8 0.1 copy.20
  112.0 0.6 collective-permute-start.9
  112.6 7.8 %collective-permute-done.9.ids_ref = s32[2,8,2048]{2,1,0:T(8,128)S(1)} collective-permute-done((s32[2,8,2048]{2,1,0:T(8,128)S(1)}, s32[2,8,2048]{2,1,0:T(8,128)S(1)}, u32[]{:S(2)}, u32[]{:S(2)}) %collective-permute-start.9) | collective-permute-done | bytes 131104 | tf_op jit(solution)/shard_map/ppermute | solution.py:293
  120.3 3.6 %collective-permute-done.11.refs_1_ = bf16[2,256,256]{2,1,0:T(8,128)(2,1)S(1)} collective-permute-done((bf16[2,256,256]{2,1,0:T(8,128)(2,1)}, bf16[2,256,256]{2,1,0:T(8,128)(2,1)S(1)}, u32[]{:S(2)}, u32[]{:S(2)}) %collective-permute-start.11) | collective-permute-done | bytes 262176 | tf_op jit(solution)/shard_map/ppermute | solution.py:272
  124.0 0.0 collective-permute-done.10
  124.0 2.1 %all-to-all-done.1 = bf16[4,2,512,128]{3,2,1,0:T(8,128)(2,1)S(1)} async-done(((bf16[4,2,512,128]{3,2,1,0:T(8,128)(2,1)}), bf16[4,2,512,128]{3,2,1,0:T(8,128)(2,1)S(1)}, u32[]{:S(2)}, u32[]{:S(2)}) %all-to-all-start.1) | async-done | bytes 1048608 | tf_op jit(solution)/shard_map/all_to_all | solution.py:278
  126.1 1.1 broadcast_in_dim.5
  127.2 0.0 copy-done.2
  127.2 4.0 %all-to-all-start.2 = ((bf16[4,2,512,128]{3,2,1,0:T(8,128)(2,1)}), bf16[4,2,512,128]{3,2,1,0:T(8,128)(2,1)S(1)}, u32[]{:S(2)}, u32[]{:S(2)}) async-start(bf16[4,2,512,128]{3,2,1,0:T(8,128)(2,1)} %broadcast_in_dim.5), calls=%async_computation.2 | async-start | bytes 2097152 | tf_op jit(solution)/shard_map/all_to_all | solution.py:278
  131.1 0.0 collective-permute-start.12
  131.2 1.1 collective-permute-start.13
  132.2 6.8 %expand.4.refs_0_ = bf16[32,2048,128]{2,1,0:T(8,128)(2,1)} custom-call(s32[2,8,2048]{2,1,0:T(8,128)S(1)} %reshape.46.ids_ref, bf16[8,512,128]{2,1,0:T(8,128)(2,1)S(1)} %bitcast.96), custom_call_target="tpu_custom_call" | custom-call | flops 4294967296 | bytes 5242880 | tf_op jit(solution)/shard_map/expand/pallas_call | solution.py:156
  139.1 0.0 collective-permute-done.12.attended_ref
  139.1 6.8 %expand.5.refs_0_ = bf16[32,2048,128]{2,1,0:T(8,128)(2,1)} custom-call(s32[2,8,2048]{2,1,0:T(8,128)S(1)} %reshape.46.ids_ref, bf16[8,512,128]{2,1,0:T(8,128)(2,1)S(1)} %collective-permute-done.12.attended_ref, bf16[32,2048,128]{2,1,0:T(8,128)(2,1)} %expand.4.refs_0_), custom_call_target="tpu_custom_call", output_to_operand_aliasing={{}: (2, {})} | custom-call | flops 4294967296 | bytes 5242880 | tf_op jit(solution)/shard_map/expand/pallas_call | solution.py:156
  145.9 3.7 %collective-permute-done.13.refs_2_ = bf16[3,256,256]{2,1,0:T(8,128)(2,1)S(1)} collective-permute-done((bf16[3,256,256]{2,1,0:T(8,128)(2,1)S(1)}, bf16[3,256,256]{2,1,0:T(8,128)(2,1)S(1)}, u32[]{:S(2)}, u32[]{:S(2)}) %collective-permute-start.13) | collective-permute-done | bytes 393248 | tf_op jit(solution)/shard_map/ppermute | solution.py:272
  149.6 0.7 copy-done
  150.4 1.5 all-to-all-done.2
  151.9 0.0 collective-permute-start.14
  151.9 0.1 pad_add_fusion.places_ref
  151.9 2.0 %collective-permute-start.15 = (bf16[2,256,256]{2,1,0:T(8,128)(2,1)}, bf16[2,256,256]{2,1,0:T(8,128)(2,1)S(1)}, u32[]{:S(2)}, u32[]{:S(2)}) collective-permute-start(bf16[2,256,256]{2,1,0:T(8,128)(2,1)} %get-tuple-element.39), channel_id=1, source_target_pairs={{0,16},{2,18},{4,20},{6,22},{8,24},{10,26},{12,28},{14,30},{16,0},... | collective-permute-start | bytes 786440 | tf_op jit(solution)/shard_map/ppermute | solution.py:272
  153.9 6.8 %expand.6.refs_0_ = bf16[32,2048,128]{2,1,0:T(8,128)(2,1)} custom-call(s32[2,8,2048]{2,1,0:T(8,128)S(1)} %collective-permute-done.9.ids_ref, bf16[8,512,128]{2,1,0:T(8,128)(2,1)S(1)} %bitcast.98, bf16[32,2048,128]{2,1,0:T(8,128)(2,1)} %expand.5.refs_0_), custom_call_target="tpu_custom_call", output_to_operand_aliasing={{}: (2, {})} | custom-call | flops 4294967296 | bytes 5242880 | tf_op jit(solution)/shard_map/expand/pallas_call | solution.py:156
  160.7 0.0 collective-permute-done.14.attended_ref
  160.8 6.8 %expand.7.features_ref = bf16[32,2048,128]{2,1,0:T(8,128)(2,1)} custom-call(s32[2,8,2048]{2,1,0:T(8,128)S(1)} %collective-permute-done.9.ids_ref, bf16[8,512,128]{2,1,0:T(8,128)(2,1)S(1)} %collective-permute-done.14.attended_ref, bf16[32,2048,128]{2,1,0:T(8,128)(2,1)} %expand.6.refs_0_), custom_call_target="tpu_custom_call", output_to_operand_aliasing={{}: (2, {})} | custom-call | flops 4294967296 | bytes 5242880 | tf_op jit(solution)/shard_map/expand/pallas_call | solution.py:156
  167.6 0.0 collective-permute-done.15.refs_3_
  167.6 9.0 %project.1 = bf16[2048,256]{1,0:T(8,128)(2,1)S(1)} custom-call(s32[4]{0:T(128)S(1)} %pad_add_fusion.places_ref, bf16[32,2048,128]{2,1,0:T(8,128)(2,1)} %expand.7.features_ref, bf16[8,288,256]{2,1,0:T(8,128)(2,1)S(1)} %bitcast_dynamic-update-slice_fusion.near_ref, bf16[1,256,256]{2,1,0:T(8,128)(2,1)S(1)} %copy-done.5, bf16[2,256,256]{2,1,0:T(8,128)(2,1)S(1)} %copy-done.3, ...), custom_call_target="tpu_custom_call" | custom-call | flops 4294967296 | bytes 19922944 | tf_op jit(solution)/shard_map/project/pallas_call | solution.py:199
  176.6 18.6 %all_to_all.20 = bf16[8,256,256]{2,1,0:T(8,128)(2,1)S(1)} all-to-all(bf16[8,256,256]{2,1,0:T(8,128)(2,1)S(1)} %bitcast.99), channel_id=1, replica_groups={{0,2,4,6,8,10,12,14},{16,18,20,22,24,26,28,30},{1,3,5,7,9,11,13,15},{17..., dimensions={0} | all-to-all | bytes 2097152 | tf_op jit(solution)/shard_map/all_to_all | solution.py:311
  195.2 1.1 copy.30
  (49 shorter events, 0.5 us)
Async XLA Ops:
  0.0 2.4 %copy-start.8 = (bf16[256,16,128]{2,1,0:T(8,128)(2,1)S(1)}, bf16[256,16,128]{2,1,0:T(8,128)(2,1)}, u32[]{:S(2)}) copy-start(bf16[256,16,128]{2,1,0:T(8,128)(2,1)} %param.6) | copy-start | bytes 3145732
  0.0 2.4 %copy-start.7 = (bf16[256,16,128]{2,1,0:T(8,128)(2,1)S(1)}, bf16[256,16,128]{2,1,0:T(8,128)(2,1)}, u32[]{:S(2)}) copy-start(bf16[256,16,128]{2,1,0:T(8,128)(2,1)} %param.7) | copy-start | bytes 3145732
  4.8 7.6 %copy-start.6 = (bf16[256,2048]{1,0:T(8,128)(2,1)S(1)}, bf16[256,2048]{1,0:T(8,128)(2,1)}, u32[]{:S(2)}) copy-start(bf16[256,2048]{1,0:T(8,128)(2,1)} %param.9) | copy-start | bytes 3145732
  4.8 75.5 %all-to-all-start = ((bf16[16,784,128]{2,1,0:T(8,128)(2,1)}), bf16[16,784,128]{2,1,0:T(8,128)(2,1)}, u32[]{:S(2)}, u32[]{:S(2)}) async-start(bf16[16,784,128]{2,1,0:T(8,128)(2,1)} %pad_maximum_fusion), calls=%async_computation | async-start | bytes 6422528 | tf_op jit(solution)/shard_map/all_to_all | solution.py:257
  15.2 5.1 %collective-permute-start = (bf16[288,256]{1,0:T(8,128)(2,1)S(1)}, bf16[288,256]{1,0:T(8,128)(2,1)S(1)}, u32[]{:S(2)}, u32[]{:S(2)}) collective-permute-start(bf16[288,256]{1,0:T(8,128)(2,1)S(1)} %get-tuple-element.50), channel_id=1, source_target_pairs={{0,2},{2,0},{4,6},{6,4},{8,10},{10,8},{12,14},{14,12},{16,18},{18,... | collective-permute-start | bytes 442376 | tf_op jit(solution)/shard_map/ppermute | solution.py:265
  15.7 60.2 %collective-permute-start.5 = (bf16[288,256]{1,0:T(8,128)(2,1)S(1)}, bf16[288,256]{1,0:T(8,128)(2,1)S(1)}, u32[]{:S(2)}, u32[]{:S(2)}) collective-permute-start(bf16[288,256]{1,0:T(8,128)(2,1)S(1)} %pad_maximum_fusion.2), channel_id=1, source_target_pairs={{0,12},{2,14},{4,8},{6,10},{8,4},{10,6},{12,0},{14,2},{16,28},{18,... | collective-permute-start | bytes 442376 | tf_op jit(solution)/shard_map/ppermute | solution.py:265
  18.3 19.0 %collective-permute-start.1 = (bf16[288,256]{1,0:T(8,128)(2,1)S(1)}, bf16[288,256]{1,0:T(8,128)(2,1)S(1)}, u32[]{:S(2)}, u32[]{:S(2)}) collective-permute-start(bf16[288,256]{1,0:T(8,128)(2,1)S(1)} %get-tuple-element.51), channel_id=1, source_target_pairs={{0,4},{2,6},{4,0},{6,2},{8,12},{10,14},{12,8},{14,10},{16,20},{18,... | collective-permute-start | bytes 442376 | tf_op jit(solution)/shard_map/ppermute | solution.py:265
  18.9 25.9 %collective-permute-start.2 = (bf16[288,256]{1,0:T(8,128)(2,1)S(1)}, bf16[288,256]{1,0:T(8,128)(2,1)S(1)}, u32[]{:S(2)}, u32[]{:S(2)}) collective-permute-start(bf16[288,256]{1,0:T(8,128)(2,1)S(1)} %get-tuple-element.52), channel_id=1, source_target_pairs={{0,6},{2,4},{4,2},{6,0},{8,14},{10,12},{12,10},{14,8},{16,22},{18,... | collective-permute-start | bytes 442376 | tf_op jit(solution)/shard_map/ppermute | solution.py:265
  19.7 53.0 %collective-permute-start.3 = (bf16[288,256]{1,0:T(8,128)(2,1)S(1)}, bf16[288,256]{1,0:T(8,128)(2,1)S(1)}, u32[]{:S(2)}, u32[]{:S(2)}) collective-permute-start(bf16[288,256]{1,0:T(8,128)(2,1)S(1)} %get-tuple-element.53), channel_id=1, source_target_pairs={{0,8},{2,10},{4,12},{6,14},{8,0},{10,2},{12,4},{14,6},{16,24},{18,... | collective-permute-start | bytes 442376 | tf_op jit(solution)/shard_map/ppermute | solution.py:265
  20.4 55.5 %collective-permute-start.4 = (bf16[288,256]{1,0:T(8,128)(2,1)S(1)}, bf16[288,256]{1,0:T(8,128)(2,1)S(1)}, u32[]{:S(2)}, u32[]{:S(2)}) collective-permute-start(bf16[288,256]{1,0:T(8,128)(2,1)S(1)} %get-tuple-element.54), channel_id=1, source_target_pairs={{0,10},{2,8},{4,14},{6,12},{8,2},{10,0},{12,6},{14,4},{16,26},{18,... | collective-permute-start | bytes 442376 | tf_op jit(solution)/shard_map/ppermute | solution.py:265
  37.3 43.0 %collective-permute-start.6 = (bf16[288,256]{1,0:T(8,128)(2,1)S(1)}, bf16[288,256]{1,0:T(8,128)(2,1)S(1)}, u32[]{:S(2)}, u32[]{:S(2)}) collective-permute-start(bf16[288,256]{1,0:T(8,128)(2,1)S(1)} %get-tuple-element.49), channel_id=1, source_target_pairs={{0,14},{2,12},{4,10},{6,8},{8,6},{10,4},{12,2},{14,0},{16,30},{18,... | collective-permute-start | bytes 442376 | tf_op jit(solution)/shard_map/ppermute | solution.py:265
  80.4 14.7 %collective-permute-start.7 = (bf16[1,256,256]{2,1,0:T(8,128)(2,1)S(1)}, bf16[1,256,256]{2,1,0:T(8,128)(2,1)S(1)}, u32[]{:S(2)}, u32[]{:S(2)}) collective-permute-start(bf16[1,256,256]{2,1,0:T(8,128)(2,1)S(1)} %slice.21), channel_id=1, source_target_pairs={{0,16},{2,18},{4,20},{6,22},{8,24},{10,26},{12,28},{14,30},{16,0},... | collective-permute-start | bytes 393224 | tf_op jit(solution)/shard_map/ppermute | solution.py:269
  95.1 0.7 copy-start.4
  95.8 6.5 %collective-permute-start.8 = (bf16[512,128]{1,0:T(8,128)(2,1)S(1)}, bf16[512,128]{1,0:T(8,128)(2,1)S(1)}, u32[]{:S(2)}, u32[]{:S(2)}) collective-permute-start(bf16[512,128]{1,0:T(8,128)(2,1)S(1)} %attend.1), channel_id=1, source_target_pairs={{0,16},{2,18},{4,20},{6,22},{8,24},{10,26},{12,28},{14,30},{16,0},... | collective-permute-start | bytes 393224 | tf_op jit(solution)/shard_map/ppermute | solution.py:283
  103.5 22.6 %all-to-all-start.1 = ((bf16[4,2,512,128]{3,2,1,0:T(8,128)(2,1)}), bf16[4,2,512,128]{3,2,1,0:T(8,128)(2,1)S(1)}, u32[]{:S(2)}, u32[]{:S(2)}) async-start(bf16[4,2,512,128]{3,2,1,0:T(8,128)(2,1)} %broadcast_in_dim.4), calls=%async_computation.1 | async-start | bytes 2097152 | tf_op jit(solution)/shard_map/all_to_all | solution.py:278
  109.1 14.9 %collective-permute-start.11 = (bf16[2,256,256]{2,1,0:T(8,128)(2,1)}, bf16[2,256,256]{2,1,0:T(8,128)(2,1)S(1)}, u32[]{:S(2)}, u32[]{:S(2)}) collective-permute-start(bf16[2,256,256]{2,1,0:T(8,128)(2,1)} %get-tuple-element.40), channel_id=1, source_target_pairs={{0,16},{2,18},{4,20},{6,22},{8,24},{10,26},{12,28},{14,30},{16,0},... | collective-permute-start | bytes 786440 | tf_op jit(solution)/shard_map/ppermute | solution.py:272
  110.3 13.7 %collective-permute-start.10 = (bf16[2,512,128]{2,1,0:T(8,128)(2,1)S(1)}, bf16[2,512,128]{2,1,0:T(8,128)(2,1)S(1)}, u32[]{:S(2)}, u32[]{:S(2)}) collective-permute-start(bf16[2,512,128]{2,1,0:T(8,128)(2,1)S(1)} %pad_maximum_fusion.17), channel_id=1, source_target_pairs={{0,1},{1,0},{2,3},{3,2},{4,5},{5,4},{6,7},{7,6},{8,9},{9,8},{10,11... | collective-permute-start | bytes 786440 | tf_op jit(solution)/shard_map/ppermute | solution.py:284
  112.0 8.4 %collective-permute-start.9 = (s32[2,8,2048]{2,1,0:T(8,128)S(1)}, s32[2,8,2048]{2,1,0:T(8,128)S(1)}, u32[]{:S(2)}, u32[]{:S(2)}) collective-permute-start(s32[2,8,2048]{2,1,0:T(8,128)S(1)} %reshape.46.ids_ref), channel_id=1, source_target_pairs={{0,1},{1,0},{2,3},{3,2},{4,5},{5,4},{6,7},{7,6},{8,9},{9,8},{10,11... | collective-permute-start | bytes 393224 | tf_op jit(solution)/shard_map/ppermute | solution.py:293
  124.0 3.2 %copy-start.2 = (bf16[2,256,256]{2,1,0:T(8,128)(2,1)}, bf16[2,256,256]{2,1,0:T(8,128)(2,1)S(1)}, u32[]{:S(2)}) copy-start(bf16[2,256,256]{2,1,0:T(8,128)(2,1)S(1)} %collective-permute-done.11.refs_1_) | copy-start | bytes 786436
  127.2 24.7 %all-to-all-start.2 = ((bf16[4,2,512,128]{3,2,1,0:T(8,128)(2,1)}), bf16[4,2,512,128]{3,2,1,0:T(8,128)(2,1)S(1)}, u32[]{:S(2)}, u32[]{:S(2)}) async-start(bf16[4,2,512,128]{3,2,1,0:T(8,128)(2,1)} %broadcast_in_dim.5), calls=%async_computation.2 | async-start | bytes 2097152 | tf_op jit(solution)/shard_map/all_to_all | solution.py:278
  131.1 8.0 %collective-permute-start.12 = (bf16[8,512,128]{2,1,0:T(8,128)(2,1)S(1)}, bf16[8,512,128]{2,1,0:T(8,128)(2,1)S(1)}, u32[]{:S(2)}, u32[]{:S(2)}) collective-permute-start(bf16[8,512,128]{2,1,0:T(8,128)(2,1)S(1)} %bitcast.95), channel_id=1, source_target_pairs={{0,2},{2,0},{4,6},{6,4},{8,10},{10,8},{12,14},{14,12},{16,18},{18,... | collective-permute-start | bytes 3145736 | tf_op jit(solution)/shard_map/ppermute | solution.py:298
  131.2 18.5 %collective-permute-start.13 = (bf16[3,256,256]{2,1,0:T(8,128)(2,1)S(1)}, bf16[3,256,256]{2,1,0:T(8,128)(2,1)S(1)}, u32[]{:S(2)}, u32[]{:S(2)}) collective-permute-start(bf16[3,256,256]{2,1,0:T(8,128)(2,1)S(1)} %slice.26), channel_id=1, source_target_pairs={{0,16},{2,18},{4,20},{6,22},{8,24},{10,26},{12,28},{14,30},{16,0},... | collective-permute-start | bytes 1179656 | tf_op jit(solution)/shard_map/ppermute | solution.py:272
  149.6 0.7 copy-start
  151.9 8.9 %collective-permute-start.14 = (bf16[8,512,128]{2,1,0:T(8,128)(2,1)S(1)}, bf16[8,512,128]{2,1,0:T(8,128)(2,1)S(1)}, u32[]{:S(2)}, u32[]{:S(2)}) collective-permute-start(bf16[8,512,128]{2,1,0:T(8,128)(2,1)S(1)} %bitcast.97), channel_id=1, source_target_pairs={{0,2},{2,0},{4,6},{6,4},{8,10},{10,8},{12,14},{14,12},{16,18},{18,... | collective-permute-start | bytes 3145736 | tf_op jit(solution)/shard_map/ppermute | solution.py:306
  151.9 15.7 %collective-permute-start.15 = (bf16[2,256,256]{2,1,0:T(8,128)(2,1)}, bf16[2,256,256]{2,1,0:T(8,128)(2,1)S(1)}, u32[]{:S(2)}, u32[]{:S(2)}) collective-permute-start(bf16[2,256,256]{2,1,0:T(8,128)(2,1)} %get-tuple-element.39), channel_id=1, source_target_pairs={{0,16},{2,18},{4,20},{6,22},{8,24},{10,26},{12,28},{14,30},{16,0},... | collective-permute-start | bytes 786440 | tf_op jit(solution)/shard_map/ppermute | solution.py:272
  160.7 6.9 %copy-start.1 = (bf16[3,256,256]{2,1,0:T(8,128)(2,1)S(1)}, bf16[3,256,256]{2,1,0:T(8,128)(2,1)}, u32[]{:S(2)}) copy-start(bf16[3,256,256]{2,1,0:T(8,128)(2,1)} %copy-done) | copy-start | bytes 1179652
  160.7 6.9 %copy-start.3 = (bf16[2,256,256]{2,1,0:T(8,128)(2,1)S(1)}, bf16[2,256,256]{2,1,0:T(8,128)(2,1)}, u32[]{:S(2)}) copy-start(bf16[2,256,256]{2,1,0:T(8,128)(2,1)} %copy-done.2) | copy-start | bytes 786436
  160.7 6.9 %copy-start.5 = (bf16[1,256,256]{2,1,0:T(8,128)(2,1)S(1)}, bf16[1,256,256]{2,1,0:T(8,128)(2,1)}, u32[]{:S(2)}) copy-start(bf16[1,256,256]{2,1,0:T(8,128)(2,1)} %copy-done.4) | copy-start | bytes 393220

commit v15 on v13

--- a/solution.py
+++ b/solution.py
@@ -234,10 +234,8 @@
     id_rows = -(-2 * tok_rows // (16 * e_width)) * 16
     coded = jnp.concatenate([high, low], axis=1)
     coded = jnp.pad(coded, ((0, 0), (0, id_rows * e_width - 2 * tok_rows)))
-    packed = jnp.concatenate(
-        [x.transpose(1, 0, 2) for x in (queries, keys, values)] + [coded.reshape(head_count, id_rows, e_width)],
-        axis=1,
-    )
+    coded = coded.reshape(head_count, id_rows, e_width).transpose(1, 0, 2)
+    packed = jnp.concatenate([queries, keys, values, coded], axis=0).transpose(1, 0, 2)
     packed, out_weight, high, low = lax.optimization_barrier((packed, out_weight, high, low))
     moved = lax.all_to_all(packed, "seq", split_axis=0, concat_axis=0, tiled=True)
 

time: 197 us -> 197 us (level)
    unnamed x42 -> x38, local copies, waits for them, and re-layouts: 3.48 us -> 4.84 us
  transfers between devices with their start and end apart: 19 -> 19, of which waited for: 11 -> 11; matrix products, arithmetic and copies ran while one was open for 2% -> 2% of each run, Pallas kernels for 18% -> 17%
where the time goes in v15:
time: 197 us
  waiting for transfers between devices  83.5 us (42%)
  Pallas kernels  43.3 us (22%)
  starting transfers between devices  36.1 us (18%)
  blocking collectives  18.6 us (9%)
  local copies, waits for them, and re-layouts  11.9 us (6%)
  other arithmetic  3.02 us (2%)
    ppermute x7, waiting for transfers between devices, by_head(): lax.ppermute(block, 'seq', [(i, i ^ k) for i in range(n_seq)])  58.3 us
    pallas_call x4, Pallas kernels, expand(): pl.pallas_call(expand_kernel, out_shape=jax.ShapeDtypeStruct((pieces * he...  27.3 us
    all_to_all x1, blocking collectives, by_head(): lax.all_to_all(near_out.reshape(half, tok_rows, cols_each), 'seq', split_...  18.6 us
    ppermute x4, starting transfers between devices, by_head(): lax.ppermute(near[a:b, :rows], 'seq', swap_halves)  11.7 us
    pallas_call x1, Pallas kernels, project(): pl.pallas_call(project_kernel, out_shape=jax.ShapeDtypeStruct((tokens, co...  8.98 us
    all_to_all x2, starting transfers between devices, spread(): lax.all_to_all(copies, 'seq', split_axis=0, concat_axis=0, axis_index_gro...  8.1 us
    ppermute x1, waiting for transfers between devices, by_head(): far_ids = lax.ppermute(slot_ids, 'head', swap_heads)  7.78 us
    all_to_all x1, starting transfers between devices, by_head(): lax.all_to_all(packed, 'seq', split_axis=0, concat_axis=0, tiled=True)  7.56 us
  transfers between devices with their start and end apart: 19, of which 11 were waited for; matrix products, arithmetic and copies ran while one was open for 2% of the time, Pallas kernels for 17%

profile of v15, /device:TPU:0, one launch (start us, length us, event | category | flops | bytes accessed | tf_op | source)
XLA Modules:
  0.0 196.9 jit_solution(2612043292055053759)
XLA Ops:
  0.0 0.8 fusion.6
  0.9 1.5 copy.10
  2.4 0.0 copy-start.7
  2.4 0.3 copy.11
  2.7 0.9 copy-done.7
  3.6 0.3 copy.9
  3.9 1.8 maximum_bitcast_fusion
  5.7 7.6 %all-to-all-start = ((bf16[16,784,128]{2,1,0:T(8,128)(2,1)}), bf16[16,784,128]{2,1,0:T(8,128)(2,1)}, u32[]{:S(2)}, u32[]{:S(2)}) async-start(bf16[16,784,128]{2,1,0:T(8,128)(2,1)} %maximum_bitcast_fusion), calls=%async_computation | async-start | bytes 6422528 | tf_op jit(solution)/shard_map/all_to_all | solution.py:240
  13.3 0.3 copy.32
  13.7 2.2 %constant_dynamic-slice_fusion = (bf16[256,1,256]{2,1,0:T(2,128)(2,1)S(1)}, bf16[256,1,256]{2,1,0:T(2,128)(2,1)S(1)}, bf16[256,1,256]{2,1,0:T(2,128)(2,1)S(1)}, ...) fusion(bf16[256,8,256]{2,1,0:T(8,128)(2,1)S(1)} %bitcast.92, ...), kind=kLoop, calls=%fused_computation.65 | loop fusion | bytes 2097184 | tf_op jit(solution)/shard_map/dynamic-slice.7
  16.0 0.1 pad_maximum_fusion
  16.1 0.4 collective-permute-start
  16.5 2.6 %collective-permute-start.5 = (bf16[288,256]{1,0:T(8,128)(2,1)S(1)}, bf16[288,256]{1,0:T(8,128)(2,1)S(1)}, u32[]{:S(2)}, u32[]{:S(2)}) collective-permute-start(bf16[288,256]{1,0:T(8,128)(2,1)S(1)} %pad_maximum_fusion.1), channel_id=1, source_target_pairs={{0,12},{2,14},{4,8},{6,10},{8,4},{10,6},{12,0},{14,2},{16,28},{18,... | collective-permute-start | bytes 442376 | tf_op jit(solution)/shard_map/ppermute | solution.py:248
  19.2 0.6 collective-permute-start.1
  19.7 0.9 collective-permute-start.2
  20.6 0.6 collective-permute-start.3
  21.2 0.0 collective-permute-done
  21.2 1.6 collective-permute-start.4
  22.8 15.4 %collective-permute-done.1 = bf16[288,256]{1,0:T(8,128)(2,1)S(1)} collective-permute-done((bf16[288,256]{1,0:T(8,128)(2,1)S(1)}, bf16[288,256]{1,0:T(8,128)(2,1)S(1)}, u32[]{:S(2)}, u32[]{:S(2)}) %collective-permute-start.1) | collective-permute-done | bytes 147488 | tf_op jit(solution)/shard_map/ppermute | solution.py:248
  38.2 0.0 collective-permute-start.6
  38.2 7.4 %collective-permute-done.2 = bf16[288,256]{1,0:T(8,128)(2,1)S(1)} collective-permute-done((bf16[288,256]{1,0:T(8,128)(2,1)S(1)}, bf16[288,256]{1,0:T(8,128)(2,1)S(1)}, u32[]{:S(2)}, u32[]{:S(2)}) %collective-permute-start.2) | collective-permute-done | bytes 147488 | tf_op jit(solution)/shard_map/ppermute | solution.py:248
  45.7 27.9 %collective-permute-done.3 = bf16[288,256]{1,0:T(8,128)(2,1)S(1)} collective-permute-done((bf16[288,256]{1,0:T(8,128)(2,1)S(1)}, bf16[288,256]{1,0:T(8,128)(2,1)S(1)}, u32[]{:S(2)}, u32[]{:S(2)}) %collective-permute-start.3) | collective-permute-done | bytes 147488 | tf_op jit(solution)/shard_map/ppermute | solution.py:248
  73.6 3.1 %collective-permute-done.4 = bf16[288,256]{1,0:T(8,128)(2,1)S(1)} collective-permute-done((bf16[288,256]{1,0:T(8,128)(2,1)S(1)}, bf16[288,256]{1,0:T(8,128)(2,1)S(1)}, u32[]{:S(2)}, u32[]{:S(2)}) %collective-permute-start.4) | collective-permute-done | bytes 147488 | tf_op jit(solution)/shard_map/ppermute | solution.py:248
  76.7 0.0 collective-permute-done.5
  76.8 4.5 %collective-permute-done.6 = bf16[288,256]{1,0:T(8,128)(2,1)S(1)} collective-permute-done((bf16[288,256]{1,0:T(8,128)(2,1)S(1)}, bf16[288,256]{1,0:T(8,128)(2,1)S(1)}, u32[]{:S(2)}, u32[]{:S(2)}) %collective-permute-start.6) | collective-permute-done | bytes 147488 | tf_op jit(solution)/shard_map/ppermute | solution.py:248
  81.2 0.0 all-to-all-done.refs_0_
  81.3 7.5 %collective-permute-start.7 = (bf16[1,256,256]{2,1,0:T(8,128)(2,1)S(1)}, bf16[1,256,256]{2,1,0:T(8,128)(2,1)S(1)}, u32[]{:S(2)}, u32[]{:S(2)}) collective-permute-start(bf16[1,256,256]{2,1,0:T(8,128)(2,1)S(1)} %slice.21), channel_id=1, source_target_pairs={{0,16},{2,18},{4,20},{6,22},{8,24},{10,26},{12,28},{14,30},{16,0},... | collective-permute-start | bytes 393224 | tf_op jit(solution)/shard_map/ppermute | solution.py:252
  88.7 7.0 %attend.1 = bf16[512,128]{1,0:T(8,128)(2,1)S(1)} custom-call(bf16[16,784,128]{2,1,0:T(8,128)(2,1)} %all-to-all-done.refs_0_), custom_call_target="tpu_custom_call" | custom-call | flops 2147483648 | bytes 3211264 | tf_op jit(solution)/shard_map/attend/pallas_call | solution.py:104
  95.7 0.0 collective-permute-done.7.refs_0_
  95.8 0.6 copy-done.4
  96.4 0.1 collective-permute-start.8
  96.5 6.4 %collective-permute-done.8 = bf16[512,128]{1,0:T(8,128)(2,1)S(1)} collective-permute-done((bf16[512,128]{1,0:T(8,128)(2,1)S(1)}, bf16[512,128]{1,0:T(8,128)(2,1)S(1)}, u32[]{:S(2)}, u32[]{:S(2)}) %collective-permute-start.8) | collective-permute-done | bytes 131104 | tf_op jit(solution)/shard_map/ppermute | solution.py:266
  103.0 1.1 broadcast_in_dim.4
  104.1 4.1 %all-to-all-start.1 = ((bf16[4,2,512,128]{3,2,1,0:T(8,128)(2,1)}), bf16[4,2,512,128]{3,2,1,0:T(8,128)(2,1)S(1)}, u32[]{:S(2)}, u32[]{:S(2)}) async-start(bf16[4,2,512,128]{3,2,1,0:T(8,128)(2,1)} %broadcast_in_dim.4), calls=%async_computation.1 | async-start | bytes 2097152 | tf_op jit(solution)/shard_map/all_to_all | solution.py:261
  108.3 0.1 reshape.45
  108.5 0.4 rev.7
  108.9 0.8 fusion.11
  109.7 1.2 collective-permute-start.11
  110.9 1.5 collective-permute-start.10
  112.4 0.1 broadcast_select_fusion
  112.5 0.1 copy.20
  112.6 0.6 collective-permute-start.9
  113.2 7.8 %collective-permute-done.9.ids_ref = s32[2,8,2048]{2,1,0:T(8,128)S(1)} collective-permute-done((s32[2,8,2048]{2,1,0:T(8,128)S(1)}, s32[2,8,2048]{2,1,0:T(8,128)S(1)}, u32[]{:S(2)}, u32[]{:S(2)}) %collective-permute-start.9) | collective-permute-done | bytes 131104 | tf_op jit(solution)/shard_map/ppermute | solution.py:276
  121.0 3.6 %collective-permute-done.11.refs_1_ = bf16[2,256,256]{2,1,0:T(8,128)(2,1)S(1)} collective-permute-done((bf16[2,256,256]{2,1,0:T(8,128)(2,1)}, bf16[2,256,256]{2,1,0:T(8,128)(2,1)S(1)}, u32[]{:S(2)}, u32[]{:S(2)}) %collective-permute-start.11) | collective-permute-done | bytes 262176 | tf_op jit(solution)/shard_map/ppermute | solution.py:255
  124.6 0.0 collective-permute-done.10
  124.6 2.1 %all-to-all-done.1 = bf16[4,2,512,128]{3,2,1,0:T(8,128)(2,1)S(1)} async-done(((bf16[4,2,512,128]{3,2,1,0:T(8,128)(2,1)}), bf16[4,2,512,128]{3,2,1,0:T(8,128)(2,1)S(1)}, u32[]{:S(2)}, u32[]{:S(2)}) %all-to-all-start.1) | async-done | bytes 1048608 | tf_op jit(solution)/shard_map/all_to_all | solution.py:261
  126.7 1.1 broadcast_in_dim.5
  127.8 4.0 %all-to-all-start.2 = ((bf16[4,2,512,128]{3,2,1,0:T(8,128)(2,1)}), bf16[4,2,512,128]{3,2,1,0:T(8,128)(2,1)S(1)}, u32[]{:S(2)}, u32[]{:S(2)}) async-start(bf16[4,2,512,128]{3,2,1,0:T(8,128)(2,1)} %broadcast_in_dim.5), calls=%async_computation.2 | async-start | bytes 2097152 | tf_op jit(solution)/shard_map/all_to_all | solution.py:261
  131.7 0.0 collective-permute-start.12
  131.8 1.1 collective-permute-start.13
  132.8 6.8 %expand.4.refs_0_ = bf16[32,2048,128]{2,1,0:T(8,128)(2,1)} custom-call(s32[2,8,2048]{2,1,0:T(8,128)S(1)} %reshape.46.ids_ref, bf16[8,512,128]{2,1,0:T(8,128)(2,1)S(1)} %bitcast.87), custom_call_target="tpu_custom_call" | custom-call | flops 4294967296 | bytes 5242880 | tf_op jit(solution)/shard_map/expand/pallas_call | solution.py:141
  139.6 6.8 %expand.5.refs_0_ = bf16[32,2048,128]{2,1,0:T(8,128)(2,1)} custom-call(s32[2,8,2048]{2,1,0:T(8,128)S(1)} %reshape.46.ids_ref, bf16[8,512,128]{2,1,0:T(8,128)(2,1)S(1)} %collective-permute-done.12.attended_ref, bf16[32,2048,128]{2,1,0:T(8,128)(2,1)} %expand.4.refs_0_), custom_call_target="tpu_custom_call", output_to_operand_aliasing={{}: (2, {})} | custom-call | flops 4294967296 | bytes 5242880 | tf_op jit(solution)/shard_map/expand/pallas_call | solution.py:141
  146.5 3.8 %collective-permute-done.13.refs_2_ = bf16[3,256,256]{2,1,0:T(8,128)(2,1)S(1)} collective-permute-done((bf16[3,256,256]{2,1,0:T(8,128)(2,1)S(1)}, bf16[3,256,256]{2,1,0:T(8,128)(2,1)S(1)}, u32[]{:S(2)}, u32[]{:S(2)}) %collective-permute-start.13) | collective-permute-done | bytes 393248 | tf_op jit(solution)/shard_map/ppermute | solution.py:255
  150.3 0.7 copy-done
  151.0 1.5 all-to-all-done.2
  152.5 0.1 pad_add_fusion.places_ref
  152.6 2.0 %collective-permute-start.15 = (bf16[2,256,256]{2,1,0:T(8,128)(2,1)}, bf16[2,256,256]{2,1,0:T(8,128)(2,1)S(1)}, u32[]{:S(2)}, u32[]{:S(2)}) collective-permute-start(bf16[2,256,256]{2,1,0:T(8,128)(2,1)} %get-tuple-element.39), channel_id=1, source_target_pairs={{0,16},{2,18},{4,20},{6,22},{8,24},{10,26},{12,28},{14,30},{16,0},... | collective-permute-start | bytes 786440 | tf_op jit(solution)/shard_map/ppermute | solution.py:255
  154.5 6.8 %expand.6.refs_0_ = bf16[32,2048,128]{2,1,0:T(8,128)(2,1)} custom-call(s32[2,8,2048]{2,1,0:T(8,128)S(1)} %collective-permute-done.9.ids_ref, bf16[8,512,128]{2,1,0:T(8,128)(2,1)S(1)} %bitcast.89, bf16[32,2048,128]{2,1,0:T(8,128)(2,1)} %expand.5.refs_0_), custom_call_target="tpu_custom_call", output_to_operand_aliasing={{}: (2, {})} | custom-call | flops 4294967296 | bytes 5242880 | tf_op jit(solution)/shard_map/expand/pallas_call | solution.py:141
  161.4 0.0 collective-permute-done.14.attended_ref
  161.4 6.8 %expand.7.features_ref = bf16[32,2048,128]{2,1,0:T(8,128)(2,1)} custom-call(s32[2,8,2048]{2,1,0:T(8,128)S(1)} %collective-permute-done.9.ids_ref, bf16[8,512,128]{2,1,0:T(8,128)(2,1)S(1)} %collective-permute-done.14.attended_ref, bf16[32,2048,128]{2,1,0:T(8,128)(2,1)} %expand.6.refs_0_), custom_call_target="tpu_custom_call", output_to_operand_aliasing={{}: (2, {})} | custom-call | flops 4294967296 | bytes 5242880 | tf_op jit(solution)/shard_map/expand/pallas_call | solution.py:141
  168.2 0.0 collective-permute-done.15.refs_3_
  168.2 9.0 %project.1 = bf16[2048,256]{1,0:T(8,128)(2,1)S(1)} custom-call(s32[4]{0:T(128)S(1)} %pad_add_fusion.places_ref, bf16[32,2048,128]{2,1,0:T(8,128)(2,1)} %expand.7.features_ref, bf16[8,288,256]{2,1,0:T(8,128)(2,1)S(1)} %bitcast_dynamic-update-slice_fusion.near_ref, bf16[1,256,256]{2,1,0:T(8,128)(2,1)S(1)} %copy-done.5, bf16[2,256,256]{2,1,0:T(8,128)(2,1)S(1)} %copy-done.3, ...), custom_call_target="tpu_custom_call" | custom-call | flops 4294967296 | bytes 19922944 | tf_op jit(solution)/shard_map/project/pallas_call | solution.py:184
  177.2 18.6 %all_to_all.20 = bf16[8,256,256]{2,1,0:T(8,128)(2,1)S(1)} all-to-all(bf16[8,256,256]{2,1,0:T(8,128)(2,1)S(1)} %bitcast.90), channel_id=1, replica_groups={{0,2,4,6,8,10,12,14},{16,18,20,22,24,26,28,30},{1,3,5,7,9,11,13,15},{17..., dimensions={0} | all-to-all | bytes 2097152 | tf_op jit(solution)/shard_map/all_to_all | solution.py:294
  195.8 1.1 copy.30
  (47 shorter events, 0.6 us)
Async XLA Ops:
  0.0 2.4 %copy-start.6 = (bf16[256,16,128]{2,1,0:T(8,128)(2,1)S(1)}, bf16[256,16,128]{2,1,0:T(8,128)(2,1)}, u32[]{:S(2)}) copy-start(bf16[256,16,128]{2,1,0:T(8,128)(2,1)} %param.7) | copy-start | bytes 3145732
  2.4 1.2 copy-start.7
  5.7 7.6 %copy-start.8 = (bf16[256,2048]{1,0:T(8,128)(2,1)S(1)}, bf16[256,2048]{1,0:T(8,128)(2,1)}, u32[]{:S(2)}) copy-start(bf16[256,2048]{1,0:T(8,128)(2,1)} %param.9) | copy-start | bytes 3145732
  5.7 75.5 %all-to-all-start = ((bf16[16,784,128]{2,1,0:T(8,128)(2,1)}), bf16[16,784,128]{2,1,0:T(8,128)(2,1)}, u32[]{:S(2)}, u32[]{:S(2)}) async-start(bf16[16,784,128]{2,1,0:T(8,128)(2,1)} %maximum_bitcast_fusion), calls=%async_computation | async-start | bytes 6422528 | tf_op jit(solution)/shard_map/all_to_all | solution.py:240
  16.1 5.1 %collective-permute-start = (bf16[288,256]{1,0:T(8,128)(2,1)S(1)}, bf16[288,256]{1,0:T(8,128)(2,1)S(1)}, u32[]{:S(2)}, u32[]{:S(2)}) collective-permute-start(bf16[288,256]{1,0:T(8,128)(2,1)S(1)} %get-tuple-element.50), channel_id=1, source_target_pairs={{0,2},{2,0},{4,6},{6,4},{8,10},{10,8},{12,14},{14,12},{16,18},{18,... | collective-permute-start | bytes 442376 | tf_op jit(solution)/shard_map/ppermute | solution.py:248
  16.5 60.2 %collective-permute-start.5 = (bf16[288,256]{1,0:T(8,128)(2,1)S(1)}, bf16[288,256]{1,0:T(8,128)(2,1)S(1)}, u32[]{:S(2)}, u32[]{:S(2)}) collective-permute-start(bf16[288,256]{1,0:T(8,128)(2,1)S(1)} %pad_maximum_fusion.1), channel_id=1, source_target_pairs={{0,12},{2,14},{4,8},{6,10},{8,4},{10,6},{12,0},{14,2},{16,28},{18,... | collective-permute-start | bytes 442376 | tf_op jit(solution)/shard_map/ppermute | solution.py:248
  19.2 19.1 %collective-permute-start.1 = (bf16[288,256]{1,0:T(8,128)(2,1)S(1)}, bf16[288,256]{1,0:T(8,128)(2,1)S(1)}, u32[]{:S(2)}, u32[]{:S(2)}) collective-permute-start(bf16[288,256]{1,0:T(8,128)(2,1)S(1)} %get-tuple-element.51), channel_id=1, source_target_pairs={{0,4},{2,6},{4,0},{6,2},{8,12},{10,14},{12,8},{14,10},{16,20},{18,... | collective-permute-start | bytes 442376 | tf_op jit(solution)/shard_map/ppermute | solution.py:248
  19.7 25.9 %collective-permute-start.2 = (bf16[288,256]{1,0:T(8,128)(2,1)S(1)}, bf16[288,256]{1,0:T(8,128)(2,1)S(1)}, u32[]{:S(2)}, u32[]{:S(2)}) collective-permute-start(bf16[288,256]{1,0:T(8,128)(2,1)S(1)} %get-tuple-element.52), channel_id=1, source_target_pairs={{0,6},{2,4},{4,2},{6,0},{8,14},{10,12},{12,10},{14,8},{16,22},{18,... | collective-permute-start | bytes 442376 | tf_op jit(solution)/shard_map/ppermute | solution.py:248
  20.6 53.0 %collective-permute-start.3 = (bf16[288,256]{1,0:T(8,128)(2,1)S(1)}, bf16[288,256]{1,0:T(8,128)(2,1)S(1)}, u32[]{:S(2)}, u32[]{:S(2)}) collective-permute-start(bf16[288,256]{1,0:T(8,128)(2,1)S(1)} %get-tuple-element.53), channel_id=1, source_target_pairs={{0,8},{2,10},{4,12},{6,14},{8,0},{10,2},{12,4},{14,6},{16,24},{18,... | collective-permute-start | bytes 442376 | tf_op jit(solution)/shard_map/ppermute | solution.py:248
  21.2 55.5 %collective-permute-start.4 = (bf16[288,256]{1,0:T(8,128)(2,1)S(1)}, bf16[288,256]{1,0:T(8,128)(2,1)S(1)}, u32[]{:S(2)}, u32[]{:S(2)}) collective-permute-start(bf16[288,256]{1,0:T(8,128)(2,1)S(1)} %get-tuple-element.54), channel_id=1, source_target_pairs={{0,10},{2,8},{4,14},{6,12},{8,2},{10,0},{12,6},{14,4},{16,26},{18,... | collective-permute-start | bytes 442376 | tf_op jit(solution)/shard_map/ppermute | solution.py:248
  38.2 43.0 %collective-permute-start.6 = (bf16[288,256]{1,0:T(8,128)(2,1)S(1)}, bf16[288,256]{1,0:T(8,128)(2,1)S(1)}, u32[]{:S(2)}, u32[]{:S(2)}) collective-permute-start(bf16[288,256]{1,0:T(8,128)(2,1)S(1)} %get-tuple-element.49), channel_id=1, source_target_pairs={{0,14},{2,12},{4,10},{6,8},{8,6},{10,4},{12,2},{14,0},{16,30},{18,... | collective-permute-start | bytes 442376 | tf_op jit(solution)/shard_map/ppermute | solution.py:248
  81.3 14.5 %collective-permute-start.7 = (bf16[1,256,256]{2,1,0:T(8,128)(2,1)S(1)}, bf16[1,256,256]{2,1,0:T(8,128)(2,1)S(1)}, u32[]{:S(2)}, u32[]{:S(2)}) collective-permute-start(bf16[1,256,256]{2,1,0:T(8,128)(2,1)S(1)} %slice.21), channel_id=1, source_target_pairs={{0,16},{2,18},{4,20},{6,22},{8,24},{10,26},{12,28},{14,30},{16,0},... | collective-permute-start | bytes 393224 | tf_op jit(solution)/shard_map/ppermute | solution.py:252
  95.8 0.6 copy-start.4
  96.4 6.5 %collective-permute-start.8 = (bf16[512,128]{1,0:T(8,128)(2,1)S(1)}, bf16[512,128]{1,0:T(8,128)(2,1)S(1)}, u32[]{:S(2)}, u32[]{:S(2)}) collective-permute-start(bf16[512,128]{1,0:T(8,128)(2,1)S(1)} %attend.1), channel_id=1, source_target_pairs={{0,16},{2,18},{4,20},{6,22},{8,24},{10,26},{12,28},{14,30},{16,0},... | collective-permute-start | bytes 393224 | tf_op jit(solution)/shard_map/ppermute | solution.py:266
  104.1 22.6 %all-to-all-start.1 = ((bf16[4,2,512,128]{3,2,1,0:T(8,128)(2,1)}), bf16[4,2,512,128]{3,2,1,0:T(8,128)(2,1)S(1)}, u32[]{:S(2)}, u32[]{:S(2)}) async-start(bf16[4,2,512,128]{3,2,1,0:T(8,128)(2,1)} %broadcast_in_dim.4), calls=%async_computation.1 | async-start | bytes 2097152 | tf_op jit(solution)/shard_map/all_to_all | solution.py:261
  109.7 14.9 %collective-permute-start.11 = (bf16[2,256,256]{2,1,0:T(8,128)(2,1)}, bf16[2,256,256]{2,1,0:T(8,128)(2,1)S(1)}, u32[]{:S(2)}, u32[]{:S(2)}) collective-permute-start(bf16[2,256,256]{2,1,0:T(8,128)(2,1)} %get-tuple-element.40), channel_id=1, source_target_pairs={{0,16},{2,18},{4,20},{6,22},{8,24},{10,26},{12,28},{14,30},{16,0},... | collective-permute-start | bytes 786440 | tf_op jit(solution)/shard_map/ppermute | solution.py:255
  110.9 13.7 %collective-permute-start.10 = (bf16[2,512,128]{2,1,0:T(8,128)(2,1)S(1)}, bf16[2,512,128]{2,1,0:T(8,128)(2,1)S(1)}, u32[]{:S(2)}, u32[]{:S(2)}) collective-permute-start(bf16[2,512,128]{2,1,0:T(8,128)(2,1)S(1)} %pad_maximum_fusion.16), channel_id=1, source_target_pairs={{0,1},{1,0},{2,3},{3,2},{4,5},{5,4},{6,7},{7,6},{8,9},{9,8},{10,11... | collective-permute-start | bytes 786440 | tf_op jit(solution)/shard_map/ppermute | solution.py:267
  112.6 8.4 %collective-permute-start.9 = (s32[2,8,2048]{2,1,0:T(8,128)S(1)}, s32[2,8,2048]{2,1,0:T(8,128)S(1)}, u32[]{:S(2)}, u32[]{:S(2)}) collective-permute-start(s32[2,8,2048]{2,1,0:T(8,128)S(1)} %reshape.46.ids_ref), channel_id=1, source_target_pairs={{0,1},{1,0},{2,3},{3,2},{4,5},{5,4},{6,7},{7,6},{8,9},{9,8},{10,11... | collective-permute-start | bytes 393224 | tf_op jit(solution)/shard_map/ppermute | solution.py:276
  124.6 3.2 %copy-start.2 = (bf16[2,256,256]{2,1,0:T(8,128)(2,1)}, bf16[2,256,256]{2,1,0:T(8,128)(2,1)S(1)}, u32[]{:S(2)}) copy-start(bf16[2,256,256]{2,1,0:T(8,128)(2,1)S(1)} %collective-permute-done.11.refs_1_) | copy-start | bytes 786436
  127.8 24.7 %all-to-all-start.2 = ((bf16[4,2,512,128]{3,2,1,0:T(8,128)(2,1)}), bf16[4,2,512,128]{3,2,1,0:T(8,128)(2,1)S(1)}, u32[]{:S(2)}, u32[]{:S(2)}) async-start(bf16[4,2,512,128]{3,2,1,0:T(8,128)(2,1)} %broadcast_in_dim.5), calls=%async_computation.2 | async-start | bytes 2097152 | tf_op jit(solution)/shard_map/all_to_all | solution.py:261
  131.7 7.9 %collective-permute-start.12 = (bf16[8,512,128]{2,1,0:T(8,128)(2,1)S(1)}, bf16[8,512,128]{2,1,0:T(8,128)(2,1)S(1)}, u32[]{:S(2)}, u32[]{:S(2)}) collective-permute-start(bf16[8,512,128]{2,1,0:T(8,128)(2,1)S(1)} %bitcast.86), channel_id=1, source_target_pairs={{0,2},{2,0},{4,6},{6,4},{8,10},{10,8},{12,14},{14,12},{16,18},{18,... | collective-permute-start | bytes 3145736 | tf_op jit(solution)/shard_map/ppermute | solution.py:281
  131.8 18.5 %collective-permute-start.13 = (bf16[3,256,256]{2,1,0:T(8,128)(2,1)S(1)}, bf16[3,256,256]{2,1,0:T(8,128)(2,1)S(1)}, u32[]{:S(2)}, u32[]{:S(2)}) collective-permute-start(bf16[3,256,256]{2,1,0:T(8,128)(2,1)S(1)} %slice.26), channel_id=1, source_target_pairs={{0,16},{2,18},{4,20},{6,22},{8,24},{10,26},{12,28},{14,30},{16,0},... | collective-permute-start | bytes 1179656 | tf_op jit(solution)/shard_map/ppermute | solution.py:255
  150.3 0.7 copy-start
  152.5 8.9 %collective-permute-start.14 = (bf16[8,512,128]{2,1,0:T(8,128)(2,1)S(1)}, bf16[8,512,128]{2,1,0:T(8,128)(2,1)S(1)}, u32[]{:S(2)}, u32[]{:S(2)}) collective-permute-start(bf16[8,512,128]{2,1,0:T(8,128)(2,1)S(1)} %bitcast.88), channel_id=1, source_target_pairs={{0,2},{2,0},{4,6},{6,4},{8,10},{10,8},{12,14},{14,12},{16,18},{18,... | collective-permute-start | bytes 3145736 | tf_op jit(solution)/shard_map/ppermute | solution.py:289
  152.6 15.6 %collective-permute-start.15 = (bf16[2,256,256]{2,1,0:T(8,128)(2,1)}, bf16[2,256,256]{2,1,0:T(8,128)(2,1)S(1)}, u32[]{:S(2)}, u32[]{:S(2)}) collective-permute-start(bf16[2,256,256]{2,1,0:T(8,128)(2,1)} %get-tuple-element.39), channel_id=1, source_target_pairs={{0,16},{2,18},{4,20},{6,22},{8,24},{10,26},{12,28},{14,30},{16,0},... | collective-permute-start | bytes 786440 | tf_op jit(solution)/shard_map/ppermute | solution.py:255
  161.4 6.8 %copy-start.1 = (bf16[3,256,256]{2,1,0:T(8,128)(2,1)S(1)}, bf16[3,256,256]{2,1,0:T(8,128)(2,1)}, u32[]{:S(2)}) copy-start(bf16[3,256,256]{2,1,0:T(8,128)(2,1)} %copy-done) | copy-start | bytes 1179652
  161.4 6.8 %copy-start.3 = (bf16[2,256,256]{2,1,0:T(8,128)(2,1)S(1)}, bf16[2,256,256]{2,1,0:T(8,128)(2,1)}, u32[]{:S(2)}) copy-start(bf16[2,256,256]{2,1,0:T(8,128)(2,1)} %copy-done.2) | copy-start | bytes 786436
  161.4 6.8 %copy-start.5 = (bf16[1,256,256]{2,1,0:T(8,128)(2,1)S(1)}, bf16[1,256,256]{2,1,0:T(8,128)(2,1)}, u32[]{:S(2)}) copy-start(bf16[1,256,256]{2,1,0:T(8,128)(2,1)} %copy-done.4) | copy-start | bytes 393220
